TPU v7x, 128 devices: a whole 4x4x4 slice. The times are simulated.
128 devices in a mesh: row: 8 (over y, core), col: 16 (over x, z).
Axes of the slice: x: 4, y: 4, z: 4, core: 2. Of those that a mesh axis runs over, the one named last changes fastest.
Arguments:
- matrix: float32 [8, 2048, 4, 4096], P(None, 'row', None, 'col'), may hold values from -6 to 6
- diag_inverses: float32 [2, 256, 256], replicated, as said below
- band: int32 [64, 64], replicated, may hold values from 0 to 2, as said below
Outputs:
- trailing: float32 [8, 2048, 4, 4096], P(None, 'row', None, 'col')
- panel_second: float32 [8, 2048, 256], P(None, 'row')
Inputs may be any that keep to these rules, and one draw needn't show every extreme that they name: band is 0 on the diagonal tiles. `diag_inverses`: each is lower triangular with a positive diagonal.
All inputs are finite; a program needn't handle non-finite values.
Results may differ from a plain program's by a relative error of at most 0.0003.
Values sent between devices are 32-bit elements; how exact they have to be, the bound alone decides.
No kernel may reach another device: no remote copies, remote signals or barrier semaphores. Data moves between devices by JAX's collectives and lax.ppermute only.
A program may use at most 128 MiB of HBM per device.

v0:
```python
import jax
import jax.numpy as jnp
from jax import lax
from jax.sharding import PartitionSpec as P


def from_root(value, axis, source):
    kept = jnp.where(lax.axis_index(axis) == source, value, 0).astype(value.dtype)
    return lax.psum(kept, axis)


def solve_rows(tiles, inverse):
    return jnp.einsum(
        "xab,kb->xak",
        tiles,
        inverse,
        precision=lax.Precision.HIGHEST,
        preferred_element_type=jnp.float32,
    )


def panel_rows(tiles, inverse, root):
    return from_root(solve_rows(tiles, inverse), "col", root)


def panel_columns(rows_panel, col_index, rows_count, tc_count):
    width = rows_panel.shape[1]
    grouped = rows_panel.reshape(tc_count, rows_panel.shape[0] // tc_count, width, width)
    picked = lax.dynamic_index_in_dim(grouped, col_index // rows_count, 1, keepdims=False)
    return from_root(picked, "row", col_index % rows_count)


def contribution(rows_panel, cols_panel, classes):
    full = jnp.einsum(
        "xak,ybk->xayb",
        rows_panel,
        cols_panel,
        precision=lax.Precision.HIGHEST,
        preferred_element_type=jnp.float32,
    )
    low = jnp.einsum(
        "xak,ybk->xayb",
        rows_panel.astype(jnp.bfloat16),
        cols_panel.astype(jnp.bfloat16),
        preferred_element_type=jnp.float32,
    )
    return jnp.where(classes == 0, full, jnp.where(classes == 1, low, jnp.zeros_like(full)))


def body(matrix, diag_inverses, band):
    rows_count = lax.axis_size("row")
    cols_count = lax.axis_size("col")
    row_index = lax.axis_index("row")
    col_index = lax.axis_index("col")
    tr_count, width, tc_count, _ = matrix.shape
    grid = band.reshape(tr_count, rows_count, tc_count, cols_count)
    classes = lax.dynamic_slice(grid, (0, row_index, 0, col_index), (tr_count, 1, tc_count, 1))
    column = matrix[:, :, 0, :]
    rows_first = panel_rows(column, diag_inverses[0], 0)
    cols_first = panel_columns(rows_first, col_index, rows_count, tc_count)
    matrix = matrix - contribution(rows_first, cols_first, classes)
    rows_second = panel_rows(matrix[:, :, 0, :], diag_inverses[1], 1)
    cols_second = panel_columns(rows_second, col_index, rows_count, tc_count)
    matrix = matrix - contribution(rows_second, cols_second, classes)
    return (matrix, rows_second)


def solution(mesh):
    in_specs = (P(None, "row", None, "col"), P(), P())
    out_specs = (P(None, "row", None, "col"), P(None, "row", None))
    return jax.shard_map(body, mesh=mesh, in_specs=in_specs, out_specs=out_specs, check_vma=False)
```

profile of v0, /device:TPU:1, one launch (start us, length us, event | category | flops | bytes accessed | tf_op | source)
XLA Modules:
  0.0 376.6 jit_solution(16056566483336288917)
XLA Ops:
  7.2 1.6 slice-done
  8.8 0.1 copy-done.6
  8.9 3.2 fusion.6
  12.2 92.5 %all-reduce.5.cloned.1.call-done = f32[8,256,256]{2,1,0:T(8,128)} async-done(((f32[8,256,256]{2,1,0:T(8,128)}), f32[8,256,256]{2,1,0:T(8,128)}) %all-reduce.5.cloned.1.call-update) | async-done | bytes 2097168 | tf_op jit(solution)/shard_map/psum | solution.py:9
  104.7 2.4 fusion.9
  107.1 0.2 all-reduce.9.cloned.1.call-start
  107.4 0.1 reshape.19
  107.5 0.1 constant_dynamic-slice_fusion
  107.6 0.1 copy.17
  107.7 0.1 copy.6
  107.8 0.1 copy.9
  107.9 60.7 %all-reduce.7.cloned.1.call-done = f32[4,256,256]{2,1,0:T(8,128)} async-done(((f32[4,256,256]{2,1,0:T(8,128)}), f32[4,256,256]{2,1,0:T(8,128)}) %all-reduce.7.cloned.1.call-update) | async-done | bytes 1048592 | tf_op jit(solution)/shard_map/psum | solution.py:9
  168.6 8.2 %fusion.4 = f32[8,256,4,256]{3,1,2,0:T(8,128)S(1)} fusion(f32[8,256,256]{2,1,0:T(8,128)S(1)} %copy-done.3, f32[4,256,256]{2,1,0:T(8,128)} %all-reduce.7.cloned.1.call-done), kind=kOutput, calls=%fused_computation.8 | convolution fusion | flops 6442450944 | bytes 11534336 | tf_op jit(solution)/shard_map/xak,ybk->xayb/dot_general | solution.py:34
  176.8 5.9 %copy_subtract_fusion = f32[8,256,4,256]{3,1,2,0:T(8,128)S(1)} fusion(f32[8,256,4,256]{3,2,1,0:T(4,128)} %param.3, f32[8,256,4,256]{3,1,2,0:T(8,128)S(1)} %fusion.4, pred[8,4]{1,0:T(8,128)(4,1)S(1)} %copy.9, pred[8,4]{1,0:T(8,128)(4,1)S(1)} %copy.6, f32[8,256,256]{2,1,0:T(8,128)S(1)} %copy-done.3, f32[4,256,256]{2,1,0:T(8,128)S(1)} %copy-done.4), kind=kOutput, calls=%fused_computation | convolution fusion | flops 1080819712 | bytes 28311616 | tf_op jit(solution)/shard_map/xak,ybk->xayb/dot_general | solution.py:41
  182.8 3.4 copy-done
  186.1 3.2 fusion.7
  189.3 0.3 all-reduce.11.cloned.1.call-start
  189.6 90.5 %all-reduce.9.cloned.1.call-done = f32[8,256,256]{2,1,0:T(8,128)} async-done(((f32[8,256,256]{2,1,0:T(8,128)}), f32[8,256,256]{2,1,0:T(8,128)}) %all-reduce.9.cloned.1.call-update) | async-done | bytes 2097168 | tf_op jit(solution)/shard_map/psum | solution.py:9
  280.1 2.4 fusion.8
  282.6 61.2 %all-reduce.11.cloned.1.call-done = f32[4,256,256]{2,1,0:T(8,128)} async-done(((f32[4,256,256]{2,1,0:T(8,128)}), f32[4,256,256]{2,1,0:T(8,128)}) %all-reduce.11.cloned.1.call-update) | async-done | bytes 1048592 | tf_op jit(solution)/shard_map/psum | solution.py:9
  343.7 8.3 %fusion.2 = f32[8,256,4,256]{3,1,2,0:T(8,128)S(1)} fusion(f32[8,256,256]{2,1,0:T(8,128)S(1)} %copy-done.2, f32[4,256,256]{2,1,0:T(8,128)} %all-reduce.11.cloned.1.call-done), kind=kOutput, calls=%fused_computation.6 | convolution fusion | flops 6442450944 | bytes 11534336 | tf_op jit(solution)/shard_map/xak,ybk->xayb/dot_general | solution.py:34
  352.0 4.5 %select_subtract_fusion = f32[8,256,4,256]{3,1,2,0:T(8,128)} fusion(f32[8,256,4,256]{3,1,2,0:T(8,128)S(1)} %copy-done.1, f32[8,256,4,256]{3,1,2,0:T(8,128)S(1)} %fusion.2, pred[8,4]{1,0:T(8,128)(4,1)S(1)} %copy.9, pred[8,4]{1,0:T(8,128)(4,1)S(1)} %copy.6, f32[8,256,256]{2,1,0:T(8,128)S(1)} %copy-done.2, f32[4,256,256]{2,1,0:T(8,128)S(1)} %copy-done.5), kind=kOutput, calls=%fused_computation.1 | convolution fusion | flops 1080819712 | bytes 28311616 | tf_op jit(solution)/shard_map/xak,ybk->xayb/dot_general | solution.py:41
  356.6 12.2 %copy.12 = f32[8,256,4,256]{3,2,1,0:T(4,128)} copy(f32[8,256,4,256]{3,1,2,0:T(8,128)} %select_subtract_fusion) | data formatting | bytes 16777216
  368.7 1.3 copy.30
  (22 shorter events, 0.2 us)
Async XLA Ops:
  7.2 97.5 %all-reduce.5.cloned.1.call-start = ((), (), s32[]{:S(2)}) async-start(), calls=%async_computation | async-start | bytes 4194304 | tf_op jit(solution)/shard_map/psum | solution.py:9
  7.2 1.6 slice-start
  7.2 1.7 copy-start.6
  12.1 95.3 %copy-start.7 = (s32[64,64]{1,0:T(8,128)S(1)}, s32[64,64]{1,0:T(8,128)}, u32[]{:S(2)}) copy-start(s32[64,64]{1,0:T(8,128)} %param.5) | copy-start | bytes 49156
  12.1 156.5 %all-reduce.7.cloned.1.call-start = ((), (), s32[]{:S(2)}) async-start(), calls=%async_computation.1 | async-start | bytes 2097152 | tf_op jit(solution)/shard_map/psum | solution.py:9
  104.7 63.9 %copy-start.3 = (f32[8,256,256]{2,1,0:T(8,128)S(1)}, f32[8,256,256]{2,1,0:T(8,128)}, u32[]{:S(2)}) copy-start(f32[8,256,256]{2,1,0:T(8,128)} %all-reduce.5.cloned.1.call-done) | copy-start | bytes 6291460
  107.1 173.0 %all-reduce.9.cloned.1.call-start = ((), (), s32[]{:S(2)}) async-start(), calls=%async_computation.2 | async-start | bytes 4194304 | tf_op jit(solution)/shard_map/psum | solution.py:9
  168.6 8.2 %copy-start.4 = (f32[4,256,256]{2,1,0:T(8,128)S(1)}, f32[4,256,256]{2,1,0:T(8,128)}, u32[]{:S(2)}) copy-start(f32[4,256,256]{2,1,0:T(8,128)} %all-reduce.7.cloned.1.call-done) | copy-start | bytes 3145732
  182.7 3.4 copy-start
  189.3 154.4 %all-reduce.11.cloned.1.call-start = ((), (), s32[]{:S(2)}) async-start(), calls=%async_computation.3 | async-start | bytes 2097152 | tf_op jit(solution)/shard_map/psum | solution.py:9
  280.1 63.6 %copy-start.2 = (f32[8,256,256]{2,1,0:T(8,128)S(1)}, f32[8,256,256]{2,1,0:T(8,128)}, u32[]{:S(2)}) copy-start(f32[8,256,256]{2,1,0:T(8,128)} %all-reduce.9.cloned.1.call-done) | copy-start | bytes 6291460
  343.7 8.3 %copy-start.1 = (f32[8,256,4,256]{3,1,2,0:T(8,128)S(1)}, f32[8,256,4,256]{3,1,2,0:T(8,128)}, u32[]{:S(2)}) copy-start(f32[8,256,4,256]{3,1,2,0:T(8,128)} %copy-done) | copy-start | bytes 25165828
  343.7 8.3 %copy-start.5 = (f32[4,256,256]{2,1,0:T(8,128)S(1)}, f32[4,256,256]{2,1,0:T(8,128)}, u32[]{:S(2)}) copy-start(f32[4,256,256]{2,1,0:T(8,128)} %all-reduce.11.cloned.1.call-done) | copy-start | bytes 3145732
Sparse Core Ops, SparseCore 0:
  12.2 92.4 all-reduce.4
  107.7 60.8 all-reduce.6
  189.4 90.5 all-reduce.8
  282.9 60.8 all-reduce.10
where the time goes:
time: 378 us; the launch traced here: 377 us
  waiting for transfers between devices  305 us (81%)
  matrix products  33.2 us (9%)
  local copies, waits for them, and re-layouts  19.1 us (5%)
  between operations  13.9 us (4%)
  other arithmetic  4.88 us (1%)
    psum x4, waiting for transfers between devices, from_root(): return lax.psum(kept, axis)  305 us
    unnamed x19, local copies, waits for them, and re-layouts  17.1 us
    dot_general x2, matrix products, contribution(): jnp.einsum('xak,ybk->xayb', rows_panel, cols_panel, precision=lax.Precisi...  16.5 us
    dot_general x2, matrix products, contribution(): jnp.einsum('xak,ybk->xayb', rows_panel.astype(jnp.bfloat16), cols_panel.a...  10.5 us
  transfers between devices with their start and end apart: 4, of which 4 were waited for; matrix products, arithmetic and copies ran while one was open for 0% of the time, Pallas kernels for 0%

commit v1 on v0

v1 whole, which is shorter than its diff:
```python
import jax
import jax.numpy as jnp
from jax import lax
from jax.experimental import pallas as pl
from jax.experimental.pallas import tpu as pltpu
from jax.sharding import PartitionSpec as P

NB = 256
HALF = 128
TR = 8
TC = 4
N_ROW = 8
N_COL = 16
SIDE = 4
F32 = jnp.float32
BF16 = jnp.bfloat16


def split(value):
    high = value.astype(BF16)
    return high, (value - high.astype(F32)).astype(BF16)


def dot(a, b):
    return jnp.dot(a, b, preferred_element_type=F32)


def dot3(a, b_high, b_low):
    a_high, a_low = split(a)
    return dot(a_high, b_high) + (dot(a_high, b_low) + dot(a_low, b_high))


def shift_x(value, by):
    pairs = [(x * SIDE + z, (x + by) % SIDE * SIDE + z) for x in range(SIDE) for z in range(SIDE)]
    return lax.ppermute(value, "col", pairs)


def shift_z(value, by):
    pairs = [(x * SIDE + z, x * SIDE + (z + by) % SIDE) for x in range(SIDE) for z in range(SIDE)]
    return lax.ppermute(value, "col", pairs)


def shift_y(value, by):
    pairs = [(y * 2 + k, (y + by) % SIDE * 2 + k) for y in range(SIDE) for k in range(2)]
    return lax.ppermute(value, "row", pairs)


def swap_core(value):
    return lax.ppermute(value, "row", [(r, r ^ 1) for r in range(N_ROW)])


def to_columns(value, shift):
    pairs = []
    for r in range(N_ROW):
        for c in range(N_COL):
            k = (c - shift) % N_COL
            column = r + N_ROW * (k // 2 % 2)
            place = k // 4 * 2 + k % 2
            pairs.append((r * N_COL + c, place * N_COL + column))
    return lax.ppermute(value, ("row", "col"), pairs)


def gather_plane(own, first, second):
    got = {(0, 0): own}
    got[1, 0] = first(own, 1)
    got[3, 0] = first(own, -1)
    got[2, 0] = first(got[1, 0], 1)
    for a in (0, 1, 3, 2):
        got[a, 1] = second(got[a, 0], 1)
        got[a, 3] = second(got[a, 0], -1)
    for a in (0, 1, 3, 2):
        got[a, 2] = second(got[a, 1], 1) if a < 2 else second(got[a, 3], -1)
    return got


def gather_rows(own):
    got = {0: own}
    got[1] = shift_y(own, 1)
    got[3] = shift_y(own, -1)
    got[2] = shift_y(got[1], 1)
    return {(a, b): (swap_core(got[a]) if b else got[a]) for a in range(SIDE) for b in range(2)}


def pick_kernel(*refs):
    sources, first, second, sems = refs[:N_COL], refs[N_COL], refs[N_COL + 1], refs[N_COL + 2]
    me = lax.axis_index("col")
    for d in range(N_COL):

        @pl.when(me == d)
        def _():
            pltpu.make_async_copy(sources[d], first, sems.at[0]).start()

        @pl.when(lax.rem(me + N_COL - 1, N_COL) == d)
        def _():
            pltpu.make_async_copy(sources[d], second, sems.at[1]).start()

    pltpu.make_async_copy(sources[0], first, sems.at[0]).wait()
    pltpu.make_async_copy(sources[0], second, sems.at[1]).wait()


def pick(sources):
    shape = jax.ShapeDtypeStruct((HALF, NB), F32)
    return pl.pallas_call(
        pick_kernel,
        out_shape=(shape, shape),
        in_specs=[pl.BlockSpec(memory_space=pl.ANY)] * N_COL,
        out_specs=[pl.BlockSpec(memory_space=pl.ANY)] * 2,
        scratch_shapes=[pltpu.SemaphoreType.DMA((2,))],
        name="pick_pieces",
    )(*sources)


ROWS = TR * NB
COLS = TC * NB


def solve_kernel(*refs):
    n = SIDE * SIDE
    first, second, cols = refs[:n], refs[n : 2 * n], refs[2 * n : 2 * n + N_ROW]
    pivot, inv, row_class, col_class = refs[2 * n + N_ROW : 2 * n + N_ROW + 4]
    row_high, row_low, col_high, col_low, panel = refs[2 * n + N_ROW + 4 : 2 * n + N_ROW + 9]
    raw, = refs[2 * n + N_ROW + 9 :]
    r, c = lax.axis_index("row"), lax.axis_index("col")
    x, z = lax.div(c, SIDE), lax.rem(c, SIDE)
    y, core = lax.div(r, 2), lax.rem(r, 2)
    for a in range(SIDE):
        for b in range(SIDE):
            k = lax.rem(x + SIDE - b, SIDE) * SIDE + lax.rem(z + SIDE - a, SIDE)
            raw[0, pl.ds(pl.multiple_of(k * HALF, HALF), HALF), :] = first[a * SIDE + b][...]
            k = lax.rem(x + SIDE - a, SIDE) * SIDE + lax.rem(z + SIDE - b, SIDE)
            k = lax.rem(k + N_COL - 1, N_COL)
            raw[1, pl.ds(pl.multiple_of(k * HALF, HALF), HALF), :] = second[a * SIDE + b][...]
    for a in range(SIDE):
        for b in range(2):
            k = lax.rem(y + SIDE - a, SIDE) * 2 + lax.rem(core + b, 2)
            at = pl.ds(pl.multiple_of(ROWS + k * HALF, HALF), HALF)
            raw[0, at, :] = cols[a * 2 + b][0]
            raw[1, at, :] = cols[a * 2 + b][1]
    inv0 = split(inv[0].T)
    inv1 = split(inv[1].T)
    one_high, one_low = split(dot3(pivot[...], *inv0).T)

    def solve(at, code):
        p1 = dot3(raw[0, at, :], *inv0)
        high, low = split(p1)
        full = dot(high, one_high)
        rest = dot(high, one_low) + dot(low, one_high)
        used = jnp.where(code == 2, 0.0, full + jnp.where(code == 0, rest, 0.0))
        return high, low, dot3(raw[1, at, :] - used, *inv1)

    def rows(p, carry):
        at = pl.ds(pl.multiple_of(p * NB, NB), NB)
        high, low, p2 = solve(at, row_class[p, 0])
        panel[p] = p2
        row_high[p, :, :NB], row_low[p, :, :NB] = high, low
        row_high[p, :, NB:], row_low[p, :, NB:] = split(p2)
        return carry

    def columns(q, carry):
        at = pl.ds(pl.multiple_of(ROWS + q * NB, NB), NB)
        high, low, p2 = solve(at, col_class[q, 0])
        col_high[q, :NB, :] = high.astype(F32).T.astype(BF16)
        col_low[q, :NB, :] = low.astype(F32).T.astype(BF16)
        col_high[q, NB:, :], col_low[q, NB:, :] = split(p2.T)
        return carry

    lax.fori_loop(0, TC, columns, 0)
    lax.fori_loop(0, TR, rows, 0)


def solve_panels(first, second, cols, pivot, inv, row_class, col_class):
    vmem = pl.BlockSpec(memory_space=pltpu.VMEM)
    smem = pl.BlockSpec(memory_space=pltpu.SMEM)
    arrays = [*first, *second, *cols, pivot, inv]
    return pl.pallas_call(
        solve_kernel,
        out_shape=(
            jax.ShapeDtypeStruct((TR, NB, 2 * NB), BF16),
            jax.ShapeDtypeStruct((TR, NB, 2 * NB), BF16),
            jax.ShapeDtypeStruct((TC, 2 * NB, NB), BF16),
            jax.ShapeDtypeStruct((TC, 2 * NB, NB), BF16),
            jax.ShapeDtypeStruct((TR, NB, NB), F32),
        ),
        in_specs=[vmem] * len(arrays) + [smem] * 2,
        out_specs=[vmem] * 5,
        scratch_shapes=[pltpu.VMEM((2, ROWS + COLS, NB), F32)],
        compiler_params=pltpu.CompilerParams(vmem_limit_bytes=40 * 1024 * 1024),
        name="solve_panels",
    )(*arrays, row_class, col_class)


def update_kernel(classes, matrix, row_high, row_low, col_high, col_low, out):
    p = pl.program_id(0)
    for q in range(TC):
        code = classes[p, q]

        def write(acc):
            for b in range(2):
                at = pl.ds(b * TC + q, NB, stride=2 * TC)
                out[0, at, :] = matrix[0, at, :] - acc[:, b * HALF : (b + 1) * HALF]

        @pl.when(code == 0)
        def _():
            high = row_high[0]
            acc = dot(high, col_high[q]) + (dot(high, col_low[q]) + dot(row_low[0], col_high[q]))
            write(acc)

        @pl.when(code == 1)
        def _():
            write(dot(row_high[0], col_high[q]))

        @pl.when(code == 2)
        def _():
            for b in range(2):
                at = pl.ds(b * TC + q, NB, stride=2 * TC)
                out[0, at, :] = matrix[0, at, :]


def update(matrix, classes, row_high, row_low, col_high, col_low):
    lines = NB * TC * 2
    view = matrix.reshape(TR, NB, TC, 2, HALF).transpose(0, 1, 3, 2, 4).reshape(TR, lines, HALF)
    block = pl.BlockSpec((1, lines, HALF), lambda p: (p, 0, 0))
    rows = pl.BlockSpec((1, NB, 2 * NB), lambda p: (p, 0, 0))
    whole = pl.BlockSpec((TC, 2 * NB, NB), lambda p: (0, 0, 0))
    out = pl.pallas_call(
        update_kernel,
        grid=(TR,),
        out_shape=jax.ShapeDtypeStruct((TR, lines, HALF), F32),
        in_specs=[pl.BlockSpec(memory_space=pltpu.SMEM), block, rows, rows, whole, whole],
        out_specs=block,
        compiler_params=pltpu.CompilerParams(vmem_limit_bytes=40 * 1024 * 1024),
        name="update_tiles",
    )(classes, view, row_high, row_low, col_high, col_low)
    return out.reshape(TR, NB, 2, TC, HALF).transpose(0, 1, 3, 2, 4).reshape(TR, NB, TC, NB)


def body(matrix, diag_inverses, band):
    row, col = lax.axis_index("row"), lax.axis_index("col")
    grid = band.reshape(TR, N_ROW, TC, N_COL)
    classes = lax.dynamic_slice(grid, (0, row, 0, col), (TR, 1, TC, 1)).reshape(TR, TC)
    second_class = band[:, 1]
    row_class = lax.dynamic_slice(second_class.reshape(TR, N_ROW), (0, row), (TR, 1))
    col_class = lax.dynamic_slice(second_class.reshape(TC, N_COL), (0, col), (TC, 1))

    column = matrix[:, :, 0, :]
    pivot = lax.psum(jnp.where((row == 1) & (col == 0), column[0], 0.0), ("row", "col"))
    pieces = column.reshape(N_COL, HALF, NB)
    sent = [pieces[0]]
    for d in range(1, N_COL):
        sent.append(lax.ppermute(pieces[d], "col", [(0, d), (1, (d + 1) % N_COL)]))
    piece1, piece2 = pick(sent)
    own_cols = jnp.stack([to_columns(piece1, 0), to_columns(piece2, 1)])
    got1 = gather_plane(piece1, shift_z, shift_x)
    got2 = gather_plane(piece2, shift_x, shift_z)
    got_cols = gather_rows(own_cols)
    order = [(a, b) for a in range(SIDE) for b in range(SIDE)]
    first = [got1[k] for k in order]
    second = [got2[k] for k in order]
    cols = [got_cols[a, b] for a in range(SIDE) for b in range(2)]
    row_high, row_low, col_high, col_low, panel = solve_panels(
        first, second, cols, pivot, diag_inverses, row_class, col_class
    )
    return update(matrix, classes, row_high, row_low, col_high, col_low), panel


def solution(mesh):
    in_specs = (P(None, "row", None, "col"), P(), P())
    out_specs = (P(None, "row", None, "col"), P(None, "row", None))
    return jax.shard_map(body, mesh=mesh, in_specs=in_specs, out_specs=out_specs, check_vma=False)
```

time: 378 us -> 310 us (0.82)
  waiting for transfers between devices: 305 us -> 144 us
  starting transfers between devices: 0.56 us -> 85.5 us
  Pallas kernels: 0 us -> 36.2 us
  matrix products: 33.2 us -> 0 us
  local copies, waits for them, and re-layouts: 19.1 us -> 26.3 us
    psum x4 -> x1, waiting for transfers between devices: 305 us -> 128 us  [body(): lax.psum(jnp.where((row == 1) & (col == 0), column[0], 0.0), ('row', 'col'))]
    ppermute x0 -> x54, starting transfers between devices: none -> 85.5 us  [the longest x15 26.8 us: body(): sent.append(lax.ppermute(pieces[d], 'col', [(0, d), (1, (d + 1) % N_COL)]))]
    pallas_call x0 -> x3, Pallas kernels: none -> 36.2 us  [the longest x1 13.8 us: update(): pl.pallas_call(update_kernel, grid=(TR,), out_shape=jax.ShapeDtypeStruct(...]
    dot_general x6 -> x0, matrix products: 33.2 us -> none  [the longest x2 16.5 us: contribution(): jnp.einsum('xak,ybk->xayb', rows_panel, cols_panel, precision=lax.Precisi...]
    ppermute x0 -> x54, waiting for transfers between devices: none -> 16.5 us  [the longest x15 8.66 us: body(): sent.append(lax.ppermute(pieces[d], 'col', [(0, d), (1, (d + 1) % N_COL)]))]
    unnamed x19 -> x100, local copies, waits for them, and re-layouts: 17.1 us -> 17.5 us
  transfers between devices with their start and end apart: 4 -> 55, of which waited for: 4 -> 14; matrix products, arithmetic and copies ran while one was open for 0% -> 3% of each run, Pallas kernels for 0% -> 0%
where the time goes in v1:
time: 310 us; the launch traced here: 308 us
  waiting for transfers between devices  144 us (46%)
  starting transfers between devices  85.5 us (28%)
  Pallas kernels  36.2 us (12%)
  local copies, waits for them, and re-layouts  26.3 us (8%)
  between operations  14.7 us (5%)
    psum x1, waiting for transfers between devices, body(): lax.psum(jnp.where((row == 1) & (col == 0), column[0], 0.0), ('row', 'col'))  128 us
    ppermute x15, starting transfers between devices, body(): sent.append(lax.ppermute(pieces[d], 'col', [(0, d), (1, (d + 1) % N_COL)]))  26.8 us
    ppermute x15, starting transfers between devices, shift_z(): return lax.ppermute(value, 'col', pairs)  22.5 us
    ppermute x15, starting transfers between devices, shift_x(): return lax.ppermute(value, 'col', pairs)  19.3 us
    unnamed x100, local copies, waits for them, and re-layouts  17.5 us
    pallas_call x1, Pallas kernels, update(): pl.pallas_call(update_kernel, grid=(TR,), out_shape=jax.ShapeDtypeStruct(...  13.8 us
    pallas_call x1, Pallas kernels, solve_panels(): pl.pallas_call(solve_kernel, out_shape=(jax.ShapeDtypeStruct((TR, NB, 2 *...  13.3 us
    ppermute x4, starting transfers between devices, swap_core(): return lax.ppermute(value, 'row', [(r, r ^ 1) for r in range(N_ROW)])  9.59 us
  transfers between devices with their start and end apart: 55, of which 14 were waited for; matrix products, arithmetic and copies ran while one was open for 3% of the time, Pallas kernels for 0%

profile of v1, /device:TPU:1, one launch (start us, length us, event | category | flops | bytes accessed | tf_op | source)
XLA Modules:
  0.0 308.3 jit_solution(10381588345840641479)
XLA Ops:
  7.2 1.5 slice-done
  9.8 8.7 %collective-permute-start.14 = (f32[128,256]{1,0:T(8,128)S(1)}, f32[128,256]{1,0:T(8,128)S(1)}, u32[]{:S(2)}, u32[]{:S(2)}) collective-permute-start(f32[128,256]{1,0:T(8,128)S(1)} %get-tuple-element.16), channel_id=1, source_target_pairs={{0,15},{1,0},{16,31},{17,16},{32,47},{33,32},{48,63},{49,48},{64,7... | collective-permute-start | bytes 393224 | tf_op jit(solution)/shard_map/ppermute | solution.py:250
  41.1 1.5 collective-permute-done.4.refs_5_
  42.7 2.8 collective-permute-done.3.refs_4_
  46.3 9.1 %pick_pieces.1 = (f32[128,256]{1,0:T(8,128)}, f32[128,256]{1,0:T(8,128)}) custom-call(f32[128,256]{1,0:T(8,128)} %get-tuple-element.31.refs_0_, f32[128,256]{1,0:T(8,128)} %copy-done.48, f32[128,256]{1,0:T(8,128)} %copy-done.47, f32[128,256]{1,0:T(8,128)} %copy-done.46, f32[128,256]{1,0:T(8,128)} %copy-done.45, f32[128,256]{1,0:T(8,128)} %copy-done.44, ...), custom_call_target="tpu_custom_call" | custom-call | tf_op jit(solution)/shard_map/pick_pieces/pallas_call | solution.py:103
  55.3 5.3 %collective-permute-start.45 = (f32[128,256]{1,0:T(8,128)}, f32[128,256]{1,0:T(8,128)S(1)}, u32[]{:S(2)}, u32[]{:S(2)}) collective-permute-start(f32[128,256]{1,0:T(8,128)} %get-tuple-element.9.refs_0_), channel_id=1, source_target_pairs={{0,0},{1,16},{2,8},{3,24},{4,32},{5,48},{6,40},{7,56},{8,64},{9,80... | collective-permute-start | bytes 393224 | tf_op jit(solution)/shard_map/ppermute | solution.py:60
  62.2 4.8 %collective-permute-start.17 = (f32[128,256]{1,0:T(8,128)}, f32[128,256]{1,0:T(8,128)S(1)}, u32[]{:S(2)}, u32[]{:S(2)}) collective-permute-start(f32[128,256]{1,0:T(8,128)} %get-tuple-element.9.refs_0_), channel_id=1, source_target_pairs={{0,12},{1,13},{2,14},{3,15},{4,0},{5,1},{6,2},{7,3},{8,4},{9,5},{1... | collective-permute-start | bytes 393224 | tf_op jit(solution)/shard_map/ppermute | solution.py:35
  67.1 4.1 %collective-permute-start.41 = (f32[128,256]{1,0:T(8,128)}, f32[128,256]{1,0:T(8,128)S(1)}, u32[]{:S(2)}, u32[]{:S(2)}) collective-permute-start(f32[128,256]{1,0:T(8,128)} %get-tuple-element.10.refs_16_), channel_id=1, source_target_pairs={{0,12},{1,13},{2,14},{3,15},{4,0},{5,1},{6,2},{7,3},{8,4},{9,5},{1... | collective-permute-start | bytes 393224 | tf_op jit(solution)/shard_map/ppermute | solution.py:35
  72.2 2.0 collective-permute-done.15.refs_1_
  74.2 4.7 %collective-permute-start.30 = (f32[128,256]{1,0:T(8,128)}, f32[128,256]{1,0:T(8,128)S(1)}, u32[]{:S(2)}, u32[]{:S(2)}) collective-permute-start(f32[128,256]{1,0:T(8,128)} %get-tuple-element.10.refs_16_), channel_id=1, source_target_pairs={{0,1},{1,2},{2,3},{3,0},{4,5},{5,6},{6,7},{7,4},{8,9},{9,10},{10,1... | collective-permute-start | bytes 393224 | tf_op jit(solution)/shard_map/ppermute | solution.py:40
  78.9 3.8 %collective-permute-start.28 = (f32[128,256]{1,0:T(8,128)S(1)}, f32[128,256]{1,0:T(8,128)S(1)}, u32[]{:S(2)}, u32[]{:S(2)}) collective-permute-start(f32[128,256]{1,0:T(8,128)S(1)} %collective-permute-done.26.refs_12_), channel_id=1, source_target_pairs={{0,12},{1,13},{2,14},{3,15},{4,0},{5,1},{6,2},{7,3},{8,4},{9,5},{1... | collective-permute-start | bytes 393224 | tf_op jit(solution)/shard_map/ppermute | solution.py:35
  82.7 4.1 %collective-permute-start.22 = (f32[128,256]{1,0:T(8,128)S(1)}, f32[128,256]{1,0:T(8,128)S(1)}, u32[]{:S(2)}, u32[]{:S(2)}) collective-permute-start(f32[128,256]{1,0:T(8,128)S(1)} %collective-permute-done.18.refs_4_), channel_id=1, source_target_pairs={{0,1},{1,2},{2,3},{3,0},{4,5},{5,6},{6,7},{7,4},{8,9},{9,10},{10,1... | collective-permute-start | bytes 393224 | tf_op jit(solution)/shard_map/ppermute | solution.py:40
  89.0 2.0 collective-permute-start.43
  102.8 2.1 slice.76
  105.0 1.9 collective-permute-start.52
  106.9 6.9 %collective-permute-start.47 = (f32[2,128,256]{2,1,0:T(8,128)S(1)}, f32[2,128,256]{2,1,0:T(8,128)S(1)}, u32[]{:S(2)}, u32[]{:S(2)}) collective-permute-start(f32[2,128,256]{2,1,0:T(8,128)S(1)} %pad_maximum_fusion.refs_32_), channel_id=1, source_target_pairs={{0,16},{16,0},{32,48},{48,32},{64,80},{80,64},{96,112},{112,96},{1... | collective-permute-start | bytes 786440 | tf_op jit(solution)/shard_map/ppermute | solution.py:49
  115.3 1.7 fusion
  117.0 1.9 collective-permute-done.39.refs_27_
  121.0 1.5 reshape.27
  126.7 2.0 collective-permute-start.25
  128.8 2.4 collective-permute-start.40
  132.2 127.5 %all-reduce.2.cloned.1.call-done.refs_40_ = f32[256,256]{1,0:T(8,128)} async-done(((f32[256,256]{1,0:T(8,128)}), f32[256,256]{1,0:T(8,128)}) %all-reduce.2.cloned.1.call-update) | async-done | bytes 262160 | tf_op jit(solution)/shard_map/psum | solution.py:246
  274.3 13.3 %solve_panels.1 = (bf16[8,256,512]{2,1,0:T(8,128)(2,1)S(1)}, bf16[8,256,512]{2,1,0:T(8,128)(2,1)S(1)}, bf16[4,512,256]{2,1,0:T(8,128)(2,1)S(1)}, bf16[4,512,256]{2,1,0:T(8,128)(2,1)S(1)}, f32[8,256,256]{2,1,0:T(8,128)}) custom-call(f32[128,256]{1,0:T(8,128)S(1)} %copy-done.2, f32[128,256]{1,0:T(8,128)S(1)} %collective-permute-done.15.refs_1_, ...), custom_call_target="tpu_custom_call" | custom-call | tf_op jit(solution)/shard_map/solve_panels/pallas_call | solution.py:175
  287.7 13.8 %update_tiles.1 = f32[8,2048,128]{2,1,0:T(8,128)} custom-call(s32[8,4]{1,0:T(8,128)S(1)} %copy.14.classes, f32[8,2048,128]{2,1,0:T(8,128)} %bitcast.48, bf16[8,256,512]{2,1,0:T(8,128)(2,1)S(1)} %get-tuple-element.11.row_high, bf16[8,256,512]{2,1,0:T(8,128)(2,1)S(1)} %get-tuple-element.12.row_low, bf16[4,512,256]{2,1,0:T(8,128)(2,1)S(1)} %get-tuple-element.13.col_high, ...), custom_call_target="tpu_custom_call" | custom-call | tf_op jit(solution)/shard_map/update_tiles/pallas_call | solution.py:225
  (204 shorter events, 64.3 us)
Async XLA Ops:
  7.2 252.6 %all-reduce.2.cloned.1.call-start = ((), (), s32[]{:S(2)}) async-start(), calls=%async_computation | async-start | bytes 524288 | tf_op jit(solution)/shard_map/psum | solution.py:246
  9.8 13.9 %collective-permute-start.14 = (f32[128,256]{1,0:T(8,128)S(1)}, f32[128,256]{1,0:T(8,128)S(1)}, u32[]{:S(2)}, u32[]{:S(2)}) collective-permute-start(f32[128,256]{1,0:T(8,128)S(1)} %get-tuple-element.16), channel_id=1, source_target_pairs={{0,15},{1,0},{16,31},{17,16},{32,47},{33,32},{48,63},{49,48},{64,7... | collective-permute-start | bytes 393224 | tf_op jit(solution)/shard_map/ppermute | solution.py:250
  30.3 9.5 %collective-permute-start.5 = (f32[128,256]{1,0:T(8,128)S(1)}, f32[128,256]{1,0:T(8,128)S(1)}, u32[]{:S(2)}, u32[]{:S(2)}) collective-permute-start(f32[128,256]{1,0:T(8,128)S(1)} %get-tuple-element.25), channel_id=1, source_target_pairs={{0,6},{1,7},{16,22},{17,23},{32,38},{33,39},{48,54},{49,55},{64,70... | collective-permute-start | bytes 393224 | tf_op jit(solution)/shard_map/ppermute | solution.py:250
  31.7 11.0 %collective-permute-start.4 = (f32[128,256]{1,0:T(8,128)S(1)}, f32[128,256]{1,0:T(8,128)S(1)}, u32[]{:S(2)}, u32[]{:S(2)}) collective-permute-start(f32[128,256]{1,0:T(8,128)S(1)} %get-tuple-element.26), channel_id=1, source_target_pairs={{0,5},{1,6},{16,21},{17,22},{32,37},{33,38},{48,53},{49,54},{64,69... | collective-permute-start | bytes 393224 | tf_op jit(solution)/shard_map/ppermute | solution.py:250
  33.0 12.5 %collective-permute-start.3 = (f32[128,256]{1,0:T(8,128)S(1)}, f32[128,256]{1,0:T(8,128)S(1)}, u32[]{:S(2)}, u32[]{:S(2)}) collective-permute-start(f32[128,256]{1,0:T(8,128)S(1)} %get-tuple-element.27), channel_id=1, source_target_pairs={{0,4},{1,5},{16,20},{17,21},{32,36},{33,37},{48,52},{49,53},{64,68... | collective-permute-start | bytes 393224 | tf_op jit(solution)/shard_map/ppermute | solution.py:250
  34.3 11.2 %collective-permute-start.2 = (f32[128,256]{1,0:T(8,128)S(1)}, f32[128,256]{1,0:T(8,128)S(1)}, u32[]{:S(2)}, u32[]{:S(2)}) collective-permute-start(f32[128,256]{1,0:T(8,128)S(1)} %get-tuple-element.28), channel_id=1, source_target_pairs={{0,3},{1,4},{16,19},{17,20},{32,35},{33,36},{48,51},{49,52},{64,67... | collective-permute-start | bytes 393224 | tf_op jit(solution)/shard_map/ppermute | solution.py:250
  55.3 11.7 %collective-permute-start.45 = (f32[128,256]{1,0:T(8,128)}, f32[128,256]{1,0:T(8,128)S(1)}, u32[]{:S(2)}, u32[]{:S(2)}) collective-permute-start(f32[128,256]{1,0:T(8,128)} %get-tuple-element.9.refs_0_), channel_id=1, source_target_pairs={{0,0},{1,16},{2,8},{3,24},{4,32},{5,48},{6,40},{7,56},{8,64},{9,80... | collective-permute-start | bytes 393224 | tf_op jit(solution)/shard_map/ppermute | solution.py:60
  60.8 10.4 %collective-permute-start.18 = (f32[128,256]{1,0:T(8,128)}, f32[128,256]{1,0:T(8,128)S(1)}, u32[]{:S(2)}, u32[]{:S(2)}) collective-permute-start(f32[128,256]{1,0:T(8,128)} %get-tuple-element.9.refs_0_), channel_id=1, source_target_pairs={{0,1},{1,2},{2,3},{3,0},{4,5},{5,6},{6,7},{7,4},{8,9},{9,10},{10,1... | collective-permute-start | bytes 393224 | tf_op jit(solution)/shard_map/ppermute | solution.py:40
  67.1 11.9 %collective-permute-start.46 = (f32[128,256]{1,0:T(8,128)}, f32[128,256]{1,0:T(8,128)S(1)}, u32[]{:S(2)}, u32[]{:S(2)}) collective-permute-start(f32[128,256]{1,0:T(8,128)} %get-tuple-element.10.refs_16_), channel_id=1, source_target_pairs={{0,120},{1,0},{2,16},{3,8},{4,24},{5,32},{6,48},{7,40},{8,56},{9,6... | collective-permute-start | bytes 393224 | tf_op jit(solution)/shard_map/ppermute | solution.py:60
  67.1 15.6 %collective-permute-start.41 = (f32[128,256]{1,0:T(8,128)}, f32[128,256]{1,0:T(8,128)S(1)}, u32[]{:S(2)}, u32[]{:S(2)}) collective-permute-start(f32[128,256]{1,0:T(8,128)} %get-tuple-element.10.refs_16_), channel_id=1, source_target_pairs={{0,12},{1,13},{2,14},{3,15},{4,0},{5,1},{6,2},{7,3},{8,4},{9,5},{1... | collective-permute-start | bytes 393224 | tf_op jit(solution)/shard_map/ppermute | solution.py:35
  71.1 11.6 %collective-permute-start.33 = (f32[128,256]{1,0:T(8,128)}, f32[128,256]{1,0:T(8,128)S(1)}, u32[]{:S(2)}, u32[]{:S(2)}) collective-permute-start(f32[128,256]{1,0:T(8,128)} %get-tuple-element.10.refs_16_), channel_id=1, source_target_pairs={{0,4},{1,5},{2,6},{3,7},{4,8},{5,9},{6,10},{7,11},{8,12},{9,13},{1... | collective-permute-start | bytes 393224 | tf_op jit(solution)/shard_map/ppermute | solution.py:35
  71.2 15.7 %collective-permute-start.32 = (f32[128,256]{1,0:T(8,128)}, f32[128,256]{1,0:T(8,128)S(1)}, u32[]{:S(2)}, u32[]{:S(2)}) collective-permute-start(f32[128,256]{1,0:T(8,128)} %get-tuple-element.10.refs_16_), channel_id=1, source_target_pairs={{0,3},{1,0},{2,1},{3,2},{4,7},{5,4},{6,5},{7,6},{8,11},{9,8},{10,9... | collective-permute-start | bytes 393224 | tf_op jit(solution)/shard_map/ppermute | solution.py:40
  74.2 12.6 %collective-permute-start.30 = (f32[128,256]{1,0:T(8,128)}, f32[128,256]{1,0:T(8,128)S(1)}, u32[]{:S(2)}, u32[]{:S(2)}) collective-permute-start(f32[128,256]{1,0:T(8,128)} %get-tuple-element.10.refs_16_), channel_id=1, source_target_pairs={{0,1},{1,2},{2,3},{3,0},{4,5},{5,6},{6,7},{7,4},{8,9},{9,10},{10,1... | collective-permute-start | bytes 393224 | tf_op jit(solution)/shard_map/ppermute | solution.py:40
  78.9 9.4 %collective-permute-start.28 = (f32[128,256]{1,0:T(8,128)S(1)}, f32[128,256]{1,0:T(8,128)S(1)}, u32[]{:S(2)}, u32[]{:S(2)}) collective-permute-start(f32[128,256]{1,0:T(8,128)S(1)} %collective-permute-done.26.refs_12_), channel_id=1, source_target_pairs={{0,12},{1,13},{2,14},{3,15},{4,0},{5,1},{6,2},{7,3},{8,4},{9,5},{1... | collective-permute-start | bytes 393224 | tf_op jit(solution)/shard_map/ppermute | solution.py:35
  98.3 17.0 %collective-permute-start.48 = (f32[2,128,256]{2,1,0:T(8,128)S(1)}, f32[2,128,256]{2,1,0:T(8,128)S(1)}, u32[]{:S(2)}, u32[]{:S(2)}) collective-permute-start(f32[2,128,256]{2,1,0:T(8,128)S(1)} %pad_maximum_fusion.refs_32_), channel_id=1, source_target_pairs={{0,32},{16,48},{32,64},{48,80},{64,96},{80,112},{96,0},{112,16},{1... | collective-permute-start | bytes 786440 | tf_op jit(solution)/shard_map/ppermute | solution.py:45
  101.3 12.5 %collective-permute-start.20 = (f32[128,256]{1,0:T(8,128)S(1)}, f32[128,256]{1,0:T(8,128)}, u32[]{:S(2)}, u32[]{:S(2)}) collective-permute-start(f32[128,256]{1,0:T(8,128)S(1)} %collective-permute-done.19.refs_5_), channel_id=1, source_target_pairs={{0,4},{1,5},{2,6},{3,7},{4,8},{5,9},{6,10},{7,11},{8,12},{9,13},{1... | collective-permute-start | bytes 393224 | tf_op jit(solution)/shard_map/ppermute | solution.py:35
  102.2 12.6 %collective-permute-start.44 = (f32[128,256]{1,0:T(8,128)S(1)}, f32[128,256]{1,0:T(8,128)}, u32[]{:S(2)}, u32[]{:S(2)}) collective-permute-start(f32[128,256]{1,0:T(8,128)S(1)} %collective-permute-done.43.refs_31_), channel_id=1, source_target_pairs={{0,3},{1,0},{2,1},{3,2},{4,7},{5,4},{6,5},{7,6},{8,11},{9,8},{10,9... | collective-permute-start | bytes 393224 | tf_op jit(solution)/shard_map/ppermute | solution.py:40
  105.0 18.8 %collective-permute-start.52 = (f32[2,128,256]{2,1,0:T(8,128)S(1)}, f32[2,128,256]{2,1,0:T(8,128)S(1)}, u32[]{:S(2)}, u32[]{:S(2)}) collective-permute-start(f32[2,128,256]{2,1,0:T(8,128)S(1)} %pad_maximum_fusion.refs_32_), channel_id=1, source_target_pairs={{0,96},{16,112},{32,0},{48,16},{64,32},{80,48},{96,64},{112,80},{1... | collective-permute-start | bytes 786440 | tf_op jit(solution)/shard_map/ppermute | solution.py:45
  106.9 21.9 %collective-permute-start.47 = (f32[2,128,256]{2,1,0:T(8,128)S(1)}, f32[2,128,256]{2,1,0:T(8,128)S(1)}, u32[]{:S(2)}, u32[]{:S(2)}) collective-permute-start(f32[2,128,256]{2,1,0:T(8,128)S(1)} %pad_maximum_fusion.refs_32_), channel_id=1, source_target_pairs={{0,16},{16,0},{32,48},{48,32},{64,80},{80,64},{96,112},{112,96},{1... | collective-permute-start | bytes 786440 | tf_op jit(solution)/shard_map/ppermute | solution.py:49
  122.5 137.2 %collective-permute-start.49 = (f32[2,128,256]{2,1,0:T(8,128)S(1)}, f32[2,128,256]{2,1,0:T(8,128)S(1)}, u32[]{:S(2)}, u32[]{:S(2)}) collective-permute-start(f32[2,128,256]{2,1,0:T(8,128)S(1)} %collective-permute-done.48.refs_34_), channel_id=1, source_target_pairs={{0,16},{16,0},{32,48},{48,32},{64,80},{80,64},{96,112},{112,96},{1... | collective-permute-start | bytes 786440 | tf_op jit(solution)/shard_map/ppermute | solution.py:49
  123.8 136.0 %collective-permute-start.53 = (f32[2,128,256]{2,1,0:T(8,128)S(1)}, f32[2,128,256]{2,1,0:T(8,128)S(1)}, u32[]{:S(2)}, u32[]{:S(2)}) collective-permute-start(f32[2,128,256]{2,1,0:T(8,128)S(1)} %collective-permute-done.52.refs_38_), channel_id=1, source_target_pairs={{0,16},{16,0},{32,48},{48,32},{64,80},{80,64},{96,112},{112,96},{1... | collective-permute-start | bytes 786440 | tf_op jit(solution)/shard_map/ppermute | solution.py:49
  123.9 135.9 %collective-permute-start.51 = (f32[2,128,256]{2,1,0:T(8,128)S(1)}, f32[2,128,256]{2,1,0:T(8,128)S(1)}, u32[]{:S(2)}, u32[]{:S(2)}) collective-permute-start(f32[2,128,256]{2,1,0:T(8,128)S(1)} %collective-permute-done.50.refs_36_), channel_id=1, source_target_pairs={{0,16},{16,0},{32,48},{48,32},{64,80},{80,64},{96,112},{112,96},{1... | collective-permute-start | bytes 786440 | tf_op jit(solution)/shard_map/ppermute | solution.py:49
  126.7 133.0 %collective-permute-start.25 = (f32[128,256]{1,0:T(8,128)}, f32[128,256]{1,0:T(8,128)}, u32[]{:S(2)}, u32[]{:S(2)}) collective-permute-start(f32[128,256]{1,0:T(8,128)} %collective-permute-done.24.refs_11_), channel_id=1, source_target_pairs={{0,12},{1,13},{2,14},{3,15},{4,0},{5,1},{6,2},{7,3},{8,4},{9,5},{1... | collective-permute-start | bytes 393224 | tf_op jit(solution)/shard_map/ppermute | solution.py:35
  128.8 131.0 %collective-permute-start.40 = (f32[128,256]{1,0:T(8,128)}, f32[128,256]{1,0:T(8,128)}, u32[]{:S(2)}, u32[]{:S(2)}) collective-permute-start(f32[128,256]{1,0:T(8,128)} %collective-permute-done.39.refs_27_), channel_id=1, source_target_pairs={{0,3},{1,0},{2,1},{3,2},{4,7},{5,4},{6,5},{7,6},{8,11},{9,8},{10,9... | collective-permute-start | bytes 393224 | tf_op jit(solution)/shard_map/ppermute | solution.py:40
  (81 other events, 1285.3 us)
Sparse Core Ops, SparseCore 0:
  117.2 142.5 all-reduce.1

commit v2 on v0

v2 whole, which is shorter than its diff:
```python
import jax
import jax.numpy as jnp
from jax import lax
from jax.experimental import pallas as pl
from jax.experimental.pallas import tpu as pltpu
from jax.sharding import PartitionSpec as P

NB = 256
HALF = 128
TR = 8
TC = 4
N_ROW = 8
N_COL = 16
SIDE = 4
F32 = jnp.float32
BF16 = jnp.bfloat16


def split(value):
    high = value.astype(BF16)
    return high, (value - high.astype(F32)).astype(BF16)


def dot(a, b):
    return jnp.dot(a, b, preferred_element_type=F32)


def dot3(a, weights):
    high, low = split(a)
    return dot(jnp.concatenate([high, high, low], axis=1), weights)


def deep(value):
    high, low = split(value)
    return jnp.concatenate([high, low, high], axis=0)


def shift_x(value, by):
    pairs = [(x * SIDE + z, (x + by) % SIDE * SIDE + z) for x in range(SIDE) for z in range(SIDE)]
    return lax.ppermute(value, "col", pairs)


def shift_z(value, by):
    pairs = [(x * SIDE + z, x * SIDE + (z + by) % SIDE) for x in range(SIDE) for z in range(SIDE)]
    return lax.ppermute(value, "col", pairs)


def shift_y(value, by):
    pairs = [(y * 2 + k, (y + by) % SIDE * 2 + k) for y in range(SIDE) for k in range(2)]
    return lax.ppermute(value, "row", pairs)


def swap_core(value):
    return lax.ppermute(value, "row", [(r, r ^ 1) for r in range(N_ROW)])


def to_columns(value):
    pairs = []
    for r in range(N_ROW):
        for c in range(N_COL):
            column = r + N_ROW * (c // 2 % 2)
            place = c // 4 * 2 + c % 2
            pairs.append((r * N_COL + c, place * N_COL + column))
    return lax.ppermute(value, ("row", "col"), pairs)


def spread_pivot(tile, row):
    def along_y(by):
        return {1: (1 + 2 * by) % N_ROW}

    up = lax.ppermute(tile, "row", complete(along_y(1), N_ROW))
    down = lax.ppermute(tile, "row", complete(along_y(-1), N_ROW))
    far = lax.ppermute(tile, "row", complete(along_y(2), N_ROW))
    odd = jnp.where(row == 3, up, jnp.where(row == 7, down, jnp.where(row == 5, far, tile)))
    return jnp.where(row % 2 == 1, odd, swap_core(odd))


def complete(moves, size):
    pairs = dict(moves)
    for device in range(size):
        if device not in pairs and device not in pairs.values():
            pairs[device] = device
    free = [device for device in range(size) if device not in pairs.values()]
    for device in range(size):
        if device not in pairs:
            pairs[device] = free.pop(0)
    return sorted(pairs.items())


ORDER = (4, 12, 1, 8, 3, 5, 13, 9, 2, 7, 15, 11, 6, 14, 10)


def scatter_pieces(column, col):
    pieces = column.reshape(SIDE, SIDE, HALF, NB)
    turned = jnp.concatenate([pieces[:, 1:], pieces[:, :1]], axis=1)
    pieces = jnp.where(col == 1, turned, pieces).reshape(N_COL, HALF, NB)
    piece1 = piece2 = pieces[0]
    got = {}
    for d in ORDER:
        other = d // SIDE * SIDE + (d + 1) % SIDE
        got[d] = lax.ppermute(pieces[d], "col", complete({0: d, 1: other}, N_COL))
    for d in ORDER:
        other = d // SIDE * SIDE + (d + 1) % SIDE
        piece1 = jnp.where(col == d, got[d], piece1)
        piece2 = jnp.where(col == other, got[d], piece2)
    return piece1, piece2


RELAY = (0, 1, 3, 2)


def gather_all(piece1, piece2):
    barrier = lax.optimization_barrier
    z_near, z_back, x_near, x_back, own = barrier((
        shift_z(piece1, 1),
        shift_z(piece1, -1),
        shift_x(piece2, 1),
        shift_x(piece2, -1),
        to_columns(jnp.concatenate([piece1, piece2], axis=0)),
    ))
    z_far, x_far, y_near, y_back = barrier((
        shift_z(z_near, 1),
        shift_x(x_near, 1),
        shift_y(own, 1),
        shift_y(own, -1),
    ))
    line1 = jnp.stack([piece1, z_near, z_back, z_far])
    line2 = jnp.stack([piece2, x_near, x_back, x_far])
    near1, back1, near2, back2, y_far = barrier((
        shift_x(line1, 1),
        shift_x(line1, -1),
        shift_z(line2, 1),
        shift_z(line2, -1),
        shift_y(y_near, 1),
    ))
    cols = jnp.stack([own, y_near, y_back, y_far])
    far1, far2, other1, other2, other_cols = barrier((
        shift_x(near1[:2], 1),
        shift_x(back1[2:], -1),
        shift_z(near2[:2], 1),
        shift_z(back2[2:], -1),
        swap_core(cols),
    ))
    pieces1 = [line1, near1, back1, far1, far2]
    pieces2 = [line2, near2, back2, other1, other2]
    return pieces1, pieces2, [cols, other_cols]


def find_piece(pieces, x, z):
    line, near, back, far_near, far_back = pieces
    far = jnp.concatenate([far_near, far_back], axis=0)
    block = jnp.where(x == 0, line, jnp.where(x == 1, near, jnp.where(x == 3, back, far)))
    place = jnp.where(z < 2, z, 5 - z)
    return lax.dynamic_index_in_dim(block, place, 0, keepdims=False)


VMEM = pl.BlockSpec(memory_space=pltpu.VMEM)
SMEM = pl.BlockSpec(memory_space=pltpu.SMEM)
ANY = pl.BlockSpec(memory_space=pl.ANY)
LIMIT = pltpu.CompilerParams(vmem_limit_bytes=40 * 1024 * 1024)
ROWS = TR * NB
COLS = TC * NB


def rows_at(index, size):
    return pl.ds(pl.multiple_of(index * size, size), size)


def plane_copies(pieces, raw, sems, swapped):
    c = lax.axis_index("col")
    x, z = lax.div(c, SIDE), lax.rem(c, SIDE)
    line, near, back, far_near, far_back = pieces
    sources = [(line.at[i], RELAY[i], 0) for i in range(4)]
    sources += [(near.at[i], RELAY[i], 1) for i in range(4)]
    sources += [(back.at[i], RELAY[i], 3) for i in range(4)]
    sources += [(far_near.at[i], RELAY[i], 2) for i in range(2)]
    sources += [(far_back.at[i], RELAY[i + 2], 2) for i in range(2)]
    copies = []
    for n, (ref, first, second) in enumerate(sources):
        dx, dz = (first, second) if swapped else (second, first)
        k = lax.rem(x + SIDE - dx, SIDE) * SIDE + lax.rem(z + SIDE - dz, SIDE)
        copies.append(pltpu.make_async_copy(ref, raw.at[rows_at(k, HALF), :], sems.at[n]))
    return copies


def column_copies(pieces, raw, sems, at, size):
    r = lax.axis_index("row")
    y, core = lax.div(r, 2), lax.rem(r, 2)
    copies = []
    for b in range(2):
        for i in range(SIDE):
            k = lax.rem(y + SIDE - RELAY[i], SIDE) * 2 + lax.rem(core + b, 2)
            ref = pieces[b].at[i, pl.ds(at, size), :]
            copies.append(pltpu.make_async_copy(ref, raw.at[rows_at(k, size), :], sems.at[b * SIDE + i]))
    return copies


def first_kernel(*refs):
    pieces, cols, inv = refs[:5], refs[5:7], refs[7]
    row_high, row_low, col_high, col_low, turned_high, turned_low = refs[8:14]
    raw, raw_cols, sems, col_sems = refs[14:]
    copies = plane_copies(pieces, raw, sems, False)
    col_copies = column_copies(cols, raw_cols, col_sems, 0, HALF)
    for copy in col_copies + copies:
        copy.start()
    weights = deep(inv[0].T)
    for copy in col_copies:
        copy.wait()

    def column(q, carry):
        solved = dot3(raw_cols[rows_at(q, NB), :], weights)
        col_high[q], col_low[q] = split(solved)
        turned_high[q], turned_low[q] = split(solved.T)
        return carry

    def row(p, carry):
        solved = dot3(raw[rows_at(p, 2 * NB), :], weights).reshape(2, NB, NB)
        high, low = split(solved)
        row_high[pl.ds(2 * p, 2)] = high
        row_low[pl.ds(2 * p, 2)] = low
        return carry

    lax.fori_loop(0, TC, column, 0, unroll=2)
    for copy in copies:
        copy.wait()
    lax.fori_loop(0, TR // 2, row, 0)


def solve_first(pieces, cols, inv):
    shapes = [jax.ShapeDtypeStruct((n, NB, NB), BF16) for n in (TR, TR, TC, TC, TC, TC)]
    return pl.pallas_call(
        first_kernel,
        out_shape=shapes,
        in_specs=[ANY] * 7 + [VMEM],
        out_specs=[VMEM] * 6,
        scratch_shapes=[
            pltpu.VMEM((ROWS, NB), F32),
            pltpu.VMEM((COLS, NB), F32),
            pltpu.SemaphoreType.DMA((N_COL,)),
            pltpu.SemaphoreType.DMA((N_ROW,)),
        ],
        compiler_params=LIMIT,
        cost_estimate=pl.CostEstimate(flops=12 * 3 * 2 * NB**3, bytes_accessed=6 * 2**20, transcendentals=0),
        name="solve_first",
    )(*pieces, *cols, inv)


def second_kernel(*refs):
    pieces, cols, inv, pivot, row_class, col_class = refs[:5], refs[5:7], *refs[7:11]
    row_high1, row_low1, col_high1, col_low1 = refs[11:15]
    panel, row_high, row_low, turned_high, turned_low = refs[15:20]
    raw, raw_cols, sems, col_sems = refs[20:]
    copies = plane_copies(pieces, raw, sems, True)
    col_copies = column_copies(cols, raw_cols, col_sems, HALF, HALF)
    for copy in col_copies + copies:
        copy.start()
    weights0 = deep(inv[0].T)
    weights1 = deep(inv[1].T)
    one = dot3(pivot[...], weights0).T
    one_high, one_low = split(one)
    rest_weights = jnp.concatenate([one_low, one_high], axis=0)

    def used(high, low, code):
        full = dot(high, one_high)
        rest = dot(jnp.concatenate([high, low], axis=1), rest_weights)
        return jnp.where(code == 2, 0.0, full + jnp.where(code == 0, rest, 0.0))

    for copy in col_copies:
        copy.wait()

    def column(q, carry):
        tile = raw_cols[rows_at(q, NB), :] - used(col_high1[q], col_low1[q], col_class[q, 0])
        solved = dot3(tile, weights1)
        turned_high[q], turned_low[q] = split(solved.T)
        return carry

    def row(p, carry):
        tile = raw[rows_at(p, NB), :] - used(row_high1[p], row_low1[p], row_class[p, 0])
        solved = dot3(tile, weights1)
        panel[p] = solved
        row_high[p], row_low[p] = split(solved)
        return carry

    lax.fori_loop(0, TC, column, 0, unroll=2)
    for copy in copies:
        copy.wait()
    lax.fori_loop(0, TR, row, 0, unroll=2)


def solve_second(pieces, cols, inv, pivot, row_class, col_class, first):
    shapes = [jax.ShapeDtypeStruct((TR, NB, NB), F32)]
    shapes += [jax.ShapeDtypeStruct((n, NB, NB), BF16) for n in (TR, TR, TC, TC)]
    return pl.pallas_call(
        second_kernel,
        out_shape=shapes,
        in_specs=[ANY] * 7 + [VMEM] * 2 + [SMEM] * 2 + [VMEM] * 4,
        out_specs=[VMEM] * 5,
        scratch_shapes=[
            pltpu.VMEM((ROWS, NB), F32),
            pltpu.VMEM((COLS, NB), F32),
            pltpu.SemaphoreType.DMA((N_COL,)),
            pltpu.SemaphoreType.DMA((N_ROW,)),
        ],
        compiler_params=LIMIT,
        cost_estimate=pl.CostEstimate(flops=24 * 3 * 2 * NB**3, bytes_accessed=12 * 2**20, transcendentals=0),
        name="solve_second",
    )(*pieces, *cols, inv, pivot, row_class, col_class, *first)


STEP = 2


def update_kernel(classes, matrix, high1, low1, high2, low2, chigh1, clow1, chigh2, clow2, out, product):
    step = pl.program_id(0)
    size = STEP * NB
    high = jnp.concatenate([high1[...].reshape(size, NB), high2[...].reshape(size, NB)], axis=1)
    low = jnp.concatenate([low1[...].reshape(size, NB), low2[...].reshape(size, NB)], axis=1)
    both = jnp.concatenate([high, low], axis=1)
    for q in range(TC):
        col_high = jnp.concatenate([chigh1[q], chigh2[q]], axis=0)
        col_low = jnp.concatenate([clow1[q], clow2[q]], axis=0)
        full = dot(high, col_high)
        rest = dot(both, jnp.concatenate([col_low, col_high], axis=0))
        for p in range(STEP):
            code = classes[step * STEP + p, q]
            at = slice(p * NB, (p + 1) * NB)
            total = jnp.where(code == 2, 0.0, full[at] + jnp.where(code == 0, rest[at], 0.0))
            for b in range(2):
                product[b * TC + q, at, :] = total[:, b * HALF : (b + 1) * HALF]
    lines = 2 * TC
    part = 32
    for p in range(STEP):
        for a in range(0, NB, part):
            turned = product[:, p * NB + a : p * NB + a + part, :].transpose(1, 0, 2).reshape(part * lines, HALF)
            at = pl.ds(a * lines, part * lines)
            out[p, at, :] = matrix[p, at, :] - turned


def update(matrix, classes, rows, cols):
    lines = NB * TC * 2
    view = matrix.reshape(TR, NB, TC, 2, HALF).transpose(0, 1, 3, 2, 4).reshape(TR, lines, HALF)
    block = pl.BlockSpec((STEP, lines, HALF), lambda p: (p, 0, 0))
    row = pl.BlockSpec((STEP, NB, NB), lambda p: (p, 0, 0))
    whole = pl.BlockSpec((TC, NB, NB), lambda p: (0, 0, 0))
    out = pl.pallas_call(
        update_kernel,
        grid=(TR // STEP,),
        out_shape=jax.ShapeDtypeStruct((TR, lines, HALF), F32),
        in_specs=[SMEM, block] + [row] * 4 + [whole] * 4,
        out_specs=block,
        scratch_shapes=[pltpu.VMEM((2 * TC, STEP * NB, HALF), F32)],
        compiler_params=LIMIT,
        name="update_tiles",
    )(classes, view, *rows, *cols)
    return out.reshape(TR, NB, 2, TC, HALF).transpose(0, 1, 3, 2, 4).reshape(TR, NB, TC, NB)


def body(matrix, diag_inverses, band):
    row, col = lax.axis_index("row"), lax.axis_index("col")
    grid = band.reshape(TR, N_ROW, TC, N_COL)
    classes = lax.dynamic_slice(grid, (0, row, 0, col), (TR, 1, TC, 1)).reshape(TR, TC)
    second_class = band[:, 1]
    row_class = lax.dynamic_slice(second_class.reshape(TR, N_ROW), (0, row), (TR, 1))
    col_class = lax.dynamic_slice(second_class.reshape(TC, N_COL), (0, col), (TC, 1))

    piece1, piece2 = scatter_pieces(matrix[:, :, 0, :], col)
    pieces1, pieces2, cols = gather_all(piece1, piece2)
    x, z = col // SIDE, col % SIDE
    first_half = find_piece(pieces1, x, z)
    second_half = find_piece(pieces1, x, (z + SIDE - 1) % SIDE)
    pivot = spread_pivot(jnp.concatenate([first_half, second_half], axis=0), row)
    row_high1, row_low1, col_high1, col_low1, turned_high1, turned_low1 = solve_first(pieces1, cols, diag_inverses)
    first = (row_high1, row_low1, col_high1, col_low1)
    panel, row_high2, row_low2, turned_high2, turned_low2 = solve_second(
        pieces2, cols, diag_inverses, pivot, row_class, col_class, first
    )
    rows = (row_high1, row_low1, row_high2, row_low2)
    turned = (turned_high1, turned_low1, turned_high2, turned_low2)
    return update(matrix, classes, rows, turned), panel


def solution(mesh):
    in_specs = (P(None, "row", None, "col"), P(), P())
    out_specs = (P(None, "row", None, "col"), P(None, "row", None))
    return jax.shard_map(body, mesh=mesh, in_specs=in_specs, out_specs=out_specs, check_vma=False)
```

time: 378 us -> 180 us (0.48)
  waiting for transfers between devices: 305 us -> 42.8 us
  starting transfers between devices: 0.56 us -> 80.3 us
  matrix products: 33.2 us -> 0 us
  Pallas kernels: 0 us -> 30.4 us
  between operations: 13.9 us -> 1.18 us
  other arithmetic: 4.88 us -> 8.9 us
  local copies, waits for them, and re-layouts: 19.1 us -> 15.2 us
    psum x4 -> x0, waiting for transfers between devices: 305 us -> none  [from_root(): return lax.psum(kept, axis)]
    ppermute x0 -> x38, starting transfers between devices: none -> 80.3 us  [the longest x15 32.5 us: scatter_pieces(): got[d] = lax.ppermute(pieces[d], 'col', complete({0: d, 1: other}, N_COL))]
    ppermute x0 -> x38, waiting for transfers between devices: none -> 42.8 us  [the longest x7 15.5 us: shift_x(): return lax.ppermute(value, 'col', pairs)]
    dot_general x6 -> x0, matrix products: 33.2 us -> none  [the longest x2 16.5 us: contribution(): jnp.einsum('xak,ybk->xayb', rows_panel, cols_panel, precision=lax.Precisi...]
    pallas_call x0 -> x3, Pallas kernels: none -> 30.4 us  [the longest x1 12.2 us: update(): pl.pallas_call(update_kernel, grid=(TR // STEP,), out_shape=jax.ShapeDtyp...]
    unnamed x19 -> x28, local copies, waits for them, and re-layouts: 17.1 us -> 4.86 us
    slice x2 -> x9, local copies, waits for them, and re-layouts: 1.58 us -> 6.77 us  [the longest x2 1.59 us: body(): piece1, piece2 = scatter_pieces(matrix[:, :, 0, :], col)]
  transfers between devices with their start and end apart: 4 -> 38, of which waited for: 4 -> 15; matrix products, arithmetic and copies ran while one was open for 0% -> 4% of each run, Pallas kernels for 0% -> 4%
where the time goes in v2:
time: 180 us; the launch traced here: 179 us
  starting transfers between devices  80.3 us (45%)
  waiting for transfers between devices  42.8 us (24%)
  Pallas kernels  30.4 us (17%)
  local copies, waits for them, and re-layouts  15.2 us (8%)
  other arithmetic  8.9 us (5%)
    ppermute x15, starting transfers between devices, scatter_pieces(): got[d] = lax.ppermute(pieces[d], 'col', complete({0: d, 1: other}, N_COL))  32.5 us
    ppermute x1, starting transfers between devices, to_columns(): return lax.ppermute(value, ('row', 'col'), pairs)  21 us
    ppermute x7, waiting for transfers between devices, shift_x(): return lax.ppermute(value, 'col', pairs)  15.5 us
    pallas_call x1, Pallas kernels, update(): pl.pallas_call(update_kernel, grid=(TR // STEP,), out_shape=jax.ShapeDtyp...  12.2 us
    pallas_call x1, Pallas kernels, solve_second(): pl.pallas_call(second_kernel, out_shape=shapes, in_specs=[ANY] * 7 + [VME...  11.4 us
    ppermute x7, waiting for transfers between devices, shift_z(): return lax.ppermute(value, 'col', pairs)  10.6 us
    ppermute x15, waiting for transfers between devices, scatter_pieces(): got[d] = lax.ppermute(pieces[d], 'col', complete({0: d, 1: other}, N_COL))  8.24 us
    ppermute x3, waiting for transfers between devices, shift_y(): return lax.ppermute(value, 'row', pairs)  7.31 us
  transfers between devices with their start and end apart: 38, of which 15 were waited for; matrix products, arithmetic and copies ran while one was open for 4% of the time, Pallas kernels for 4%

profile of v2, /device:TPU:1, one launch (start us, length us, event | category | flops | bytes accessed | tf_op | source)
XLA Modules:
  0.0 178.8 jit_solution(2646389764754661155)
XLA Ops:
  7.4 3.9 %collective-permute-start.14 = (f32[128,256]{1,0:T(8,128)S(1)}, f32[128,256]{1,0:T(8,128)S(1)}, u32[]{:S(2)}, u32[]{:S(2)}) collective-permute-start(f32[128,256]{1,0:T(8,128)S(1)} %get-tuple-element.62), channel_id=1, source_target_pairs={{0,4},{1,5},{2,2},{3,3},{4,0},{5,1},{6,6},{7,7},{8,8},{9,9},{10,10... | collective-permute-start | bytes 393224 | tf_op jit(solution)/shard_map/ppermute | solution.py:101
  11.4 1.9 %collective-permute-start.13 = (f32[128,256]{1,0:T(8,128)S(1)}, f32[128,256]{1,0:T(8,128)S(1)}, u32[]{:S(2)}, u32[]{:S(2)}) collective-permute-start(f32[128,256]{1,0:T(8,128)S(1)} %get-tuple-element.63), channel_id=1, source_target_pairs={{0,12},{1,13},{2,2},{3,3},{4,4},{5,5},{6,6},{7,7},{8,8},{9,9},{10,... | collective-permute-start | bytes 393224 | tf_op jit(solution)/shard_map/ppermute | solution.py:101
  13.3 3.5 %collective-permute-start.12 = (f32[128,256]{1,0:T(8,128)S(1)}, f32[128,256]{1,0:T(8,128)S(1)}, u32[]{:S(2)}, u32[]{:S(2)}) collective-permute-start(f32[128,256]{1,0:T(8,128)S(1)} %get-tuple-element.64), channel_id=1, source_target_pairs={{0,1},{1,2},{2,0},{3,3},{4,4},{5,5},{6,6},{7,7},{8,8},{9,9},{10,10... | collective-permute-start | bytes 393224 | tf_op jit(solution)/shard_map/ppermute | solution.py:101
  22.7 1.9 %collective-permute-start.8 = (f32[128,256]{1,0:T(8,128)S(1)}, f32[128,256]{1,0:T(8,128)S(1)}, u32[]{:S(2)}, u32[]{:S(2)}) collective-permute-start(f32[128,256]{1,0:T(8,128)S(1)} %get-tuple-element.68), channel_id=1, source_target_pairs={{0,13},{1,14},{2,2},{3,3},{4,4},{5,5},{6,6},{7,7},{8,8},{9,9},{10,... | collective-permute-start | bytes 393224 | tf_op jit(solution)/shard_map/ppermute | solution.py:101
  40.2 2.3 %collective-permute-done.2 = f32[128,256]{1,0:T(8,128)S(1)} collective-permute-done((f32[128,256]{1,0:T(8,128)S(1)}, f32[128,256]{1,0:T(8,128)S(1)}, u32[]{:S(2)}, u32[]{:S(2)}) %collective-permute-start.2) | collective-permute-done | bytes 131104 | tf_op jit(solution)/shard_map/ppermute | solution.py:101
  42.4 3.9 %collective-permute-done.1 = f32[128,256]{1,0:T(8,128)S(1)} collective-permute-done((f32[128,256]{1,0:T(8,128)S(1)}, f32[128,256]{1,0:T(8,128)S(1)}, u32[]{:S(2)}, u32[]{:S(2)}) %collective-permute-start.1) | collective-permute-done | bytes 131104 | tf_op jit(solution)/shard_map/ppermute | solution.py:101
  46.3 2.0 %collective-permute-done = f32[128,256]{1,0:T(8,128)S(1)} collective-permute-done((f32[128,256]{1,0:T(8,128)S(1)}, f32[128,256]{1,0:T(8,128)S(1)}, u32[]{:S(2)}, u32[]{:S(2)}) %collective-permute-start) | collective-permute-done | bytes 131104 | tf_op jit(solution)/shard_map/ppermute | solution.py:101
  50.5 21.0 %collective-permute-start.19 = (f32[256,256]{1,0:T(8,128)S(1)}, f32[256,256]{1,0:T(8,128)S(1)}, u32[]{:S(2)}, u32[]{:S(2)}) collective-permute-start(f32[256,256]{1,0:T(8,128)S(1)} %pad_maximum_fusion.4), channel_id=1, source_target_pairs={{0,0},{1,16},{2,8},{3,24},{4,32},{5,48},{6,40},{7,56},{8,64},{9,80... | collective-permute-start | bytes 786440 | tf_op jit(solution)/shard_map/ppermute | solution.py:64
  73.1 4.2 %collective-permute-start.18 = (f32[128,256]{1,0:T(8,128)S(1)}, f32[128,256]{1,0:T(8,128)S(1)}, u32[]{:S(2)}, u32[]{:S(2)}) collective-permute-start(f32[128,256]{1,0:T(8,128)S(1)} %select_select_fusion.1), channel_id=1, source_target_pairs={{0,12},{1,13},{2,14},{3,15},{4,0},{5,1},{6,2},{7,3},{8,4},{9,5},{1... | collective-permute-start | bytes 393224 | tf_op jit(solution)/shard_map/ppermute | solution.py:40
  77.7 2.3 %collective-permute-done.18 = f32[128,256]{1,0:T(8,128)S(1)} collective-permute-done((f32[128,256]{1,0:T(8,128)S(1)}, f32[128,256]{1,0:T(8,128)S(1)}, u32[]{:S(2)}, u32[]{:S(2)}) %collective-permute-start.18) | collective-permute-done | bytes 131104 | tf_op jit(solution)/shard_map/ppermute | solution.py:40
  80.0 4.7 %collective-permute-done.17 = f32[128,256]{1,0:T(8,128)S(1)} collective-permute-done((f32[128,256]{1,0:T(8,128)S(1)}, f32[128,256]{1,0:T(8,128)S(1)}, u32[]{:S(2)}, u32[]{:S(2)}) %collective-permute-start.17) | collective-permute-done | bytes 131104 | tf_op jit(solution)/shard_map/ppermute | solution.py:40
  86.1 5.0 %collective-permute-done.20 = f32[128,256]{1,0:T(8,128)S(1)} collective-permute-done((f32[128,256]{1,0:T(8,128)S(1)}, f32[128,256]{1,0:T(8,128)S(1)}, u32[]{:S(2)}, u32[]{:S(2)}) %collective-permute-start.20) | collective-permute-done | bytes 131104 | tf_op jit(solution)/shard_map/ppermute | solution.py:45
  93.5 2.2 %collective-permute-start.27 = (f32[4,128,256]{2,1,0:T(8,128)S(1)}, f32[4,128,256]{2,1,0:T(8,128)S(1)}, u32[]{:S(2)}, u32[]{:S(2)}) collective-permute-start(f32[4,128,256]{2,1,0:T(8,128)S(1)} %pad_maximum_fusion.3.refs_0_), channel_id=1, source_target_pairs={{0,3},{1,0},{2,1},{3,2},{4,7},{5,4},{6,5},{7,6},{8,11},{9,8},{10,9... | collective-permute-start | bytes 1572872 | tf_op jit(solution)/shard_map/ppermute | solution.py:45
  96.6 6.6 %collective-permute-done.28 = f32[256,256]{1,0:T(8,128)S(1)} collective-permute-done((f32[256,256]{1,0:T(8,128)S(1)}, f32[256,256]{1,0:T(8,128)S(1)}, u32[]{:S(2)}, u32[]{:S(2)}) %collective-permute-start.28) | collective-permute-done | bytes 262176 | tf_op jit(solution)/shard_map/ppermute | solution.py:50
  104.3 2.2 %collective-permute-done.27.refs_2_ = f32[4,128,256]{2,1,0:T(8,128)S(1)} collective-permute-done((f32[4,128,256]{2,1,0:T(8,128)S(1)}, f32[4,128,256]{2,1,0:T(8,128)S(1)}, u32[]{:S(2)}, u32[]{:S(2)}) %collective-permute-start.27) | collective-permute-done | bytes 524320 | tf_op jit(solution)/shard_map/ppermute | solution.py:45
  106.5 3.0 %collective-permute-done.26.refs_1_ = f32[4,128,256]{2,1,0:T(8,128)S(1)} collective-permute-done((f32[4,128,256]{2,1,0:T(8,128)S(1)}, f32[4,128,256]{2,1,0:T(8,128)S(1)}, u32[]{:S(2)}, u32[]{:S(2)}) %collective-permute-start.26) | collective-permute-done | bytes 524320 | tf_op jit(solution)/shard_map/ppermute | solution.py:45
  117.3 5.3 %collective-permute-done.30.refs_4_ = f32[2,128,256]{2,1,0:T(8,128)S(1)} collective-permute-done((f32[2,128,256]{2,1,0:T(8,128)}, f32[2,128,256]{2,1,0:T(8,128)S(1)}, u32[]{:S(2)}, u32[]{:S(2)}) %collective-permute-start.30) | collective-permute-done | bytes 262176 | tf_op jit(solution)/shard_map/ppermute | solution.py:40
  122.6 2.2 %collective-permute-done.29.refs_3_ = f32[2,128,256]{2,1,0:T(8,128)S(1)} collective-permute-done((f32[2,128,256]{2,1,0:T(8,128)}, f32[2,128,256]{2,1,0:T(8,128)S(1)}, u32[]{:S(2)}, u32[]{:S(2)}) %collective-permute-start.29) | collective-permute-done | bytes 262176 | tf_op jit(solution)/shard_map/ppermute | solution.py:40
  129.3 4.6 %collective-permute-start.35 = (f32[256,256]{1,0:T(8,128)}, f32[256,256]{1,0:T(8,128)}, u32[]{:S(2)}, u32[]{:S(2)}) collective-permute-start(f32[256,256]{1,0:T(8,128)} %pad_maximum_fusion.5), channel_id=1, source_target_pairs={{0,0},{16,112},{32,32},{48,48},{64,64},{80,80},{96,96},{112,16},{1... | collective-permute-start | bytes 786440 | tf_op jit(solution)/shard_map/ppermute | solution.py:72
  133.9 2.4 %collective-permute-start.34 = (f32[256,256]{1,0:T(8,128)}, f32[256,256]{1,0:T(8,128)}, u32[]{:S(2)}, u32[]{:S(2)}) collective-permute-start(f32[256,256]{1,0:T(8,128)} %pad_maximum_fusion.5), channel_id=1, source_target_pairs={{0,0},{16,48},{32,32},{48,16},{64,64},{80,80},{96,96},{112,112},{1... | collective-permute-start | bytes 786440 | tf_op jit(solution)/shard_map/ppermute | solution.py:71
  143.0 2.1 %collective-permute-start.37 = (f32[256,256]{1,0:T(8,128)}, f32[256,256]{1,0:T(8,128)}, u32[]{:S(2)}, u32[]{:S(2)}) collective-permute-start(f32[256,256]{1,0:T(8,128)} %select_select_fusion), channel_id=1, source_target_pairs={{0,16},{16,0},{32,48},{48,32},{64,80},{80,64},{96,112},{112,96},{1... | collective-permute-start | bytes 786440 | tf_op jit(solution)/shard_map/ppermute | solution.py:54
  147.3 6.9 %solve_first.1 = (bf16[8,256,256]{2,1,0:T(8,128)(2,1)S(1)}, bf16[8,256,256]{2,1,0:T(8,128)(2,1)S(1)}, bf16[4,256,256]{2,1,0:T(8,128)(2,1)S(1)}, bf16[4,256,256]{...) custom-call(f32[4,128,256]{2,1,0:T(8,128)S(1)} %pad_maximum_fusion.2.refs_0_, ...), custom_call_target="tpu_custom_call" | custom-call | flops 1207959552 | bytes 6291456 | tf_op jit(solution)/shard_map/solve_first/pallas_call | solution.py:231
  155.2 11.4 %solve_second.1 = (f32[8,256,256]{2,1,0:T(8,128)}, bf16[8,256,256]{2,1,0:T(8,128)(2,1)S(1)}, bf16[8,256,256]{2,1,0:T(8,128)(2,1)S(1)}, bf16[4,256,256]{2,1,0:T(8,128)(2,1)S(1)}, bf16[4,256,256]{2,1,0:T(8,128)(2,1)S(1)}) custom-call(f32[4,128,256]{2,1,0:T(8,128)S(1)} %copy-done.3, f32[4,128,256]{2,1,0:T(8,128)S(1)} %copy-done.7, ...), custom_call_target="tpu_custom_call" | custom-call | flops 2415919104 | bytes 12582912 | tf_op jit(solution)/shard_map/solve_second/pallas_call | solution.py:293
  166.6 12.2 %update_tiles.1 = f32[8,2048,128]{2,1,0:T(8,128)} custom-call(s32[8,4]{1,0:T(8,128)S(1)} %copy.12.classes, f32[8,2048,128]{2,1,0:T(8,128)} %bitcast.70, bf16[8,256,256]{2,1,0:T(8,128)(2,1)S(1)} %get-tuple-element.49.refs_11_.high1, bf16[8,256,256]{2,1,0:T(8,128)(2,1)S(1)} %get-tuple-element.50.refs_12_.low1, ...), custom_call_target="tpu_custom_call" | custom-call | tf_op jit(solution)/shard_map/update_tiles/pallas_call | solution.py:345
  (113 shorter events, 59.8 us)
Async XLA Ops:
  7.4 13.3 %collective-permute-start.14 = (f32[128,256]{1,0:T(8,128)S(1)}, f32[128,256]{1,0:T(8,128)S(1)}, u32[]{:S(2)}, u32[]{:S(2)}) collective-permute-start(f32[128,256]{1,0:T(8,128)S(1)} %get-tuple-element.62), channel_id=1, source_target_pairs={{0,4},{1,5},{2,2},{3,3},{4,0},{5,1},{6,6},{7,7},{8,8},{9,9},{10,10... | collective-permute-start | bytes 393224 | tf_op jit(solution)/shard_map/ppermute | solution.py:101
  11.4 11.3 %collective-permute-start.13 = (f32[128,256]{1,0:T(8,128)S(1)}, f32[128,256]{1,0:T(8,128)S(1)}, u32[]{:S(2)}, u32[]{:S(2)}) collective-permute-start(f32[128,256]{1,0:T(8,128)S(1)} %get-tuple-element.63), channel_id=1, source_target_pairs={{0,12},{1,13},{2,2},{3,3},{4,4},{5,5},{6,6},{7,7},{8,8},{9,9},{10,... | collective-permute-start | bytes 393224 | tf_op jit(solution)/shard_map/ppermute | solution.py:101
  13.3 11.3 %collective-permute-start.12 = (f32[128,256]{1,0:T(8,128)S(1)}, f32[128,256]{1,0:T(8,128)S(1)}, u32[]{:S(2)}, u32[]{:S(2)}) collective-permute-start(f32[128,256]{1,0:T(8,128)S(1)} %get-tuple-element.64), channel_id=1, source_target_pairs={{0,1},{1,2},{2,0},{3,3},{4,4},{5,5},{6,6},{7,7},{8,8},{9,9},{10,10... | collective-permute-start | bytes 393224 | tf_op jit(solution)/shard_map/ppermute | solution.py:101
  16.9 9.7 %collective-permute-start.11 = (f32[128,256]{1,0:T(8,128)S(1)}, f32[128,256]{1,0:T(8,128)S(1)}, u32[]{:S(2)}, u32[]{:S(2)}) collective-permute-start(f32[128,256]{1,0:T(8,128)S(1)} %get-tuple-element.65), channel_id=1, source_target_pairs={{0,8},{1,9},{2,2},{3,3},{4,4},{5,5},{6,6},{7,7},{8,0},{9,1},{10,10... | collective-permute-start | bytes 393224 | tf_op jit(solution)/shard_map/ppermute | solution.py:101
  18.8 9.7 %collective-permute-start.10 = (f32[128,256]{1,0:T(8,128)S(1)}, f32[128,256]{1,0:T(8,128)S(1)}, u32[]{:S(2)}, u32[]{:S(2)}) collective-permute-start(f32[128,256]{1,0:T(8,128)S(1)} %get-tuple-element.66), channel_id=1, source_target_pairs={{0,3},{1,0},{2,2},{3,1},{4,4},{5,5},{6,6},{7,7},{8,8},{9,9},{10,10... | collective-permute-start | bytes 393224 | tf_op jit(solution)/shard_map/ppermute | solution.py:101
  20.7 9.7 %collective-permute-start.9 = (f32[128,256]{1,0:T(8,128)S(1)}, f32[128,256]{1,0:T(8,128)S(1)}, u32[]{:S(2)}, u32[]{:S(2)}) collective-permute-start(f32[128,256]{1,0:T(8,128)S(1)} %get-tuple-element.67), channel_id=1, source_target_pairs={{0,5},{1,6},{2,2},{3,3},{4,4},{5,0},{6,1},{7,7},{8,8},{9,9},{10,10... | collective-permute-start | bytes 393224 | tf_op jit(solution)/shard_map/ppermute | solution.py:101
  22.7 9.7 %collective-permute-start.8 = (f32[128,256]{1,0:T(8,128)S(1)}, f32[128,256]{1,0:T(8,128)S(1)}, u32[]{:S(2)}, u32[]{:S(2)}) collective-permute-start(f32[128,256]{1,0:T(8,128)S(1)} %get-tuple-element.68), channel_id=1, source_target_pairs={{0,13},{1,14},{2,2},{3,3},{4,4},{5,5},{6,6},{7,7},{8,8},{9,9},{10,... | collective-permute-start | bytes 393224 | tf_op jit(solution)/shard_map/ppermute | solution.py:101
  24.6 9.7 %collective-permute-start.7 = (f32[128,256]{1,0:T(8,128)S(1)}, f32[128,256]{1,0:T(8,128)S(1)}, u32[]{:S(2)}, u32[]{:S(2)}) collective-permute-start(f32[128,256]{1,0:T(8,128)S(1)} %get-tuple-element.69), channel_id=1, source_target_pairs={{0,9},{1,10},{2,2},{3,3},{4,4},{5,5},{6,6},{7,7},{8,8},{9,0},{10,1... | collective-permute-start | bytes 393224 | tf_op jit(solution)/shard_map/ppermute | solution.py:101
  26.5 9.7 %collective-permute-start.6 = (f32[128,256]{1,0:T(8,128)S(1)}, f32[128,256]{1,0:T(8,128)S(1)}, u32[]{:S(2)}, u32[]{:S(2)}) collective-permute-start(f32[128,256]{1,0:T(8,128)S(1)} %get-tuple-element.70), channel_id=1, source_target_pairs={{0,2},{1,3},{2,0},{3,1},{4,4},{5,5},{6,6},{7,7},{8,8},{9,9},{10,10... | collective-permute-start | bytes 393224 | tf_op jit(solution)/shard_map/ppermute | solution.py:101
  28.5 9.7 %collective-permute-start.5 = (f32[128,256]{1,0:T(8,128)S(1)}, f32[128,256]{1,0:T(8,128)S(1)}, u32[]{:S(2)}, u32[]{:S(2)}) collective-permute-start(f32[128,256]{1,0:T(8,128)S(1)} %get-tuple-element.71), channel_id=1, source_target_pairs={{0,7},{1,4},{2,2},{3,3},{4,0},{5,5},{6,6},{7,1},{8,8},{9,9},{10,10... | collective-permute-start | bytes 393224 | tf_op jit(solution)/shard_map/ppermute | solution.py:101
  30.4 9.7 %collective-permute-start.4 = (f32[128,256]{1,0:T(8,128)S(1)}, f32[128,256]{1,0:T(8,128)S(1)}, u32[]{:S(2)}, u32[]{:S(2)}) collective-permute-start(f32[128,256]{1,0:T(8,128)S(1)} %get-tuple-element.72), channel_id=1, source_target_pairs={{0,15},{1,12},{2,2},{3,3},{4,4},{5,5},{6,6},{7,7},{8,8},{9,9},{10,... | collective-permute-start | bytes 393224 | tf_op jit(solution)/shard_map/ppermute | solution.py:101
  36.2 10.1 %collective-permute-start.1 = (f32[128,256]{1,0:T(8,128)S(1)}, f32[128,256]{1,0:T(8,128)S(1)}, u32[]{:S(2)}, u32[]{:S(2)}) collective-permute-start(f32[128,256]{1,0:T(8,128)S(1)} %get-tuple-element.75), channel_id=1, source_target_pairs={{0,14},{1,15},{2,2},{3,3},{4,4},{5,5},{6,6},{7,7},{8,8},{9,9},{10,... | collective-permute-start | bytes 393224 | tf_op jit(solution)/shard_map/ppermute | solution.py:101
  38.2 10.2 %collective-permute-start = (f32[128,256]{1,0:T(8,128)S(1)}, f32[128,256]{1,0:T(8,128)S(1)}, u32[]{:S(2)}, u32[]{:S(2)}) collective-permute-start(f32[128,256]{1,0:T(8,128)S(1)} %get-tuple-element.76), channel_id=1, source_target_pairs={{0,10},{1,11},{2,2},{3,3},{4,4},{5,5},{6,6},{7,7},{8,8},{9,9},{10,... | collective-permute-start | bytes 393224 | tf_op jit(solution)/shard_map/ppermute | solution.py:101
  50.5 34.1 %collective-permute-start.19 = (f32[256,256]{1,0:T(8,128)S(1)}, f32[256,256]{1,0:T(8,128)S(1)}, u32[]{:S(2)}, u32[]{:S(2)}) collective-permute-start(f32[256,256]{1,0:T(8,128)S(1)} %pad_maximum_fusion.4), channel_id=1, source_target_pairs={{0,0},{1,16},{2,8},{3,24},{4,32},{5,48},{6,40},{7,56},{8,64},{9,80... | collective-permute-start | bytes 786440 | tf_op jit(solution)/shard_map/ppermute | solution.py:64
  91.9 11.3 %collective-permute-start.25 = (f32[4,128,256]{2,1,0:T(8,128)S(1)}, f32[4,128,256]{2,1,0:T(8,128)S(1)}, u32[]{:S(2)}, u32[]{:S(2)}) collective-permute-start(f32[4,128,256]{2,1,0:T(8,128)S(1)} %pad_maximum_fusion.2.refs_0_), channel_id=1, source_target_pairs={{0,12},{1,13},{2,14},{3,15},{4,0},{5,1},{6,2},{7,3},{8,4},{9,5},{1... | collective-permute-start | bytes 1572872 | tf_op jit(solution)/shard_map/ppermute | solution.py:40
  92.0 12.3 %collective-permute-start.24 = (f32[4,128,256]{2,1,0:T(8,128)S(1)}, f32[4,128,256]{2,1,0:T(8,128)S(1)}, u32[]{:S(2)}, u32[]{:S(2)}) collective-permute-start(f32[4,128,256]{2,1,0:T(8,128)S(1)} %pad_maximum_fusion.2.refs_0_), channel_id=1, source_target_pairs={{0,4},{1,5},{2,6},{3,7},{4,8},{5,9},{6,10},{7,11},{8,12},{9,13},{1... | collective-permute-start | bytes 1572872 | tf_op jit(solution)/shard_map/ppermute | solution.py:40
  93.5 13.0 %collective-permute-start.27 = (f32[4,128,256]{2,1,0:T(8,128)S(1)}, f32[4,128,256]{2,1,0:T(8,128)S(1)}, u32[]{:S(2)}, u32[]{:S(2)}) collective-permute-start(f32[4,128,256]{2,1,0:T(8,128)S(1)} %pad_maximum_fusion.3.refs_0_), channel_id=1, source_target_pairs={{0,3},{1,0},{2,1},{3,2},{4,7},{5,4},{6,5},{7,6},{8,11},{9,8},{10,9... | collective-permute-start | bytes 1572872 | tf_op jit(solution)/shard_map/ppermute | solution.py:45
  95.7 13.8 %collective-permute-start.26 = (f32[4,128,256]{2,1,0:T(8,128)S(1)}, f32[4,128,256]{2,1,0:T(8,128)S(1)}, u32[]{:S(2)}, u32[]{:S(2)}) collective-permute-start(f32[4,128,256]{2,1,0:T(8,128)S(1)} %pad_maximum_fusion.3.refs_0_), channel_id=1, source_target_pairs={{0,1},{1,2},{2,3},{3,0},{4,5},{5,6},{6,7},{7,4},{8,9},{9,10},{10,1... | collective-permute-start | bytes 1572872 | tf_op jit(solution)/shard_map/ppermute | solution.py:45
  109.6 15.2 %collective-permute-start.33 = (f32[4,256,256]{2,1,0:T(8,128)S(1)}, f32[4,256,256]{2,1,0:T(8,128)}, u32[]{:S(2)}, u32[]{:S(2)}) collective-permute-start(f32[4,256,256]{2,1,0:T(8,128)S(1)} %pad_maximum_fusion.1.refs_5_), channel_id=1, source_target_pairs={{0,16},{16,0},{32,48},{48,32},{64,80},{80,64},{96,112},{112,96},{1... | collective-permute-start | bytes 3145736 | tf_op jit(solution)/shard_map/ppermute | solution.py:54
  115.7 9.1 %collective-permute-start.29 = (f32[2,128,256]{2,1,0:T(8,128)}, f32[2,128,256]{2,1,0:T(8,128)S(1)}, u32[]{:S(2)}, u32[]{:S(2)}) collective-permute-start(f32[2,128,256]{2,1,0:T(8,128)} %slice.91), channel_id=1, source_target_pairs={{0,4},{1,5},{2,6},{3,7},{4,8},{5,9},{6,10},{7,11},{8,12},{9,13},{1... | collective-permute-start | bytes 786440 | tf_op jit(solution)/shard_map/ppermute | solution.py:40
  115.8 9.0 %collective-permute-start.32 = (f32[2,128,256]{2,1,0:T(8,128)}, f32[2,128,256]{2,1,0:T(8,128)S(1)}, u32[]{:S(2)}, u32[]{:S(2)}) collective-permute-start(f32[2,128,256]{2,1,0:T(8,128)} %slice.94), channel_id=1, source_target_pairs={{0,3},{1,0},{2,1},{3,2},{4,7},{5,4},{6,5},{7,6},{8,11},{9,8},{10,9... | collective-permute-start | bytes 786440 | tf_op jit(solution)/shard_map/ppermute | solution.py:45
  127.4 12.9 %collective-permute-start.36 = (f32[256,256]{1,0:T(8,128)}, f32[256,256]{1,0:T(8,128)}, u32[]{:S(2)}, u32[]{:S(2)}) collective-permute-start(f32[256,256]{1,0:T(8,128)} %pad_maximum_fusion.5), channel_id=1, source_target_pairs={{0,0},{16,80},{32,32},{48,48},{64,64},{80,16},{96,96},{112,112},{1... | collective-permute-start | bytes 786440 | tf_op jit(solution)/shard_map/ppermute | solution.py:73
  129.3 11.0 %collective-permute-start.35 = (f32[256,256]{1,0:T(8,128)}, f32[256,256]{1,0:T(8,128)}, u32[]{:S(2)}, u32[]{:S(2)}) collective-permute-start(f32[256,256]{1,0:T(8,128)} %pad_maximum_fusion.5), channel_id=1, source_target_pairs={{0,0},{16,112},{32,32},{48,48},{64,64},{80,80},{96,96},{112,16},{1... | collective-permute-start | bytes 786440 | tf_op jit(solution)/shard_map/ppermute | solution.py:72
  143.0 11.1 %collective-permute-start.37 = (f32[256,256]{1,0:T(8,128)}, f32[256,256]{1,0:T(8,128)}, u32[]{:S(2)}, u32[]{:S(2)}) collective-permute-start(f32[256,256]{1,0:T(8,128)} %select_select_fusion), channel_id=1, source_target_pairs={{0,16},{16,0},{32,48},{48,32},{64,80},{80,64},{96,112},{112,96},{1... | collective-permute-start | bytes 786440 | tf_op jit(solution)/shard_map/ppermute | solution.py:54
  (28 other events, 229.3 us)

commit v3 on v2

v3 whole, which is shorter than its diff:
```python
import functools

import jax
import jax.numpy as jnp
from jax import lax
from jax.experimental import pallas as pl
from jax.experimental.pallas import tpu as pltpu
from jax.sharding import PartitionSpec as P

NB = 256
HALF = 128
TR = 8
TC = 4
N_ROW = 8
N_COL = 16
SIDE = 4
F32 = jnp.float32
BF16 = jnp.bfloat16


def split(value):
    high = value.astype(BF16)
    return high, (value - high.astype(F32)).astype(BF16)


def dot(a, b):
    return jnp.dot(a, b, preferred_element_type=F32)


def dot3(a, weights):
    high, low = split(a)
    return dot(jnp.concatenate([high, high, low], axis=1), weights)


def deep(value):
    high, low = split(value)
    return jnp.concatenate([high, low, high], axis=0)


def shift_x(value, by):
    pairs = [(x * SIDE + z, (x + by) % SIDE * SIDE + z) for x in range(SIDE) for z in range(SIDE)]
    return lax.ppermute(value, "col", pairs)


def shift_z(value, by):
    pairs = [(x * SIDE + z, x * SIDE + (z + by) % SIDE) for x in range(SIDE) for z in range(SIDE)]
    return lax.ppermute(value, "col", pairs)


def shift_y(value, by):
    pairs = [(y * 2 + k, (y + by) % SIDE * 2 + k) for y in range(SIDE) for k in range(2)]
    return lax.ppermute(value, "row", pairs)


def swap_core(value):
    return lax.ppermute(value, "row", [(r, r ^ 1) for r in range(N_ROW)])


def to_columns(along_x, along_z, x, z):
    first, second = [], []
    for r in range(N_ROW):
        for a in range(SIDE):
            for b in range(SIDE):
                source = r * N_COL + a * SIDE + b
                first.append((source, (a // 2 * SIDE + b) * N_COL + r + N_ROW * (a % 2)))
                tile = b if a < 2 else (b + SIDE - 1) % SIDE
                second.append((source, (tile // 2 * SIDE + a) * N_COL + r + N_ROW * (tile % 2)))
    one = lax.dynamic_slice(along_x, (z * HALF, 0), (HALF, NB))
    two = lax.dynamic_slice(along_z, (x * HALF, 0), (HALF, NB))
    return lax.ppermute(one, ("row", "col"), first), lax.ppermute(two, ("row", "col"), second)


def choose(place, own, near, far, back):
    return jnp.where(place == 0, own, jnp.where(place == 1, near, jnp.where(place == 2, far, back)))


def join(one, two):
    return jnp.concatenate([one, two], axis=0)


def gather_all(raw, row, col):
    barrier = lax.optimization_barrier
    x, z = col // SIDE, col % SIDE
    after_z = (z + SIDE - 1) % SIDE

    xn, xb, zn, zb = barrier((
        shift_x(raw[NB : 2 * NB + HALF], 1),
        shift_x(raw[2 * NB + HALF : 4 * NB], -1),
        shift_z(raw[5 * NB : 6 * NB + HALF], 1),
        shift_z(raw[6 * NB + HALF :], -1),
    ))
    xc, xd, zc, zd = barrier((
        shift_x(xn[NB:], 1),
        shift_x(xb[:HALF], -1),
        shift_z(zn[NB:], 1),
        shift_z(zb[:HALF], -1),
    ))
    tile_a = choose(x, raw[:NB], xn[:NB], join(xc, xd), xb[HALF:])
    line_b = raw[4 * NB : 5 * NB], zn[:NB], join(zc, zd), zb[HALF:]
    tile_b = join(choose(z, *line_b), choose(after_z, *line_b))

    bn, bb, an, ab = barrier((
        shift_x(tile_b, 1),
        shift_x(tile_b, -1),
        shift_z(tile_a, 1),
        shift_z(tile_a, -1),
    ))
    bc, bd, ac, ad = barrier((
        shift_x(bn[:NB], 1),
        shift_x(bb[NB:], -1),
        shift_z(an[:HALF], 1),
        shift_z(ab[HALF:], -1),
    ))
    line_a = tile_a, an, join(ac, ad), ab
    along_x = join(choose(z, *line_a), choose(after_z, *line_a))
    along_z = choose(x, tile_b, bn, join(bc, bd), bb)

    corner = [(N_COL + z, N_COL + 2 * SIDE + z) for z in range(SIDE)]
    xn, xb, zn, zb, (part_a, part_b), pivot = barrier((
        shift_x(along_x, 1),
        shift_x(along_x, -1),
        shift_z(along_z, 1),
        shift_z(along_z, -1),
        to_columns(along_x, along_z, x, z),
        lax.ppermute(along_x[:NB], ("row", "col"), corner),
    ))
    own = join(part_a, part_b)
    pivot = choose(x, along_x[:NB], xn[:NB], pivot, xb[:NB])
    xc, xd, zc, zd, yn, yb, pivot_up, pivot_down = barrier((
        shift_x(xn[:NB], 1),
        shift_x(xb[NB:], -1),
        shift_z(zn[:NB], 1),
        shift_z(zb[NB:], -1),
        shift_y(own, 1),
        shift_y(own, -1),
        lax.ppermute(pivot, "row", [(1, 3)]),
        lax.ppermute(pivot, "row", [(1, 7)]),
    ))
    panel1 = [(along_x, 0), (xn, 0), (xc, 0), (xb, 0), (along_z, 0), (zn, 0), (zc, 0), (zb, 0)]
    panel2 = [(along_x, NB), (xn, NB), (xd, 0), (xb, NB), (along_z, NB), (zn, NB), (zd, 0), (zb, NB)]
    yc, yd, pivot_far = barrier((
        shift_y(yn[:HALF], 1),
        shift_y(yb[HALF:], -1),
        lax.ppermute(pivot_up, "row", [(3, 5)]),
    ))
    odd = jnp.where(row == 1, pivot, pivot_up + pivot_down + pivot_far)
    here = jnp.stack([own, yn, join(yc, yd), yb])
    there = swap_core(here)
    pivot = jnp.where(row % 2 == 1, odd, swap_core(odd))
    return panel1, panel2, [here, there], pivot


VMEM = pl.BlockSpec(memory_space=pltpu.VMEM)
SMEM = pl.BlockSpec(memory_space=pltpu.SMEM)
ANY = pl.BlockSpec(memory_space=pl.ANY)
LIMIT = pltpu.CompilerParams(vmem_limit_bytes=40 * 1024 * 1024)
ROWS = TR * NB
COLS = TC * NB


def rows_at(index, size):
    return pl.ds(pl.multiple_of(index * size, size), size)


def plane_copies(refs, starts, raw, sems, root):
    c = lax.axis_index("col")
    x, z = lax.div(c, SIDE), lax.rem(c, SIDE)
    copies = []
    for n in range(TR):
        line = x if n < SIDE else z + SIDE - root
        place = lax.rem(line + SIDE - n % SIDE, SIDE) + n // SIDE * SIDE
        source = refs[n].at[pl.ds(starts[n], NB), :]
        copies.append(pltpu.make_async_copy(source, raw.at[rows_at(place, NB), :], sems.at[n]))
    return copies


def column_copies(pieces, raw, sems):
    r = lax.axis_index("row")
    y, core = lax.div(r, 2), lax.rem(r, 2)
    copies = []
    for b in range(2):
        for i in range(SIDE):
            k = lax.rem(y + SIDE - i, SIDE) * 2 + lax.rem(core + b, 2)
            panel = lax.div(lax.rem(k, SIDE), 2)
            at = lax.div(k, SIDE) * 2 + lax.rem(k, 2)
            for part in range(2):
                source = pieces[b].at[i, pl.ds(part * HALF, HALF), :]
                target = raw.at[panel, rows_at(at + part * SIDE, HALF), :]
                copies.append(pltpu.make_async_copy(source, target, sems.at[(b * SIDE + i) * 2 + part]))
    return copies


def first_kernel(starts, *refs):
    pieces, inv, row_high, row_low, raw, sems = refs[:TR], *refs[TR:]
    copies = plane_copies(pieces, starts, raw, sems, 0)
    for copy in copies:
        copy.start()
    weights = deep(inv[0].T)
    for copy in copies:
        copy.wait()

    def row(p, carry):
        solved = dot3(raw[rows_at(p, 2 * NB), :], weights).reshape(2, NB, NB)
        high, low = split(solved)
        row_high[pl.ds(2 * p, 2)] = high
        row_low[pl.ds(2 * p, 2)] = low
        return carry

    lax.fori_loop(0, TR // 2, row, 0)


def solve_first(pieces, inv):
    return pl.pallas_call(
        functools.partial(first_kernel, tuple(start for _, start in pieces)),
        out_shape=[jax.ShapeDtypeStruct((TR, NB, NB), BF16)] * 2,
        in_specs=[ANY] * TR + [VMEM],
        out_specs=[VMEM] * 2,
        scratch_shapes=[pltpu.VMEM((ROWS, NB), F32), pltpu.SemaphoreType.DMA((TR,))],
        compiler_params=LIMIT,
        cost_estimate=pl.CostEstimate(flops=8 * 3 * 2 * NB**3, bytes_accessed=4 * 2**20, transcendentals=0),
        name="solve_first",
    )(*[array for array, _ in pieces], inv)


def second_kernel(starts, *refs):
    pieces, cols = refs[:TR], refs[TR : TR + 2]
    inv, pivot, row_class, col_class, row_high1, row_low1 = refs[TR + 2 : TR + 8]
    panel, row_high, row_low, high1, low1, high2, low2 = refs[TR + 8 : TR + 15]
    raw, raw_cols, sems, col_sems = refs[TR + 15 :]
    copies = plane_copies(pieces, starts, raw, sems, 1)
    col_copies = column_copies(cols, raw_cols, col_sems)
    for copy in copies + col_copies:
        copy.start()
    weights0 = deep(inv[0].T)
    weights1 = deep(inv[1].T)
    one_high, one_low = split(dot3(pivot[...], weights0).T)
    rest_weights = join(one_low, one_high)

    def used(high, low, code):
        full = dot(high, one_high)
        rest = dot(jnp.concatenate([high, low], axis=1), rest_weights)
        return jnp.where(code == 2, 0.0, full + jnp.where(code == 0, rest, 0.0))

    def row(p, carry):
        tile = raw[rows_at(p, NB), :] - used(row_high1[p], row_low1[p], row_class[p, 0])
        solved = dot3(tile, weights1)
        panel[p] = solved
        row_high[p], row_low[p] = split(solved)
        return carry

    def column(q, carry):
        first = dot3(raw_cols[0, rows_at(q, NB), :], weights0)
        high1[q], low1[q] = split(first.T)
        high, low = split(first)
        tile = raw_cols[1, rows_at(q, NB), :] - used(high, low, col_class[q, 0])
        high2[q], low2[q] = split(dot3(tile, weights1).T)
        return carry

    for copy in copies:
        copy.wait()
    lax.fori_loop(0, TR, row, 0, unroll=2)
    for copy in col_copies:
        copy.wait()
    lax.fori_loop(0, TC, column, 0, unroll=2)


def solve_second(pieces, cols, inv, pivot, row_class, col_class, first):
    shapes = [jax.ShapeDtypeStruct((TR, NB, NB), F32)]
    shapes += [jax.ShapeDtypeStruct((n, NB, NB), BF16) for n in (TR, TR, TC, TC, TC, TC)]
    return pl.pallas_call(
        functools.partial(second_kernel, tuple(start for _, start in pieces)),
        out_shape=shapes,
        in_specs=[ANY] * (TR + 2) + [VMEM] * 2 + [SMEM] * 2 + [VMEM] * 2,
        out_specs=[VMEM] * 7,
        scratch_shapes=[
            pltpu.VMEM((ROWS, NB), F32),
            pltpu.VMEM((2, COLS, NB), F32),
            pltpu.SemaphoreType.DMA((TR,)),
            pltpu.SemaphoreType.DMA((N_COL,)),
        ],
        compiler_params=LIMIT,
        cost_estimate=pl.CostEstimate(flops=28 * 3 * 2 * NB**3, bytes_accessed=12 * 2**20, transcendentals=0),
        name="solve_second",
    )(*[array for array, _ in pieces], *cols, inv, pivot, row_class, col_class, *first)


STEP = 2


def update_kernel(classes, matrix, high1, low1, high2, low2, chigh1, clow1, chigh2, clow2, out, product):
    step = pl.program_id(0)
    size = STEP * NB
    high = jnp.concatenate([high1[...].reshape(size, NB), high2[...].reshape(size, NB)], axis=1)
    low = jnp.concatenate([low1[...].reshape(size, NB), low2[...].reshape(size, NB)], axis=1)
    both = jnp.concatenate([high, low], axis=1)
    for q in range(TC):
        col_high = jnp.concatenate([chigh1[q], chigh2[q]], axis=0)
        col_low = jnp.concatenate([clow1[q], clow2[q]], axis=0)
        full = dot(high, col_high)
        rest = dot(both, jnp.concatenate([col_low, col_high], axis=0))
        for p in range(STEP):
            code = classes[step * STEP + p, q]
            at = slice(p * NB, (p + 1) * NB)
            total = jnp.where(code == 2, 0.0, full[at] + jnp.where(code == 0, rest[at], 0.0))
            for b in range(2):
                product[b * TC + q, at, :] = total[:, b * HALF : (b + 1) * HALF]
    lines = 2 * TC
    part = 32
    for p in range(STEP):
        for a in range(0, NB, part):
            turned = product[:, p * NB + a : p * NB + a + part, :].transpose(1, 0, 2).reshape(part * lines, HALF)
            at = pl.ds(a * lines, part * lines)
            out[p, at, :] = matrix[p, at, :] - turned


def update(matrix, classes, rows, cols):
    lines = NB * TC * 2
    view = matrix.reshape(TR, NB, TC, 2, HALF).transpose(0, 1, 3, 2, 4).reshape(TR, lines, HALF)
    block = pl.BlockSpec((STEP, lines, HALF), lambda p: (p, 0, 0))
    row = pl.BlockSpec((STEP, NB, NB), lambda p: (p, 0, 0))
    whole = pl.BlockSpec((TC, NB, NB), lambda p: (0, 0, 0))
    out = pl.pallas_call(
        update_kernel,
        grid=(TR // STEP,),
        out_shape=jax.ShapeDtypeStruct((TR, lines, HALF), F32),
        in_specs=[SMEM, block] + [row] * 4 + [whole] * 4,
        out_specs=block,
        scratch_shapes=[pltpu.VMEM((2 * TC, STEP * NB, HALF), F32)],
        compiler_params=LIMIT,
        name="update_tiles",
    )(classes, view, *rows, *cols)
    return out.reshape(TR, NB, 2, TC, HALF).transpose(0, 1, 3, 2, 4).reshape(TR, NB, TC, NB)


def body(matrix, diag_inverses, band):
    row, col = lax.axis_index("row"), lax.axis_index("col")
    grid = band.reshape(TR, N_ROW, TC, N_COL)
    classes = lax.dynamic_slice(grid, (0, row, 0, col), (TR, 1, TC, 1)).reshape(TR, TC)
    second_class = band[:, 1]
    row_class = lax.dynamic_slice(second_class.reshape(TR, N_ROW), (0, row), (TR, 1))
    col_class = lax.dynamic_slice(second_class.reshape(TC, N_COL), (0, col), (TC, 1))

    raw = matrix[:, :, 0, :].reshape(ROWS, NB)
    panel1, panel2, cols, pivot = gather_all(raw, row, col)
    first = solve_first(panel1, diag_inverses)
    panel, row_high2, row_low2, high1, low1, high2, low2 = solve_second(
        panel2, cols, diag_inverses, pivot, row_class, col_class, first
    )
    rows = (*first, row_high2, row_low2)
    return update(matrix, classes, rows, (high1, low1, high2, low2)), panel


def solution(mesh):
    in_specs = (P(None, "row", None, "col"), P(), P())
    out_specs = (P(None, "row", None, "col"), P(None, "row", None))
    return jax.shard_map(body, mesh=mesh, in_specs=in_specs, out_specs=out_specs, check_vma=False)
```

time: 180 us -> 156 us (0.87)
  starting transfers between devices: 80.3 us -> 56.4 us
  waiting for transfers between devices: 42.8 us -> 54.8 us
  Pallas kernels: 30.4 us -> 22.2 us
  other arithmetic: 8.9 us -> 6.49 us
    ppermute x19 -> x6, starting transfers between devices: 62.4 us -> 26.7 us  [the longest x1 9.05 us: to_columns(): lax.ppermute(one, ('row', 'col'), first)]
    ppermute x7 -> x12, waiting for transfers between devices: 10.6 us -> 28.7 us  [shift_z(): return lax.ppermute(value, 'col', pairs)]
    ppermute x7 -> x12, waiting for transfers between devices: 15.5 us -> 3.13 us  [shift_x(): return lax.ppermute(value, 'col', pairs)]
    ppermute x7 -> x12, starting transfers between devices: 5.25 us -> 14.6 us  [shift_z(): return lax.ppermute(value, 'col', pairs)]
    ppermute x19 -> x6, waiting for transfers between devices: 9.34 us -> 18.2 us  [the longest x1 13.4 us: to_columns(): lax.ppermute(two, ('row', 'col'), second)]
    pallas_call x2, Pallas kernels: 18.2 us -> 10 us  [the longest x1 8.13 us: solve_second(): pl.pallas_call(functools.partial(second_kernel, tuple((start for _, start...]
    ppermute x3 -> x4, starting transfers between devices: 1.58 us -> 4.51 us  [shift_y(): return lax.ppermute(value, 'row', pairs)]
    ppermute x3 -> x4, waiting for transfers between devices: 7.31 us -> 4.81 us  [shift_y(): return lax.ppermute(value, 'row', pairs)]
  transfers between devices with their start and end apart: 38 -> 36, of which waited for: 15 -> 19; matrix products, arithmetic and copies ran while one was open for 4% -> 7% of each run, Pallas kernels for 4% -> 1%
where the time goes in v3:
time: 156 us; the launch traced here: 155 us
  starting transfers between devices  56.4 us (36%)
  waiting for transfers between devices  54.8 us (35%)
  Pallas kernels  22.2 us (14%)
  local copies, waits for them, and re-layouts  13.9 us (9%)
  other arithmetic  6.49 us (4%)
    ppermute x12, waiting for transfers between devices, shift_z(): return lax.ppermute(value, 'col', pairs)  28.7 us
    ppermute x12, starting transfers between devices, shift_z(): return lax.ppermute(value, 'col', pairs)  14.6 us
    ppermute x1, waiting for transfers between devices, to_columns(): lax.ppermute(two, ('row', 'col'), second)  13.4 us
    pallas_call x1, Pallas kernels, update(): pl.pallas_call(update_kernel, grid=(TR // STEP,), out_shape=jax.ShapeDtyp...  12.2 us
    ppermute x1, starting transfers between devices, to_columns(): lax.ppermute(one, ('row', 'col'), first)  9.05 us
    ppermute x12, starting transfers between devices, shift_x(): return lax.ppermute(value, 'col', pairs)  8.77 us
    pallas_call x1, Pallas kernels, solve_second(): pl.pallas_call(functools.partial(second_kernel, tuple((start for _, start...  8.13 us
    ppermute x1, starting transfers between devices, gather_all(): lax.ppermute(along_x[:NB], ('row', 'col'), corner)  6.9 us
  transfers between devices with their start and end apart: 36, of which 19 were waited for; matrix products, arithmetic and copies ran while one was open for 7% of the time, Pallas kernels for 1%

profile of v3, /device:TPU:1, one launch (start us, length us, event | category | flops | bytes accessed | tf_op | source)
XLA Modules:
  0.0 155.1 jit_solution(7695797292483404692)
XLA Ops:
  2.5 4.7 %collective-permute-start.3 = (f32[384,256]{1,0:T(8,128)S(1)}, f32[384,256]{1,0:T(8,128)S(1)}, u32[]{:S(2)}, u32[]{:S(2)}) collective-permute-start(f32[384,256]{1,0:T(8,128)S(1)} %get-tuple-element.90), channel_id=1, source_target_pairs={{0,3},{1,0},{2,1},{3,2},{4,7},{5,4},{6,5},{7,6},{8,11},{9,8},{10,9... | collective-permute-start | bytes 1179656 | tf_op jit(solution)/shard_map/ppermute | solution.py:47
  7.2 2.5 %collective-permute-start.1 = (f32[384,256]{1,0:T(8,128)S(1)}, f32[384,256]{1,0:T(8,128)S(1)}, u32[]{:S(2)}, u32[]{:S(2)}) collective-permute-start(f32[384,256]{1,0:T(8,128)S(1)} %get-tuple-element.92), channel_id=1, source_target_pairs={{0,12},{1,13},{2,14},{3,15},{4,0},{5,1},{6,2},{7,3},{8,4},{9,5},{1... | collective-permute-start | bytes 1179656 | tf_op jit(solution)/shard_map/ppermute | solution.py:42
  9.7 5.3 %collective-permute-done.3 = f32[384,256]{1,0:T(8,128)S(1)} collective-permute-done((f32[384,256]{1,0:T(8,128)S(1)}, f32[384,256]{1,0:T(8,128)S(1)}, u32[]{:S(2)}, u32[]{:S(2)}) %collective-permute-start.3) | collective-permute-done | bytes 393248 | tf_op jit(solution)/shard_map/ppermute | solution.py:47
  15.0 3.1 %collective-permute-done.2 = f32[384,256]{1,0:T(8,128)S(1)} collective-permute-done((f32[384,256]{1,0:T(8,128)S(1)}, f32[384,256]{1,0:T(8,128)S(1)}, u32[]{:S(2)}, u32[]{:S(2)}) %collective-permute-start.2) | collective-permute-done | bytes 393248 | tf_op jit(solution)/shard_map/ppermute | solution.py:47
  18.1 2.2 %collective-permute-done = f32[384,256]{1,0:T(8,128)S(1)} collective-permute-done((f32[384,256]{1,0:T(8,128)S(1)}, f32[384,256]{1,0:T(8,128)S(1)}, u32[]{:S(2)}, u32[]{:S(2)}) %collective-permute-start) | collective-permute-done | bytes 393248 | tf_op jit(solution)/shard_map/ppermute | solution.py:42
  20.3 2.5 %collective-permute-start.7 = (f32[128,256]{1,0:T(8,128)S(1)}, f32[128,256]{1,0:T(8,128)S(1)}, u32[]{:S(2)}, u32[]{:S(2)}) collective-permute-start(f32[128,256]{1,0:T(8,128)S(1)} %slice.101), channel_id=1, source_target_pairs={{0,3},{1,0},{2,1},{3,2},{4,7},{5,4},{6,5},{7,6},{8,11},{9,8},{10,9... | collective-permute-start | bytes 393224 | tf_op jit(solution)/shard_map/ppermute | solution.py:47
  24.7 3.1 %collective-permute-done.6 = f32[128,256]{1,0:T(8,128)S(1)} collective-permute-done((f32[128,256]{1,0:T(8,128)S(1)}, f32[128,256]{1,0:T(8,128)S(1)}, u32[]{:S(2)}, u32[]{:S(2)}) %collective-permute-start.6) | collective-permute-done | bytes 131104 | tf_op jit(solution)/shard_map/ppermute | solution.py:47
  30.8 3.0 %collective-permute-start.11 = (f32[256,256]{1,0:T(8,128)S(1)}, f32[256,256]{1,0:T(8,128)S(1)}, u32[]{:S(2)}, u32[]{:S(2)}) collective-permute-start(f32[256,256]{1,0:T(8,128)S(1)} %fusion.3), channel_id=1, source_target_pairs={{0,3},{1,0},{2,1},{3,2},{4,7},{5,4},{6,5},{7,6},{8,11},{9,8},{10,9... | collective-permute-start | bytes 786440 | tf_op jit(solution)/shard_map/ppermute | solution.py:47
  33.8 3.3 %collective-permute-done.11 = f32[256,256]{1,0:T(8,128)S(1)} collective-permute-done((f32[256,256]{1,0:T(8,128)S(1)}, f32[256,256]{1,0:T(8,128)S(1)}, u32[]{:S(2)}, u32[]{:S(2)}) %collective-permute-start.11) | collective-permute-done | bytes 262176 | tf_op jit(solution)/shard_map/ppermute | solution.py:47
  37.1 3.4 %collective-permute-done.10 = f32[256,256]{1,0:T(8,128)S(1)} collective-permute-done((f32[256,256]{1,0:T(8,128)S(1)}, f32[256,256]{1,0:T(8,128)S(1)}, u32[]{:S(2)}, u32[]{:S(2)}) %collective-permute-start.10) | collective-permute-done | bytes 262176 | tf_op jit(solution)/shard_map/ppermute | solution.py:47
  44.9 2.5 %collective-permute-done.15 = f32[128,256]{1,0:T(8,128)S(1)} collective-permute-done((f32[128,256]{1,0:T(8,128)}, f32[128,256]{1,0:T(8,128)S(1)}, u32[]{:S(2)}, u32[]{:S(2)}) %collective-permute-start.15) | collective-permute-done | bytes 131104 | tf_op jit(solution)/shard_map/ppermute | solution.py:47
  47.5 2.8 %collective-permute-done.14 = f32[128,256]{1,0:T(8,128)} collective-permute-done((f32[128,256]{1,0:T(8,128)}, f32[128,256]{1,0:T(8,128)}, u32[]{:S(2)}, u32[]{:S(2)}) %collective-permute-start.14) | collective-permute-done | bytes 131104 | tf_op jit(solution)/shard_map/ppermute | solution.py:47
  53.9 9.0 %collective-permute-start.20 = (f32[128,256]{1,0:T(8,128)}, f32[128,256]{1,0:T(8,128)S(1)}, u32[]{:S(2)}, u32[]{:S(2)}) collective-permute-start(f32[128,256]{1,0:T(8,128)} %fusion.4), channel_id=1, source_target_pairs={{0,0},{1,16},{2,32},{3,48},{4,8},{5,24},{6,40},{7,56},{8,64},{9,80... | collective-permute-start | bytes 393224 | tf_op jit(solution)/shard_map/ppermute | solution.py:70
  66.1 4.5 %collective-permute-start.21 = (f32[128,256]{1,0:T(8,128)S(1)}, f32[128,256]{1,0:T(8,128)S(1)}, u32[]{:S(2)}, u32[]{:S(2)}) collective-permute-start(f32[128,256]{1,0:T(8,128)S(1)} %constant_dynamic-slice_fusion.2), channel_id=1, source_target_pairs={{0,0},{1,8},{2,64},{3,72},{4,16},{5,24},{6,80},{7,88},{8,104},{9,3... | collective-permute-start | bytes 393224 | tf_op jit(solution)/shard_map/ppermute | solution.py:70
  70.6 13.4 %collective-permute-done.21 = f32[128,256]{1,0:T(8,128)S(1)} collective-permute-done((f32[128,256]{1,0:T(8,128)S(1)}, f32[128,256]{1,0:T(8,128)S(1)}, u32[]{:S(2)}, u32[]{:S(2)}) %collective-permute-start.21) | collective-permute-done | bytes 131104 | tf_op jit(solution)/shard_map/ppermute | solution.py:70
  84.0 6.9 %collective-permute-start.22 = (f32[256,256]{1,0:T(8,128)S(1)}, f32[256,256]{1,0:T(8,128)S(1)}, u32[]{:S(2)}, u32[]{:S(2)}) collective-permute-start(f32[256,256]{1,0:T(8,128)S(1)} %get-tuple-element.96), channel_id=1, source_target_pairs={{16,24},{17,25},{18,26},{19,27}} | collective-permute-start | bytes 786440 | tf_op jit(solution)/shard_map/ppermute | solution.py:125
  90.9 3.3 %collective-permute-done.22 = f32[256,256]{1,0:T(8,128)S(1)} collective-permute-done((f32[256,256]{1,0:T(8,128)S(1)}, f32[256,256]{1,0:T(8,128)S(1)}, u32[]{:S(2)}, u32[]{:S(2)}) %collective-permute-start.22) | collective-permute-done | bytes 262176 | tf_op jit(solution)/shard_map/ppermute | solution.py:125
  98.5 4.5 %collective-permute-done.26.refs_6_ = f32[256,256]{1,0:T(8,128)S(1)} collective-permute-done((f32[256,256]{1,0:T(8,128)S(1)}, f32[256,256]{1,0:T(8,128)S(1)}, u32[]{:S(2)}, u32[]{:S(2)}) %collective-permute-start.26) | collective-permute-done | bytes 262176 | tf_op jit(solution)/shard_map/ppermute | solution.py:47
  104.3 4.3 %collective-permute-start.30 = (f32[256,256]{1,0:T(8,128)S(1)}, f32[256,256]{1,0:T(8,128)S(1)}, u32[]{:S(2)}, u32[]{:S(2)}) collective-permute-start(f32[256,256]{1,0:T(8,128)S(1)} %get-tuple-element.98), channel_id=1, source_target_pairs={{16,112},{17,113},{18,114},{19,115},{20,116},{21,117},{22,118},{23... | collective-permute-start | bytes 786440 | tf_op jit(solution)/shard_map/ppermute | solution.py:137
  113.9 2.4 %collective-permute-start.32 = (f32[128,256]{1,0:T(8,128)S(1)}, f32[128,256]{1,0:T(8,128)S(1)}, u32[]{:S(2)}, u32[]{:S(2)}) collective-permute-start(f32[128,256]{1,0:T(8,128)S(1)} %slice.117), channel_id=1, source_target_pairs={{0,96},{16,112},{32,0},{48,16},{64,32},{80,48},{96,64},{112,80},{1... | collective-permute-start | bytes 393224 | tf_op jit(solution)/shard_map/ppermute | solution.py:52
  116.9 2.6 %collective-permute-done.32 = f32[128,256]{1,0:T(8,128)S(1)} collective-permute-done((f32[128,256]{1,0:T(8,128)S(1)}, f32[128,256]{1,0:T(8,128)S(1)}, u32[]{:S(2)}, u32[]{:S(2)}) %collective-permute-start.32) | collective-permute-done | bytes 131104 | tf_op jit(solution)/shard_map/ppermute | solution.py:52
  119.5 2.2 %collective-permute-done.31 = f32[128,256]{1,0:T(8,128)S(1)} collective-permute-done((f32[128,256]{1,0:T(8,128)S(1)}, f32[128,256]{1,0:T(8,128)S(1)}, u32[]{:S(2)}, u32[]{:S(2)}) %collective-permute-start.31) | collective-permute-done | bytes 131104 | tf_op jit(solution)/shard_map/ppermute | solution.py:52
  134.7 8.1 %solve_second.1 = (f32[8,256,256]{2,1,0:T(8,128)}, bf16[8,256,256]{2,1,0:T(8,128)(2,1)S(1)}, bf16[8,256,256]{2,1,0:T(8,128)(2,1)S(1)}, bf16[4,256,256]{2,1,0:T(8...) custom-call(f32[512,256]{1,0:T(8,128)S(1)} %pad_maximum_fusion.1.ref, ...), custom_call_target="tpu_custom_call" | custom-call | flops 2818572288 | bytes 12582912 | tf_op jit(solution)/shard_map/solve_second/pallas_call | solution.py:270
  142.9 12.2 %update_tiles.1 = f32[8,2048,128]{2,1,0:T(8,128)} custom-call(s32[8,4]{1,0:T(8,128)S(1)} %copy.16.classes, f32[8,2048,128]{2,1,0:T(8,128)} %bitcast.27, bf16[8,256,256]{2,1,0:T(8,128)(2,1)S(1)} %get-tuple-element.70.refs_14_.high1, bf16[8,256,256]{2,1,0:T(8,128)(2,1)S(1)} %get-tuple-element.71.refs_15_.low1, ...), custom_call_target="tpu_custom_call" | custom-call | tf_op jit(solution)/shard_map/update_tiles/pallas_call | solution.py:322
  (138 shorter events, 42.2 us)
Async XLA Ops:
  2.5 12.4 %collective-permute-start.3 = (f32[384,256]{1,0:T(8,128)S(1)}, f32[384,256]{1,0:T(8,128)S(1)}, u32[]{:S(2)}, u32[]{:S(2)}) collective-permute-start(f32[384,256]{1,0:T(8,128)S(1)} %get-tuple-element.90), channel_id=1, source_target_pairs={{0,3},{1,0},{2,1},{3,2},{4,7},{5,4},{6,5},{7,6},{8,11},{9,8},{10,9... | collective-permute-start | bytes 1179656 | tf_op jit(solution)/shard_map/ppermute | solution.py:47
  7.2 10.9 %collective-permute-start.2 = (f32[384,256]{1,0:T(8,128)S(1)}, f32[384,256]{1,0:T(8,128)S(1)}, u32[]{:S(2)}, u32[]{:S(2)}) collective-permute-start(f32[384,256]{1,0:T(8,128)S(1)} %get-tuple-element.91), channel_id=1, source_target_pairs={{0,1},{1,2},{2,3},{3,0},{4,5},{5,6},{6,7},{7,4},{8,9},{9,10},{10,1... | collective-permute-start | bytes 1179656 | tf_op jit(solution)/shard_map/ppermute | solution.py:47
  7.2 10.9 %collective-permute-start.1 = (f32[384,256]{1,0:T(8,128)S(1)}, f32[384,256]{1,0:T(8,128)S(1)}, u32[]{:S(2)}, u32[]{:S(2)}) collective-permute-start(f32[384,256]{1,0:T(8,128)S(1)} %get-tuple-element.92), channel_id=1, source_target_pairs={{0,12},{1,13},{2,14},{3,15},{4,0},{5,1},{6,2},{7,3},{8,4},{9,5},{1... | collective-permute-start | bytes 1179656 | tf_op jit(solution)/shard_map/ppermute | solution.py:42
  9.7 10.6 %collective-permute-start = (f32[384,256]{1,0:T(8,128)S(1)}, f32[384,256]{1,0:T(8,128)S(1)}, u32[]{:S(2)}, u32[]{:S(2)}) collective-permute-start(f32[384,256]{1,0:T(8,128)S(1)} %get-tuple-element.93), channel_id=1, source_target_pairs={{0,4},{1,5},{2,6},{3,7},{4,8},{5,9},{6,10},{7,11},{8,12},{9,13},{1... | collective-permute-start | bytes 1179656 | tf_op jit(solution)/shard_map/ppermute | solution.py:42
  28.2 12.3 %collective-permute-start.9 = (f32[512,256]{1,0:T(8,128)S(1)}, f32[512,256]{1,0:T(8,128)S(1)}, u32[]{:S(2)}, u32[]{:S(2)}) collective-permute-start(f32[512,256]{1,0:T(8,128)S(1)} %pad_maximum_fusion.2), channel_id=1, source_target_pairs={{0,12},{1,13},{2,14},{3,15},{4,0},{5,1},{6,2},{7,3},{8,4},{9,5},{1... | collective-permute-start | bytes 1572872 | tf_op jit(solution)/shard_map/ppermute | solution.py:42
  28.3 12.2 %collective-permute-start.8 = (f32[512,256]{1,0:T(8,128)S(1)}, f32[512,256]{1,0:T(8,128)S(1)}, u32[]{:S(2)}, u32[]{:S(2)}) collective-permute-start(f32[512,256]{1,0:T(8,128)S(1)} %pad_maximum_fusion.2), channel_id=1, source_target_pairs={{0,4},{1,5},{2,6},{3,7},{4,8},{5,9},{6,10},{7,11},{8,12},{9,13},{1... | collective-permute-start | bytes 1572872 | tf_op jit(solution)/shard_map/ppermute | solution.py:42
  40.6 9.7 %collective-permute-start.13 = (f32[256,256]{1,0:T(8,128)S(1)}, f32[256,256]{1,0:T(8,128)S(1)}, u32[]{:S(2)}, u32[]{:S(2)}) collective-permute-start(f32[256,256]{1,0:T(8,128)S(1)} %slice.108), channel_id=1, source_target_pairs={{0,12},{1,13},{2,14},{3,15},{4,0},{5,1},{6,2},{7,3},{8,4},{9,5},{1... | collective-permute-start | bytes 786440 | tf_op jit(solution)/shard_map/ppermute | solution.py:42
  41.9 8.3 %collective-permute-start.12 = (f32[256,256]{1,0:T(8,128)S(1)}, f32[256,256]{1,0:T(8,128)S(1)}, u32[]{:S(2)}, u32[]{:S(2)}) collective-permute-start(f32[256,256]{1,0:T(8,128)S(1)} %slice.107), channel_id=1, source_target_pairs={{0,4},{1,5},{2,6},{3,7},{4,8},{5,9},{6,10},{7,11},{8,12},{9,13},{1... | collective-permute-start | bytes 786440 | tf_op jit(solution)/shard_map/ppermute | solution.py:42
  51.6 42.6 %collective-permute-start.17 = (f32[512,256]{1,0:T(8,128)S(1)}, f32[512,256]{1,0:T(8,128)S(1)}, u32[]{:S(2)}, u32[]{:S(2)}) collective-permute-start(f32[512,256]{1,0:T(8,128)S(1)} %pad_maximum_fusion.1.refs_0_), channel_id=1, source_target_pairs={{0,12},{1,13},{2,14},{3,15},{4,0},{5,1},{6,2},{7,3},{8,4},{9,5},{1... | collective-permute-start | bytes 1572872 | tf_op jit(solution)/shard_map/ppermute | solution.py:42
  53.3 40.9 %collective-permute-start.16 = (f32[512,256]{1,0:T(8,128)S(1)}, f32[512,256]{1,0:T(8,128)S(1)}, u32[]{:S(2)}, u32[]{:S(2)}) collective-permute-start(f32[512,256]{1,0:T(8,128)S(1)} %pad_maximum_fusion.1.refs_0_), channel_id=1, source_target_pairs={{0,4},{1,5},{2,6},{3,7},{4,8},{5,9},{6,10},{7,11},{8,12},{9,13},{1... | collective-permute-start | bytes 1572872 | tf_op jit(solution)/shard_map/ppermute | solution.py:42
  53.9 12.2 %collective-permute-start.20 = (f32[128,256]{1,0:T(8,128)}, f32[128,256]{1,0:T(8,128)S(1)}, u32[]{:S(2)}, u32[]{:S(2)}) collective-permute-start(f32[128,256]{1,0:T(8,128)} %fusion.4), channel_id=1, source_target_pairs={{0,0},{1,16},{2,32},{3,48},{4,8},{5,24},{6,40},{7,56},{8,64},{9,80... | collective-permute-start | bytes 393224 | tf_op jit(solution)/shard_map/ppermute | solution.py:70
  64.2 30.0 %collective-permute-start.19 = (f32[512,256]{1,0:T(8,128)S(1)}, f32[512,256]{1,0:T(8,128)S(1)}, u32[]{:S(2)}, u32[]{:S(2)}) collective-permute-start(f32[512,256]{1,0:T(8,128)S(1)} %fusion.1.refs_4_), channel_id=1, source_target_pairs={{0,3},{1,0},{2,1},{3,2},{4,7},{5,4},{6,5},{7,6},{8,11},{9,8},{10,9... | collective-permute-start | bytes 1572872 | tf_op jit(solution)/shard_map/ppermute | solution.py:47
  64.3 29.9 %collective-permute-start.18 = (f32[512,256]{1,0:T(8,128)S(1)}, f32[512,256]{1,0:T(8,128)S(1)}, u32[]{:S(2)}, u32[]{:S(2)}) collective-permute-start(f32[512,256]{1,0:T(8,128)S(1)} %fusion.1.refs_4_), channel_id=1, source_target_pairs={{0,1},{1,2},{2,3},{3,0},{4,5},{5,6},{6,7},{7,4},{8,9},{9,10},{10,1... | collective-permute-start | bytes 1572872 | tf_op jit(solution)/shard_map/ppermute | solution.py:47
  66.1 17.8 %collective-permute-start.21 = (f32[128,256]{1,0:T(8,128)S(1)}, f32[128,256]{1,0:T(8,128)S(1)}, u32[]{:S(2)}, u32[]{:S(2)}) collective-permute-start(f32[128,256]{1,0:T(8,128)S(1)} %constant_dynamic-slice_fusion.2), channel_id=1, source_target_pairs={{0,0},{1,8},{2,64},{3,72},{4,16},{5,24},{6,80},{7,88},{8,104},{9,3... | collective-permute-start | bytes 393224 | tf_op jit(solution)/shard_map/ppermute | solution.py:70
  84.0 10.2 %collective-permute-start.22 = (f32[256,256]{1,0:T(8,128)S(1)}, f32[256,256]{1,0:T(8,128)S(1)}, u32[]{:S(2)}, u32[]{:S(2)}) collective-permute-start(f32[256,256]{1,0:T(8,128)S(1)} %get-tuple-element.96), channel_id=1, source_target_pairs={{16,24},{17,25},{18,26},{19,27}} | collective-permute-start | bytes 786440 | tf_op jit(solution)/shard_map/ppermute | solution.py:125
  94.2 14.3 %collective-permute-start.28 = (f32[256,256]{1,0:T(8,128)S(1)}, f32[256,256]{1,0:T(8,128)S(1)}, u32[]{:S(2)}, u32[]{:S(2)}) collective-permute-start(f32[256,256]{1,0:T(8,128)S(1)} %constant_dynamic-update-slice_fusion.4), channel_id=1, source_target_pairs={{0,96},{16,112},{32,0},{48,16},{64,32},{80,48},{96,64},{112,80},{1... | collective-permute-start | bytes 786440 | tf_op jit(solution)/shard_map/ppermute | solution.py:52
  94.3 15.6 %collective-permute-start.27 = (f32[256,256]{1,0:T(8,128)S(1)}, f32[256,256]{1,0:T(8,128)S(1)}, u32[]{:S(2)}, u32[]{:S(2)}) collective-permute-start(f32[256,256]{1,0:T(8,128)S(1)} %constant_dynamic-update-slice_fusion.4), channel_id=1, source_target_pairs={{0,32},{16,48},{32,64},{48,80},{64,96},{80,112},{96,0},{112,16},{1... | collective-permute-start | bytes 786440 | tf_op jit(solution)/shard_map/ppermute | solution.py:52
  95.8 7.1 %collective-permute-start.26 = (f32[256,256]{1,0:T(8,128)S(1)}, f32[256,256]{1,0:T(8,128)S(1)}, u32[]{:S(2)}, u32[]{:S(2)}) collective-permute-start(f32[256,256]{1,0:T(8,128)S(1)} %slice.114), channel_id=1, source_target_pairs={{0,3},{1,0},{2,1},{3,2},{4,7},{5,4},{6,5},{7,6},{8,11},{9,8},{10,9... | collective-permute-start | bytes 786440 | tf_op jit(solution)/shard_map/ppermute | solution.py:47
  95.9 8.4 %collective-permute-start.25 = (f32[256,256]{1,0:T(8,128)S(1)}, f32[256,256]{1,0:T(8,128)S(1)}, u32[]{:S(2)}, u32[]{:S(2)}) collective-permute-start(f32[256,256]{1,0:T(8,128)S(1)} %slice.113), channel_id=1, source_target_pairs={{0,1},{1,2},{2,3},{3,0},{4,5},{5,6},{6,7},{7,4},{8,9},{9,10},{10,1... | collective-permute-start | bytes 786440 | tf_op jit(solution)/shard_map/ppermute | solution.py:47
  98.4 11.5 %collective-permute-start.23 = (f32[256,256]{1,0:T(8,128)S(1)}, f32[256,256]{1,0:T(8,128)S(1)}, u32[]{:S(2)}, u32[]{:S(2)}) collective-permute-start(f32[256,256]{1,0:T(8,128)S(1)} %get-tuple-element.99), channel_id=1, source_target_pairs={{0,4},{1,5},{2,6},{3,7},{4,8},{5,9},{6,10},{7,11},{8,12},{9,13},{1... | collective-permute-start | bytes 786440 | tf_op jit(solution)/shard_map/ppermute | solution.py:42
  103.7 7.6 %collective-permute-start.24 = (f32[256,256]{1,0:T(8,128)S(1)}, f32[256,256]{1,0:T(8,128)S(1)}, u32[]{:S(2)}, u32[]{:S(2)}) collective-permute-start(f32[256,256]{1,0:T(8,128)S(1)} %get-tuple-element.100), channel_id=1, source_target_pairs={{0,12},{1,13},{2,14},{3,15},{4,0},{5,1},{6,2},{7,3},{8,4},{9,5},{1... | collective-permute-start | bytes 786440 | tf_op jit(solution)/shard_map/ppermute | solution.py:42
  104.3 7.7 %collective-permute-start.30 = (f32[256,256]{1,0:T(8,128)S(1)}, f32[256,256]{1,0:T(8,128)S(1)}, u32[]{:S(2)}, u32[]{:S(2)}) collective-permute-start(f32[256,256]{1,0:T(8,128)S(1)} %get-tuple-element.98), channel_id=1, source_target_pairs={{16,112},{17,113},{18,114},{19,115},{20,116},{21,117},{22,118},{23... | collective-permute-start | bytes 786440 | tf_op jit(solution)/shard_map/ppermute | solution.py:137
  113.2 8.5 %collective-permute-start.33 = (f32[256,256]{1,0:T(8,128)S(1)}, f32[256,256]{1,0:T(8,128)S(1)}, u32[]{:S(2)}, u32[]{:S(2)}) collective-permute-start(f32[256,256]{1,0:T(8,128)S(1)} %collective-permute-done.29), channel_id=1, source_target_pairs={{48,80},{49,81},{50,82},{51,83},{52,84},{53,85},{54,86},{55,87},{5... | collective-permute-start | bytes 786440 | tf_op jit(solution)/shard_map/ppermute | solution.py:144
  123.5 11.2 %collective-permute-start.34 = (f32[4,256,256]{2,1,0:T(8,128)}, f32[4,256,256]{2,1,0:T(8,128)}, u32[]{:S(2)}, u32[]{:S(2)}) collective-permute-start(f32[4,256,256]{2,1,0:T(8,128)} %pad_maximum_fusion.refs_8_), channel_id=1, source_target_pairs={{0,16},{16,0},{32,48},{48,32},{64,80},{80,64},{96,112},{112,96},{1... | collective-permute-start | bytes 3145736 | tf_op jit(solution)/shard_map/ppermute | solution.py:56
  (34 other events, 227.6 us)

commit v4 on v3

v4 whole, which is shorter than its diff:
```python
import functools

import jax
import jax.numpy as jnp
from jax import lax
from jax.experimental import pallas as pl
from jax.experimental.pallas import tpu as pltpu
from jax.sharding import PartitionSpec as P

NB = 256
HALF = 128
TR = 8
TC = 4
N_ROW = 8
N_COL = 16
SIDE = 4
F32 = jnp.float32
BF16 = jnp.bfloat16


def split(value):
    high = value.astype(BF16)
    return high, (value - high.astype(F32)).astype(BF16)


def dot(a, b):
    return jnp.dot(a, b, preferred_element_type=F32)


def dot3(a, weights):
    high, low = split(a)
    return dot(jnp.concatenate([high, high, low], axis=1), weights)


def deep(value):
    high, low = split(value)
    return jnp.concatenate([high, low, high], axis=0)


def shift_plane(value, by, swapped):
    pairs = []
    for r in range(N_ROW):
        for x in range(SIDE):
            for z in range(SIDE):
                along_z = (r % 2 == 1) != swapped
                to = (x, (z + by) % SIDE) if along_z else ((x + by) % SIDE, z)
                pairs.append((r * N_COL + x * SIDE + z, r * N_COL + to[0] * SIDE + to[1]))
    return lax.ppermute(value, ("row", "col"), pairs)


def shift_line(value, by):
    return shift_plane(value, by, False)


def shift_cross(value, by):
    return shift_plane(value, by, True)


def send_far(value):
    pairs = []
    for r in range(N_ROW):
        for root in range(2):
            to = root + 2 if r % 2 else 2 * SIDE + root
            pairs.append((r * N_COL + root, r * N_COL + to))
    return lax.ppermute(value, ("row", "col"), pairs)


def shift_y(value, by):
    pairs = [(y * 2 + k, (y + by) % SIDE * 2 + k) for y in range(SIDE) for k in range(2)]
    return lax.ppermute(value, "row", pairs)


def swap_core(value):
    return lax.ppermute(value, "row", [(r, r ^ 1) for r in range(N_ROW)])


def to_columns(value):
    pairs = []
    for r in range(N_ROW):
        for x in range(SIDE):
            for z in range(SIDE):
                line, cross = (z, x) if r % 2 else (x, z)
                panel, odd = cross // 2, cross % 2
                quarter = (line - panel * (r % 2)) % SIDE
                target = (quarter * 2 + panel) * N_COL + r + N_ROW * odd
                pairs.append((r * N_COL + x * SIDE + z, target))
    return lax.ppermute(value, ("row", "col"), pairs)


def relay_y(near, back, core):
    pairs = [(r, (r + (2 if r % 2 == 0 else -2)) % N_ROW) for r in range(N_ROW)]
    return lax.ppermute(jnp.where(core == 0, near, back), "row", pairs)


def choose(place, own, near, far, back):
    return jnp.where(place == 0, own, jnp.where(place == 1, near, jnp.where(place == 2, far, back)))


def join(one, two):
    return jnp.concatenate([one, two], axis=0)


PAIR = 2 * NB


def gather_all(raw, row, col):
    barrier = lax.optimization_barrier
    x, z, core = col // SIDE, col % SIDE, row % 2
    line, cross = jnp.where(core == 0, x, z), jnp.where(core == 0, z, x)

    near, back, far = barrier((
        shift_line(raw[PAIR : 2 * PAIR], 1),
        shift_line(raw[3 * PAIR :], -1),
        send_far(raw[2 * PAIR : 3 * PAIR]),
    ))
    places = raw[:PAIR], near, far, back
    own1 = choose(line, *places)
    own2 = choose((line + SIDE - 1) % SIDE, *places)

    both = join(own1, own2)
    near, back = barrier((shift_cross(both, 1), shift_cross(both, -1)))
    far1, far2 = barrier((shift_cross(near[:PAIR], 1), shift_cross(back[PAIR:], -1)))
    block1 = choose(cross, own1, near[:PAIR], far1, back[:PAIR])
    after = (cross + SIDE - 1) % SIDE
    block2 = jnp.where(
        core == 0,
        choose(after, own1, near[:PAIR], far1, back[:PAIR]),
        choose(cross, own2, near[PAIR:], far2, back[PAIR:]),
    )
    block = join(block1, block2)
    tile = lax.dynamic_slice(block, (cross * NB, 0), (NB, NB))
    block, tile, pivot = barrier((block, tile, block1[:NB]))

    corner = [(N_COL + SIDE * a, N_COL + SIDE * a + 2) for a in range(SIDE)]
    near, back, own, pivot_far = barrier((
        shift_line(block, 1),
        shift_line(block, -1),
        to_columns(tile),
        lax.ppermute(pivot, ("row", "col"), corner),
    ))
    pivot = choose(z, pivot, near[:NB], pivot_far, back[:NB])
    far1, far2, up, down, own_other, pivot_up, pivot_down = barrier((
        shift_line(near[:PAIR], 1),
        shift_line(back[PAIR:], -1),
        shift_y(own, 1),
        shift_y(own, -1),
        swap_core(own),
        lax.ppermute(pivot, "row", [(1, 3)]),
        lax.ppermute(pivot, "row", [(1, 7)]),
    ))
    panel1 = [(block, 0), (near, 0), (far1, 0), (back, 0)]
    panel2 = [(block, PAIR), (near, PAIR), (far2, 0), (back, PAIR)]
    last, up_other, down_other, pivot_far = barrier((
        relay_y(up, down, core),
        swap_core(up),
        swap_core(down),
        lax.ppermute(pivot_up, "row", [(3, 5)]),
    ))
    odd = jnp.where(row == 1, pivot, pivot_up + pivot_down + pivot_far)
    cols = [own, up, last, down, own_other, up_other, swap_core(last), down_other]
    pivot = jnp.where(core == 1, odd, swap_core(odd))
    return panel1, panel2, cols, pivot


VMEM = pl.BlockSpec(memory_space=pltpu.VMEM)
SMEM = pl.BlockSpec(memory_space=pltpu.SMEM)
ANY = pl.BlockSpec(memory_space=pl.ANY)
LIMIT = pltpu.CompilerParams(vmem_limit_bytes=24 * 1024 * 1024)
ROWS = TR * NB
COLS = TC * NB


def rows_at(index, size):
    return pl.ds(pl.multiple_of(index * size, size), size)


def plane_copies(refs, starts, raw, sems, panel):
    c, core = lax.axis_index("col"), lax.rem(lax.axis_index("row"), 2)
    x, z = lax.div(c, SIDE), lax.rem(c, SIDE)
    line = jnp.where(core == 0, x, z + SIDE - panel)
    copies = []
    for n in range(SIDE):
        place = lax.rem(line + SIDE - n, SIDE)
        source = refs[n].at[pl.ds(starts[n], PAIR), :]
        copies.append(pltpu.make_async_copy(source, raw.at[rows_at(place, PAIR), :], sems.at[n]))
    return copies


def column_copies(tiles, raw, sems):
    r = lax.axis_index("row")
    y, core = lax.div(r, 2), lax.rem(r, 2)
    copies = []
    for n in range(N_ROW):
        k = lax.rem(y + SIDE - n % SIDE, SIDE) * 2 + lax.rem(core + n // SIDE, 2)
        target = raw.at[lax.rem(k, 2), rows_at(lax.div(k, 2), NB), :]
        copies.append(pltpu.make_async_copy(tiles[n], target, sems.at[n]))
    return copies


def first_kernel(starts, *refs):
    pieces, inv, row_high, row_low, raw, sems = refs[:SIDE], *refs[SIDE:]
    copies = plane_copies(pieces, starts, raw, sems, 0)
    for copy in copies:
        copy.start()
    weights = deep(inv[0].T)
    for copy in copies:
        copy.wait()

    def row(p, carry):
        solved = dot3(raw[rows_at(p, 2 * NB), :], weights).reshape(2, NB, NB)
        high, low = split(solved)
        row_high[pl.ds(2 * p, 2)] = high
        row_low[pl.ds(2 * p, 2)] = low
        return carry

    lax.fori_loop(0, TR // 2, row, 0)


def solve_first(pieces, inv):
    return pl.pallas_call(
        functools.partial(first_kernel, tuple(start for _, start in pieces)),
        out_shape=[jax.ShapeDtypeStruct((TR, NB, NB), BF16)] * 2,
        in_specs=[ANY] * SIDE + [VMEM],
        out_specs=[VMEM] * 2,
        scratch_shapes=[pltpu.VMEM((ROWS, NB), F32), pltpu.SemaphoreType.DMA((SIDE,))],
        compiler_params=LIMIT,
        cost_estimate=pl.CostEstimate(flops=8 * 3 * 2 * NB**3, bytes_accessed=4 * 2**20, transcendentals=0),
        name="solve_first",
    )(*[array for array, _ in pieces], inv)


def second_kernel(starts, *refs):
    pieces, cols = refs[:SIDE], refs[SIDE : SIDE + N_ROW]
    inv, pivot, band, row_high1, row_low1, *refs = refs[SIDE + N_ROW :]
    panel, row_high, row_low, high1, low1, high2, low2, raw, raw_cols, sems, col_sems = refs
    r, c = lax.axis_index("row"), lax.axis_index("col")
    copies = plane_copies(pieces, starts, raw, sems, 1)
    col_copies = column_copies(cols, raw_cols, col_sems)
    for copy in copies + col_copies:
        copy.start()
    weights0 = deep(inv[0].T)
    weights1 = deep(inv[1].T)
    one_high, one_low = split(dot3(pivot[...], weights0).T)
    rest_weights = join(one_low, one_high)

    def used(high, low, code):
        full = dot(high, one_high)
        rest = dot(jnp.concatenate([high, low], axis=1), rest_weights)
        return jnp.where(code == 2, 0.0, full + jnp.where(code == 0, rest, 0.0))

    def row(p, carry):
        tile = raw[rows_at(p, NB), :] - used(row_high1[p], row_low1[p], band[p * N_ROW + r, 1])
        solved = dot3(tile, weights1)
        panel[p] = solved
        row_high[p], row_low[p] = split(solved)
        return carry

    def column(q, carry):
        first = dot3(raw_cols[0, rows_at(q, NB), :], weights0)
        high1[q], low1[q] = split(first.T)
        high, low = split(first)
        tile = raw_cols[1, rows_at(q, NB), :] - used(high, low, band[q * N_COL + c, 1])
        high2[q], low2[q] = split(dot3(tile, weights1).T)
        return carry

    for copy in copies:
        copy.wait()
    lax.fori_loop(0, TR, row, 0, unroll=2)
    for copy in col_copies:
        copy.wait()
    lax.fori_loop(0, TC, column, 0, unroll=2)


def solve_second(pieces, cols, inv, pivot, band, first):
    shapes = [jax.ShapeDtypeStruct((TR, NB, NB), F32)]
    shapes += [jax.ShapeDtypeStruct((n, NB, NB), BF16) for n in (TR, TR, TC, TC, TC, TC)]
    return pl.pallas_call(
        functools.partial(second_kernel, tuple(start for _, start in pieces)),
        out_shape=shapes,
        in_specs=[ANY] * (SIDE + N_ROW) + [VMEM] * 2 + [SMEM] + [VMEM] * 2,
        out_specs=[VMEM] * 7,
        scratch_shapes=[
            pltpu.VMEM((ROWS, NB), F32),
            pltpu.VMEM((2, COLS, NB), F32),
            pltpu.SemaphoreType.DMA((SIDE,)),
            pltpu.SemaphoreType.DMA((N_ROW,)),
        ],
        compiler_params=LIMIT,
        cost_estimate=pl.CostEstimate(flops=28 * 3 * 2 * NB**3, bytes_accessed=12 * 2**20, transcendentals=0),
        name="solve_second",
    )(*[array for array, _ in pieces], *cols, inv, pivot, band, *first)


STEP = 2


def update_kernel(band, matrix, high1, low1, high2, low2, chigh1, clow1, chigh2, clow2, out, product):
    step = pl.program_id(0)
    r, c = lax.axis_index("row"), lax.axis_index("col")
    size = STEP * NB
    high = jnp.concatenate([high1[...].reshape(size, NB), high2[...].reshape(size, NB)], axis=1)
    low = jnp.concatenate([low1[...].reshape(size, NB), low2[...].reshape(size, NB)], axis=1)
    both = jnp.concatenate([high, low], axis=1)
    for q in range(TC):
        col_high = jnp.concatenate([chigh1[q], chigh2[q]], axis=0)
        col_low = jnp.concatenate([clow1[q], clow2[q]], axis=0)
        full = dot(high, col_high)
        rest = dot(both, jnp.concatenate([col_low, col_high], axis=0))
        for p in range(STEP):
            code = band[(step * STEP + p) * N_ROW + r, q * N_COL + c]
            at = slice(p * NB, (p + 1) * NB)
            total = jnp.where(code == 2, 0.0, full[at] + jnp.where(code == 0, rest[at], 0.0))
            for b in range(2):
                product[b * TC + q, at, :] = total[:, b * HALF : (b + 1) * HALF]
    lines = 2 * TC
    part = 32
    for p in range(STEP):
        for a in range(0, NB, part):
            turned = product[:, p * NB + a : p * NB + a + part, :].transpose(1, 0, 2).reshape(part * lines, HALF)
            at = pl.ds(a * lines, part * lines)
            out[p, at, :] = matrix[p, at, :] - turned


def update(matrix, band, rows, cols):
    lines = NB * TC * 2
    view = matrix.reshape(TR, NB, TC, 2, HALF).transpose(0, 1, 3, 2, 4).reshape(TR, lines, HALF)
    block = pl.BlockSpec((STEP, lines, HALF), lambda p: (p, 0, 0))
    row = pl.BlockSpec((STEP, NB, NB), lambda p: (p, 0, 0))
    whole = pl.BlockSpec((TC, NB, NB), lambda p: (0, 0, 0))
    out = pl.pallas_call(
        update_kernel,
        grid=(TR // STEP,),
        out_shape=jax.ShapeDtypeStruct((TR, lines, HALF), F32),
        in_specs=[SMEM, block] + [row] * 4 + [whole] * 4,
        out_specs=block,
        scratch_shapes=[pltpu.VMEM((2 * TC, STEP * NB, HALF), F32)],
        compiler_params=LIMIT,
        name="update_tiles",
    )(band, view, *rows, *cols)
    return out.reshape(TR, NB, 2, TC, HALF).transpose(0, 1, 3, 2, 4).reshape(TR, NB, TC, NB)


def body(matrix, diag_inverses, band):
    raw = matrix[:, :, 0, :].reshape(ROWS, NB)
    panel1, panel2, cols, pivot = gather_all(raw, lax.axis_index("row"), lax.axis_index("col"))
    first = solve_first(panel1, diag_inverses)
    panel, row_high2, row_low2, high1, low1, high2, low2 = solve_second(
        panel2, cols, diag_inverses, pivot, band, first
    )
    rows = (*first, row_high2, row_low2)
    return update(matrix, band, rows, (high1, low1, high2, low2)), panel


def solution(mesh):
    in_specs = (P(None, "row", None, "col"), P(), P())
    out_specs = (P(None, "row", None, "col"), P(None, "row", None))
    return jax.shard_map(body, mesh=mesh, in_specs=in_specs, out_specs=out_specs, check_vma=False)
```

time: 156 us -> 144 us (0.923)
  starting transfers between devices: 56.4 us -> 49.2 us
  waiting for transfers between devices: 54.8 us -> 47.9 us
  local copies, waits for them, and re-layouts: 13.9 us -> 18.4 us
    ppermute x27 -> x14, starting transfers between devices: 43.8 us -> 26.3 us  [the longest x10 11.8 us: shift_plane(): return lax.ppermute(value, ('row', 'col'), pairs)]
    ppermute x1, starting transfers between devices: 4.31 us -> 12.2 us  [gather_all(): lax.ppermute(pivot, 'row', [(1, 7)])]
    ppermute x27 -> x14, waiting for transfers between devices: 48.8 us -> 41.1 us  [the longest x10 29.8 us: shift_plane(): return lax.ppermute(value, ('row', 'col'), pairs)]
    unnamed x47 -> x26, local copies, waits for them, and re-layouts: 6.27 us -> 11.7 us
    slice x17 -> x5, local copies, waits for them, and re-layouts: 3.67 us -> 6.64 us  [the longest x1 4.91 us: gather_all(): raw[2 * PAIR:3 * PAIR]]
    ppermute x2 -> x5, starting transfers between devices: 1.81 us -> 4.22 us  [swap_core(): return lax.ppermute(value, 'row', [(r, r ^ 1) for r in range(N_ROW)])]
    ppermute x4 -> x2, waiting for transfers between devices: 4.81 us -> 6.72 us  [shift_y(): return lax.ppermute(value, 'row', pairs)]
    select_n x5 -> x3, other arithmetic: 3.38 us -> 1.52 us  [choose(): jnp.where(place == 0, own, jnp.where(place == 1, near, jnp.where(place ==...]
  transfers between devices with their start and end apart: 36 -> 24, of which waited for: 19 -> 11; matrix products, arithmetic and copies ran while one was open for 7% -> 1% of each run, Pallas kernels for 1% -> 1%
where the time goes in v4:
time: 144 us
  starting transfers between devices  49.2 us (34%)
  waiting for transfers between devices  47.9 us (33%)
  Pallas kernels  21.2 us (15%)
  local copies, waits for them, and re-layouts  18.4 us (13%)
  other arithmetic  6.17 us (4%)
    ppermute x10, waiting for transfers between devices, shift_plane(): return lax.ppermute(value, ('row', 'col'), pairs)  29.8 us
    ppermute x1, starting transfers between devices, gather_all(): lax.ppermute(pivot, 'row', [(1, 7)])  12.2 us
    ppermute x10, starting transfers between devices, shift_plane(): return lax.ppermute(value, ('row', 'col'), pairs)  11.8 us
    unnamed x26, local copies, waits for them, and re-layouts  11.7 us
    pallas_call x1, Pallas kernels, update(): pl.pallas_call(update_kernel, grid=(TR // STEP,), out_shape=jax.ShapeDtyp...  11.5 us
    pallas_call x1, Pallas kernels, solve_second(): pl.pallas_call(functools.partial(second_kernel, tuple((start for _, start...  7.89 us
    ppermute x1, starting transfers between devices, gather_all(): lax.ppermute(pivot, ('row', 'col'), corner)  7.03 us
    ppermute x2, waiting for transfers between devices, shift_y(): return lax.ppermute(value, 'row', pairs)  6.72 us
  transfers between devices with their start and end apart: 24, of which 11 were waited for; matrix products, arithmetic and copies ran while one was open for 1% of the time, Pallas kernels for 1%

profile of v4, /device:TPU:1, one launch (start us, length us, event | category | flops | bytes accessed | tf_op | source)
XLA Modules:
  0.0 143.7 jit_solution(11849260649859688491)
XLA Ops:
  0.6 4.9 %fusion.1 = (f32[2,256,1,256]{3,2,1,0:T(1,128)S(1)}, f32[2,256,1,256]{3,2,1,0:T(1,128)S(1)}, f32[2,256,1,256]{3,2,1,0:T(1,128)S(1)}, f32[2,256,1,256]{3,2,1,0:T(1,128)S(1)}) fusion(f32[8,256,4,256]{3,2,1,0:T(4,128)} %param.3), kind=kLoop, calls=%fused_computation.13 | loop fusion | bytes 4194304 | tf_op jit(solution)/shard_map/slice | solution.py:114
  5.6 2.5 %collective-permute-start = (f32[512,256]{1,0:T(8,128)S(1)}, f32[512,256]{1,0:T(8,128)S(1)}, u32[]{:S(2)}, u32[]{:S(2)}) collective-permute-start(f32[512,256]{1,0:T(8,128)S(1)} %bitcast.18), channel_id=1, source_target_pairs={{0,4},{1,5},{2,6},{3,7},{4,8},{5,9},{6,10},{7,11},{8,12},{9,13},{1... | collective-permute-start | bytes 1572872 | tf_op jit(solution)/shard_map/ppermute | solution.py:48
  8.2 2.2 %collective-permute-start.1 = (f32[512,256]{1,0:T(8,128)S(1)}, f32[512,256]{1,0:T(8,128)S(1)}, u32[]{:S(2)}, u32[]{:S(2)}) collective-permute-start(f32[512,256]{1,0:T(8,128)S(1)} %bitcast.19), channel_id=1, source_target_pairs={{0,12},{1,13},{2,14},{3,15},{4,0},{5,1},{6,2},{7,3},{8,4},{9,5},{1... | collective-permute-start | bytes 1572872 | tf_op jit(solution)/shard_map/ppermute | solution.py:48
  11.2 3.2 %collective-permute-start.2 = (f32[512,256]{1,0:T(8,128)}, f32[512,256]{1,0:T(8,128)S(1)}, u32[]{:S(2)}, u32[]{:S(2)}) collective-permute-start(f32[512,256]{1,0:T(8,128)} %bitcast.6), channel_id=1, source_target_pairs={{0,8},{1,9},{16,18},{17,19},{32,40},{33,41},{48,50},{49,51},{64,72... | collective-permute-start | bytes 1572872 | tf_op jit(solution)/shard_map/ppermute | solution.py:65
  14.5 2.6 %collective-permute-done = f32[512,256]{1,0:T(8,128)S(1)} collective-permute-done((f32[512,256]{1,0:T(8,128)S(1)}, f32[512,256]{1,0:T(8,128)S(1)}, u32[]{:S(2)}, u32[]{:S(2)}) %collective-permute-start) | collective-permute-done | bytes 524320 | tf_op jit(solution)/shard_map/ppermute | solution.py:48
  17.1 5.0 %collective-permute-done.1 = f32[512,256]{1,0:T(8,128)S(1)} collective-permute-done((f32[512,256]{1,0:T(8,128)S(1)}, f32[512,256]{1,0:T(8,128)S(1)}, u32[]{:S(2)}, u32[]{:S(2)}) %collective-permute-start.1) | collective-permute-done | bytes 524320 | tf_op jit(solution)/shard_map/ppermute | solution.py:48
  23.9 12.5 %collective-permute-done.4 = f32[1024,256]{1,0:T(8,128)S(1)} collective-permute-done((f32[1024,256]{1,0:T(8,128)S(1)}, f32[1024,256]{1,0:T(8,128)S(1)}, u32[]{:S(2)}, u32[]{:S(2)}) %collective-permute-start.4) | collective-permute-done | bytes 1048608 | tf_op jit(solution)/shard_map/ppermute | solution.py:48
  40.8 7.2 %collective-permute-done.6 = f32[512,256]{1,0:T(8,128)} collective-permute-done((f32[512,256]{1,0:T(8,128)}, f32[512,256]{1,0:T(8,128)}, u32[]{:S(2)}, u32[]{:S(2)}) %collective-permute-start.6) | collective-permute-done | bytes 524320 | tf_op jit(solution)/shard_map/ppermute | solution.py:48
  51.4 2.5 %collective-permute-start.8 = (f32[1024,256]{1,0:T(8,128)S(1)}, f32[1024,256]{1,0:T(8,128)S(1)}, u32[]{:S(2)}, u32[]{:S(2)}) collective-permute-start(f32[1024,256]{1,0:T(8,128)S(1)} %pad_maximum_fusion.refs_0_), channel_id=1, source_target_pairs={{0,12},{1,13},{2,14},{3,15},{4,0},{5,1},{6,2},{7,3},{8,4},{9,5},{1... | collective-permute-start | bytes 3145736 | tf_op jit(solution)/shard_map/ppermute | solution.py:48
  53.9 4.2 %collective-permute-start.9 = (f32[256,256]{1,0:T(8,128)}, f32[256,256]{1,0:T(8,128)}, u32[]{:S(2)}, u32[]{:S(2)}) collective-permute-start(f32[256,256]{1,0:T(8,128)} %get-tuple-element.44), channel_id=1, source_target_pairs={{0,0},{1,8},{2,16},{3,24},{4,32},{5,40},{6,48},{7,56},{8,64},{9,72... | collective-permute-start | bytes 786440 | tf_op jit(solution)/shard_map/ppermute | solution.py:87
  58.1 7.0 %collective-permute-start.10 = (f32[256,256]{1,0:T(8,128)S(1)}, f32[256,256]{1,0:T(8,128)}, u32[]{:S(2)}, u32[]{:S(2)}) collective-permute-start(f32[256,256]{1,0:T(8,128)S(1)} %get-tuple-element.45), channel_id=1, source_target_pairs={{16,18},{20,22},{24,26},{28,30}} | collective-permute-start | bytes 786440 | tf_op jit(solution)/shard_map/ppermute | solution.py:139
  65.2 6.2 %collective-permute-done.9.refs_4_ = f32[256,256]{1,0:T(8,128)} collective-permute-done((f32[256,256]{1,0:T(8,128)}, f32[256,256]{1,0:T(8,128)}, u32[]{:S(2)}, u32[]{:S(2)}) %collective-permute-start.9) | collective-permute-done | bytes 262176 | tf_op jit(solution)/shard_map/ppermute | solution.py:87
  71.4 2.7 %collective-permute-done.10 = f32[256,256]{1,0:T(8,128)} collective-permute-done((f32[256,256]{1,0:T(8,128)S(1)}, f32[256,256]{1,0:T(8,128)}, u32[]{:S(2)}, u32[]{:S(2)}) %collective-permute-start.10) | collective-permute-done | bytes 262176 | tf_op jit(solution)/shard_map/ppermute | solution.py:139
  74.1 12.2 %collective-permute-start.17 = (f32[256,256]{1,0:T(8,128)S(1)}, f32[256,256]{1,0:T(8,128)}, u32[]{:S(2)}, u32[]{:S(2)}) collective-permute-start(f32[256,256]{1,0:T(8,128)S(1)} %select_select_fusion.2), channel_id=1, source_target_pairs={{16,112},{17,113},{18,114},{19,115},{20,116},{21,117},{22,118},{23... | collective-permute-start | bytes 786440 | tf_op jit(solution)/shard_map/ppermute | solution.py:149
  86.3 2.0 %collective-permute-start.16 = (f32[256,256]{1,0:T(8,128)S(1)}, f32[256,256]{1,0:T(8,128)}, u32[]{:S(2)}, u32[]{:S(2)}) collective-permute-start(f32[256,256]{1,0:T(8,128)S(1)} %select_select_fusion.2), channel_id=1, source_target_pairs={{16,48},{17,49},{18,50},{19,51},{20,52},{21,53},{22,54},{23,55},{2... | collective-permute-start | bytes 786440 | tf_op jit(solution)/shard_map/ppermute | solution.py:148
  89.9 2.4 %collective-permute-start.14 = (f32[256,256]{1,0:T(8,128)}, f32[256,256]{1,0:T(8,128)S(1)}, u32[]{:S(2)}, u32[]{:S(2)}) collective-permute-start(f32[256,256]{1,0:T(8,128)} %collective-permute-done.9.refs_4_), channel_id=1, source_target_pairs={{0,96},{16,112},{32,0},{48,16},{64,32},{80,48},{96,64},{112,80},{1... | collective-permute-start | bytes 786440 | tf_op jit(solution)/shard_map/ppermute | solution.py:70
  93.8 3.8 %collective-permute-done.14.refs_7_ = f32[256,256]{1,0:T(8,128)S(1)} collective-permute-done((f32[256,256]{1,0:T(8,128)}, f32[256,256]{1,0:T(8,128)S(1)}, u32[]{:S(2)}, u32[]{:S(2)}) %collective-permute-start.14) | collective-permute-done | bytes 262176 | tf_op jit(solution)/shard_map/ppermute | solution.py:70
  97.6 2.9 %collective-permute-done.13.refs_5_ = f32[256,256]{1,0:T(8,128)} collective-permute-done((f32[256,256]{1,0:T(8,128)}, f32[256,256]{1,0:T(8,128)}, u32[]{:S(2)}, u32[]{:S(2)}) %collective-permute-start.13) | collective-permute-done | bytes 262176 | tf_op jit(solution)/shard_map/ppermute | solution.py:70
  104.3 2.0 %collective-permute-start.19 = (f32[256,256]{1,0:T(8,128)}, f32[256,256]{1,0:T(8,128)}, u32[]{:S(2)}, u32[]{:S(2)}) collective-permute-start(f32[256,256]{1,0:T(8,128)} %collective-permute-done.13.refs_5_), channel_id=1, source_target_pairs={{0,16},{16,0},{32,48},{48,32},{64,80},{80,64},{96,112},{112,96},{1... | collective-permute-start | bytes 786440 | tf_op jit(solution)/shard_map/ppermute | solution.py:74
  106.2 2.5 %collective-permute-done.18.refs_6_ = f32[256,256]{1,0:T(8,128)} collective-permute-done((f32[256,256]{1,0:T(8,128)}, f32[256,256]{1,0:T(8,128)}, u32[]{:S(2)}, u32[]{:S(2)}) %collective-permute-start.18) | collective-permute-done | bytes 262176 | tf_op jit(solution)/shard_map/ppermute | solution.py:92
  110.7 2.2 %collective-permute-start.23 = (f32[256,256]{1,0:T(8,128)}, f32[256,256]{1,0:T(8,128)}, u32[]{:S(2)}, u32[]{:S(2)}) collective-permute-start(f32[256,256]{1,0:T(8,128)} %add_select_fusion), channel_id=1, source_target_pairs={{0,16},{16,0},{32,48},{48,32},{64,80},{80,64},{96,112},{112,96},{1... | collective-permute-start | bytes 786440 | tf_op jit(solution)/shard_map/ppermute | solution.py:74
  120.9 7.9 %solve_second.1 = (f32[8,256,256]{2,1,0:T(8,128)}, bf16[8,256,256]{2,1,0:T(8,128)(2,1)S(1)}, bf16[8,256,256]{2,1,0:T(8,128)(2,1)S(1)}, bf16[4,256,256]{2,1,0:T(8...) custom-call(f32[1024,256]{1,0:T(8,128)S(1)} %pad_maximum_fusion.refs, ...), custom_call_target="tpu_custom_call" | custom-call | flops 2818572288 | bytes 12582912 | tf_op jit(solution)/shard_map/solve_second/pallas_call | solution.py:277
  128.8 3.4 %copy-done = f32[8,256,4,256]{3,2,1,0:T(4,128)S(1)} copy-done((f32[8,256,4,256]{3,2,1,0:T(4,128)S(1)}, f32[8,256,4,256]{3,2,1,0:T(4,128)}, u32[]{:S(2)}) %copy-start) | copy-done | bytes 8388632
  132.2 11.5 %update_tiles.1 = f32[8,2048,128]{2,1,0:T(8,128)} custom-call(s32[64,64]{1,0:T(8,128)S(1)} %copy-done.5, f32[8,2048,128]{2,1,0:T(8,128)S(1)} %bitcast.16, bf16[8,256,256]{2,1,0:T(8,128)(2,1)S(1)} %get-tuple-element.51.refs_15_.high1, bf16[8,256,256]{2,1,0:T(8,128)(2,1)S(1)} %get-tuple-element.52.refs_16_.low1, ...), custom_call_target="tpu_custom_call" | custom-call | tf_op jit(solution)/shard_map/update_tiles/pallas_call | solution.py:330
  (67 shorter events, 27.3 us)
Async XLA Ops:
  5.6 11.5 %collective-permute-start = (f32[512,256]{1,0:T(8,128)S(1)}, f32[512,256]{1,0:T(8,128)S(1)}, u32[]{:S(2)}, u32[]{:S(2)}) collective-permute-start(f32[512,256]{1,0:T(8,128)S(1)} %bitcast.18), channel_id=1, source_target_pairs={{0,4},{1,5},{2,6},{3,7},{4,8},{5,9},{6,10},{7,11},{8,12},{9,13},{1... | collective-permute-start | bytes 1572872 | tf_op jit(solution)/shard_map/ppermute | solution.py:48
  8.2 14.0 %collective-permute-start.1 = (f32[512,256]{1,0:T(8,128)S(1)}, f32[512,256]{1,0:T(8,128)S(1)}, u32[]{:S(2)}, u32[]{:S(2)}) collective-permute-start(f32[512,256]{1,0:T(8,128)S(1)} %bitcast.19), channel_id=1, source_target_pairs={{0,12},{1,13},{2,14},{3,15},{4,0},{5,1},{6,2},{7,3},{8,4},{9,5},{1... | collective-permute-start | bytes 1572872 | tf_op jit(solution)/shard_map/ppermute | solution.py:48
  11.2 10.9 %collective-permute-start.2 = (f32[512,256]{1,0:T(8,128)}, f32[512,256]{1,0:T(8,128)S(1)}, u32[]{:S(2)}, u32[]{:S(2)}) collective-permute-start(f32[512,256]{1,0:T(8,128)} %bitcast.6), channel_id=1, source_target_pairs={{0,8},{1,9},{16,18},{17,19},{32,40},{33,41},{48,50},{49,51},{64,72... | collective-permute-start | bytes 1572872 | tf_op jit(solution)/shard_map/ppermute | solution.py:65
  22.3 14.0 %collective-permute-start.4 = (f32[1024,256]{1,0:T(8,128)S(1)}, f32[1024,256]{1,0:T(8,128)S(1)}, u32[]{:S(2)}, u32[]{:S(2)}) collective-permute-start(f32[1024,256]{1,0:T(8,128)S(1)} %pad_maximum_fusion.1), channel_id=1, source_target_pairs={{0,3},{1,0},{2,1},{3,2},{4,7},{5,4},{6,5},{7,6},{8,11},{9,8},{10,9... | collective-permute-start | bytes 3145736 | tf_op jit(solution)/shard_map/ppermute | solution.py:48
  22.4 15.2 %collective-permute-start.3 = (f32[1024,256]{1,0:T(8,128)S(1)}, f32[1024,256]{1,0:T(8,128)S(1)}, u32[]{:S(2)}, u32[]{:S(2)}) collective-permute-start(f32[1024,256]{1,0:T(8,128)S(1)} %pad_maximum_fusion.1), channel_id=1, source_target_pairs={{0,1},{1,2},{2,3},{3,0},{4,5},{5,6},{6,7},{7,4},{8,9},{9,10},{10,1... | collective-permute-start | bytes 3145736 | tf_op jit(solution)/shard_map/ppermute | solution.py:48
  39.3 8.6 %collective-permute-start.6 = (f32[512,256]{1,0:T(8,128)}, f32[512,256]{1,0:T(8,128)}, u32[]{:S(2)}, u32[]{:S(2)}) collective-permute-start(f32[512,256]{1,0:T(8,128)} %slice.69), channel_id=1, source_target_pairs={{0,3},{1,0},{2,1},{3,2},{4,7},{5,4},{6,5},{7,6},{8,11},{9,8},{10,9... | collective-permute-start | bytes 1572872 | tf_op jit(solution)/shard_map/ppermute | solution.py:48
  39.3 9.9 %collective-permute-start.5 = (f32[512,256]{1,0:T(8,128)}, f32[512,256]{1,0:T(8,128)}, u32[]{:S(2)}, u32[]{:S(2)}) collective-permute-start(f32[512,256]{1,0:T(8,128)} %slice.68), channel_id=1, source_target_pairs={{0,1},{1,2},{2,3},{3,0},{4,5},{5,6},{6,7},{7,4},{8,9},{9,10},{10,1... | collective-permute-start | bytes 1572872 | tf_op jit(solution)/shard_map/ppermute | solution.py:48
  51.4 22.7 %collective-permute-start.8 = (f32[1024,256]{1,0:T(8,128)S(1)}, f32[1024,256]{1,0:T(8,128)S(1)}, u32[]{:S(2)}, u32[]{:S(2)}) collective-permute-start(f32[1024,256]{1,0:T(8,128)S(1)} %pad_maximum_fusion.refs_0_), channel_id=1, source_target_pairs={{0,12},{1,13},{2,14},{3,15},{4,0},{5,1},{6,2},{7,3},{8,4},{9,5},{1... | collective-permute-start | bytes 3145736 | tf_op jit(solution)/shard_map/ppermute | solution.py:48
  53.9 20.2 %collective-permute-start.7 = (f32[1024,256]{1,0:T(8,128)S(1)}, f32[1024,256]{1,0:T(8,128)S(1)}, u32[]{:S(2)}, u32[]{:S(2)}) collective-permute-start(f32[1024,256]{1,0:T(8,128)S(1)} %pad_maximum_fusion.refs_0_), channel_id=1, source_target_pairs={{0,4},{1,5},{2,6},{3,7},{4,8},{5,9},{6,10},{7,11},{8,12},{9,13},{1... | collective-permute-start | bytes 3145736 | tf_op jit(solution)/shard_map/ppermute | solution.py:48
  53.9 17.5 %collective-permute-start.9 = (f32[256,256]{1,0:T(8,128)}, f32[256,256]{1,0:T(8,128)}, u32[]{:S(2)}, u32[]{:S(2)}) collective-permute-start(f32[256,256]{1,0:T(8,128)} %get-tuple-element.44), channel_id=1, source_target_pairs={{0,0},{1,8},{2,16},{3,24},{4,32},{5,40},{6,48},{7,56},{8,64},{9,72... | collective-permute-start | bytes 786440 | tf_op jit(solution)/shard_map/ppermute | solution.py:87
  58.1 15.9 %collective-permute-start.10 = (f32[256,256]{1,0:T(8,128)S(1)}, f32[256,256]{1,0:T(8,128)}, u32[]{:S(2)}, u32[]{:S(2)}) collective-permute-start(f32[256,256]{1,0:T(8,128)S(1)} %get-tuple-element.45), channel_id=1, source_target_pairs={{16,18},{20,22},{24,26},{28,30}} | collective-permute-start | bytes 786440 | tf_op jit(solution)/shard_map/ppermute | solution.py:139
  74.1 15.8 %collective-permute-start.17 = (f32[256,256]{1,0:T(8,128)S(1)}, f32[256,256]{1,0:T(8,128)}, u32[]{:S(2)}, u32[]{:S(2)}) collective-permute-start(f32[256,256]{1,0:T(8,128)S(1)} %select_select_fusion.2), channel_id=1, source_target_pairs={{16,112},{17,113},{18,114},{19,115},{20,116},{21,117},{22,118},{23... | collective-permute-start | bytes 786440 | tf_op jit(solution)/shard_map/ppermute | solution.py:149
  86.3 6.0 %collective-permute-start.16 = (f32[256,256]{1,0:T(8,128)S(1)}, f32[256,256]{1,0:T(8,128)}, u32[]{:S(2)}, u32[]{:S(2)}) collective-permute-start(f32[256,256]{1,0:T(8,128)S(1)} %select_select_fusion.2), channel_id=1, source_target_pairs={{16,48},{17,49},{18,50},{19,51},{20,52},{21,53},{22,54},{23,55},{2... | collective-permute-start | bytes 786440 | tf_op jit(solution)/shard_map/ppermute | solution.py:148
  88.4 12.1 %collective-permute-start.12 = (f32[512,256]{1,0:T(8,128)S(1)}, f32[512,256]{1,0:T(8,128)S(1)}, u32[]{:S(2)}, u32[]{:S(2)}) collective-permute-start(f32[512,256]{1,0:T(8,128)S(1)} %slice.74), channel_id=1, source_target_pairs={{0,12},{1,13},{2,14},{3,15},{4,0},{5,1},{6,2},{7,3},{8,4},{9,5},{1... | collective-permute-start | bytes 1572872 | tf_op jit(solution)/shard_map/ppermute | solution.py:48
  88.5 12.9 %collective-permute-start.11 = (f32[512,256]{1,0:T(8,128)S(1)}, f32[512,256]{1,0:T(8,128)S(1)}, u32[]{:S(2)}, u32[]{:S(2)}) collective-permute-start(f32[512,256]{1,0:T(8,128)S(1)} %slice.73), channel_id=1, source_target_pairs={{0,4},{1,5},{2,6},{3,7},{4,8},{5,9},{6,10},{7,11},{8,12},{9,13},{1... | collective-permute-start | bytes 1572872 | tf_op jit(solution)/shard_map/ppermute | solution.py:48
  89.9 3.2 %collective-permute-start.15 = (f32[256,256]{1,0:T(8,128)}, f32[256,256]{1,0:T(8,128)S(1)}, u32[]{:S(2)}, u32[]{:S(2)}) collective-permute-start(f32[256,256]{1,0:T(8,128)} %collective-permute-done.9.refs_4_), channel_id=1, source_target_pairs={{0,16},{16,0},{32,48},{48,32},{64,80},{80,64},{96,112},{112,96},{1... | collective-permute-start | bytes 786440 | tf_op jit(solution)/shard_map/ppermute | solution.py:74
  89.9 7.7 %collective-permute-start.14 = (f32[256,256]{1,0:T(8,128)}, f32[256,256]{1,0:T(8,128)S(1)}, u32[]{:S(2)}, u32[]{:S(2)}) collective-permute-start(f32[256,256]{1,0:T(8,128)} %collective-permute-done.9.refs_4_), channel_id=1, source_target_pairs={{0,96},{16,112},{32,0},{48,16},{64,32},{80,48},{96,64},{112,80},{1... | collective-permute-start | bytes 786440 | tf_op jit(solution)/shard_map/ppermute | solution.py:70
  92.3 8.2 %collective-permute-start.13 = (f32[256,256]{1,0:T(8,128)}, f32[256,256]{1,0:T(8,128)}, u32[]{:S(2)}, u32[]{:S(2)}) collective-permute-start(f32[256,256]{1,0:T(8,128)} %collective-permute-done.9.refs_4_), channel_id=1, source_target_pairs={{0,32},{16,48},{32,64},{48,80},{64,96},{80,112},{96,0},{112,16},{1... | collective-permute-start | bytes 786440 | tf_op jit(solution)/shard_map/ppermute | solution.py:70
  102.9 5.8 %collective-permute-start.18 = (f32[256,256]{1,0:T(8,128)}, f32[256,256]{1,0:T(8,128)}, u32[]{:S(2)}, u32[]{:S(2)}) collective-permute-start(f32[256,256]{1,0:T(8,128)} %broadcast_select_fusion.1), channel_id=1, source_target_pairs={{0,32},{16,112},{32,64},{48,16},{64,96},{80,48},{96,0},{112,80},{1... | collective-permute-start | bytes 786440 | tf_op jit(solution)/shard_map/ppermute | solution.py:92
  102.9 5.8 %collective-permute-start.21 = (f32[256,256]{1,0:T(8,128)}, f32[256,256]{1,0:T(8,128)}, u32[]{:S(2)}, u32[]{:S(2)}) collective-permute-start(f32[256,256]{1,0:T(8,128)} %collective-permute-done.16), channel_id=1, source_target_pairs={{48,80},{49,81},{50,82},{51,83},{52,84},{53,85},{54,86},{55,87},{5... | collective-permute-start | bytes 786440 | tf_op jit(solution)/shard_map/ppermute | solution.py:157
  104.3 4.5 %collective-permute-start.19 = (f32[256,256]{1,0:T(8,128)}, f32[256,256]{1,0:T(8,128)}, u32[]{:S(2)}, u32[]{:S(2)}) collective-permute-start(f32[256,256]{1,0:T(8,128)} %collective-permute-done.13.refs_5_), channel_id=1, source_target_pairs={{0,16},{16,0},{32,48},{48,32},{64,80},{80,64},{96,112},{112,96},{1... | collective-permute-start | bytes 786440 | tf_op jit(solution)/shard_map/ppermute | solution.py:74
  106.2 2.5 %collective-permute-start.20 = (f32[256,256]{1,0:T(8,128)S(1)}, f32[256,256]{1,0:T(8,128)}, u32[]{:S(2)}, u32[]{:S(2)}) collective-permute-start(f32[256,256]{1,0:T(8,128)S(1)} %collective-permute-done.14.refs_7_), channel_id=1, source_target_pairs={{0,16},{16,0},{32,48},{48,32},{64,80},{80,64},{96,112},{112,96},{1... | collective-permute-start | bytes 786440 | tf_op jit(solution)/shard_map/ppermute | solution.py:74
  110.7 6.2 %collective-permute-start.23 = (f32[256,256]{1,0:T(8,128)}, f32[256,256]{1,0:T(8,128)}, u32[]{:S(2)}, u32[]{:S(2)}) collective-permute-start(f32[256,256]{1,0:T(8,128)} %add_select_fusion), channel_id=1, source_target_pairs={{0,16},{16,0},{32,48},{48,32},{64,80},{80,64},{96,112},{112,96},{1... | collective-permute-start | bytes 786440 | tf_op jit(solution)/shard_map/ppermute | solution.py:74
  112.9 5.0 %collective-permute-start.22 = (f32[256,256]{1,0:T(8,128)}, f32[256,256]{1,0:T(8,128)S(1)}, u32[]{:S(2)}, u32[]{:S(2)}) collective-permute-start(f32[256,256]{1,0:T(8,128)} %collective-permute-done.18.refs_6_), channel_id=1, source_target_pairs={{0,16},{16,0},{32,48},{48,32},{64,80},{80,64},{96,112},{112,96},{1... | collective-permute-start | bytes 786440 | tf_op jit(solution)/shard_map/ppermute | solution.py:74
  (11 other events, 108.3 us)

commit v5 on v4

v5 whole, which is shorter than its diff:
```python
import functools

import jax
import jax.numpy as jnp
from jax import lax
from jax.experimental import pallas as pl
from jax.experimental.pallas import tpu as pltpu
from jax.sharding import PartitionSpec as P

NB = 256
HALF = 128
TR = 8
TC = 4
N_ROW = 8
N_COL = 16
SIDE = 4
F32 = jnp.float32
BF16 = jnp.bfloat16


def split(value):
    high = value.astype(BF16)
    return high, (value - high.astype(F32)).astype(BF16)


def dot(a, b):
    return jnp.dot(a, b, preferred_element_type=F32)


def dot3(a, weights):
    high, low = split(a)
    return dot(jnp.concatenate([high, high, low], axis=1), weights)


def deep(value):
    high, low = split(value)
    return jnp.concatenate([high, low, high], axis=0)


def shift_plane(value, by, swapped):
    pairs = []
    for r in range(N_ROW):
        for x in range(SIDE):
            for z in range(SIDE):
                along_z = (r % 2 == 1) != swapped
                to = (x, (z + by) % SIDE) if along_z else ((x + by) % SIDE, z)
                pairs.append((r * N_COL + x * SIDE + z, r * N_COL + to[0] * SIDE + to[1]))
    return lax.ppermute(value, ("row", "col"), pairs)


def shift_line(value, by):
    return shift_plane(value, by, False)


def shift_cross(value, by):
    return shift_plane(value, by, True)


def send_far(value):
    pairs = []
    for r in range(N_ROW):
        for root in range(2):
            to = root + 2 if r % 2 else 2 * SIDE + root
            pairs.append((r * N_COL + root, r * N_COL + to))
    return lax.ppermute(value, ("row", "col"), pairs)


def shift_y(value, by):
    pairs = [(y * 2 + k, (y + by) % SIDE * 2 + k) for y in range(SIDE) for k in range(2)]
    return lax.ppermute(value, "row", pairs)


def swap_core(value):
    return lax.ppermute(value, "row", [(r, r ^ 1) for r in range(N_ROW)])


def to_columns(value):
    pairs = []
    for r in range(N_ROW):
        for x in range(SIDE):
            for z in range(SIDE):
                line, cross = (z, x) if r % 2 else (x, z)
                panel, odd = cross // 2, cross % 2
                quarter = (line - panel * (r % 2)) % SIDE
                target = (quarter * 2 + panel) * N_COL + r + N_ROW * odd
                pairs.append((r * N_COL + x * SIDE + z, target))
    return lax.ppermute(value, ("row", "col"), pairs)


def relay_y(near, back, core):
    pairs = [(r, (r + (2 if r % 2 == 0 else -2)) % N_ROW) for r in range(N_ROW)]
    return lax.ppermute(jnp.where(core == 0, near, back), "row", pairs)


def choose(place, own, near, far, back):
    return jnp.where(place == 0, own, jnp.where(place == 1, near, jnp.where(place == 2, far, back)))


def join(one, two):
    return jnp.concatenate([one, two], axis=0)


PAIR = 2 * NB


def gather_all(raw, row, col):
    barrier = lax.optimization_barrier
    x, z, core = col // SIDE, col % SIDE, row % 2
    line, cross = jnp.where(core == 0, x, z), jnp.where(core == 0, z, x)

    near, back, far = barrier((
        shift_line(raw[PAIR : 2 * PAIR], 1),
        shift_line(raw[3 * PAIR :], -1),
        send_far(raw[2 * PAIR : 3 * PAIR]),
    ))
    places = raw[:PAIR], near, far, back
    own1 = choose(line, *places)
    own2 = choose((line + SIDE - 1) % SIDE, *places)

    near1, back2 = shift_cross(own1, 1), shift_cross(own2, -1)
    back1, near2 = shift_cross(own1, -1), shift_cross(own2, 1)
    far1, far2 = shift_cross(near1, 1), shift_cross(back2, -1)
    near1, far1, back1, near2, far2, back2 = barrier((near1, far1, back1, near2, far2, back2))
    after = (cross + SIDE - 1) % SIDE
    block1 = choose(cross, own1, near1, far1, back1)
    block2 = jnp.where(
        core == 0,
        choose(after, own1, near1, far1, back1),
        choose(cross, own2, near2, far2, back2),
    )
    half = jnp.where(cross < 2, block1, block2)
    tile = lax.dynamic_slice(half, (cross % 2 * NB, 0), (NB, NB))
    block1, block2, tile, pivot = barrier((block1, block2, tile, block1[:NB]))

    corner = [(N_COL + SIDE * a, N_COL + SIDE * a + 2) for a in range(SIDE)]
    near1, back2 = shift_line(block1, 1), shift_line(block2, -1)
    back1, near2 = shift_line(block1, -1), shift_line(block2, 1)
    own, pivot_far = to_columns(tile), lax.ppermute(pivot, ("row", "col"), corner)
    pivot = choose(z, pivot, near1[:NB], pivot_far, back1[:NB])
    far1, far2, up, down, own_other, pivot_up, pivot_down, pivot_swap = barrier((
        shift_line(near1, 1),
        shift_line(back2, -1),
        shift_y(own, 1),
        shift_y(own, -1),
        swap_core(own),
        lax.ppermute(pivot, "row", [(1, 3)]),
        lax.ppermute(pivot, "row", [(1, 7)]),
        lax.ppermute(pivot, "row", [(1, 0)]),
    ))
    panel1 = [block1, near1, far1, back1]
    panel2 = [block2, near2, far2, back2]
    ends = pivot_up + pivot_down
    last, up_other, down_other, pivot_far, ends_swap = barrier((
        relay_y(up, down, core),
        swap_core(up),
        swap_core(down),
        lax.ppermute(ends, "row", [(3, 5)]),
        lax.ppermute(ends, "row", [(3, 2), (7, 6)]),
    ))
    cols = [own, up, last, down, own_other, up_other, swap_core(last), down_other]
    far_swap = lax.ppermute(pivot_far, "row", [(5, 4)])
    pivots = [pivot_swap, pivot, ends_swap, ends, far_swap, pivot_far]
    return panel1, panel2, cols, pivots


VMEM = pl.BlockSpec(memory_space=pltpu.VMEM)
SMEM = pl.BlockSpec(memory_space=pltpu.SMEM)
ANY = pl.BlockSpec(memory_space=pl.ANY)
ROWS = TR * NB
COLS = TC * NB


def rows_at(index, size):
    return pl.ds(pl.multiple_of(index * size, size), size)


def plane_copies(refs, raw, sems, panel):
    c, core = lax.axis_index("col"), lax.rem(lax.axis_index("row"), 2)
    x, z = lax.div(c, SIDE), lax.rem(c, SIDE)
    line = jnp.where(core == 0, x, z + SIDE - panel)
    copies = []
    for n in range(SIDE):
        place = lax.rem(line + SIDE - n, SIDE)
        copies.append(pltpu.make_async_copy(refs[n], raw.at[rows_at(place, PAIR), :], sems.at[n]))
    return copies


def column_copies(tiles, raw, sems):
    r = lax.axis_index("row")
    y, core = lax.div(r, 2), lax.rem(r, 2)
    copies = []
    for n in range(N_ROW):
        k = lax.rem(y + SIDE - n % SIDE, SIDE) * 2 + lax.rem(core + n // SIDE, 2)
        target = raw.at[lax.rem(k, 2), rows_at(lax.div(k, 2), NB), :]
        copies.append(pltpu.make_async_copy(tiles[n], target, sems.at[n]))
    return copies


def first_kernel(*refs):
    pieces, inv_in, row_high, row_low, raw, inv, sems = refs[:SIDE], *refs[SIDE:]
    copies = plane_copies(pieces, raw, sems, 0)
    weights_copy = pltpu.make_async_copy(inv_in.at[0], inv, sems.at[SIDE])
    for copy in [weights_copy, *copies]:
        copy.start()
    weights_copy.wait()
    weights = deep(inv[...].T)
    for copy in copies:
        copy.wait()

    def row(p, carry):
        solved = dot3(raw[rows_at(p, PAIR), :], weights).reshape(2, NB, NB)
        high, low = split(solved)
        row_high[pl.ds(2 * p, 2)] = high
        row_low[pl.ds(2 * p, 2)] = low
        return carry

    lax.fori_loop(0, TR // 2, row, 0)


def solve_first(pieces, inv):
    return pl.pallas_call(
        first_kernel,
        out_shape=[jax.ShapeDtypeStruct((TR, NB, NB), BF16)] * 2,
        in_specs=[ANY] * (SIDE + 1),
        out_specs=[VMEM] * 2,
        scratch_shapes=[
            pltpu.VMEM((ROWS, NB), F32),
            pltpu.VMEM((NB, NB), F32),
            pltpu.SemaphoreType.DMA((SIDE + 1,)),
        ],
        compiler_params=pltpu.CompilerParams(vmem_limit_bytes=16 * 1024 * 1024),
        cost_estimate=pl.CostEstimate(flops=8 * 3 * 2 * NB**3, bytes_accessed=4 * 2**20, transcendentals=0),
        name="solve_first",
    )(*pieces, inv)


STEP = 2
LINES = NB * TC * 2
PART = 32


def last_kernel(*refs):
    pieces, cols = refs[:SIDE], refs[SIDE : SIDE + N_ROW]
    pivots, refs = refs[SIDE + N_ROW : SIDE + N_ROW + 6], refs[SIDE + N_ROW + 6 :]
    matrix, inv_in, high_in, low_in, band, out, panel, *refs = refs
    tiles, raw, raw_cols, row_high1, row_low1, row_high2, row_low2, col_high, col_low, even, odd, *refs = refs
    inv, pivot, sems, col_sems, in_sems, out_sems, panel_sems, small_sems = refs
    r, c = lax.axis_index("row"), lax.axis_index("col")
    copies = plane_copies(pieces, raw, sems, 1)
    col_copies = column_copies(cols, raw_cols, col_sems)
    loads = [pltpu.make_async_copy(matrix.at[p], tiles.at[p], in_sems.at[p]) for p in range(TR)]
    small = [(inv_in, inv), (pivots[0], pivot), (high_in, row_high1), (low_in, row_low1)]
    small = [pltpu.make_async_copy(a, b, small_sems.at[n]) for n, (a, b) in enumerate(small)]
    small[0].start()
    for n, rows in enumerate(((0,), (1,), (2, 6), (3, 7), (4,), (5,))):

        @pl.when(functools.reduce(jnp.logical_or, [r == row for row in rows]))
        def _():
            pltpu.make_async_copy(pivots[n], pivot, small_sems.at[1]).start()

    for copy in small[2:] + copies + col_copies + loads:
        copy.start()
    small[0].wait()
    weights0 = deep(inv[0].T)
    weights1 = deep(inv[1].T)
    small[1].wait()
    one_high, one_low = split(dot3(pivot[...], weights0).T)
    rest_weights = join(one_low, one_high)

    def used(high, low, code):
        full = dot(high, one_high)
        rest = dot(jnp.concatenate([high, low], axis=1), rest_weights)
        return jnp.where(code == 2, 0.0, full + jnp.where(code == 0, rest, 0.0))

    def row(p, carry):
        tile = raw[rows_at(p, NB), :] - used(row_high1[p], row_low1[p], band[p * N_ROW + r, 1])
        solved = dot3(tile, weights1)
        raw[rows_at(p, NB), :] = solved
        row_high2[p], row_low2[p] = split(solved)
        return carry

    def column(q, carry):
        first = dot3(raw_cols[0, rows_at(q, NB), :], weights0)
        col_high[q, :NB, :], col_low[q, :NB, :] = split(first.T)
        high, low = split(first)
        tile = raw_cols[1, rows_at(q, NB), :] - used(high, low, band[q * N_COL + c, 1])
        col_high[q, NB:, :], col_low[q, NB:, :] = split(dot3(tile, weights1).T)
        return carry

    for copy in small[2:] + copies:
        copy.wait()
    lax.fori_loop(0, TR, row, 0, unroll=4)
    panels = [pltpu.make_async_copy(raw.at[pl.ds(p * NB, NB), :], panel.at[p], panel_sems.at[p]) for p in range(TR)]
    for copy in panels:
        copy.start()
    for copy in col_copies:
        copy.wait()
    lax.fori_loop(0, TC, column, 0, unroll=4)

    size = STEP * NB

    def multiply(step, q, product):
        at = pl.ds(step * STEP, STEP)
        high = jnp.concatenate([row_high1[at].reshape(size, NB), row_high2[at].reshape(size, NB)], axis=1)
        low = jnp.concatenate([row_low1[at].reshape(size, NB), row_low2[at].reshape(size, NB)], axis=1)
        full = dot(high, col_high[q])
        rest = dot(jnp.concatenate([high, low], axis=1), join(col_low[q], col_high[q]))
        for p in range(STEP):
            code = band[(step * STEP + p) * N_ROW + r, q * N_COL + c]
            at = slice(p * NB, (p + 1) * NB)
            total = jnp.where(code == 2, 0.0, full[at] + jnp.where(code == 0, rest[at], 0.0))
            for b in range(2):
                product[b * TC + q, at, :] = total[:, b * HALF : (b + 1) * HALF]

    def subtract(step, share, product):
        for a in range(share * size // TC, (share + 1) * size // TC, PART):
            turned = product[:, a : a + PART, :].transpose(1, 0, 2).reshape(PART * 2 * TC, HALF)
            at = pl.ds(a % NB * 2 * TC, PART * 2 * TC)
            tiles[step * STEP + a // NB, at, :] -= turned

    steps = TR // STEP
    stores = [pltpu.make_async_copy(tiles.at[p], out.at[p], out_sems.at[p]) for p in range(TR)]
    for step in range(steps + 1):
        product, before = (even, odd) if step % 2 == 0 else (odd, even)
        if step:
            for p in range(STEP):
                loads[(step - 1) * STEP + p].wait()
        for q in range(TC):
            if step < steps:
                multiply(step, q, product)
            if step:
                subtract(step - 1, q, before)
        if step:
            for p in range(STEP):
                stores[(step - 1) * STEP + p].start()
    for copy in stores + panels:
        copy.wait()


def finish(pieces, cols, pivots, matrix, inv, first, band):
    view = matrix.reshape(TR, NB, TC, 2, HALF).transpose(0, 1, 3, 2, 4).reshape(TR, LINES, HALF)
    out, panel = pl.pallas_call(
        last_kernel,
        out_shape=(
            jax.ShapeDtypeStruct((TR, LINES, HALF), F32),
            jax.ShapeDtypeStruct((TR, NB, NB), F32),
        ),
        in_specs=[ANY] * (SIDE + N_ROW + 6 + 4) + [SMEM],
        out_specs=[ANY] * 2,
        scratch_shapes=[
            pltpu.VMEM((TR, LINES, HALF), F32),
            pltpu.VMEM((ROWS, NB), F32),
            pltpu.VMEM((2, COLS, NB), F32),
            pltpu.VMEM((TR, NB, NB), BF16),
            pltpu.VMEM((TR, NB, NB), BF16),
            pltpu.VMEM((TR, NB, NB), BF16),
            pltpu.VMEM((TR, NB, NB), BF16),
            pltpu.VMEM((TC, PAIR, NB), BF16),
            pltpu.VMEM((TC, PAIR, NB), BF16),
            pltpu.VMEM((2 * TC, STEP * NB, HALF), F32),
            pltpu.VMEM((2 * TC, STEP * NB, HALF), F32),
            pltpu.VMEM((2, NB, NB), F32),
            pltpu.VMEM((NB, NB), F32),
            pltpu.SemaphoreType.DMA((SIDE,)),
            pltpu.SemaphoreType.DMA((N_ROW,)),
            pltpu.SemaphoreType.DMA((TR,)),
            pltpu.SemaphoreType.DMA((TR,)),
            pltpu.SemaphoreType.DMA((TR,)),
            pltpu.SemaphoreType.DMA((4,)),
        ],
        compiler_params=pltpu.CompilerParams(vmem_limit_bytes=40 * 1024 * 1024),
        cost_estimate=pl.CostEstimate(flops=200 * 2 * NB**3, bytes_accessed=20 * 2**20, transcendentals=0),
        name="solve_and_update",
    )(*pieces, *cols, *pivots, view, inv, *first, band)
    return out.reshape(TR, NB, 2, TC, HALF).transpose(0, 1, 3, 2, 4).reshape(TR, NB, TC, NB), panel


def body(matrix, diag_inverses, band):
    raw = lax.optimization_barrier(matrix[:, :, 0, :].reshape(ROWS, NB))
    panel1, panel2, cols, pivots = gather_all(raw, lax.axis_index("row"), lax.axis_index("col"))
    first = solve_first(panel1, diag_inverses)
    return finish(panel2, cols, pivots, matrix, diag_inverses, first, band)


def solution(mesh):
    in_specs = (P(None, "row", None, "col"), P(), P())
    out_specs = (P(None, "row", None, "col"), P(None, "row", None))
    return jax.shard_map(body, mesh=mesh, in_specs=in_specs, out_specs=out_specs, check_vma=False)
```

time: 144 us -> 125 us (0.87)
  local copies, waits for them, and re-layouts: 18.4 us -> 3.81 us
  waiting for transfers between devices: 47.9 us -> 41.1 us
  starting transfers between devices: 49.2 us -> 53.3 us
  other arithmetic: 6.17 us -> 4.11 us
    unnamed x26 -> x17, local copies, waits for them, and re-layouts: 11.7 us -> 1.05 us
    ppermute x2, starting transfers between devices: 3.17 us -> 10.9 us  [shift_y(): return lax.ppermute(value, 'row', pairs)]
    ppermute x1, starting transfers between devices: 12.2 us -> 4.73 us  [gather_all(): lax.ppermute(pivot, 'row', [(1, 7)])]
    ppermute x2, waiting for transfers between devices: 6.72 us -> 0.01 us  [shift_y(): return lax.ppermute(value, 'row', pairs)]
    ppermute x10 -> x14, waiting for transfers between devices: 29.8 us -> 24.1 us  [shift_plane(): return lax.ppermute(value, ('row', 'col'), pairs)]
    ppermute x1, waiting for transfers between devices: 6.19 us -> 0.99 us  [to_columns(): return lax.ppermute(value, ('row', 'col'), pairs)]
    ppermute x1, waiting for transfers between devices: 0.01 us -> 4.9 us  [send_far(): return lax.ppermute(value, ('row', 'col'), pairs)]
    ppermute x1 -> x4, starting transfers between devices: 1.37 us -> 5.28 us  [the longest x1 3.25 us: gather_all(): lax.ppermute(pivot, 'row', [(1, 0)])]
  transfers between devices with their start and end apart: 24 -> 30, of which waited for: 11 -> 13; matrix products, arithmetic and copies ran while one was open for 1% -> 1% of each run, Pallas kernels for 1% -> 2%
where the time goes in v5:
time: 125 us
  starting transfers between devices  53.3 us (43%)
  waiting for transfers between devices  41.1 us (33%)
  Pallas kernels  21.5 us (17%)
  other arithmetic  4.11 us (3%)
  local copies, waits for them, and re-layouts  3.81 us (3%)
    ppermute x14, waiting for transfers between devices, shift_plane(): return lax.ppermute(value, ('row', 'col'), pairs)  24.1 us
    pallas_call x1, Pallas kernels, finish(): pl.pallas_call(last_kernel, out_shape=(jax.ShapeDtypeStruct((TR, LINES, H...  18.7 us
    ppermute x14, starting transfers between devices, shift_plane(): return lax.ppermute(value, ('row', 'col'), pairs)  12 us
    ppermute x2, starting transfers between devices, shift_y(): return lax.ppermute(value, 'row', pairs)  10.9 us
    ppermute x1, starting transfers between devices, send_far(): return lax.ppermute(value, ('row', 'col'), pairs)  6.35 us
    ppermute x1, starting transfers between devices, gather_all(): lax.ppermute(pivot, ('row', 'col'), corner)  6.34 us
    ppermute x1, waiting for transfers between devices, send_far(): return lax.ppermute(value, ('row', 'col'), pairs)  4.9 us
    ppermute x1, starting transfers between devices, gather_all(): lax.ppermute(pivot, 'row', [(1, 7)])  4.73 us
  transfers between devices with their start and end apart: 30, of which 13 were waited for; matrix products, arithmetic and copies ran while one was open for 1% of the time, Pallas kernels for 2%

profile of v5, /device:TPU:1, one launch (start us, length us, event | category | flops | bytes accessed | tf_op | source)
XLA Modules:
  0.0 124.8 jit_solution(8179063338396007304)
XLA Ops:
  0.6 1.6 %slice-done = f32[8,256,1,256]{3,2,1,0:T(1,128)S(1)} async-done(((f32[8,256,4,256]{3,2,1,0:T(4,128)}), f32[8,256,1,256]{3,2,1,0:T(1,128)S(1)}, s32[]{:S(2)}) %slice-start) | async-done | bytes 2097176 | tf_op jit(solution)/shard_map/slice | solution.py:379
  3.6 6.3 %collective-permute-start.2 = (f32[512,256]{1,0:T(8,128)}, f32[512,256]{1,0:T(8,128)S(1)}, u32[]{:S(2)}, u32[]{:S(2)}) collective-permute-start(f32[512,256]{1,0:T(8,128)} %get-tuple-element.66), channel_id=1, source_target_pairs={{0,8},{1,9},{16,18},{17,19},{32,40},{33,41},{48,50},{49,51},{64,72... | collective-permute-start | bytes 1572872 | tf_op jit(solution)/shard_map/ppermute | solution.py:65
  10.1 1.5 %collective-permute-start = (f32[512,256]{1,0:T(8,128)}, f32[512,256]{1,0:T(8,128)}, u32[]{:S(2)}, u32[]{:S(2)}) collective-permute-start(f32[512,256]{1,0:T(8,128)} %get-tuple-element.68), channel_id=1, source_target_pairs={{0,4},{1,5},{2,6},{3,7},{4,8},{5,9},{6,10},{7,11},{8,12},{9,13},{1... | collective-permute-start | bytes 1572872 | tf_op jit(solution)/shard_map/ppermute | solution.py:48
  11.5 4.9 %collective-permute-done.2 = f32[512,256]{1,0:T(8,128)S(1)} collective-permute-done((f32[512,256]{1,0:T(8,128)}, f32[512,256]{1,0:T(8,128)S(1)}, u32[]{:S(2)}, u32[]{:S(2)}) %collective-permute-start.2) | collective-permute-done | bytes 524320 | tf_op jit(solution)/shard_map/ppermute | solution.py:65
  16.4 6.7 %collective-permute-done.1 = f32[512,256]{1,0:T(8,128)S(1)} collective-permute-done((f32[512,256]{1,0:T(8,128)}, f32[512,256]{1,0:T(8,128)S(1)}, u32[]{:S(2)}, u32[]{:S(2)}) %collective-permute-start.1) | collective-permute-done | bytes 524320 | tf_op jit(solution)/shard_map/ppermute | solution.py:48
  23.9 1.5 %select_select_fusion.2 = (f32[512,256]{1,0:T(8,128)S(1)}, f32[512,256]{1,0:T(8,128)S(1)}) fusion(f32[512,256]{1,0:T(8,128)} %collective-permute-done, f32[512,256]{1,0:T(8,128)} %copy-done.3, f32[512,256]{1,0:T(8,128)} %copy-done.4, f32[2048,256]{1,0:T(8,128)S(1)} %bitcast.12, pred[]{:T(512)S(6)} %eq.68, pred[]{:T(512)S(6)} %eq.67, pred[]{:T(512)S(6)} %eq.66, ...), kind=kLoop, calls=%fused_computation.2 | loop fusion | flops 786432 | bytes 3145734 | tf_op jit(solution)/shard_map/jit(_where)/select_n | solution.py:96
  27.0 2.6 %collective-permute-start.5 = (f32[512,256]{1,0:T(8,128)S(1)}, f32[512,256]{1,0:T(8,128)S(1)}, u32[]{:S(2)}, u32[]{:S(2)}) collective-permute-start(f32[512,256]{1,0:T(8,128)S(1)} %get-tuple-element.63), channel_id=1, source_target_pairs={{0,3},{1,0},{2,1},{3,2},{4,7},{5,4},{6,5},{7,6},{8,11},{9,8},{10,9... | collective-permute-start | bytes 1572872 | tf_op jit(solution)/shard_map/ppermute | solution.py:48
  29.6 4.2 %collective-permute-done.7 = f32[512,256]{1,0:T(8,128)S(1)} collective-permute-done((f32[512,256]{1,0:T(8,128)S(1)}, f32[512,256]{1,0:T(8,128)S(1)}, u32[]{:S(2)}, u32[]{:S(2)}) %collective-permute-start.7) | collective-permute-done | bytes 524320 | tf_op jit(solution)/shard_map/ppermute | solution.py:48
  35.3 5.5 %collective-permute-done.6 = f32[512,256]{1,0:T(8,128)S(1)} collective-permute-done((f32[512,256]{1,0:T(8,128)S(1)}, f32[512,256]{1,0:T(8,128)S(1)}, u32[]{:S(2)}, u32[]{:S(2)}) %collective-permute-start.6) | collective-permute-done | bytes 524320 | tf_op jit(solution)/shard_map/ppermute | solution.py:48
  40.8 4.3 %collective-permute-done.8 = f32[512,256]{1,0:T(8,128)} collective-permute-done((f32[512,256]{1,0:T(8,128)S(1)}, f32[512,256]{1,0:T(8,128)}, u32[]{:S(2)}, u32[]{:S(2)}) %collective-permute-start.8) | collective-permute-done | bytes 524320 | tf_op jit(solution)/shard_map/ppermute | solution.py:48
  46.3 1.5 %select_select_fusion = (f32[512,256]{1,0:T(8,128)S(1)}, f32[512,256]{1,0:T(8,128)S(1)}) fusion(f32[512,256]{1,0:T(8,128)S(1)} %get-tuple-element.62, f32[512,256]{1,0:T(8,128)} %copy-done.5, f32[512,256]{1,0:T(8,128)} %collective-permute-done.8, f32[512,256]{1,0:T(8,128)S(1)} %collective-permute-done.7, f32[512,256]{1,0:T(8,128)S(1)} %get-tuple-element.63, ...), kind=kLoop, calls=%fused_computation | loop fusion | flops 1310720 | bytes 5242887 | tf_op jit(solution)/shard_map/jit(_where)/select_n | solution.py:126
  47.9 1.9 %collective-permute-start.12 = (f32[512,256]{1,0:T(8,128)S(1)}, f32[512,256]{1,0:T(8,128)}, u32[]{:S(2)}, u32[]{:S(2)}) collective-permute-start(f32[512,256]{1,0:T(8,128)S(1)} %get-tuple-element.41.refs_0_), channel_id=1, source_target_pairs={{0,12},{1,13},{2,14},{3,15},{4,0},{5,1},{6,2},{7,3},{8,4},{9,5},{1... | collective-permute-start | bytes 1572872 | tf_op jit(solution)/shard_map/ppermute | solution.py:48
  51.3 3.4 %collective-permute-start.14 = (f32[256,256]{1,0:T(8,128)S(1)}, f32[256,256]{1,0:T(8,128)S(1)}, u32[]{:S(2)}, u32[]{:S(2)}) collective-permute-start(f32[256,256]{1,0:T(8,128)S(1)} %get-tuple-element.43), channel_id=1, source_target_pairs={{0,0},{1,8},{2,16},{3,24},{4,32},{5,40},{6,48},{7,56},{8,64},{9,72... | collective-permute-start | bytes 786440 | tf_op jit(solution)/shard_map/ppermute | solution.py:87
  54.6 6.3 %collective-permute-start.18 = (f32[256,256]{1,0:T(8,128)S(1)}, f32[256,256]{1,0:T(8,128)S(1)}, u32[]{:S(2)}, u32[]{:S(2)}) collective-permute-start(f32[256,256]{1,0:T(8,128)S(1)} %get-tuple-element.44), channel_id=1, source_target_pairs={{16,18},{20,22},{24,26},{28,30}} | collective-permute-start | bytes 786440 | tf_op jit(solution)/shard_map/ppermute | solution.py:138
  62.0 3.8 %collective-permute-done.18 = f32[256,256]{1,0:T(8,128)S(1)} collective-permute-done((f32[256,256]{1,0:T(8,128)S(1)}, f32[256,256]{1,0:T(8,128)S(1)}, u32[]{:S(2)}, u32[]{:S(2)}) %collective-permute-start.18) | collective-permute-done | bytes 262176 | tf_op jit(solution)/shard_map/ppermute | solution.py:138
  65.8 10.8 %collective-permute-start.16 = (f32[256,256]{1,0:T(8,128)S(1)}, f32[256,256]{1,0:T(8,128)S(1)}, u32[]{:S(2)}, u32[]{:S(2)}) collective-permute-start(f32[256,256]{1,0:T(8,128)S(1)} %collective-permute-done.14.refs_4_), channel_id=1, source_target_pairs={{0,96},{16,112},{32,0},{48,16},{64,32},{80,48},{96,64},{112,80},{1... | collective-permute-start | bytes 786440 | tf_op jit(solution)/shard_map/ppermute | solution.py:70
  79.3 3.2 %collective-permute-start.22 = (f32[256,256]{1,0:T(8,128)S(1)}, f32[256,256]{1,0:T(8,128)S(1)}, u32[]{:S(2)}, u32[]{:S(2)}) collective-permute-start(f32[256,256]{1,0:T(8,128)S(1)} %fusion.1.refs_13_), channel_id=1, source_target_pairs={{16,0},{17,1},{18,2},{19,3},{20,4},{21,5},{22,6},{23,7},{24,8},{25... | collective-permute-start | bytes 786440 | tf_op jit(solution)/shard_map/ppermute | solution.py:148
  82.5 4.7 %collective-permute-start.21 = (f32[256,256]{1,0:T(8,128)S(1)}, f32[256,256]{1,0:T(8,128)S(1)}, u32[]{:S(2)}, u32[]{:S(2)}) collective-permute-start(f32[256,256]{1,0:T(8,128)S(1)} %fusion.1.refs_13_), channel_id=1, source_target_pairs={{16,112},{17,113},{18,114},{19,115},{20,116},{21,117},{22,118},{23... | collective-permute-start | bytes 786440 | tf_op jit(solution)/shard_map/ppermute | solution.py:147
  88.6 1.9 %collective-permute-done.21 = f32[256,256]{1,0:T(8,128)S(1)} collective-permute-done((f32[256,256]{1,0:T(8,128)S(1)}, f32[256,256]{1,0:T(8,128)S(1)}, u32[]{:S(2)}, u32[]{:S(2)}) %collective-permute-start.21) | collective-permute-done | bytes 262176 | tf_op jit(solution)/shard_map/ppermute | solution.py:147
  93.3 2.5 %collective-permute-start.23 = (f32[256,256]{1,0:T(8,128)S(1)}, f32[256,256]{1,0:T(8,128)S(1)}, u32[]{:S(2)}, u32[]{:S(2)}) collective-permute-start(f32[256,256]{1,0:T(8,128)S(1)} %broadcast_select_fusion), channel_id=1, source_target_pairs={{0,32},{16,112},{32,64},{48,16},{64,96},{80,48},{96,0},{112,80},{1... | collective-permute-start | bytes 786440 | tf_op jit(solution)/shard_map/ppermute | solution.py:92
  96.4 4.0 %collective-permute-done.23.refs_6_ = f32[256,256]{1,0:T(8,128)S(1)} collective-permute-done((f32[256,256]{1,0:T(8,128)S(1)}, f32[256,256]{1,0:T(8,128)S(1)}, u32[]{:S(2)}, u32[]{:S(2)}) %collective-permute-start.23) | collective-permute-done | bytes 262176 | tf_op jit(solution)/shard_map/ppermute | solution.py:92
  101.1 2.7 %solve_first.1 = (bf16[8,256,256]{2,1,0:T(8,128)(2,1)S(1)}, bf16[8,256,256]{2,1,0:T(8,128)(2,1)S(1)}) custom-call(f32[512,256]{1,0:T(8,128)S(1)} %get-tuple-element.42.refs_0_, f32[512,256]{1,0:T(8,128)S(1)} %collective-permute-done.10.refs_1_, f32[512,256]{1,0:T(8,128)} %collective-permute-done.11.refs_2_, f32[512,256]{1,0:T(8,128)S(1)} %collective-permute-done.19.refs_3_, ...), custom_call_target="tpu_custom_call" | custom-call | flops 805306368 | bytes 4194304 | tf_op jit(solution)/shard_map/solve_first/pallas_call | solution.py:221
  103.8 2.1 %collective-permute-done.9.refs_1_ = f32[512,256]{1,0:T(8,128)S(1)} collective-permute-done((f32[512,256]{1,0:T(8,128)S(1)}, f32[512,256]{1,0:T(8,128)S(1)}, u32[]{:S(2)}, u32[]{:S(2)}) %collective-permute-start.9) | collective-permute-done | bytes 524320 | tf_op jit(solution)/shard_map/ppermute | solution.py:48
  105.9 18.7 %solve_and_update.1 = (f32[8,2048,128]{2,1,0:T(8,128)}, f32[8,256,256]{2,1,0:T(8,128)}) custom-call(f32[512,256]{1,0:T(8,128)S(1)} %get-tuple-element.41.refs_0_, f32[512,256]{1,0:T(8,128)S(1)} %collective-permute-done.9.refs_1_, f32[512,256]{1,0:T(8,128)} %collective-permute-done.13.refs_2_, f32[512,256]{1,0:T(8,128)} %collective-permute-done.12.refs_3_, ...), custom_call_target="tpu_custom_call" | custom-call | flops 6710886400 | bytes 20971520 | tf_op jit(solution)/shard_map/solve_and_update/pallas_call | solution.py:342
  (64 shorter events, 16.8 us)
Async XLA Ops:
  3.6 12.8 %collective-permute-start.2 = (f32[512,256]{1,0:T(8,128)}, f32[512,256]{1,0:T(8,128)S(1)}, u32[]{:S(2)}, u32[]{:S(2)}) collective-permute-start(f32[512,256]{1,0:T(8,128)} %get-tuple-element.66), channel_id=1, source_target_pairs={{0,8},{1,9},{16,18},{17,19},{32,40},{33,41},{48,50},{49,51},{64,72... | collective-permute-start | bytes 1572872 | tf_op jit(solution)/shard_map/ppermute | solution.py:65
  10.0 13.1 %collective-permute-start.1 = (f32[512,256]{1,0:T(8,128)}, f32[512,256]{1,0:T(8,128)S(1)}, u32[]{:S(2)}, u32[]{:S(2)}) collective-permute-start(f32[512,256]{1,0:T(8,128)} %get-tuple-element.67), channel_id=1, source_target_pairs={{0,12},{1,13},{2,14},{3,15},{4,0},{5,1},{6,2},{7,3},{8,4},{9,5},{1... | collective-permute-start | bytes 1572872 | tf_op jit(solution)/shard_map/ppermute | solution.py:48
  10.1 13.8 %collective-permute-start = (f32[512,256]{1,0:T(8,128)}, f32[512,256]{1,0:T(8,128)}, u32[]{:S(2)}, u32[]{:S(2)}) collective-permute-start(f32[512,256]{1,0:T(8,128)} %get-tuple-element.68), channel_id=1, source_target_pairs={{0,4},{1,5},{2,6},{3,7},{4,8},{5,9},{6,10},{7,11},{8,12},{9,13},{1... | collective-permute-start | bytes 1572872 | tf_op jit(solution)/shard_map/ppermute | solution.py:48
  25.4 8.4 %collective-permute-start.7 = (f32[512,256]{1,0:T(8,128)S(1)}, f32[512,256]{1,0:T(8,128)S(1)}, u32[]{:S(2)}, u32[]{:S(2)}) collective-permute-start(f32[512,256]{1,0:T(8,128)S(1)} %get-tuple-element.62), channel_id=1, source_target_pairs={{0,3},{1,0},{2,1},{3,2},{4,7},{5,4},{6,5},{7,6},{8,11},{9,8},{10,9... | collective-permute-start | bytes 1572872 | tf_op jit(solution)/shard_map/ppermute | solution.py:48
  25.5 9.6 %collective-permute-start.3 = (f32[512,256]{1,0:T(8,128)S(1)}, f32[512,256]{1,0:T(8,128)S(1)}, u32[]{:S(2)}, u32[]{:S(2)}) collective-permute-start(f32[512,256]{1,0:T(8,128)S(1)} %get-tuple-element.63), channel_id=1, source_target_pairs={{0,1},{1,2},{2,3},{3,0},{4,5},{5,6},{6,7},{7,4},{8,9},{9,10},{10,1... | collective-permute-start | bytes 1572872 | tf_op jit(solution)/shard_map/ppermute | solution.py:48
  26.9 13.9 %collective-permute-start.6 = (f32[512,256]{1,0:T(8,128)S(1)}, f32[512,256]{1,0:T(8,128)S(1)}, u32[]{:S(2)}, u32[]{:S(2)}) collective-permute-start(f32[512,256]{1,0:T(8,128)S(1)} %get-tuple-element.62), channel_id=1, source_target_pairs={{0,1},{1,2},{2,3},{3,0},{4,5},{5,6},{6,7},{7,4},{8,9},{9,10},{10,1... | collective-permute-start | bytes 1572872 | tf_op jit(solution)/shard_map/ppermute | solution.py:48
  27.0 13.8 %collective-permute-start.5 = (f32[512,256]{1,0:T(8,128)S(1)}, f32[512,256]{1,0:T(8,128)S(1)}, u32[]{:S(2)}, u32[]{:S(2)}) collective-permute-start(f32[512,256]{1,0:T(8,128)S(1)} %get-tuple-element.63), channel_id=1, source_target_pairs={{0,3},{1,0},{2,1},{3,2},{4,7},{5,4},{6,5},{7,6},{8,11},{9,8},{10,9... | collective-permute-start | bytes 1572872 | tf_op jit(solution)/shard_map/ppermute | solution.py:48
  33.8 11.3 %collective-permute-start.8 = (f32[512,256]{1,0:T(8,128)S(1)}, f32[512,256]{1,0:T(8,128)}, u32[]{:S(2)}, u32[]{:S(2)}) collective-permute-start(f32[512,256]{1,0:T(8,128)S(1)} %collective-permute-done.7), channel_id=1, source_target_pairs={{0,3},{1,0},{2,1},{3,2},{4,7},{5,4},{6,5},{7,6},{8,11},{9,8},{10,9... | collective-permute-start | bytes 1572872 | tf_op jit(solution)/shard_map/ppermute | solution.py:48
  35.1 11.2 %collective-permute-start.4 = (f32[512,256]{1,0:T(8,128)S(1)}, f32[512,256]{1,0:T(8,128)}, u32[]{:S(2)}, u32[]{:S(2)}) collective-permute-start(f32[512,256]{1,0:T(8,128)S(1)} %collective-permute-done.3), channel_id=1, source_target_pairs={{0,1},{1,2},{2,3},{3,0},{4,5},{5,6},{6,7},{7,4},{8,9},{9,10},{10,1... | collective-permute-start | bytes 1572872 | tf_op jit(solution)/shard_map/ppermute | solution.py:48
  47.9 28.8 %collective-permute-start.12 = (f32[512,256]{1,0:T(8,128)S(1)}, f32[512,256]{1,0:T(8,128)}, u32[]{:S(2)}, u32[]{:S(2)}) collective-permute-start(f32[512,256]{1,0:T(8,128)S(1)} %get-tuple-element.41.refs_0_), channel_id=1, source_target_pairs={{0,12},{1,13},{2,14},{3,15},{4,0},{5,1},{6,2},{7,3},{8,4},{9,5},{1... | collective-permute-start | bytes 1572872 | tf_op jit(solution)/shard_map/ppermute | solution.py:48
  49.8 26.9 %collective-permute-start.19 = (f32[512,256]{1,0:T(8,128)S(1)}, f32[512,256]{1,0:T(8,128)S(1)}, u32[]{:S(2)}, u32[]{:S(2)}) collective-permute-start(f32[512,256]{1,0:T(8,128)S(1)} %get-tuple-element.42.refs_0_), channel_id=1, source_target_pairs={{0,12},{1,13},{2,14},{3,15},{4,0},{5,1},{6,2},{7,3},{8,4},{9,5},{1... | collective-permute-start | bytes 1572872 | tf_op jit(solution)/shard_map/ppermute | solution.py:48
  49.9 26.9 %collective-permute-start.10 = (f32[512,256]{1,0:T(8,128)S(1)}, f32[512,256]{1,0:T(8,128)S(1)}, u32[]{:S(2)}, u32[]{:S(2)}) collective-permute-start(f32[512,256]{1,0:T(8,128)S(1)} %get-tuple-element.42.refs_0_), channel_id=1, source_target_pairs={{0,4},{1,5},{2,6},{3,7},{4,8},{5,9},{6,10},{7,11},{8,12},{9,13},{1... | collective-permute-start | bytes 1572872 | tf_op jit(solution)/shard_map/ppermute | solution.py:48
  51.3 10.7 %collective-permute-start.14 = (f32[256,256]{1,0:T(8,128)S(1)}, f32[256,256]{1,0:T(8,128)S(1)}, u32[]{:S(2)}, u32[]{:S(2)}) collective-permute-start(f32[256,256]{1,0:T(8,128)S(1)} %get-tuple-element.43), channel_id=1, source_target_pairs={{0,0},{1,8},{2,16},{3,24},{4,32},{5,40},{6,48},{7,56},{8,64},{9,72... | collective-permute-start | bytes 786440 | tf_op jit(solution)/shard_map/ppermute | solution.py:87
  54.6 11.2 %collective-permute-start.18 = (f32[256,256]{1,0:T(8,128)S(1)}, f32[256,256]{1,0:T(8,128)S(1)}, u32[]{:S(2)}, u32[]{:S(2)}) collective-permute-start(f32[256,256]{1,0:T(8,128)S(1)} %get-tuple-element.44), channel_id=1, source_target_pairs={{16,18},{20,22},{24,26},{28,30}} | collective-permute-start | bytes 786440 | tf_op jit(solution)/shard_map/ppermute | solution.py:138
  62.0 17.3 %collective-permute-start.17 = (f32[256,256]{1,0:T(8,128)S(1)}, f32[256,256]{1,0:T(8,128)}, u32[]{:S(2)}, u32[]{:S(2)}) collective-permute-start(f32[256,256]{1,0:T(8,128)S(1)} %collective-permute-done.14.refs_4_), channel_id=1, source_target_pairs={{0,16},{16,0},{32,48},{48,32},{64,80},{80,64},{96,112},{112,96},{1... | collective-permute-start | bytes 786440 | tf_op jit(solution)/shard_map/ppermute | solution.py:74
  65.8 16.7 %collective-permute-start.16 = (f32[256,256]{1,0:T(8,128)S(1)}, f32[256,256]{1,0:T(8,128)S(1)}, u32[]{:S(2)}, u32[]{:S(2)}) collective-permute-start(f32[256,256]{1,0:T(8,128)S(1)} %collective-permute-done.14.refs_4_), channel_id=1, source_target_pairs={{0,96},{16,112},{32,0},{48,16},{64,32},{80,48},{96,64},{112,80},{1... | collective-permute-start | bytes 786440 | tf_op jit(solution)/shard_map/ppermute | solution.py:70
  76.7 10.6 %collective-permute-start.15 = (f32[256,256]{1,0:T(8,128)S(1)}, f32[256,256]{1,0:T(8,128)S(1)}, u32[]{:S(2)}, u32[]{:S(2)}) collective-permute-start(f32[256,256]{1,0:T(8,128)S(1)} %collective-permute-done.14.refs_4_), channel_id=1, source_target_pairs={{0,32},{16,48},{32,64},{48,80},{64,96},{80,112},{96,0},{112,16},{1... | collective-permute-start | bytes 786440 | tf_op jit(solution)/shard_map/ppermute | solution.py:70
  76.7 15.2 %collective-permute-start.13 = (f32[512,256]{1,0:T(8,128)}, f32[512,256]{1,0:T(8,128)}, u32[]{:S(2)}, u32[]{:S(2)}) collective-permute-start(f32[512,256]{1,0:T(8,128)} %collective-permute-done.12.refs_3_), channel_id=1, source_target_pairs={{0,12},{1,13},{2,14},{3,15},{4,0},{5,1},{6,2},{7,3},{8,4},{9,5},{1... | collective-permute-start | bytes 1572872 | tf_op jit(solution)/shard_map/ppermute | solution.py:48
  76.8 15.1 %collective-permute-start.11 = (f32[512,256]{1,0:T(8,128)S(1)}, f32[512,256]{1,0:T(8,128)}, u32[]{:S(2)}, u32[]{:S(2)}) collective-permute-start(f32[512,256]{1,0:T(8,128)S(1)} %collective-permute-done.10.refs_1_), channel_id=1, source_target_pairs={{0,4},{1,5},{2,6},{3,7},{4,8},{5,9},{6,10},{7,11},{8,12},{9,13},{1... | collective-permute-start | bytes 1572872 | tf_op jit(solution)/shard_map/ppermute | solution.py:48
  79.3 9.3 %collective-permute-start.22 = (f32[256,256]{1,0:T(8,128)S(1)}, f32[256,256]{1,0:T(8,128)S(1)}, u32[]{:S(2)}, u32[]{:S(2)}) collective-permute-start(f32[256,256]{1,0:T(8,128)S(1)} %fusion.1.refs_13_), channel_id=1, source_target_pairs={{16,0},{17,1},{18,2},{19,3},{20,4},{21,5},{22,6},{23,7},{24,8},{25... | collective-permute-start | bytes 786440 | tf_op jit(solution)/shard_map/ppermute | solution.py:148
  82.5 8.0 %collective-permute-start.21 = (f32[256,256]{1,0:T(8,128)S(1)}, f32[256,256]{1,0:T(8,128)S(1)}, u32[]{:S(2)}, u32[]{:S(2)}) collective-permute-start(f32[256,256]{1,0:T(8,128)S(1)} %fusion.1.refs_13_), channel_id=1, source_target_pairs={{16,112},{17,113},{18,114},{19,115},{20,116},{21,117},{22,118},{23... | collective-permute-start | bytes 786440 | tf_op jit(solution)/shard_map/ppermute | solution.py:147
  93.3 7.0 %collective-permute-start.23 = (f32[256,256]{1,0:T(8,128)S(1)}, f32[256,256]{1,0:T(8,128)S(1)}, u32[]{:S(2)}, u32[]{:S(2)}) collective-permute-start(f32[256,256]{1,0:T(8,128)S(1)} %broadcast_select_fusion), channel_id=1, source_target_pairs={{0,32},{16,112},{32,64},{48,16},{64,96},{80,48},{96,0},{112,80},{1... | collective-permute-start | bytes 786440 | tf_op jit(solution)/shard_map/ppermute | solution.py:92
  96.4 9.5 %collective-permute-start.9 = (f32[512,256]{1,0:T(8,128)S(1)}, f32[512,256]{1,0:T(8,128)S(1)}, u32[]{:S(2)}, u32[]{:S(2)}) collective-permute-start(f32[512,256]{1,0:T(8,128)S(1)} %get-tuple-element.41.refs_0_), channel_id=1, source_target_pairs={{0,4},{1,5},{2,6},{3,7},{4,8},{5,9},{6,10},{7,11},{8,12},{9,13},{1... | collective-permute-start | bytes 1572872 | tf_op jit(solution)/shard_map/ppermute | solution.py:48
  100.3 5.6 %collective-permute-start.28 = (f32[256,256]{1,0:T(8,128)S(1)}, f32[256,256]{1,0:T(8,128)S(1)}, u32[]{:S(2)}, u32[]{:S(2)}) collective-permute-start(f32[256,256]{1,0:T(8,128)S(1)} %collective-permute-done.23.refs_6_), channel_id=1, source_target_pairs={{0,16},{16,0},{32,48},{48,32},{64,80},{80,64},{96,112},{112,96},{1... | collective-permute-start | bytes 786440 | tf_op jit(solution)/shard_map/ppermute | solution.py:74
  (15 other events, 150.0 us)

commit v6 on v5

--- a/solution.py
+++ b/solution.py
@@ -133,16 +133,27 @@
     block1, block2, tile, pivot = barrier((block1, block2, tile, block1[:NB]))
 
     corner = [(N_COL + SIDE * a, N_COL + SIDE * a + 2) for a in range(SIDE)]
+    own, pivot_near, pivot_back, pivot_far = barrier((
+        to_columns(tile),
+        shift_line(pivot, 1),
+        shift_line(pivot, -1),
+        lax.ppermute(pivot, ("row", "col"), corner),
+    ))
+    pivot = choose(z, pivot, pivot_near, pivot_far, pivot_back)
+    block1, block2, own, pivot = barrier((block1, block2, own, pivot))
+
     near1, back2 = shift_line(block1, 1), shift_line(block2, -1)
     back1, near2 = shift_line(block1, -1), shift_line(block2, 1)
-    own, pivot_far = to_columns(tile), lax.ppermute(pivot, ("row", "col"), corner)
-    pivot = choose(z, pivot, near1[:NB], pivot_far, back1[:NB])
-    far1, far2, up, down, own_other, pivot_up, pivot_down, pivot_swap = barrier((
+    own_other = swap_core(own)
+    near1, back2, own, pivot = barrier((near1, back2, own, pivot))
+    far1, far2, back1, near2, own_other, up, down, pivot_up, pivot_down, pivot_swap = barrier((
         shift_line(near1, 1),
         shift_line(back2, -1),
+        back1,
+        near2,
+        own_other,
         shift_y(own, 1),
         shift_y(own, -1),
-        swap_core(own),
         lax.ppermute(pivot, "row", [(1, 3)]),
         lax.ppermute(pivot, "row", [(1, 7)]),
         lax.ppermute(pivot, "row", [(1, 0)]),
@@ -272,13 +283,6 @@
         rest = dot(jnp.concatenate([high, low], axis=1), rest_weights)
         return jnp.where(code == 2, 0.0, full + jnp.where(code == 0, rest, 0.0))
 
-    def row(p, carry):
-        tile = raw[rows_at(p, NB), :] - used(row_high1[p], row_low1[p], band[p * N_ROW + r, 1])
-        solved = dot3(tile, weights1)
-        raw[rows_at(p, NB), :] = solved
-        row_high2[p], row_low2[p] = split(solved)
-        return carry
-
     def column(q, carry):
         first = dot3(raw_cols[0, rows_at(q, NB), :], weights0)
         col_high[q, :NB, :], col_low[q, :NB, :] = split(first.T)
@@ -287,15 +291,20 @@
         col_high[q, NB:, :], col_low[q, NB:, :] = split(dot3(tile, weights1).T)
         return carry
 
+    panels = [pltpu.make_async_copy(raw.at[pl.ds(p * NB, NB), :], panel.at[p], panel_sems.at[p]) for p in range(TR)]
+
+    def solve(p):
+        at = pl.ds(p * NB, NB)
+        tile = raw[at, :] - used(row_high1[p], row_low1[p], band[p * N_ROW + r, 1])
+        solved = dot3(tile, weights1)
+        raw[at, :] = solved
+        row_high2[p], row_low2[p] = split(solved)
+
+    for copy in col_copies:
+        copy.wait()
+    lax.fori_loop(0, TC, column, 0, unroll=2)
     for copy in small[2:] + copies:
         copy.wait()
-    lax.fori_loop(0, TR, row, 0, unroll=4)
-    panels = [pltpu.make_async_copy(raw.at[pl.ds(p * NB, NB), :], panel.at[p], panel_sems.at[p]) for p in range(TR)]
-    for copy in panels:
-        copy.start()
-    for copy in col_copies:
-        copy.wait()
-    lax.fori_loop(0, TC, column, 0, unroll=4)
 
     size = STEP * NB
 
@@ -320,17 +329,22 @@
 
     steps = TR // STEP
     stores = [pltpu.make_async_copy(tiles.at[p], out.at[p], out_sems.at[p]) for p in range(TR)]
-    for step in range(steps + 1):
+    for step in range(-1, steps + 1):
         product, before = (even, odd) if step % 2 == 0 else (odd, even)
-        if step:
+        if step > 0:
             for p in range(STEP):
                 loads[(step - 1) * STEP + p].wait()
         for q in range(TC):
-            if step < steps:
+            if step + 1 < steps and q < STEP:
+                solve((step + 1) * STEP + q)
+            if 0 <= step < steps:
                 multiply(step, q, product)
-            if step:
+            if step > 0:
                 subtract(step - 1, q, before)
-        if step:
+        if step + 1 < steps:
+            for p in range(STEP):
+                panels[(step + 1) * STEP + p].start()
+        if step > 0:
             for p in range(STEP):
                 stores[(step - 1) * STEP + p].start()
     for copy in stores + panels:

time: 125 us -> 126 us (level); the launches traced: 125 us -> 124 us
  Pallas kernels: 21.5 us -> 19.8 us
    ppermute x2, starting transfers between devices: 10.9 us -> 4.57 us  [shift_y(): return lax.ppermute(value, 'row', pairs)]
    ppermute x4, starting transfers between devices: 0.52 us -> 5.61 us  [swap_core(): return lax.ppermute(value, 'row', [(r, r ^ 1) for r in range(N_ROW)])]
    ppermute x14 -> x16, starting transfers between devices: 12 us -> 15.3 us  [shift_plane(): return lax.ppermute(value, ('row', 'col'), pairs)]
    ppermute x14 -> x16, waiting for transfers between devices: 24.1 us -> 26.9 us  [shift_plane(): return lax.ppermute(value, ('row', 'col'), pairs)]
    ppermute x1, starting transfers between devices: 4.73 us -> 2.84 us  [gather_all(): lax.ppermute(pivot, 'row', [(1, 7)])]
    ppermute x1, starting transfers between devices: 3.25 us -> 4.86 us  [gather_all(): lax.ppermute(pivot, 'row', [(1, 0)])]
    ppermute x1, waiting for transfers between devices: 3.83 us -> 2.31 us  [gather_all(): lax.ppermute(pivot, ('row', 'col'), corner)]
  transfers between devices with their start and end apart: 30 -> 32, of which waited for: 13 -> 15; matrix products, arithmetic and copies ran while one was open for 1% -> 0% of each run, Pallas kernels for 2% -> 2%
where the time goes in v6:
time: 126 us; the launch traced here: 124 us
  starting transfers between devices  54.1 us (43%)
  waiting for transfers between devices  41.7 us (33%)
  Pallas kernels  19.8 us (16%)
  local copies, waits for them, and re-layouts  3.8 us (3%)
  other arithmetic  3.16 us (3%)
    ppermute x16, waiting for transfers between devices, shift_plane(): return lax.ppermute(value, ('row', 'col'), pairs)  26.9 us
    pallas_call x1, Pallas kernels, finish(): pl.pallas_call(last_kernel, out_shape=(jax.ShapeDtypeStruct((TR, LINES, H...  17.9 us
    ppermute x16, starting transfers between devices, shift_plane(): return lax.ppermute(value, ('row', 'col'), pairs)  15.3 us
    ppermute x1, starting transfers between devices, send_far(): return lax.ppermute(value, ('row', 'col'), pairs)  6.35 us
    ppermute x1, starting transfers between devices, gather_all(): lax.ppermute(pivot, ('row', 'col'), corner)  6.34 us
    ppermute x4, starting transfers between devices, swap_core(): return lax.ppermute(value, 'row', [(r, r ^ 1) for r in range(N_ROW)])  5.61 us
    ppermute x1, waiting for transfers between devices, send_far(): return lax.ppermute(value, ('row', 'col'), pairs)  4.9 us
    ppermute x1, starting transfers between devices, gather_all(): lax.ppermute(pivot, 'row', [(1, 0)])  4.86 us
  transfers between devices with their start and end apart: 32, of which 15 were waited for; matrix products, arithmetic and copies ran while one was open for 0% of the time, Pallas kernels for 2%

profile of v6, /device:TPU:1, one launch (start us, length us, event | category | flops | bytes accessed | tf_op | source)
XLA Modules:
  0.0 123.6 jit_solution(13377325156955573788)
XLA Ops:
  0.6 1.6 %slice-done = f32[8,256,1,256]{3,2,1,0:T(1,128)S(1)} async-done(((f32[8,256,4,256]{3,2,1,0:T(4,128)}), f32[8,256,1,256]{3,2,1,0:T(1,128)S(1)}, s32[]{:S(2)}) %slice-start) | async-done | bytes 2097176 | tf_op jit(solution)/shard_map/slice | solution.py:393
  3.6 6.3 %collective-permute-start.2 = (f32[512,256]{1,0:T(8,128)}, f32[512,256]{1,0:T(8,128)S(1)}, u32[]{:S(2)}, u32[]{:S(2)}) collective-permute-start(f32[512,256]{1,0:T(8,128)} %get-tuple-element.94), channel_id=1, source_target_pairs={{0,8},{1,9},{16,18},{17,19},{32,40},{33,41},{48,50},{49,51},{64,72... | collective-permute-start | bytes 1572872 | tf_op jit(solution)/shard_map/ppermute | solution.py:65
  11.5 4.9 %collective-permute-done.2 = f32[512,256]{1,0:T(8,128)S(1)} collective-permute-done((f32[512,256]{1,0:T(8,128)}, f32[512,256]{1,0:T(8,128)S(1)}, u32[]{:S(2)}, u32[]{:S(2)}) %collective-permute-start.2) | collective-permute-done | bytes 524320 | tf_op jit(solution)/shard_map/ppermute | solution.py:65
  16.4 6.7 %collective-permute-done.1 = f32[512,256]{1,0:T(8,128)S(1)} collective-permute-done((f32[512,256]{1,0:T(8,128)}, f32[512,256]{1,0:T(8,128)S(1)}, u32[]{:S(2)}, u32[]{:S(2)}) %collective-permute-start.1) | collective-permute-done | bytes 524320 | tf_op jit(solution)/shard_map/ppermute | solution.py:48
  23.9 1.5 %select_select_fusion.2 = (f32[512,256]{1,0:T(8,128)S(1)}, f32[512,256]{1,0:T(8,128)S(1)}) fusion(f32[512,256]{1,0:T(8,128)} %collective-permute-done, f32[512,256]{1,0:T(8,128)} %copy-done.2, f32[512,256]{1,0:T(8,128)} %copy-done.3, f32[2048,256]{1,0:T(8,128)S(1)} %bitcast.12, pred[]{:T(512)S(6)} %eq.68, pred[]{:T(512)S(6)} %eq.67, pred[]{:T(512)S(6)} %eq.66, ...), kind=kLoop, calls=%fused_computation.2 | loop fusion | flops 786432 | bytes 3145734 | tf_op jit(solution)/shard_map/jit(_where)/select_n | solution.py:96
  27.0 2.6 %collective-permute-start.5 = (f32[512,256]{1,0:T(8,128)S(1)}, f32[512,256]{1,0:T(8,128)S(1)}, u32[]{:S(2)}, u32[]{:S(2)}) collective-permute-start(f32[512,256]{1,0:T(8,128)S(1)} %get-tuple-element.91), channel_id=1, source_target_pairs={{0,3},{1,0},{2,1},{3,2},{4,7},{5,4},{6,5},{7,6},{8,11},{9,8},{10,9... | collective-permute-start | bytes 1572872 | tf_op jit(solution)/shard_map/ppermute | solution.py:48
  29.6 4.2 %collective-permute-done.7 = f32[512,256]{1,0:T(8,128)S(1)} collective-permute-done((f32[512,256]{1,0:T(8,128)S(1)}, f32[512,256]{1,0:T(8,128)S(1)}, u32[]{:S(2)}, u32[]{:S(2)}) %collective-permute-start.7) | collective-permute-done | bytes 524320 | tf_op jit(solution)/shard_map/ppermute | solution.py:48
  35.3 5.5 %collective-permute-done.6 = f32[512,256]{1,0:T(8,128)S(1)} collective-permute-done((f32[512,256]{1,0:T(8,128)S(1)}, f32[512,256]{1,0:T(8,128)S(1)}, u32[]{:S(2)}, u32[]{:S(2)}) %collective-permute-start.6) | collective-permute-done | bytes 524320 | tf_op jit(solution)/shard_map/ppermute | solution.py:48
  40.8 4.3 %collective-permute-done.8 = f32[512,256]{1,0:T(8,128)} collective-permute-done((f32[512,256]{1,0:T(8,128)S(1)}, f32[512,256]{1,0:T(8,128)}, u32[]{:S(2)}, u32[]{:S(2)}) %collective-permute-start.8) | collective-permute-done | bytes 524320 | tf_op jit(solution)/shard_map/ppermute | solution.py:48
  47.8 2.3 %collective-permute-start.9 = (f32[256,256]{1,0:T(8,128)S(1)}, f32[256,256]{1,0:T(8,128)S(1)}, u32[]{:S(2)}, u32[]{:S(2)}) collective-permute-start(f32[256,256]{1,0:T(8,128)S(1)} %get-tuple-element.57), channel_id=1, source_target_pairs={{0,0},{1,8},{2,16},{3,24},{4,32},{5,40},{6,48},{7,56},{8,64},{9,72... | collective-permute-start | bytes 786440 | tf_op jit(solution)/shard_map/ppermute | solution.py:87
  50.2 6.3 %collective-permute-start.12 = (f32[256,256]{1,0:T(8,128)S(1)}, f32[256,256]{1,0:T(8,128)S(1)}, u32[]{:S(2)}, u32[]{:S(2)}) collective-permute-start(f32[256,256]{1,0:T(8,128)S(1)} %get-tuple-element.58), channel_id=1, source_target_pairs={{16,18},{20,22},{24,26},{28,30}} | collective-permute-start | bytes 786440 | tf_op jit(solution)/shard_map/ppermute | solution.py:140
  58.1 2.3 %collective-permute-done.12 = f32[256,256]{1,0:T(8,128)S(1)} collective-permute-done((f32[256,256]{1,0:T(8,128)S(1)}, f32[256,256]{1,0:T(8,128)S(1)}, u32[]{:S(2)}, u32[]{:S(2)}) %collective-permute-start.12) | collective-permute-done | bytes 262176 | tf_op jit(solution)/shard_map/ppermute | solution.py:140
  60.4 1.8 %collective-permute-done.11 = f32[256,256]{1,0:T(8,128)S(1)} collective-permute-done((f32[256,256]{1,0:T(8,128)S(1)}, f32[256,256]{1,0:T(8,128)S(1)}, u32[]{:S(2)}, u32[]{:S(2)}) %collective-permute-start.11) | collective-permute-done | bytes 262176 | tf_op jit(solution)/shard_map/ppermute | solution.py:48
  63.3 1.7 %collective-permute-start.14 = (f32[512,256]{1,0:T(8,128)S(1)}, f32[512,256]{1,0:T(8,128)S(1)}, u32[]{:S(2)}, u32[]{:S(2)}) collective-permute-start(f32[512,256]{1,0:T(8,128)S(1)} %get-tuple-element.63.refs_0_), channel_id=1, source_target_pairs={{0,12},{1,13},{2,14},{3,15},{4,0},{5,1},{6,2},{7,3},{8,4},{9,5},{1... | collective-permute-start | bytes 1572872 | tf_op jit(solution)/shard_map/ppermute | solution.py:48
  68.3 5.1 %collective-permute-start.19 = (f32[256,256]{1,0:T(8,128)S(1)}, f32[256,256]{1,0:T(8,128)S(1)}, u32[]{:S(2)}, u32[]{:S(2)}) collective-permute-start(f32[256,256]{1,0:T(8,128)S(1)} %collective-permute-done.9.refs_4_), channel_id=1, source_target_pairs={{0,16},{16,0},{32,48},{48,32},{64,80},{80,64},{96,112},{112,96},{1... | collective-permute-start | bytes 786440 | tf_op jit(solution)/shard_map/ppermute | solution.py:74
  74.5 4.6 %collective-permute-start.21 = (f32[256,256]{1,0:T(8,128)S(1)}, f32[256,256]{1,0:T(8,128)S(1)}, u32[]{:S(2)}, u32[]{:S(2)}) collective-permute-start(f32[256,256]{1,0:T(8,128)S(1)} %collective-permute-done.9.refs_4_), channel_id=1, source_target_pairs={{0,96},{16,112},{32,0},{48,16},{64,32},{80,48},{96,64},{112,80},{1... | collective-permute-start | bytes 786440 | tf_op jit(solution)/shard_map/ppermute | solution.py:70
  80.1 1.6 %collective-permute-start.16 = (f32[512,256]{1,0:T(8,128)S(1)}, f32[512,256]{1,0:T(8,128)S(1)}, u32[]{:S(2)}, u32[]{:S(2)}) collective-permute-start(f32[512,256]{1,0:T(8,128)S(1)} %collective-permute-done.14.refs_3_), channel_id=1, source_target_pairs={{0,12},{1,13},{2,14},{3,15},{4,0},{5,1},{6,2},{7,3},{8,4},{9,5},{1... | collective-permute-start | bytes 1572872 | tf_op jit(solution)/shard_map/ppermute | solution.py:48
  81.8 4.9 %collective-permute-start.24 = (f32[256,256]{1,0:T(8,128)S(1)}, f32[256,256]{1,0:T(8,128)S(1)}, u32[]{:S(2)}, u32[]{:S(2)}) collective-permute-start(f32[256,256]{1,0:T(8,128)S(1)} %select_select_fusion.4.refs_13_), channel_id=1, source_target_pairs={{16,0},{17,1},{18,2},{19,3},{20,4},{21,5},{22,6},{23,7},{24,8},{25... | collective-permute-start | bytes 786440 | tf_op jit(solution)/shard_map/ppermute | solution.py:159
  86.6 2.8 %collective-permute-start.23 = (f32[256,256]{1,0:T(8,128)S(1)}, f32[256,256]{1,0:T(8,128)S(1)}, u32[]{:S(2)}, u32[]{:S(2)}) collective-permute-start(f32[256,256]{1,0:T(8,128)S(1)} %select_select_fusion.4.refs_13_), channel_id=1, source_target_pairs={{16,112},{17,113},{18,114},{19,115},{20,116},{21,117},{22,118},{23... | collective-permute-start | bytes 786440 | tf_op jit(solution)/shard_map/ppermute | solution.py:158
  90.8 1.9 %collective-permute-done.23 = f32[256,256]{1,0:T(8,128)S(1)} collective-permute-done((f32[256,256]{1,0:T(8,128)S(1)}, f32[256,256]{1,0:T(8,128)S(1)}, u32[]{:S(2)}, u32[]{:S(2)}) %collective-permute-start.23) | collective-permute-done | bytes 262176 | tf_op jit(solution)/shard_map/ppermute | solution.py:158
  95.5 2.5 %collective-permute-start.25 = (f32[256,256]{1,0:T(8,128)S(1)}, f32[256,256]{1,0:T(8,128)S(1)}, u32[]{:S(2)}, u32[]{:S(2)}) collective-permute-start(f32[256,256]{1,0:T(8,128)S(1)} %broadcast_select_fusion), channel_id=1, source_target_pairs={{0,32},{16,112},{32,64},{48,16},{64,96},{80,48},{96,0},{112,80},{1... | collective-permute-start | bytes 786440 | tf_op jit(solution)/shard_map/ppermute | solution.py:92
  98.6 4.3 %collective-permute-done.25.refs_6_ = f32[256,256]{1,0:T(8,128)S(1)} collective-permute-done((f32[256,256]{1,0:T(8,128)S(1)}, f32[256,256]{1,0:T(8,128)S(1)}, u32[]{:S(2)}, u32[]{:S(2)}) %collective-permute-start.25) | collective-permute-done | bytes 262176 | tf_op jit(solution)/shard_map/ppermute | solution.py:92
  103.6 1.9 %solve_first.1 = (bf16[8,256,256]{2,1,0:T(8,128)(2,1)S(1)}, bf16[8,256,256]{2,1,0:T(8,128)(2,1)S(1)}) custom-call(f32[512,256]{1,0:T(8,128)S(1)} %get-tuple-element.64.refs_0_, f32[512,256]{1,0:T(8,128)S(1)} %collective-permute-done.13.refs_1_, f32[512,256]{1,0:T(8,128)S(1)} %collective-permute-done.15.refs_2_, ...), custom_call_target="tpu_custom_call" | custom-call | flops 805306368 | bytes 4194304 | tf_op jit(solution)/shard_map/solve_first/pallas_call | solution.py:232
  105.6 17.9 %solve_and_update.1 = (f32[8,2048,128]{2,1,0:T(8,128)}, f32[8,256,256]{2,1,0:T(8,128)}) custom-call(f32[512,256]{1,0:T(8,128)S(1)} %get-tuple-element.63.refs_0_, f32[512,256]{1,0:T(8,128)S(1)} %collective-permute-done.18.refs_1_, f32[512,256]{1,0:T(8,128)S(1)} %collective-permute-done.16.refs_2_, f32[512,256]{1,0:T(8,128)S(1)} %collective-permute-done.14.refs_3_, ...), custom_call_target="tpu_custom_call" | custom-call | flops 6710886400 | bytes 20971520 | tf_op jit(solution)/shard_map/solve_and_update/pallas_call | solution.py:356
  (64 shorter events, 22.8 us)
Async XLA Ops:
  3.6 12.8 %collective-permute-start.2 = (f32[512,256]{1,0:T(8,128)}, f32[512,256]{1,0:T(8,128)S(1)}, u32[]{:S(2)}, u32[]{:S(2)}) collective-permute-start(f32[512,256]{1,0:T(8,128)} %get-tuple-element.94), channel_id=1, source_target_pairs={{0,8},{1,9},{16,18},{17,19},{32,40},{33,41},{48,50},{49,51},{64,72... | collective-permute-start | bytes 1572872 | tf_op jit(solution)/shard_map/ppermute | solution.py:65
  10.0 13.1 %collective-permute-start.1 = (f32[512,256]{1,0:T(8,128)}, f32[512,256]{1,0:T(8,128)S(1)}, u32[]{:S(2)}, u32[]{:S(2)}) collective-permute-start(f32[512,256]{1,0:T(8,128)} %get-tuple-element.95), channel_id=1, source_target_pairs={{0,12},{1,13},{2,14},{3,15},{4,0},{5,1},{6,2},{7,3},{8,4},{9,5},{1... | collective-permute-start | bytes 1572872 | tf_op jit(solution)/shard_map/ppermute | solution.py:48
  10.1 13.8 %collective-permute-start = (f32[512,256]{1,0:T(8,128)}, f32[512,256]{1,0:T(8,128)}, u32[]{:S(2)}, u32[]{:S(2)}) collective-permute-start(f32[512,256]{1,0:T(8,128)} %get-tuple-element.96), channel_id=1, source_target_pairs={{0,4},{1,5},{2,6},{3,7},{4,8},{5,9},{6,10},{7,11},{8,12},{9,13},{1... | collective-permute-start | bytes 1572872 | tf_op jit(solution)/shard_map/ppermute | solution.py:48
  25.4 8.4 %collective-permute-start.7 = (f32[512,256]{1,0:T(8,128)S(1)}, f32[512,256]{1,0:T(8,128)S(1)}, u32[]{:S(2)}, u32[]{:S(2)}) collective-permute-start(f32[512,256]{1,0:T(8,128)S(1)} %get-tuple-element.90), channel_id=1, source_target_pairs={{0,3},{1,0},{2,1},{3,2},{4,7},{5,4},{6,5},{7,6},{8,11},{9,8},{10,9... | collective-permute-start | bytes 1572872 | tf_op jit(solution)/shard_map/ppermute | solution.py:48
  25.5 9.6 %collective-permute-start.3 = (f32[512,256]{1,0:T(8,128)S(1)}, f32[512,256]{1,0:T(8,128)S(1)}, u32[]{:S(2)}, u32[]{:S(2)}) collective-permute-start(f32[512,256]{1,0:T(8,128)S(1)} %get-tuple-element.91), channel_id=1, source_target_pairs={{0,1},{1,2},{2,3},{3,0},{4,5},{5,6},{6,7},{7,4},{8,9},{9,10},{10,1... | collective-permute-start | bytes 1572872 | tf_op jit(solution)/shard_map/ppermute | solution.py:48
  26.9 13.9 %collective-permute-start.6 = (f32[512,256]{1,0:T(8,128)S(1)}, f32[512,256]{1,0:T(8,128)S(1)}, u32[]{:S(2)}, u32[]{:S(2)}) collective-permute-start(f32[512,256]{1,0:T(8,128)S(1)} %get-tuple-element.90), channel_id=1, source_target_pairs={{0,1},{1,2},{2,3},{3,0},{4,5},{5,6},{6,7},{7,4},{8,9},{9,10},{10,1... | collective-permute-start | bytes 1572872 | tf_op jit(solution)/shard_map/ppermute | solution.py:48
  27.0 13.8 %collective-permute-start.5 = (f32[512,256]{1,0:T(8,128)S(1)}, f32[512,256]{1,0:T(8,128)S(1)}, u32[]{:S(2)}, u32[]{:S(2)}) collective-permute-start(f32[512,256]{1,0:T(8,128)S(1)} %get-tuple-element.91), channel_id=1, source_target_pairs={{0,3},{1,0},{2,1},{3,2},{4,7},{5,4},{6,5},{7,6},{8,11},{9,8},{10,9... | collective-permute-start | bytes 1572872 | tf_op jit(solution)/shard_map/ppermute | solution.py:48
  33.8 11.3 %collective-permute-start.8 = (f32[512,256]{1,0:T(8,128)S(1)}, f32[512,256]{1,0:T(8,128)}, u32[]{:S(2)}, u32[]{:S(2)}) collective-permute-start(f32[512,256]{1,0:T(8,128)S(1)} %collective-permute-done.7), channel_id=1, source_target_pairs={{0,3},{1,0},{2,1},{3,2},{4,7},{5,4},{6,5},{7,6},{8,11},{9,8},{10,9... | collective-permute-start | bytes 1572872 | tf_op jit(solution)/shard_map/ppermute | solution.py:48
  35.1 11.2 %collective-permute-start.4 = (f32[512,256]{1,0:T(8,128)S(1)}, f32[512,256]{1,0:T(8,128)}, u32[]{:S(2)}, u32[]{:S(2)}) collective-permute-start(f32[512,256]{1,0:T(8,128)S(1)} %collective-permute-done.3), channel_id=1, source_target_pairs={{0,1},{1,2},{2,3},{3,0},{4,5},{5,6},{6,7},{7,4},{8,9},{9,10},{10,1... | collective-permute-start | bytes 1572872 | tf_op jit(solution)/shard_map/ppermute | solution.py:48
  47.8 10.2 %collective-permute-start.9 = (f32[256,256]{1,0:T(8,128)S(1)}, f32[256,256]{1,0:T(8,128)S(1)}, u32[]{:S(2)}, u32[]{:S(2)}) collective-permute-start(f32[256,256]{1,0:T(8,128)S(1)} %get-tuple-element.57), channel_id=1, source_target_pairs={{0,0},{1,8},{2,16},{3,24},{4,32},{5,40},{6,48},{7,56},{8,64},{9,72... | collective-permute-start | bytes 786440 | tf_op jit(solution)/shard_map/ppermute | solution.py:87
  50.2 10.2 %collective-permute-start.12 = (f32[256,256]{1,0:T(8,128)S(1)}, f32[256,256]{1,0:T(8,128)S(1)}, u32[]{:S(2)}, u32[]{:S(2)}) collective-permute-start(f32[256,256]{1,0:T(8,128)S(1)} %get-tuple-element.58), channel_id=1, source_target_pairs={{16,18},{20,22},{24,26},{28,30}} | collective-permute-start | bytes 786440 | tf_op jit(solution)/shard_map/ppermute | solution.py:140
  56.6 6.6 %collective-permute-start.10 = (f32[256,256]{1,0:T(8,128)S(1)}, f32[256,256]{1,0:T(8,128)S(1)}, u32[]{:S(2)}, u32[]{:S(2)}) collective-permute-start(f32[256,256]{1,0:T(8,128)S(1)} %get-tuple-element.58), channel_id=1, source_target_pairs={{0,4},{1,5},{2,6},{3,7},{4,8},{5,9},{6,10},{7,11},{8,12},{9,13},{1... | collective-permute-start | bytes 786440 | tf_op jit(solution)/shard_map/ppermute | solution.py:48
  63.3 10.1 %collective-permute-start.14 = (f32[512,256]{1,0:T(8,128)S(1)}, f32[512,256]{1,0:T(8,128)S(1)}, u32[]{:S(2)}, u32[]{:S(2)}) collective-permute-start(f32[512,256]{1,0:T(8,128)S(1)} %get-tuple-element.63.refs_0_), channel_id=1, source_target_pairs={{0,12},{1,13},{2,14},{3,15},{4,0},{5,1},{6,2},{7,3},{8,4},{9,5},{1... | collective-permute-start | bytes 1572872 | tf_op jit(solution)/shard_map/ppermute | solution.py:48
  65.0 9.5 %collective-permute-start.13 = (f32[512,256]{1,0:T(8,128)S(1)}, f32[512,256]{1,0:T(8,128)S(1)}, u32[]{:S(2)}, u32[]{:S(2)}) collective-permute-start(f32[512,256]{1,0:T(8,128)S(1)} %get-tuple-element.64.refs_0_), channel_id=1, source_target_pairs={{0,4},{1,5},{2,6},{3,7},{4,8},{5,9},{6,10},{7,11},{8,12},{9,13},{1... | collective-permute-start | bytes 1572872 | tf_op jit(solution)/shard_map/ppermute | solution.py:48
  65.6 14.5 %collective-permute-start.18 = (f32[512,256]{1,0:T(8,128)S(1)}, f32[512,256]{1,0:T(8,128)S(1)}, u32[]{:S(2)}, u32[]{:S(2)}) collective-permute-start(f32[512,256]{1,0:T(8,128)S(1)} %get-tuple-element.63.refs_0_), channel_id=1, source_target_pairs={{0,4},{1,5},{2,6},{3,7},{4,8},{5,9},{6,10},{7,11},{8,12},{9,13},{1... | collective-permute-start | bytes 1572872 | tf_op jit(solution)/shard_map/ppermute | solution.py:48
  67.0 14.7 %collective-permute-start.17 = (f32[512,256]{1,0:T(8,128)S(1)}, f32[512,256]{1,0:T(8,128)S(1)}, u32[]{:S(2)}, u32[]{:S(2)}) collective-permute-start(f32[512,256]{1,0:T(8,128)S(1)} %get-tuple-element.64.refs_0_), channel_id=1, source_target_pairs={{0,12},{1,13},{2,14},{3,15},{4,0},{5,1},{6,2},{7,3},{8,4},{9,5},{1... | collective-permute-start | bytes 1572872 | tf_op jit(solution)/shard_map/ppermute | solution.py:48
  68.3 10.8 %collective-permute-start.19 = (f32[256,256]{1,0:T(8,128)S(1)}, f32[256,256]{1,0:T(8,128)S(1)}, u32[]{:S(2)}, u32[]{:S(2)}) collective-permute-start(f32[256,256]{1,0:T(8,128)S(1)} %collective-permute-done.9.refs_4_), channel_id=1, source_target_pairs={{0,16},{16,0},{32,48},{48,32},{64,80},{80,64},{96,112},{112,96},{1... | collective-permute-start | bytes 786440 | tf_op jit(solution)/shard_map/ppermute | solution.py:74
  74.5 12.1 %collective-permute-start.21 = (f32[256,256]{1,0:T(8,128)S(1)}, f32[256,256]{1,0:T(8,128)S(1)}, u32[]{:S(2)}, u32[]{:S(2)}) collective-permute-start(f32[256,256]{1,0:T(8,128)S(1)} %collective-permute-done.9.refs_4_), channel_id=1, source_target_pairs={{0,96},{16,112},{32,0},{48,16},{64,32},{80,48},{96,64},{112,80},{1... | collective-permute-start | bytes 786440 | tf_op jit(solution)/shard_map/ppermute | solution.py:70
  79.1 10.4 %collective-permute-start.20 = (f32[256,256]{1,0:T(8,128)S(1)}, f32[256,256]{1,0:T(8,128)S(1)}, u32[]{:S(2)}, u32[]{:S(2)}) collective-permute-start(f32[256,256]{1,0:T(8,128)S(1)} %collective-permute-done.9.refs_4_), channel_id=1, source_target_pairs={{0,32},{16,48},{32,64},{48,80},{64,96},{80,112},{96,0},{112,16},{1... | collective-permute-start | bytes 786440 | tf_op jit(solution)/shard_map/ppermute | solution.py:70
  79.1 15.0 %collective-permute-start.15 = (f32[512,256]{1,0:T(8,128)S(1)}, f32[512,256]{1,0:T(8,128)S(1)}, u32[]{:S(2)}, u32[]{:S(2)}) collective-permute-start(f32[512,256]{1,0:T(8,128)S(1)} %collective-permute-done.13.refs_1_), channel_id=1, source_target_pairs={{0,4},{1,5},{2,6},{3,7},{4,8},{5,9},{6,10},{7,11},{8,12},{9,13},{1... | collective-permute-start | bytes 1572872 | tf_op jit(solution)/shard_map/ppermute | solution.py:48
  80.1 14.0 %collective-permute-start.16 = (f32[512,256]{1,0:T(8,128)S(1)}, f32[512,256]{1,0:T(8,128)S(1)}, u32[]{:S(2)}, u32[]{:S(2)}) collective-permute-start(f32[512,256]{1,0:T(8,128)S(1)} %collective-permute-done.14.refs_3_), channel_id=1, source_target_pairs={{0,12},{1,13},{2,14},{3,15},{4,0},{5,1},{6,2},{7,3},{8,4},{9,5},{1... | collective-permute-start | bytes 1572872 | tf_op jit(solution)/shard_map/ppermute | solution.py:48
  81.8 9.1 %collective-permute-start.24 = (f32[256,256]{1,0:T(8,128)S(1)}, f32[256,256]{1,0:T(8,128)S(1)}, u32[]{:S(2)}, u32[]{:S(2)}) collective-permute-start(f32[256,256]{1,0:T(8,128)S(1)} %select_select_fusion.4.refs_13_), channel_id=1, source_target_pairs={{16,0},{17,1},{18,2},{19,3},{20,4},{21,5},{22,6},{23,7},{24,8},{25... | collective-permute-start | bytes 786440 | tf_op jit(solution)/shard_map/ppermute | solution.py:159
  86.6 6.1 %collective-permute-start.23 = (f32[256,256]{1,0:T(8,128)S(1)}, f32[256,256]{1,0:T(8,128)S(1)}, u32[]{:S(2)}, u32[]{:S(2)}) collective-permute-start(f32[256,256]{1,0:T(8,128)S(1)} %select_select_fusion.4.refs_13_), channel_id=1, source_target_pairs={{16,112},{17,113},{18,114},{19,115},{20,116},{21,117},{22,118},{23... | collective-permute-start | bytes 786440 | tf_op jit(solution)/shard_map/ppermute | solution.py:158
  95.5 7.4 %collective-permute-start.25 = (f32[256,256]{1,0:T(8,128)S(1)}, f32[256,256]{1,0:T(8,128)S(1)}, u32[]{:S(2)}, u32[]{:S(2)}) collective-permute-start(f32[256,256]{1,0:T(8,128)S(1)} %broadcast_select_fusion), channel_id=1, source_target_pairs={{0,32},{16,112},{32,64},{48,16},{64,96},{80,48},{96,0},{112,80},{1... | collective-permute-start | bytes 786440 | tf_op jit(solution)/shard_map/ppermute | solution.py:92
  (15 other events, 149.2 us)

commit v7 on v6

--- a/solution.py
+++ b/solution.py
@@ -133,44 +133,38 @@
     block1, block2, tile, pivot = barrier((block1, block2, tile, block1[:NB]))
 
     corner = [(N_COL + SIDE * a, N_COL + SIDE * a + 2) for a in range(SIDE)]
-    own, pivot_near, pivot_back, pivot_far = barrier((
+    near1, back2, back1, near2, own, pivot_far = barrier((
+        shift_line(block1, 1),
+        shift_line(block2, -1),
+        shift_line(block1, -1),
+        shift_line(block2, 1),
         to_columns(tile),
-        shift_line(pivot, 1),
-        shift_line(pivot, -1),
         lax.ppermute(pivot, ("row", "col"), corner),
     ))
-    pivot = choose(z, pivot, pivot_near, pivot_far, pivot_back)
-    block1, block2, own, pivot = barrier((block1, block2, own, pivot))
-
-    near1, back2 = shift_line(block1, 1), shift_line(block2, -1)
-    back1, near2 = shift_line(block1, -1), shift_line(block2, 1)
-    own_other = swap_core(own)
+    pivot = choose(z, pivot, near1[:NB], pivot_far, back1[:NB])
     near1, back2, own, pivot = barrier((near1, back2, own, pivot))
-    far1, far2, back1, near2, own_other, up, down, pivot_up, pivot_down, pivot_swap = barrier((
+    far1, far2, up, down, own_other, pivot_up, pivot_down, pivot_far, pivot_swap = barrier((
         shift_line(near1, 1),
         shift_line(back2, -1),
-        back1,
-        near2,
-        own_other,
         shift_y(own, 1),
         shift_y(own, -1),
+        swap_core(own),
         lax.ppermute(pivot, "row", [(1, 3)]),
         lax.ppermute(pivot, "row", [(1, 7)]),
+        lax.ppermute(pivot, "row", [(1, 5)]),
         lax.ppermute(pivot, "row", [(1, 0)]),
     ))
     panel1 = [block1, near1, far1, back1]
     panel2 = [block2, near2, far2, back2]
-    ends = pivot_up + pivot_down
-    last, up_other, down_other, pivot_far, ends_swap = barrier((
+    odd = pivot_up + pivot_down + pivot_far
+    last, up_other, down_other, even = barrier((
         relay_y(up, down, core),
         swap_core(up),
         swap_core(down),
-        lax.ppermute(ends, "row", [(3, 5)]),
-        lax.ppermute(ends, "row", [(3, 2), (7, 6)]),
+        lax.ppermute(odd, "row", [(3, 2), (5, 4), (7, 6)]),
     ))
     cols = [own, up, last, down, own_other, up_other, swap_core(last), down_other]
-    far_swap = lax.ppermute(pivot_far, "row", [(5, 4)])
-    pivots = [pivot_swap, pivot, ends_swap, ends, far_swap, pivot_far]
+    pivots = [pivot_swap, pivot, even, odd]
     return panel1, panel2, cols, pivots
 
 
@@ -252,7 +246,7 @@
 
 def last_kernel(*refs):
     pieces, cols = refs[:SIDE], refs[SIDE : SIDE + N_ROW]
-    pivots, refs = refs[SIDE + N_ROW : SIDE + N_ROW + 6], refs[SIDE + N_ROW + 6 :]
+    pivots, refs = refs[SIDE + N_ROW : SIDE + N_ROW + 4], refs[SIDE + N_ROW + 4 :]
     matrix, inv_in, high_in, low_in, band, out, panel, *refs = refs
     tiles, raw, raw_cols, row_high1, row_low1, row_high2, row_low2, col_high, col_low, even, odd, *refs = refs
     inv, pivot, sems, col_sems, in_sems, out_sems, panel_sems, small_sems = refs
@@ -263,7 +257,7 @@
     small = [(inv_in, inv), (pivots[0], pivot), (high_in, row_high1), (low_in, row_low1)]
     small = [pltpu.make_async_copy(a, b, small_sems.at[n]) for n, (a, b) in enumerate(small)]
     small[0].start()
-    for n, rows in enumerate(((0,), (1,), (2, 6), (3, 7), (4,), (5,))):
+    for n, rows in enumerate(((0,), (1,), (2, 4, 6), (3, 5, 7))):
 
         @pl.when(functools.reduce(jnp.logical_or, [r == row for row in rows]))
         def _():
@@ -359,7 +353,7 @@
             jax.ShapeDtypeStruct((TR, LINES, HALF), F32),
             jax.ShapeDtypeStruct((TR, NB, NB), F32),
         ),
-        in_specs=[ANY] * (SIDE + N_ROW + 6 + 4) + [SMEM],
+        in_specs=[ANY] * (SIDE + N_ROW + 4 + 4) + [SMEM],
         out_specs=[ANY] * 2,
         scratch_shapes=[
             pltpu.VMEM((TR, LINES, HALF), F32),

time: 126 us -> 125 us (level)
  waiting for transfers between devices: 41.7 us -> 38.9 us
  other arithmetic: 3.16 us -> 4.84 us
    ppermute x1, starting transfers between devices: 6.34 us -> 11.7 us  [gather_all(): lax.ppermute(pivot, ('row', 'col'), corner)]
    ppermute x16 -> x14, waiting for transfers between devices: 26.9 us -> 22 us  [shift_plane(): return lax.ppermute(value, ('row', 'col'), pairs)]
    ppermute x1, starting transfers between devices: 4.86 us -> 2.35 us  [gather_all(): lax.ppermute(pivot, 'row', [(1, 0)])]
    ppermute x2, starting transfers between devices: 4.57 us -> 2.34 us  [shift_y(): return lax.ppermute(value, 'row', pairs)]
    ppermute x1, starting transfers between devices: 2.84 us -> 1.31 us  [gather_all(): lax.ppermute(pivot, 'row', [(1, 7)])]
    ppermute x2, waiting for transfers between devices: 0.01 us -> 1.49 us  [shift_y(): return lax.ppermute(value, 'row', pairs)]
    ppermute x3 -> x2, starting transfers between devices: 2.03 us -> 3.45 us  [the longest x1 2.78 us: gather_all(): lax.ppermute(pivot, 'row', [(1, 5)])]
    ppermute x16 -> x14, starting transfers between devices: 15.3 us -> 16.3 us  [shift_plane(): return lax.ppermute(value, ('row', 'col'), pairs)]
  transfers between devices with their start and end apart: 32 -> 29, of which waited for: 15 -> 14; matrix products, arithmetic and copies ran while one was open for 0% -> 0% of each run, Pallas kernels for 2% -> 2%
where the time goes in v7:
time: 125 us; the launch traced here: 123 us
  starting transfers between devices  54.7 us (44%)
  waiting for transfers between devices  38.9 us (31%)
  Pallas kernels  19.7 us (16%)
  other arithmetic  4.84 us (4%)
  local copies, waits for them, and re-layouts  3.79 us (3%)
    ppermute x14, waiting for transfers between devices, shift_plane(): return lax.ppermute(value, ('row', 'col'), pairs)  22 us
    pallas_call x1, Pallas kernels, finish(): pl.pallas_call(last_kernel, out_shape=(jax.ShapeDtypeStruct((TR, LINES, H...  17.8 us
    ppermute x14, starting transfers between devices, shift_plane(): return lax.ppermute(value, ('row', 'col'), pairs)  16.3 us
    ppermute x1, starting transfers between devices, gather_all(): lax.ppermute(pivot, ('row', 'col'), corner)  11.7 us
    ppermute x1, starting transfers between devices, send_far(): return lax.ppermute(value, ('row', 'col'), pairs)  6.35 us
    ppermute x4, starting transfers between devices, swap_core(): return lax.ppermute(value, 'row', [(r, r ^ 1) for r in range(N_ROW)])  5.13 us
    ppermute x1, waiting for transfers between devices, send_far(): return lax.ppermute(value, ('row', 'col'), pairs)  4.9 us
    ppermute x1, waiting for transfers between devices, relay_y(): return lax.ppermute(jnp.where(core == 0, near, back), 'row', pairs)  3.51 us
  transfers between devices with their start and end apart: 29, of which 14 were waited for; matrix products, arithmetic and copies ran while one was open for 0% of the time, Pallas kernels for 2%

profile of v7, /device:TPU:1, one launch (start us, length us, event | category | flops | bytes accessed | tf_op | source)
XLA Modules:
  0.0 123.0 jit_solution(12783681181187503991)
XLA Ops:
  0.6 1.6 %slice-done = f32[8,256,1,256]{3,2,1,0:T(1,128)S(1)} async-done(((f32[8,256,4,256]{3,2,1,0:T(4,128)}), f32[8,256,1,256]{3,2,1,0:T(1,128)S(1)}, s32[]{:S(2)}) %slice-start) | async-done | bytes 2097176 | tf_op jit(solution)/shard_map/slice | solution.py:387
  3.6 6.3 %collective-permute-start.2 = (f32[512,256]{1,0:T(8,128)}, f32[512,256]{1,0:T(8,128)S(1)}, u32[]{:S(2)}, u32[]{:S(2)}) collective-permute-start(f32[512,256]{1,0:T(8,128)} %get-tuple-element.86), channel_id=1, source_target_pairs={{0,8},{1,9},{16,18},{17,19},{32,40},{33,41},{48,50},{49,51},{64,72... | collective-permute-start | bytes 1572872 | tf_op jit(solution)/shard_map/ppermute | solution.py:65
  11.5 4.9 %collective-permute-done.2 = f32[512,256]{1,0:T(8,128)S(1)} collective-permute-done((f32[512,256]{1,0:T(8,128)}, f32[512,256]{1,0:T(8,128)S(1)}, u32[]{:S(2)}, u32[]{:S(2)}) %collective-permute-start.2) | collective-permute-done | bytes 524320 | tf_op jit(solution)/shard_map/ppermute | solution.py:65
  16.4 6.7 %collective-permute-done.1 = f32[512,256]{1,0:T(8,128)S(1)} collective-permute-done((f32[512,256]{1,0:T(8,128)}, f32[512,256]{1,0:T(8,128)S(1)}, u32[]{:S(2)}, u32[]{:S(2)}) %collective-permute-start.1) | collective-permute-done | bytes 524320 | tf_op jit(solution)/shard_map/ppermute | solution.py:48
  23.9 1.5 %select_select_fusion.2 = (f32[512,256]{1,0:T(8,128)S(1)}, f32[512,256]{1,0:T(8,128)S(1)}) fusion(f32[512,256]{1,0:T(8,128)} %collective-permute-done, f32[512,256]{1,0:T(8,128)} %copy-done.2, f32[512,256]{1,0:T(8,128)} %copy-done.3, f32[2048,256]{1,0:T(8,128)S(1)} %bitcast.12, pred[]{:T(512)S(6)} %eq.68, pred[]{:T(512)S(6)} %eq.67, pred[]{:T(512)S(6)} %eq.66, ...), kind=kLoop, calls=%fused_computation.2 | loop fusion | flops 786432 | bytes 3145734 | tf_op jit(solution)/shard_map/jit(_where)/select_n | solution.py:96
  27.0 2.6 %collective-permute-start.5 = (f32[512,256]{1,0:T(8,128)S(1)}, f32[512,256]{1,0:T(8,128)S(1)}, u32[]{:S(2)}, u32[]{:S(2)}) collective-permute-start(f32[512,256]{1,0:T(8,128)S(1)} %get-tuple-element.83), channel_id=1, source_target_pairs={{0,3},{1,0},{2,1},{3,2},{4,7},{5,4},{6,5},{7,6},{8,11},{9,8},{10,9... | collective-permute-start | bytes 1572872 | tf_op jit(solution)/shard_map/ppermute | solution.py:48
  29.6 4.2 %collective-permute-done.7 = f32[512,256]{1,0:T(8,128)S(1)} collective-permute-done((f32[512,256]{1,0:T(8,128)S(1)}, f32[512,256]{1,0:T(8,128)S(1)}, u32[]{:S(2)}, u32[]{:S(2)}) %collective-permute-start.7) | collective-permute-done | bytes 524320 | tf_op jit(solution)/shard_map/ppermute | solution.py:48
  35.3 5.5 %collective-permute-done.6 = f32[512,256]{1,0:T(8,128)S(1)} collective-permute-done((f32[512,256]{1,0:T(8,128)S(1)}, f32[512,256]{1,0:T(8,128)S(1)}, u32[]{:S(2)}, u32[]{:S(2)}) %collective-permute-start.6) | collective-permute-done | bytes 524320 | tf_op jit(solution)/shard_map/ppermute | solution.py:48
  40.8 4.3 %collective-permute-done.8 = f32[512,256]{1,0:T(8,128)} collective-permute-done((f32[512,256]{1,0:T(8,128)S(1)}, f32[512,256]{1,0:T(8,128)}, u32[]{:S(2)}, u32[]{:S(2)}) %collective-permute-start.8) | collective-permute-done | bytes 524320 | tf_op jit(solution)/shard_map/ppermute | solution.py:48
  48.5 2.2 %collective-permute-start.13 = (f32[256,256]{1,0:T(8,128)S(1)}, f32[256,256]{1,0:T(8,128)S(1)}, u32[]{:S(2)}, u32[]{:S(2)}) collective-permute-start(f32[256,256]{1,0:T(8,128)S(1)} %get-tuple-element.53), channel_id=1, source_target_pairs={{0,0},{1,8},{2,16},{3,24},{4,32},{5,40},{6,48},{7,56},{8,64},{9,72... | collective-permute-start | bytes 786440 | tf_op jit(solution)/shard_map/ppermute | solution.py:87
  52.1 3.6 %collective-permute-start.10 = (f32[512,256]{1,0:T(8,128)S(1)}, f32[512,256]{1,0:T(8,128)}, u32[]{:S(2)}, u32[]{:S(2)}) collective-permute-start(f32[512,256]{1,0:T(8,128)S(1)} %get-tuple-element.51.refs_0_), channel_id=1, source_target_pairs={{0,12},{1,13},{2,14},{3,15},{4,0},{5,1},{6,2},{7,3},{8,4},{9,5},{1... | collective-permute-start | bytes 1572872 | tf_op jit(solution)/shard_map/ppermute | solution.py:48
  57.8 11.7 %collective-permute-start.14 = (f32[256,256]{1,0:T(8,128)}, f32[256,256]{1,0:T(8,128)}, u32[]{:S(2)}, u32[]{:S(2)}) collective-permute-start(f32[256,256]{1,0:T(8,128)} %get-tuple-element.54), channel_id=1, source_target_pairs={{16,18},{20,22},{24,26},{28,30}} | collective-permute-start | bytes 786440 | tf_op jit(solution)/shard_map/ppermute | solution.py:142
  69.5 2.9 %collective-permute-done.14 = f32[256,256]{1,0:T(8,128)} collective-permute-done((f32[256,256]{1,0:T(8,128)}, f32[256,256]{1,0:T(8,128)}, u32[]{:S(2)}, u32[]{:S(2)}) %collective-permute-start.14) | collective-permute-done | bytes 262176 | tf_op jit(solution)/shard_map/ppermute | solution.py:142
  73.4 4.6 %collective-permute-start.19 = (f32[256,256]{1,0:T(8,128)S(1)}, f32[256,256]{1,0:T(8,128)S(1)}, u32[]{:S(2)}, u32[]{:S(2)}) collective-permute-start(f32[256,256]{1,0:T(8,128)S(1)} %collective-permute-done.13.refs_4_), channel_id=1, source_target_pairs={{0,16},{16,0},{32,48},{48,32},{64,80},{80,64},{96,112},{112,96},{1... | collective-permute-start | bytes 786440 | tf_op jit(solution)/shard_map/ppermute | solution.py:74
  78.1 2.3 %collective-permute-start.17 = (f32[256,256]{1,0:T(8,128)S(1)}, f32[256,256]{1,0:T(8,128)S(1)}, u32[]{:S(2)}, u32[]{:S(2)}) collective-permute-start(f32[256,256]{1,0:T(8,128)S(1)} %collective-permute-done.13.refs_4_), channel_id=1, source_target_pairs={{0,32},{16,48},{32,64},{48,80},{64,96},{80,112},{96,0},{112,16},{1... | collective-permute-start | bytes 786440 | tf_op jit(solution)/shard_map/ppermute | solution.py:70
  80.4 2.3 %collective-permute-start.23 = (f32[256,256]{1,0:T(8,128)S(1)}, f32[256,256]{1,0:T(8,128)S(1)}, u32[]{:S(2)}, u32[]{:S(2)}) collective-permute-start(f32[256,256]{1,0:T(8,128)S(1)} %select_select_fusion.4.refs_13_), channel_id=1, source_target_pairs={{16,0},{17,1},{18,2},{19,3},{20,4},{21,5},{22,6},{23,7},{24,8},{25... | collective-permute-start | bytes 786440 | tf_op jit(solution)/shard_map/ppermute | solution.py:155
  82.8 2.7 %collective-permute-start.16 = (f32[512,256]{1,0:T(8,128)}, f32[512,256]{1,0:T(8,128)S(1)}, u32[]{:S(2)}, u32[]{:S(2)}) collective-permute-start(f32[512,256]{1,0:T(8,128)} %collective-permute-done.10.refs_3_), channel_id=1, source_target_pairs={{0,12},{1,13},{2,14},{3,15},{4,0},{5,1},{6,2},{7,3},{8,4},{9,5},{1... | collective-permute-start | bytes 1572872 | tf_op jit(solution)/shard_map/ppermute | solution.py:48
  85.5 1.5 %collective-permute-done.18.refs_7_ = f32[256,256]{1,0:T(8,128)S(1)} collective-permute-done((f32[256,256]{1,0:T(8,128)S(1)}, f32[256,256]{1,0:T(8,128)S(1)}, u32[]{:S(2)}, u32[]{:S(2)}) %collective-permute-start.18) | collective-permute-done | bytes 262176 | tf_op jit(solution)/shard_map/ppermute | solution.py:70
  87.0 2.8 %collective-permute-start.22 = (f32[256,256]{1,0:T(8,128)S(1)}, f32[256,256]{1,0:T(8,128)S(1)}, u32[]{:S(2)}, u32[]{:S(2)}) collective-permute-start(f32[256,256]{1,0:T(8,128)S(1)} %select_select_fusion.4.refs_13_), channel_id=1, source_target_pairs={{16,80},{17,81},{18,82},{19,83},{20,84},{21,85},{22,86},{23,87},{2... | collective-permute-start | bytes 786440 | tf_op jit(solution)/shard_map/ppermute | solution.py:154
  94.4 1.5 %collective-permute-done.20 = f32[256,256]{1,0:T(8,128)S(1)} collective-permute-done((f32[256,256]{1,0:T(8,128)S(1)}, f32[256,256]{1,0:T(8,128)S(1)}, u32[]{:S(2)}, u32[]{:S(2)}) %collective-permute-start.20) | collective-permute-done | bytes 262176 | tf_op jit(solution)/shard_map/ppermute | solution.py:152
  96.7 2.3 %collective-permute-start.24 = (f32[256,256]{1,0:T(8,128)S(1)}, f32[256,256]{1,0:T(8,128)S(1)}, u32[]{:S(2)}, u32[]{:S(2)}) collective-permute-start(f32[256,256]{1,0:T(8,128)S(1)} %broadcast_select_fusion), channel_id=1, source_target_pairs={{0,32},{16,112},{32,64},{48,16},{64,96},{80,48},{96,0},{112,80},{1... | collective-permute-start | bytes 786440 | tf_op jit(solution)/shard_map/ppermute | solution.py:92
  99.5 3.5 %collective-permute-done.24.refs_6_ = f32[256,256]{1,0:T(8,128)S(1)} collective-permute-done((f32[256,256]{1,0:T(8,128)S(1)}, f32[256,256]{1,0:T(8,128)S(1)}, u32[]{:S(2)}, u32[]{:S(2)}) %collective-permute-start.24) | collective-permute-done | bytes 262176 | tf_op jit(solution)/shard_map/ppermute | solution.py:92
  103.1 1.9 %solve_first.1 = (bf16[8,256,256]{2,1,0:T(8,128)(2,1)S(1)}, bf16[8,256,256]{2,1,0:T(8,128)(2,1)S(1)}) custom-call(f32[512,256]{1,0:T(8,128)S(1)} %get-tuple-element.52.refs_0_, f32[512,256]{1,0:T(8,128)S(1)} %collective-permute-done.9.refs_1_, f32[512,256]{1,0:T(8,128)S(1)} %collective-permute-done.15.refs_2_, ...), custom_call_target="tpu_custom_call" | custom-call | flops 805306368 | bytes 4194304 | tf_op jit(solution)/shard_map/solve_first/pallas_call | solution.py:226
  105.0 17.8 %solve_and_update.1 = (f32[8,2048,128]{2,1,0:T(8,128)}, f32[8,256,256]{2,1,0:T(8,128)}) custom-call(f32[512,256]{1,0:T(8,128)S(1)} %get-tuple-element.51.refs_0_, f32[512,256]{1,0:T(8,128)S(1)} %collective-permute-done.12.refs_1_, f32[512,256]{1,0:T(8,128)S(1)} %collective-permute-done.16.refs_2_, f32[512,256]{1,0:T(8,128)} %collective-permute-done.10.refs_3_, ...), custom_call_target="tpu_custom_call" | custom-call | flops 6710886400 | bytes 20971520 | tf_op jit(solution)/shard_map/solve_and_update/pallas_call | solution.py:350
  (58 shorter events, 20.6 us)
Async XLA Ops:
  3.6 12.8 %collective-permute-start.2 = (f32[512,256]{1,0:T(8,128)}, f32[512,256]{1,0:T(8,128)S(1)}, u32[]{:S(2)}, u32[]{:S(2)}) collective-permute-start(f32[512,256]{1,0:T(8,128)} %get-tuple-element.86), channel_id=1, source_target_pairs={{0,8},{1,9},{16,18},{17,19},{32,40},{33,41},{48,50},{49,51},{64,72... | collective-permute-start | bytes 1572872 | tf_op jit(solution)/shard_map/ppermute | solution.py:65
  10.0 13.1 %collective-permute-start.1 = (f32[512,256]{1,0:T(8,128)}, f32[512,256]{1,0:T(8,128)S(1)}, u32[]{:S(2)}, u32[]{:S(2)}) collective-permute-start(f32[512,256]{1,0:T(8,128)} %get-tuple-element.87), channel_id=1, source_target_pairs={{0,12},{1,13},{2,14},{3,15},{4,0},{5,1},{6,2},{7,3},{8,4},{9,5},{1... | collective-permute-start | bytes 1572872 | tf_op jit(solution)/shard_map/ppermute | solution.py:48
  10.1 13.8 %collective-permute-start = (f32[512,256]{1,0:T(8,128)}, f32[512,256]{1,0:T(8,128)}, u32[]{:S(2)}, u32[]{:S(2)}) collective-permute-start(f32[512,256]{1,0:T(8,128)} %get-tuple-element.88), channel_id=1, source_target_pairs={{0,4},{1,5},{2,6},{3,7},{4,8},{5,9},{6,10},{7,11},{8,12},{9,13},{1... | collective-permute-start | bytes 1572872 | tf_op jit(solution)/shard_map/ppermute | solution.py:48
  25.4 8.4 %collective-permute-start.7 = (f32[512,256]{1,0:T(8,128)S(1)}, f32[512,256]{1,0:T(8,128)S(1)}, u32[]{:S(2)}, u32[]{:S(2)}) collective-permute-start(f32[512,256]{1,0:T(8,128)S(1)} %get-tuple-element.82), channel_id=1, source_target_pairs={{0,3},{1,0},{2,1},{3,2},{4,7},{5,4},{6,5},{7,6},{8,11},{9,8},{10,9... | collective-permute-start | bytes 1572872 | tf_op jit(solution)/shard_map/ppermute | solution.py:48
  25.5 9.6 %collective-permute-start.3 = (f32[512,256]{1,0:T(8,128)S(1)}, f32[512,256]{1,0:T(8,128)S(1)}, u32[]{:S(2)}, u32[]{:S(2)}) collective-permute-start(f32[512,256]{1,0:T(8,128)S(1)} %get-tuple-element.83), channel_id=1, source_target_pairs={{0,1},{1,2},{2,3},{3,0},{4,5},{5,6},{6,7},{7,4},{8,9},{9,10},{10,1... | collective-permute-start | bytes 1572872 | tf_op jit(solution)/shard_map/ppermute | solution.py:48
  26.9 13.9 %collective-permute-start.6 = (f32[512,256]{1,0:T(8,128)S(1)}, f32[512,256]{1,0:T(8,128)S(1)}, u32[]{:S(2)}, u32[]{:S(2)}) collective-permute-start(f32[512,256]{1,0:T(8,128)S(1)} %get-tuple-element.82), channel_id=1, source_target_pairs={{0,1},{1,2},{2,3},{3,0},{4,5},{5,6},{6,7},{7,4},{8,9},{9,10},{10,1... | collective-permute-start | bytes 1572872 | tf_op jit(solution)/shard_map/ppermute | solution.py:48
  27.0 13.8 %collective-permute-start.5 = (f32[512,256]{1,0:T(8,128)S(1)}, f32[512,256]{1,0:T(8,128)S(1)}, u32[]{:S(2)}, u32[]{:S(2)}) collective-permute-start(f32[512,256]{1,0:T(8,128)S(1)} %get-tuple-element.83), channel_id=1, source_target_pairs={{0,3},{1,0},{2,1},{3,2},{4,7},{5,4},{6,5},{7,6},{8,11},{9,8},{10,9... | collective-permute-start | bytes 1572872 | tf_op jit(solution)/shard_map/ppermute | solution.py:48
  33.8 11.3 %collective-permute-start.8 = (f32[512,256]{1,0:T(8,128)S(1)}, f32[512,256]{1,0:T(8,128)}, u32[]{:S(2)}, u32[]{:S(2)}) collective-permute-start(f32[512,256]{1,0:T(8,128)S(1)} %collective-permute-done.7), channel_id=1, source_target_pairs={{0,3},{1,0},{2,1},{3,2},{4,7},{5,4},{6,5},{7,6},{8,11},{9,8},{10,9... | collective-permute-start | bytes 1572872 | tf_op jit(solution)/shard_map/ppermute | solution.py:48
  35.1 11.2 %collective-permute-start.4 = (f32[512,256]{1,0:T(8,128)S(1)}, f32[512,256]{1,0:T(8,128)}, u32[]{:S(2)}, u32[]{:S(2)}) collective-permute-start(f32[512,256]{1,0:T(8,128)S(1)} %collective-permute-done.3), channel_id=1, source_target_pairs={{0,1},{1,2},{2,3},{3,0},{4,5},{5,6},{6,7},{7,4},{8,9},{9,10},{10,1... | collective-permute-start | bytes 1572872 | tf_op jit(solution)/shard_map/ppermute | solution.py:48
  48.5 9.3 %collective-permute-start.13 = (f32[256,256]{1,0:T(8,128)S(1)}, f32[256,256]{1,0:T(8,128)S(1)}, u32[]{:S(2)}, u32[]{:S(2)}) collective-permute-start(f32[256,256]{1,0:T(8,128)S(1)} %get-tuple-element.53), channel_id=1, source_target_pairs={{0,0},{1,8},{2,16},{3,24},{4,32},{5,40},{6,48},{7,56},{8,64},{9,72... | collective-permute-start | bytes 786440 | tf_op jit(solution)/shard_map/ppermute | solution.py:87
  50.7 21.7 %collective-permute-start.12 = (f32[512,256]{1,0:T(8,128)S(1)}, f32[512,256]{1,0:T(8,128)S(1)}, u32[]{:S(2)}, u32[]{:S(2)}) collective-permute-start(f32[512,256]{1,0:T(8,128)S(1)} %get-tuple-element.51.refs_0_), channel_id=1, source_target_pairs={{0,4},{1,5},{2,6},{3,7},{4,8},{5,9},{6,10},{7,11},{8,12},{9,13},{1... | collective-permute-start | bytes 1572872 | tf_op jit(solution)/shard_map/ppermute | solution.py:48
  52.1 20.3 %collective-permute-start.10 = (f32[512,256]{1,0:T(8,128)S(1)}, f32[512,256]{1,0:T(8,128)}, u32[]{:S(2)}, u32[]{:S(2)}) collective-permute-start(f32[512,256]{1,0:T(8,128)S(1)} %get-tuple-element.51.refs_0_), channel_id=1, source_target_pairs={{0,12},{1,13},{2,14},{3,15},{4,0},{5,1},{6,2},{7,3},{8,4},{9,5},{1... | collective-permute-start | bytes 1572872 | tf_op jit(solution)/shard_map/ppermute | solution.py:48
  55.7 16.7 %collective-permute-start.11 = (f32[512,256]{1,0:T(8,128)S(1)}, f32[512,256]{1,0:T(8,128)S(1)}, u32[]{:S(2)}, u32[]{:S(2)}) collective-permute-start(f32[512,256]{1,0:T(8,128)S(1)} %get-tuple-element.52.refs_0_), channel_id=1, source_target_pairs={{0,12},{1,13},{2,14},{3,15},{4,0},{5,1},{6,2},{7,3},{8,4},{9,5},{1... | collective-permute-start | bytes 1572872 | tf_op jit(solution)/shard_map/ppermute | solution.py:48
  57.1 15.3 %collective-permute-start.9 = (f32[512,256]{1,0:T(8,128)S(1)}, f32[512,256]{1,0:T(8,128)S(1)}, u32[]{:S(2)}, u32[]{:S(2)}) collective-permute-start(f32[512,256]{1,0:T(8,128)S(1)} %get-tuple-element.52.refs_0_), channel_id=1, source_target_pairs={{0,4},{1,5},{2,6},{3,7},{4,8},{5,9},{6,10},{7,11},{8,12},{9,13},{1... | collective-permute-start | bytes 1572872 | tf_op jit(solution)/shard_map/ppermute | solution.py:48
  57.8 14.6 %collective-permute-start.14 = (f32[256,256]{1,0:T(8,128)}, f32[256,256]{1,0:T(8,128)}, u32[]{:S(2)}, u32[]{:S(2)}) collective-permute-start(f32[256,256]{1,0:T(8,128)} %get-tuple-element.54), channel_id=1, source_target_pairs={{16,18},{20,22},{24,26},{28,30}} | collective-permute-start | bytes 786440 | tf_op jit(solution)/shard_map/ppermute | solution.py:142
  73.4 9.4 %collective-permute-start.19 = (f32[256,256]{1,0:T(8,128)S(1)}, f32[256,256]{1,0:T(8,128)S(1)}, u32[]{:S(2)}, u32[]{:S(2)}) collective-permute-start(f32[256,256]{1,0:T(8,128)S(1)} %collective-permute-done.13.refs_4_), channel_id=1, source_target_pairs={{0,16},{16,0},{32,48},{48,32},{64,80},{80,64},{96,112},{112,96},{1... | collective-permute-start | bytes 786440 | tf_op jit(solution)/shard_map/ppermute | solution.py:74
  78.1 8.9 %collective-permute-start.18 = (f32[256,256]{1,0:T(8,128)S(1)}, f32[256,256]{1,0:T(8,128)S(1)}, u32[]{:S(2)}, u32[]{:S(2)}) collective-permute-start(f32[256,256]{1,0:T(8,128)S(1)} %collective-permute-done.13.refs_4_), channel_id=1, source_target_pairs={{0,96},{16,112},{32,0},{48,16},{64,32},{80,48},{96,64},{112,80},{1... | collective-permute-start | bytes 786440 | tf_op jit(solution)/shard_map/ppermute | solution.py:70
  78.1 11.7 %collective-permute-start.17 = (f32[256,256]{1,0:T(8,128)S(1)}, f32[256,256]{1,0:T(8,128)S(1)}, u32[]{:S(2)}, u32[]{:S(2)}) collective-permute-start(f32[256,256]{1,0:T(8,128)S(1)} %collective-permute-done.13.refs_4_), channel_id=1, source_target_pairs={{0,32},{16,48},{32,64},{48,80},{64,96},{80,112},{96,0},{112,16},{1... | collective-permute-start | bytes 786440 | tf_op jit(solution)/shard_map/ppermute | solution.py:70
  80.4 10.7 %collective-permute-start.23 = (f32[256,256]{1,0:T(8,128)S(1)}, f32[256,256]{1,0:T(8,128)S(1)}, u32[]{:S(2)}, u32[]{:S(2)}) collective-permute-start(f32[256,256]{1,0:T(8,128)S(1)} %select_select_fusion.4.refs_13_), channel_id=1, source_target_pairs={{16,0},{17,1},{18,2},{19,3},{20,4},{21,5},{22,6},{23,7},{24,8},{25... | collective-permute-start | bytes 786440 | tf_op jit(solution)/shard_map/ppermute | solution.py:155
  82.8 13.1 %collective-permute-start.15 = (f32[512,256]{1,0:T(8,128)S(1)}, f32[512,256]{1,0:T(8,128)S(1)}, u32[]{:S(2)}, u32[]{:S(2)}) collective-permute-start(f32[512,256]{1,0:T(8,128)S(1)} %collective-permute-done.9.refs_1_), channel_id=1, source_target_pairs={{0,4},{1,5},{2,6},{3,7},{4,8},{5,9},{6,10},{7,11},{8,12},{9,13},{1... | collective-permute-start | bytes 1572872 | tf_op jit(solution)/shard_map/ppermute | solution.py:48
  82.8 13.0 %collective-permute-start.16 = (f32[512,256]{1,0:T(8,128)}, f32[512,256]{1,0:T(8,128)S(1)}, u32[]{:S(2)}, u32[]{:S(2)}) collective-permute-start(f32[512,256]{1,0:T(8,128)} %collective-permute-done.10.refs_3_), channel_id=1, source_target_pairs={{0,12},{1,13},{2,14},{3,15},{4,0},{5,1},{6,2},{7,3},{8,4},{9,5},{1... | collective-permute-start | bytes 1572872 | tf_op jit(solution)/shard_map/ppermute | solution.py:48
  87.0 6.1 %collective-permute-start.22 = (f32[256,256]{1,0:T(8,128)S(1)}, f32[256,256]{1,0:T(8,128)S(1)}, u32[]{:S(2)}, u32[]{:S(2)}) collective-permute-start(f32[256,256]{1,0:T(8,128)S(1)} %select_select_fusion.4.refs_13_), channel_id=1, source_target_pairs={{16,80},{17,81},{18,82},{19,83},{20,84},{21,85},{22,86},{23,87},{2... | collective-permute-start | bytes 786440 | tf_op jit(solution)/shard_map/ppermute | solution.py:154
  91.1 4.8 %collective-permute-start.20 = (f32[256,256]{1,0:T(8,128)S(1)}, f32[256,256]{1,0:T(8,128)S(1)}, u32[]{:S(2)}, u32[]{:S(2)}) collective-permute-start(f32[256,256]{1,0:T(8,128)S(1)} %select_select_fusion.4.refs_13_), channel_id=1, source_target_pairs={{16,48},{17,49},{18,50},{19,51},{20,52},{21,53},{22,54},{23,55},{2... | collective-permute-start | bytes 786440 | tf_op jit(solution)/shard_map/ppermute | solution.py:152
  96.7 6.4 %collective-permute-start.24 = (f32[256,256]{1,0:T(8,128)S(1)}, f32[256,256]{1,0:T(8,128)S(1)}, u32[]{:S(2)}, u32[]{:S(2)}) collective-permute-start(f32[256,256]{1,0:T(8,128)S(1)} %broadcast_select_fusion), channel_id=1, source_target_pairs={{0,32},{16,112},{32,64},{48,16},{64,96},{80,48},{96,0},{112,80},{1... | collective-permute-start | bytes 786440 | tf_op jit(solution)/shard_map/ppermute | solution.py:92
  (12 other events, 100.3 us)

commit v8 on v7

v8 whole, which is shorter than its diff:
```python
import functools

import jax
import jax.numpy as jnp
from jax import lax
from jax.experimental import pallas as pl
from jax.experimental.pallas import tpu as pltpu
from jax.sharding import PartitionSpec as P

NB = 256
HALF = 128
TR = 8
TC = 4
N_ROW = 8
N_COL = 16
SIDE = 4
F32 = jnp.float32
BF16 = jnp.bfloat16


def split(value):
    high = value.astype(BF16)
    return high, (value - high.astype(F32)).astype(BF16)


def dot(a, b):
    return jnp.dot(a, b, preferred_element_type=F32)


def dot3(a, weights):
    high, low = split(a)
    return dot(jnp.concatenate([high, high, low], axis=1), weights)


def deep(value):
    high, low = split(value)
    return jnp.concatenate([high, low, high], axis=0)


def shift_plane(value, by, swapped):
    pairs = []
    for r in range(N_ROW):
        for x in range(SIDE):
            for z in range(SIDE):
                along_z = (r % 2 == 1) != swapped
                to = (x, (z + by) % SIDE) if along_z else ((x + by) % SIDE, z)
                pairs.append((r * N_COL + x * SIDE + z, r * N_COL + to[0] * SIDE + to[1]))
    return lax.ppermute(value, ("row", "col"), pairs)


def shift_line(value, by):
    return shift_plane(value, by, False)


def shift_cross(value, by):
    return shift_plane(value, by, True)


def send_far(value):
    pairs = []
    for r in range(N_ROW):
        for root in range(2):
            to = root + 2 if r % 2 else 2 * SIDE + root
            pairs.append((r * N_COL + root, r * N_COL + to))
    return lax.ppermute(value, ("row", "col"), pairs)


def shift_y(value, by):
    pairs = [(y * 2 + k, (y + by) % SIDE * 2 + k) for y in range(SIDE) for k in range(2)]
    return lax.ppermute(value, "row", pairs)


def swap_core(value):
    return lax.ppermute(value, "row", [(r, r ^ 1) for r in range(N_ROW)])


def tile_choice(r, line, cross):
    turned = (cross - r // 4) % SIDE
    return (turned // 2, turned % 2) if r % 2 else (cross % 2, cross // 2)


def to_columns(value):
    pairs = []
    for r in range(N_ROW):
        for x in range(SIDE):
            for z in range(SIDE):
                line, cross = (z, x) if r % 2 else (x, z)
                odd, panel = tile_choice(r, line, cross)
                quarter = (line - panel * (r % 2)) % SIDE
                target = ((quarter + r // 2) % SIDE * 2 + panel) * N_COL + r + N_ROW * odd
                pairs.append((r * N_COL + x * SIDE + z, target))
    return lax.ppermute(value, ("row", "col"), pairs)


def send_corner(value, moves):
    return lax.ppermute(value, ("row", "col"), [(N_COL + a, N_COL + b) for a, b in moves])


def relay_y(near, back, core):
    pairs = [(r, (r + (2 if r % 2 == 0 else -2)) % N_ROW) for r in range(N_ROW)]
    return lax.ppermute(jnp.where(core == 0, near, back), "row", pairs)


def choose(place, own, near, far, back):
    return jnp.where(place == 0, own, jnp.where(place == 1, near, jnp.where(place == 2, far, back)))


def join(one, two):
    return jnp.concatenate([one, two], axis=0)


PAIR = 2 * NB


def gather_all(raw, row, col):
    barrier = lax.optimization_barrier
    x, z, core = col // SIDE, col % SIDE, row % 2
    line, cross = jnp.where(core == 0, x, z), jnp.where(core == 0, z, x)

    near, back, far, *spread = barrier((
        shift_line(raw[PAIR : 2 * PAIR], 1),
        shift_line(raw[3 * PAIR :], -1),
        send_far(raw[2 * PAIR : 3 * PAIR]),
        *[send_corner(raw[:NB], [(0, a)]) for a in range(1, SIDE)],
    ))
    pivot = jnp.where(z == 0, raw[:NB], sum(spread))
    places = raw[:PAIR], near, far, back
    own1 = choose(line, *places)
    own2 = choose((line + SIDE - 1) % SIDE, *places)

    near1, back2 = shift_cross(own1, 1), shift_cross(own2, -1)
    back1, near2 = shift_cross(own1, -1), shift_cross(own2, 1)
    far1, far2 = shift_cross(near1, 1), shift_cross(back2, -1)
    spread = [send_corner(pivot, [(a, b * SIDE + a) for a in range(SIDE)]) for b in range(1, SIDE)]
    near1, far1, back1, near2, far2, back2, *spread = barrier((near1, far1, back1, near2, far2, back2, *spread))
    pivot = jnp.where(x == 0, pivot, sum(spread))
    after = (cross + SIDE - 1) % SIDE
    block1 = choose(cross, own1, near1, far1, back1)
    block2 = jnp.where(
        core == 0,
        choose(after, own1, near1, far1, back1),
        choose(cross, own2, near2, far2, back2),
    )
    turned = (cross - row // 4) % SIDE
    odd = jnp.where(core == 0, cross % 2, turned // 2)
    panel = jnp.where(core == 0, cross // 2, turned % 2)
    tile = lax.dynamic_slice(jnp.where(panel == 0, block1, block2), (odd * NB, 0), (NB, NB))
    block1, block2, tile, pivot = barrier((block1, block2, tile, pivot))

    near1, back2, back1, near2, own, pivot_swap, *odd = barrier((
        shift_line(block1, 1),
        shift_line(block2, -1),
        shift_line(block1, -1),
        shift_line(block2, 1),
        to_columns(tile),
        lax.ppermute(pivot, "row", [(1, 0)]),
        *[lax.ppermute(pivot, "row", [(1, to)]) for to in (3, 5, 7)],
    ))
    near1, back2, own, odd = barrier((near1, back2, own, sum(odd)))
    far1, far2, up, down, own_other, even = barrier((
        shift_line(near1, 1),
        shift_line(back2, -1),
        shift_y(own, 1),
        shift_y(own, -1),
        swap_core(own),
        lax.ppermute(odd, "row", [(3, 2), (5, 4), (7, 6)]),
    ))
    panel1 = [block1, near1, far1, back1]
    panel2 = [block2, near2, far2, back2]
    pivots = [pivot_swap, pivot, even, odd]
    last, up_other, down_other = relay_y(up, down, core), swap_core(up), swap_core(down)
    return panel1, panel2, (own, up, last, down, own_other, up_other, down_other), pivots


VMEM = pl.BlockSpec(memory_space=pltpu.VMEM)
SMEM = pl.BlockSpec(memory_space=pltpu.SMEM)
ANY = pl.BlockSpec(memory_space=pl.ANY)
ROWS = TR * NB
COLS = TC * NB


def rows_at(index, size):
    return pl.ds(pl.multiple_of(index * size, size), size)


def plane_copies(refs, raw, sems, panel):
    c, core = lax.axis_index("col"), lax.rem(lax.axis_index("row"), 2)
    x, z = lax.div(c, SIDE), lax.rem(c, SIDE)
    line = jnp.where(core == 0, x, z + SIDE - panel)
    copies = []
    for n in range(SIDE):
        place = lax.rem(line + SIDE - n, SIDE)
        copies.append(pltpu.make_async_copy(refs[n], raw.at[rows_at(place, PAIR), :], sems.at[n]))
    return copies


def column_copies(tiles, raw, sems):
    r = lax.axis_index("row")
    y, core = lax.div(r, 2), lax.rem(r, 2)
    copies = []
    for n in range(N_ROW):
        k = lax.rem(y + SIDE - n % SIDE, SIDE) * 2 + lax.rem(core + n // SIDE, 2)
        source_y = lax.div(lax.rem(lax.axis_index("col"), N_ROW), 2)
        tile = lax.rem(lax.div(k, 2) + SIDE - source_y, SIDE)
        target = raw.at[lax.rem(k, 2), rows_at(tile, NB), :]
        copies.append(pltpu.make_async_copy(tiles[n], target, sems.at[n]))
    return copies


def rows_kernel(*refs):
    pieces1, pieces2, pivots = refs[:SIDE], refs[SIDE : 2 * SIDE], refs[2 * SIDE : 3 * SIDE]
    inv_in, band, high1, low1, high2, low2, one, panel, raw1, raw2, inv, pivot, *sems = refs[3 * SIDE :]
    sems1, sems2, small_sems, panel_sems = sems
    r = lax.axis_index("row")
    copies1 = plane_copies(pieces1, raw1, sems1, 0)
    copies2 = plane_copies(pieces2, raw2, sems2, 1)
    pltpu.make_async_copy(inv_in, inv, small_sems.at[0]).start()
    for n, rows in enumerate(((0,), (1,), (2, 4, 6), (3, 5, 7))):

        @pl.when(functools.reduce(jnp.logical_or, [r == row for row in rows]))
        def _():
            pltpu.make_async_copy(pivots[n], pivot, small_sems.at[1]).start()

    for copy in copies1 + copies2:
        copy.start()
    pltpu.make_async_copy(inv_in, inv, small_sems.at[0]).wait()
    weights0 = deep(inv[0].T)
    weights1 = deep(inv[1].T)
    pltpu.make_async_copy(pivots[0], pivot, small_sems.at[1]).wait()
    one_high, one_low = split(dot3(pivot[...], weights0).T)
    one[:NB], one[NB:] = one_high, one_low
    rest_weights = join(one_low, one_high)
    for copy in copies1 + copies2:
        copy.wait()

    def solve(i, carry):
        at, tiles = rows_at(i, PAIR), pl.ds(2 * i, 2)
        high, low = split(dot3(raw1[at, :], weights0))
        high1[tiles], low1[tiles] = high.reshape(2, NB, NB), low.reshape(2, NB, NB)
        full = dot(high, one_high)
        rest = dot(jnp.concatenate([high, low], axis=1), rest_weights)
        used = []
        for n in range(2):
            code, part = band[(2 * i + n) * N_ROW + r, 1], slice(n * NB, (n + 1) * NB)
            used.append(jnp.where(code == 2, 0.0, full[part] + jnp.where(code == 0, rest[part], 0.0)))
        solved = dot3(raw2[at, :] - join(*used), weights1)
        raw2[at, :] = solved
        high, low = split(solved)
        high2[tiles], low2[tiles] = high.reshape(2, NB, NB), low.reshape(2, NB, NB)
        return carry

    lax.fori_loop(0, TR // 2, solve, 0, unroll=2)
    panels = [pltpu.make_async_copy(raw2.at[pl.ds(p * NB, NB), :], panel.at[p], panel_sems.at[p]) for p in range(TR)]
    for copy in panels:
        copy.start()
    for copy in panels:
        copy.wait()


def solve_rows(pieces1, pieces2, pivots, inv, band):
    half = jax.ShapeDtypeStruct((TR, NB, NB), BF16)
    return pl.pallas_call(
        rows_kernel,
        out_shape=[half] * 4 + [jax.ShapeDtypeStruct((PAIR, NB), BF16), jax.ShapeDtypeStruct((TR, NB, NB), F32)],
        in_specs=[ANY] * (3 * SIDE + 1) + [SMEM],
        out_specs=[VMEM] * 5 + [ANY],
        scratch_shapes=[
            pltpu.VMEM((ROWS, NB), F32),
            pltpu.VMEM((ROWS, NB), F32),
            pltpu.VMEM((2, NB, NB), F32),
            pltpu.VMEM((NB, NB), F32),
            pltpu.SemaphoreType.DMA((SIDE,)),
            pltpu.SemaphoreType.DMA((SIDE,)),
            pltpu.SemaphoreType.DMA((2,)),
            pltpu.SemaphoreType.DMA((TR,)),
        ],
        compiler_params=pltpu.CompilerParams(vmem_limit_bytes=24 * 1024 * 1024),
        cost_estimate=pl.CostEstimate(flops=80 * 2 * NB**3, bytes_accessed=10 * 2**20, transcendentals=0),
        name="solve_rows",
    )(*pieces1, *pieces2, *pivots, inv, band)


STEP = 2
LINES = NB * TC * 2
PART = 32


def last_kernel(*refs):
    cols, refs = refs[:N_ROW], refs[N_ROW:]
    matrix, inv_in, *rows_in, one_in, band, out, tiles, raw_cols = refs[:11]
    row_high1, row_low1, row_high2, row_low2, one, col_high, col_low, even, odd, inv, *sems = refs[11:]
    col_sems, in_sems, out_sems, small_sems = sems
    r, c = lax.axis_index("row"), lax.axis_index("col")
    col_copies = column_copies(cols, raw_cols, col_sems)
    loads = [pltpu.make_async_copy(matrix.at[p], tiles.at[p], in_sems.at[p]) for p in range(TR)]
    small = [(inv_in, inv), (one_in, one), *zip(rows_in, (row_high1, row_low1, row_high2, row_low2))]
    small = [pltpu.make_async_copy(a, b, small_sems.at[n]) for n, (a, b) in enumerate(small)]
    for copy in small[:2] + col_copies + small[2:] + loads:
        copy.start()
    small[0].wait()
    weights0 = deep(inv[0].T)
    weights1 = deep(inv[1].T)
    small[1].wait()
    one_high = one[:NB]
    rest_weights = join(one[NB:], one_high)
    for copy in col_copies:
        copy.wait()

    def column(q, carry):
        first = dot3(raw_cols[0, rows_at(q, NB), :], weights0)
        col_high[q, :NB, :], col_low[q, :NB, :] = split(first.T)
        high, low = split(first)
        code = band[q * N_COL + c, 1]
        rest = dot(jnp.concatenate([high, low], axis=1), rest_weights)
        used = jnp.where(code == 2, 0.0, dot(high, one_high) + jnp.where(code == 0, rest, 0.0))
        solved = dot3(raw_cols[1, rows_at(q, NB), :] - used, weights1)
        col_high[q, NB:, :], col_low[q, NB:, :] = split(solved.T)
        return carry

    lax.fori_loop(0, TC, column, 0, unroll=2)
    for copy in small[2:]:
        copy.wait()
    size = STEP * NB

    def multiply(step, q, product):
        at = pl.ds(step * STEP, STEP)
        high = jnp.concatenate([row_high1[at].reshape(size, NB), row_high2[at].reshape(size, NB)], axis=1)
        low = jnp.concatenate([row_low1[at].reshape(size, NB), row_low2[at].reshape(size, NB)], axis=1)
        full = dot(high, col_high[q])
        rest = dot(jnp.concatenate([high, low], axis=1), join(col_low[q], col_high[q]))
        for p in range(STEP):
            code = band[(step * STEP + p) * N_ROW + r, q * N_COL + c]
            at = slice(p * NB, (p + 1) * NB)
            total = jnp.where(code == 2, 0.0, full[at] + jnp.where(code == 0, rest[at], 0.0))
            for b in range(2):
                product[b * TC + q, at, :] = total[:, b * HALF : (b + 1) * HALF]

    def subtract(step, share, product):
        for a in range(share * size // TC, (share + 1) * size // TC, PART):
            turned = product[:, a : a + PART, :].transpose(1, 0, 2).reshape(PART * 2 * TC, HALF)
            at = pl.ds(a % NB * 2 * TC, PART * 2 * TC)
            tiles[step * STEP + a // NB, at, :] -= turned

    steps = TR // STEP
    stores = [pltpu.make_async_copy(tiles.at[p], out.at[p], out_sems.at[p]) for p in range(TR)]
    for step in range(steps + 1):
        product, before = (even, odd) if step % 2 == 0 else (odd, even)
        if step > 0:
            for p in range(STEP):
                loads[(step - 1) * STEP + p].wait()
        for q in range(TC):
            if step < steps:
                multiply(step, q, product)
            if step > 0:
                subtract(step - 1, q, before)
        if step > 0:
            for p in range(STEP):
                stores[(step - 1) * STEP + p].start()
    for copy in stores:
        copy.wait()


def finish(cols, matrix, inv, rows, one, band):
    view = matrix.reshape(TR, NB, TC, 2, HALF).transpose(0, 1, 3, 2, 4).reshape(TR, LINES, HALF)
    half = pltpu.VMEM((TR, NB, NB), BF16)
    out = pl.pallas_call(
        last_kernel,
        out_shape=jax.ShapeDtypeStruct((TR, LINES, HALF), F32),
        in_specs=[ANY] * (N_ROW + 7) + [SMEM],
        out_specs=ANY,
        scratch_shapes=[
            pltpu.VMEM((TR, LINES, HALF), F32),
            pltpu.VMEM((2, COLS, NB), F32),
            half,
            half,
            half,
            half,
            pltpu.VMEM((PAIR, NB), BF16),
            pltpu.VMEM((TC, PAIR, NB), BF16),
            pltpu.VMEM((TC, PAIR, NB), BF16),
            pltpu.VMEM((2 * TC, STEP * NB, HALF), F32),
            pltpu.VMEM((2 * TC, STEP * NB, HALF), F32),
            pltpu.VMEM((2, NB, NB), F32),
            pltpu.SemaphoreType.DMA((N_ROW,)),
            pltpu.SemaphoreType.DMA((TR,)),
            pltpu.SemaphoreType.DMA((TR,)),
            pltpu.SemaphoreType.DMA((6,)),
        ],
        compiler_params=pltpu.CompilerParams(vmem_limit_bytes=42 * 1024 * 1024),
        cost_estimate=pl.CostEstimate(flops=220 * 2 * NB**3, bytes_accessed=20 * 2**20, transcendentals=0),
        name="update_tiles",
    )(*cols, view, inv, *rows, one, band)
    return out.reshape(TR, NB, 2, TC, HALF).transpose(0, 1, 3, 2, 4).reshape(TR, NB, TC, NB)


def body(matrix, diag_inverses, band):
    raw = lax.optimization_barrier(matrix[:, :, 0, :].reshape(ROWS, NB))
    panel1, panel2, cols, pivots = gather_all(raw, lax.axis_index("row"), lax.axis_index("col"))
    *rows, one, panel = solve_rows(panel1, panel2, pivots, diag_inverses, band)
    cols, rows = lax.optimization_barrier((cols, rows))
    own, up, last, down, own_other, up_other, down_other = cols
    cols = [own, up, last, down, own_other, up_other, swap_core(last), down_other]
    return finish(cols, matrix, diag_inverses, rows, one, band), panel


def solution(mesh):
    in_specs = (P(None, "row", None, "col"), P(), P())
    out_specs = (P(None, "row", None, "col"), P(None, "row", None))
    return jax.shard_map(body, mesh=mesh, in_specs=in_specs, out_specs=out_specs, check_vma=False)
```

time: 125 us -> 134 us (1.072)
  Pallas kernels: 19.7 us -> 22.8 us
  waiting for transfers between devices: 38.9 us -> 41.9 us
  local copies, waits for them, and re-layouts: 3.79 us -> 6.01 us
    ppermute x4 -> x9, waiting for transfers between devices: 6.35 us -> 22.3 us  [the longest x6 22.3 us: send_corner(): lax.ppermute(value, ('row', 'col'), [(N_COL + a, N_COL + b) for a, b in m...]
    ppermute x14, waiting for transfers between devices: 22 us -> 9.99 us  [shift_plane(): return lax.ppermute(value, ('row', 'col'), pairs)]
    ppermute x14, starting transfers between devices: 16.3 us -> 22.5 us  [shift_plane(): return lax.ppermute(value, ('row', 'col'), pairs)]
    ppermute x4 -> x9, starting transfers between devices: 17 us -> 23.1 us  [the longest x6 19.2 us: send_corner(): lax.ppermute(value, ('row', 'col'), [(N_COL + a, N_COL + b) for a, b in m...]
    ppermute x2, waiting for transfers between devices: 1.49 us -> 7.2 us  [shift_y(): return lax.ppermute(value, 'row', pairs)]
    ppermute x1, starting transfers between devices: 6.35 us -> 1.31 us  [send_far(): return lax.ppermute(value, ('row', 'col'), pairs)]
    ppermute x1, waiting for transfers between devices: 4.9 us -> 0.01 us  [send_far(): return lax.ppermute(value, ('row', 'col'), pairs)]
    ppermute x1, waiting for transfers between devices: 3.51 us -> 0.01 us  [relay_y(): return lax.ppermute(jnp.where(core == 0, near, back), 'row', pairs)]
  transfers between devices with their start and end apart: 29 -> 34, of which waited for: 14 -> 12; matrix products, arithmetic and copies ran while one was open for 0% -> 2% of each run, Pallas kernels for 2% -> 6%
where the time goes in v8:
time: 134 us; the launch traced here: 132 us
  starting transfers between devices  54.6 us (41%)
  waiting for transfers between devices  41.9 us (31%)
  Pallas kernels  22.8 us (17%)
  local copies, waits for them, and re-layouts  6.01 us (4%)
  other arithmetic  5.43 us (4%)
    ppermute x14, starting transfers between devices, shift_plane(): return lax.ppermute(value, ('row', 'col'), pairs)  22.5 us
    ppermute x6, waiting for transfers between devices, send_corner(): lax.ppermute(value, ('row', 'col'), [(N_COL + a, N_COL + b) for a, b in m...  22.3 us
    ppermute x6, starting transfers between devices, send_corner(): lax.ppermute(value, ('row', 'col'), [(N_COL + a, N_COL + b) for a, b in m...  19.2 us
    pallas_call x1, Pallas kernels, finish(): pl.pallas_call(last_kernel, out_shape=jax.ShapeDtypeStruct((TR, LINES, HA...  15.2 us
    ppermute x14, waiting for transfers between devices, shift_plane(): return lax.ppermute(value, ('row', 'col'), pairs)  9.99 us
    pallas_call x1, Pallas kernels, solve_rows(): pl.pallas_call(rows_kernel, out_shape=[half] * 4 + [jax.ShapeDtypeStruct(...  7.55 us
    ppermute x2, waiting for transfers between devices, shift_y(): return lax.ppermute(value, 'row', pairs)  7.2 us
    ppermute x3, starting transfers between devices, gather_all(): lax.ppermute(pivot, 'row', [(1, to)])  3.92 us
  transfers between devices with their start and end apart: 34, of which 12 were waited for; matrix products, arithmetic and copies ran while one was open for 2% of the time, Pallas kernels for 6%

profile of v8, /device:TPU:1, one launch (start us, length us, event | category | flops | bytes accessed | tf_op | source)
XLA Modules:
  0.0 131.8 jit_solution(14226739512471570891)
XLA Ops:
  0.6 1.6 %slice-done = f32[8,256,1,256]{3,2,1,0:T(1,128)S(1)} async-done(((f32[8,256,4,256]{3,2,1,0:T(4,128)}), f32[8,256,1,256]{3,2,1,0:T(1,128)S(1)}, s32[]{:S(2)}) %slice-start) | async-done | bytes 2097176 | tf_op jit(solution)/shard_map/slice | solution.py:397
  3.2 7.2 %collective-permute-start.5 = (f32[256,256]{1,0:T(8,128)}, f32[256,256]{1,0:T(8,128)}, u32[]{:S(2)}, u32[]{:S(2)}) collective-permute-start(f32[256,256]{1,0:T(8,128)} %slice.31), channel_id=1, source_target_pairs={{16,19}} | collective-permute-start | bytes 786440 | tf_op jit(solution)/shard_map/ppermute | solution.py:96
  13.0 1.5 %collective-permute-start = (f32[512,256]{1,0:T(8,128)}, f32[512,256]{1,0:T(8,128)}, u32[]{:S(2)}, u32[]{:S(2)}) collective-permute-start(f32[512,256]{1,0:T(8,128)} %get-tuple-element.118), channel_id=1, source_target_pairs={{0,4},{1,5},{2,6},{3,7},{4,8},{5,9},{6,10},{7,11},{8,12},{9,13},{1... | collective-permute-start | bytes 1572872 | tf_op jit(solution)/shard_map/ppermute | solution.py:48
  14.4 2.1 %collective-permute-start.4 = (f32[256,256]{1,0:T(8,128)}, f32[256,256]{1,0:T(8,128)S(1)}, u32[]{:S(2)}, u32[]{:S(2)}) collective-permute-start(f32[256,256]{1,0:T(8,128)} %slice.31), channel_id=1, source_target_pairs={{16,18}} | collective-permute-start | bytes 786440 | tf_op jit(solution)/shard_map/ppermute | solution.py:96
  16.5 2.0 %collective-permute-start.3 = (f32[256,256]{1,0:T(8,128)}, f32[256,256]{1,0:T(8,128)}, u32[]{:S(2)}, u32[]{:S(2)}) collective-permute-start(f32[256,256]{1,0:T(8,128)} %slice.31), channel_id=1, source_target_pairs={{16,17}} | collective-permute-start | bytes 786440 | tf_op jit(solution)/shard_map/ppermute | solution.py:96
  18.5 9.2 %collective-permute-done.4 = f32[256,256]{1,0:T(8,128)S(1)} collective-permute-done((f32[256,256]{1,0:T(8,128)}, f32[256,256]{1,0:T(8,128)S(1)}, u32[]{:S(2)}, u32[]{:S(2)}) %collective-permute-start.4) | collective-permute-done | bytes 262176 | tf_op jit(solution)/shard_map/ppermute | solution.py:96
  27.7 4.1 %collective-permute-done.3 = f32[256,256]{1,0:T(8,128)} collective-permute-done((f32[256,256]{1,0:T(8,128)}, f32[256,256]{1,0:T(8,128)}, u32[]{:S(2)}, u32[]{:S(2)}) %collective-permute-start.3) | collective-permute-done | bytes 262176 | tf_op jit(solution)/shard_map/ppermute | solution.py:96
  33.4 1.5 %select_select_fusion.2 = (f32[512,256]{1,0:T(8,128)S(1)}, f32[512,256]{1,0:T(8,128)S(1)}) fusion(f32[512,256]{1,0:T(8,128)} %collective-permute-done, f32[512,256]{1,0:T(8,128)} %copy-done.2, f32[512,256]{1,0:T(8,128)} %copy-done.3, f32[2048,256]{1,0:T(8,128)S(1)} %bitcast.13, pred[]{:T(512)S(6)} %eq.72, pred[]{:T(512)S(6)} %eq.71, pred[]{:T(512)S(6)} %eq.70, ...), kind=kLoop, calls=%fused_computation.2 | loop fusion | flops 786432 | bytes 3145734 | tf_op jit(solution)/shard_map/jit(_where)/select_n | solution.py:105
  37.6 3.9 %collective-permute-start.14 = (f32[256,256]{1,0:T(8,128)S(1)}, f32[256,256]{1,0:T(8,128)}, u32[]{:S(2)}, u32[]{:S(2)}) collective-permute-start(f32[256,256]{1,0:T(8,128)S(1)} %add_select_fusion.1), channel_id=1, source_target_pairs={{16,28},{17,29},{18,30},{19,31}} | collective-permute-start | bytes 786440 | tf_op jit(solution)/shard_map/ppermute | solution.py:96
  44.1 3.4 %collective-permute-start.8 = (f32[512,256]{1,0:T(8,128)S(1)}, f32[512,256]{1,0:T(8,128)S(1)}, u32[]{:S(2)}, u32[]{:S(2)}) collective-permute-start(f32[512,256]{1,0:T(8,128)S(1)} %get-tuple-element.113), channel_id=1, source_target_pairs={{0,3},{1,0},{2,1},{3,2},{4,7},{5,4},{6,5},{7,6},{8,11},{9,8},{10,9... | collective-permute-start | bytes 1572872 | tf_op jit(solution)/shard_map/ppermute | solution.py:48
  49.7 2.6 %collective-permute-start.12 = (f32[256,256]{1,0:T(8,128)S(1)}, f32[256,256]{1,0:T(8,128)}, u32[]{:S(2)}, u32[]{:S(2)}) collective-permute-start(f32[256,256]{1,0:T(8,128)S(1)} %add_select_fusion.1), channel_id=1, source_target_pairs={{16,20},{17,21},{18,22},{19,23}} | collective-permute-start | bytes 786440 | tf_op jit(solution)/shard_map/ppermute | solution.py:96
  52.4 7.9 %collective-permute-done.12 = f32[256,256]{1,0:T(8,128)} collective-permute-done((f32[256,256]{1,0:T(8,128)S(1)}, f32[256,256]{1,0:T(8,128)}, u32[]{:S(2)}, u32[]{:S(2)}) %collective-permute-start.12) | collective-permute-done | bytes 262176 | tf_op jit(solution)/shard_map/ppermute | solution.py:96
  60.2 1.5 %select_select_fusion = (f32[512,256]{1,0:T(8,128)S(1)}, f32[512,256]{1,0:T(8,128)S(1)}) fusion(f32[512,256]{1,0:T(8,128)S(1)} %get-tuple-element.112, f32[512,256]{1,0:T(8,128)S(1)} %collective-permute-done.9, f32[512,256]{1,0:T(8,128)S(1)} %collective-permute-done.11, f32[512,256]{1,0:T(8,128)} %collective-permute-done.10, ...), kind=kLoop, calls=%fused_computation | loop fusion | flops 1310720 | bytes 5242887 | tf_op jit(solution)/shard_map/jit(_where)/select_n | solution.py:139
  63.0 1.9 %collective-permute-start.19 = (f32[256,256]{1,0:T(8,128)S(1)}, f32[256,256]{1,0:T(8,128)S(1)}, u32[]{:S(2)}, u32[]{:S(2)}) collective-permute-start(f32[256,256]{1,0:T(8,128)S(1)} %get-tuple-element.74), channel_id=1, source_target_pairs={{0,0},{1,8},{2,16},{3,24},{4,32},{5,40},{6,48},{7,56},{8,64},{9,72... | collective-permute-start | bytes 786440 | tf_op jit(solution)/shard_map/ppermute | solution.py:92
  68.8 9.0 %collective-permute-start.17 = (f32[512,256]{1,0:T(8,128)S(1)}, f32[512,256]{1,0:T(8,128)S(1)}, u32[]{:S(2)}, u32[]{:S(2)}) collective-permute-start(f32[512,256]{1,0:T(8,128)S(1)} %get-tuple-element.72.refs_0_), channel_id=1, source_target_pairs={{0,12},{1,13},{2,14},{3,15},{4,0},{5,1},{6,2},{7,3},{8,4},{9,5},{1... | collective-permute-start | bytes 1572872 | tf_op jit(solution)/shard_map/ppermute | solution.py:48
  77.9 2.7 %collective-permute-start.16 = (f32[512,256]{1,0:T(8,128)S(1)}, f32[512,256]{1,0:T(8,128)S(1)}, u32[]{:S(2)}, u32[]{:S(2)}) collective-permute-start(f32[512,256]{1,0:T(8,128)S(1)} %get-tuple-element.73.refs_4_), channel_id=1, source_target_pairs={{0,12},{1,13},{2,14},{3,15},{4,0},{5,1},{6,2},{7,3},{8,4},{9,5},{1... | collective-permute-start | bytes 1572872 | tf_op jit(solution)/shard_map/ppermute | solution.py:48
  84.0 3.1 %collective-permute-done.15.refs_1_ = f32[512,256]{1,0:T(8,128)S(1)} collective-permute-done((f32[512,256]{1,0:T(8,128)S(1)}, f32[512,256]{1,0:T(8,128)S(1)}, u32[]{:S(2)}, u32[]{:S(2)}) %collective-permute-start.15) | collective-permute-done | bytes 524320 | tf_op jit(solution)/shard_map/ppermute | solution.py:48
  87.1 5.9 %collective-permute-done.18.refs_5_ = f32[512,256]{1,0:T(8,128)S(1)} collective-permute-done((f32[512,256]{1,0:T(8,128)S(1)}, f32[512,256]{1,0:T(8,128)S(1)}, u32[]{:S(2)}, u32[]{:S(2)}) %collective-permute-start.18) | collective-permute-done | bytes 524320 | tf_op jit(solution)/shard_map/ppermute | solution.py:48
  93.8 2.7 %collective-permute-start.25 = (f32[512,256]{1,0:T(8,128)S(1)}, f32[512,256]{1,0:T(8,128)S(1)}, u32[]{:S(2)}, u32[]{:S(2)}) collective-permute-start(f32[512,256]{1,0:T(8,128)S(1)} %collective-permute-done.16.refs_7_), channel_id=1, source_target_pairs={{0,12},{1,13},{2,14},{3,15},{4,0},{5,1},{6,2},{7,3},{8,4},{9,5},{1... | collective-permute-start | bytes 1572872 | tf_op jit(solution)/shard_map/ppermute | solution.py:48
  96.5 1.5 %collective-permute-start.26 = (f32[256,256]{1,0:T(8,128)S(1)}, f32[256,256]{1,0:T(8,128)S(1)}, u32[]{:S(2)}, u32[]{:S(2)}) collective-permute-start(f32[256,256]{1,0:T(8,128)S(1)} %collective-permute-done.19.refs_0_), channel_id=1, source_target_pairs={{0,32},{16,48},{32,64},{48,80},{64,96},{80,112},{96,0},{112,16},{1... | collective-permute-start | bytes 786440 | tf_op jit(solution)/shard_map/ppermute | solution.py:70
  98.0 5.8 %collective-permute-done.27.refs_3_ = f32[256,256]{1,0:T(8,128)S(1)} collective-permute-done((f32[256,256]{1,0:T(8,128)S(1)}, f32[256,256]{1,0:T(8,128)S(1)}, u32[]{:S(2)}, u32[]{:S(2)}) %collective-permute-start.27) | collective-permute-done | bytes 262176 | tf_op jit(solution)/shard_map/ppermute | solution.py:70
  105.5 1.6 %collective-permute-start.31 = (f32[256,256]{1,0:T(8,128)S(1)}, f32[256,256]{1,0:T(8,128)S(1)}, u32[]{:S(2)}, u32[]{:S(2)}) collective-permute-start(f32[256,256]{1,0:T(8,128)S(1)} %collective-permute-done.26.refs_1_), channel_id=1, source_target_pairs={{0,16},{16,0},{32,48},{48,32},{64,80},{80,64},{96,112},{112,96},{1... | collective-permute-start | bytes 786440 | tf_op jit(solution)/shard_map/ppermute | solution.py:74
  107.1 7.6 %solve_rows.1 = (bf16[8,256,256]{2,1,0:T(8,128)(2,1)S(1)}, bf16[8,256,256]{2,1,0:T(8,128)(2,1)S(1)}, bf16[8,256,256]{2,1,0:T(8,128)(2,1)S(1)}, bf16[8,256,256]{2...) custom-call(f32[512,256]{1,0:T(8,128)S(1)} %get-tuple-element.72.refs_0_, ...), custom_call_target="tpu_custom_call" | custom-call | flops 2684354560 | bytes 10485760 | tf_op jit(solution)/shard_map/solve_rows/pallas_call | solution.py:262
  116.4 15.2 %update_tiles.1 = f32[8,2048,128]{2,1,0:T(8,128)} custom-call(f32[256,256]{1,0:T(8,128)S(1)} %collective-permute-done.19.refs_0_, f32[256,256]{1,0:T(8,128)S(1)} %collective-permute-done.26.refs_1_, f32[256,256]{1,0:T(8,128)S(1)} %collective-permute-done.30.refs_2_, f32[256,256]{1,0:T(8,128)S(1)} %collective-permute-done.27.refs_3_, ...), custom_call_target="tpu_custom_call" | custom-call | flops 7381975040 | bytes 20971520 | tf_op jit(solution)/shard_map/update_tiles/pallas_call | solution.py:366
  (71 shorter events, 25.4 us)
Async XLA Ops:
  3.2 13.3 %collective-permute-start.5 = (f32[256,256]{1,0:T(8,128)}, f32[256,256]{1,0:T(8,128)}, u32[]{:S(2)}, u32[]{:S(2)}) collective-permute-start(f32[256,256]{1,0:T(8,128)} %slice.31), channel_id=1, source_target_pairs={{16,19}} | collective-permute-start | bytes 786440 | tf_op jit(solution)/shard_map/ppermute | solution.py:96
  11.6 20.3 %collective-permute-start.2 = (f32[512,256]{1,0:T(8,128)}, f32[512,256]{1,0:T(8,128)S(1)}, u32[]{:S(2)}, u32[]{:S(2)}) collective-permute-start(f32[512,256]{1,0:T(8,128)} %get-tuple-element.116), channel_id=1, source_target_pairs={{0,8},{1,9},{16,18},{17,19},{32,40},{33,41},{48,50},{49,51},{64,72... | collective-permute-start | bytes 1572872 | tf_op jit(solution)/shard_map/ppermute | solution.py:65
  12.9 19.0 %collective-permute-start.1 = (f32[512,256]{1,0:T(8,128)}, f32[512,256]{1,0:T(8,128)S(1)}, u32[]{:S(2)}, u32[]{:S(2)}) collective-permute-start(f32[512,256]{1,0:T(8,128)} %get-tuple-element.117), channel_id=1, source_target_pairs={{0,12},{1,13},{2,14},{3,15},{4,0},{5,1},{6,2},{7,3},{8,4},{9,5},{1... | collective-permute-start | bytes 1572872 | tf_op jit(solution)/shard_map/ppermute | solution.py:48
  13.0 20.5 %collective-permute-start = (f32[512,256]{1,0:T(8,128)}, f32[512,256]{1,0:T(8,128)}, u32[]{:S(2)}, u32[]{:S(2)}) collective-permute-start(f32[512,256]{1,0:T(8,128)} %get-tuple-element.118), channel_id=1, source_target_pairs={{0,4},{1,5},{2,6},{3,7},{4,8},{5,9},{6,10},{7,11},{8,12},{9,13},{1... | collective-permute-start | bytes 1572872 | tf_op jit(solution)/shard_map/ppermute | solution.py:48
  14.4 13.3 %collective-permute-start.4 = (f32[256,256]{1,0:T(8,128)}, f32[256,256]{1,0:T(8,128)S(1)}, u32[]{:S(2)}, u32[]{:S(2)}) collective-permute-start(f32[256,256]{1,0:T(8,128)} %slice.31), channel_id=1, source_target_pairs={{16,18}} | collective-permute-start | bytes 786440 | tf_op jit(solution)/shard_map/ppermute | solution.py:96
  16.5 15.3 %collective-permute-start.3 = (f32[256,256]{1,0:T(8,128)}, f32[256,256]{1,0:T(8,128)}, u32[]{:S(2)}, u32[]{:S(2)}) collective-permute-start(f32[256,256]{1,0:T(8,128)} %slice.31), channel_id=1, source_target_pairs={{16,17}} | collective-permute-start | bytes 786440 | tf_op jit(solution)/shard_map/ppermute | solution.py:96
  34.9 12.6 %collective-permute-start.10 = (f32[512,256]{1,0:T(8,128)S(1)}, f32[512,256]{1,0:T(8,128)}, u32[]{:S(2)}, u32[]{:S(2)}) collective-permute-start(f32[512,256]{1,0:T(8,128)S(1)} %get-tuple-element.112), channel_id=1, source_target_pairs={{0,3},{1,0},{2,1},{3,2},{4,7},{5,4},{6,5},{7,6},{8,11},{9,8},{10,9... | collective-permute-start | bytes 1572872 | tf_op jit(solution)/shard_map/ppermute | solution.py:48
  35.0 12.6 %collective-permute-start.6 = (f32[512,256]{1,0:T(8,128)S(1)}, f32[512,256]{1,0:T(8,128)}, u32[]{:S(2)}, u32[]{:S(2)}) collective-permute-start(f32[512,256]{1,0:T(8,128)S(1)} %get-tuple-element.113), channel_id=1, source_target_pairs={{0,1},{1,2},{2,3},{3,0},{4,5},{5,6},{6,7},{7,4},{8,9},{9,10},{10,1... | collective-permute-start | bytes 1572872 | tf_op jit(solution)/shard_map/ppermute | solution.py:48
  42.8 17.4 %collective-permute-start.9 = (f32[512,256]{1,0:T(8,128)S(1)}, f32[512,256]{1,0:T(8,128)S(1)}, u32[]{:S(2)}, u32[]{:S(2)}) collective-permute-start(f32[512,256]{1,0:T(8,128)S(1)} %get-tuple-element.112), channel_id=1, source_target_pairs={{0,1},{1,2},{2,3},{3,0},{4,5},{5,6},{6,7},{7,4},{8,9},{9,10},{10,1... | collective-permute-start | bytes 1572872 | tf_op jit(solution)/shard_map/ppermute | solution.py:48
  44.1 16.1 %collective-permute-start.8 = (f32[512,256]{1,0:T(8,128)S(1)}, f32[512,256]{1,0:T(8,128)S(1)}, u32[]{:S(2)}, u32[]{:S(2)}) collective-permute-start(f32[512,256]{1,0:T(8,128)S(1)} %get-tuple-element.113), channel_id=1, source_target_pairs={{0,3},{1,0},{2,1},{3,2},{4,7},{5,4},{6,5},{7,6},{8,11},{9,8},{10,9... | collective-permute-start | bytes 1572872 | tf_op jit(solution)/shard_map/ppermute | solution.py:48
  47.5 12.7 %collective-permute-start.11 = (f32[512,256]{1,0:T(8,128)}, f32[512,256]{1,0:T(8,128)S(1)}, u32[]{:S(2)}, u32[]{:S(2)}) collective-permute-start(f32[512,256]{1,0:T(8,128)} %collective-permute-done.10), channel_id=1, source_target_pairs={{0,3},{1,0},{2,1},{3,2},{4,7},{5,4},{6,5},{7,6},{8,11},{9,8},{10,9... | collective-permute-start | bytes 1572872 | tf_op jit(solution)/shard_map/ppermute | solution.py:48
  47.6 12.7 %collective-permute-start.7 = (f32[512,256]{1,0:T(8,128)}, f32[512,256]{1,0:T(8,128)S(1)}, u32[]{:S(2)}, u32[]{:S(2)}) collective-permute-start(f32[512,256]{1,0:T(8,128)} %collective-permute-done.6), channel_id=1, source_target_pairs={{0,1},{1,2},{2,3},{3,0},{4,5},{5,6},{6,7},{7,4},{8,9},{9,10},{10,1... | collective-permute-start | bytes 1572872 | tf_op jit(solution)/shard_map/ppermute | solution.py:48
  49.7 10.5 %collective-permute-start.12 = (f32[256,256]{1,0:T(8,128)S(1)}, f32[256,256]{1,0:T(8,128)}, u32[]{:S(2)}, u32[]{:S(2)}) collective-permute-start(f32[256,256]{1,0:T(8,128)S(1)} %add_select_fusion.1), channel_id=1, source_target_pairs={{16,20},{17,21},{18,22},{19,23}} | collective-permute-start | bytes 786440 | tf_op jit(solution)/shard_map/ppermute | solution.py:96
  63.0 14.9 %collective-permute-start.19 = (f32[256,256]{1,0:T(8,128)S(1)}, f32[256,256]{1,0:T(8,128)S(1)}, u32[]{:S(2)}, u32[]{:S(2)}) collective-permute-start(f32[256,256]{1,0:T(8,128)S(1)} %get-tuple-element.74), channel_id=1, source_target_pairs={{0,0},{1,8},{2,16},{3,24},{4,32},{5,40},{6,48},{7,56},{8,64},{9,72... | collective-permute-start | bytes 786440 | tf_op jit(solution)/shard_map/ppermute | solution.py:92
  64.9 13.0 %collective-permute-start.23 = (f32[256,256]{1,0:T(8,128)S(1)}, f32[256,256]{1,0:T(8,128)S(1)}, u32[]{:S(2)}, u32[]{:S(2)}) collective-permute-start(f32[256,256]{1,0:T(8,128)S(1)} %get-tuple-element.75.refs_9_), channel_id=1, source_target_pairs={{16,112},{17,113},{18,114},{19,115},{20,116},{21,117},{22,118},{23... | collective-permute-start | bytes 786440 | tf_op jit(solution)/shard_map/ppermute | solution.py:157
  66.2 11.7 %collective-permute-start.22 = (f32[256,256]{1,0:T(8,128)S(1)}, f32[256,256]{1,0:T(8,128)S(1)}, u32[]{:S(2)}, u32[]{:S(2)}) collective-permute-start(f32[256,256]{1,0:T(8,128)S(1)} %get-tuple-element.75.refs_9_), channel_id=1, source_target_pairs={{16,80},{17,81},{18,82},{19,83},{20,84},{21,85},{22,86},{23,87},{2... | collective-permute-start | bytes 786440 | tf_op jit(solution)/shard_map/ppermute | solution.py:157
  67.5 13.1 %collective-permute-start.21 = (f32[256,256]{1,0:T(8,128)S(1)}, f32[256,256]{1,0:T(8,128)S(1)}, u32[]{:S(2)}, u32[]{:S(2)}) collective-permute-start(f32[256,256]{1,0:T(8,128)S(1)} %get-tuple-element.75.refs_9_), channel_id=1, source_target_pairs={{16,48},{17,49},{18,50},{19,51},{20,52},{21,53},{22,54},{23,55},{2... | collective-permute-start | bytes 786440 | tf_op jit(solution)/shard_map/ppermute | solution.py:157
  68.8 15.1 %collective-permute-start.17 = (f32[512,256]{1,0:T(8,128)S(1)}, f32[512,256]{1,0:T(8,128)S(1)}, u32[]{:S(2)}, u32[]{:S(2)}) collective-permute-start(f32[512,256]{1,0:T(8,128)S(1)} %get-tuple-element.72.refs_0_), channel_id=1, source_target_pairs={{0,12},{1,13},{2,14},{3,15},{4,0},{5,1},{6,2},{7,3},{8,4},{9,5},{1... | collective-permute-start | bytes 1572872 | tf_op jit(solution)/shard_map/ppermute | solution.py:48
  77.8 9.2 %collective-permute-start.15 = (f32[512,256]{1,0:T(8,128)S(1)}, f32[512,256]{1,0:T(8,128)S(1)}, u32[]{:S(2)}, u32[]{:S(2)}) collective-permute-start(f32[512,256]{1,0:T(8,128)S(1)} %get-tuple-element.72.refs_0_), channel_id=1, source_target_pairs={{0,4},{1,5},{2,6},{3,7},{4,8},{5,9},{6,10},{7,11},{8,12},{9,13},{1... | collective-permute-start | bytes 1572872 | tf_op jit(solution)/shard_map/ppermute | solution.py:48
  77.8 15.1 %collective-permute-start.18 = (f32[512,256]{1,0:T(8,128)S(1)}, f32[512,256]{1,0:T(8,128)S(1)}, u32[]{:S(2)}, u32[]{:S(2)}) collective-permute-start(f32[512,256]{1,0:T(8,128)S(1)} %get-tuple-element.73.refs_4_), channel_id=1, source_target_pairs={{0,4},{1,5},{2,6},{3,7},{4,8},{5,9},{6,10},{7,11},{8,12},{9,13},{1... | collective-permute-start | bytes 1572872 | tf_op jit(solution)/shard_map/ppermute | solution.py:48
  77.9 15.1 %collective-permute-start.16 = (f32[512,256]{1,0:T(8,128)S(1)}, f32[512,256]{1,0:T(8,128)S(1)}, u32[]{:S(2)}, u32[]{:S(2)}) collective-permute-start(f32[512,256]{1,0:T(8,128)S(1)} %get-tuple-element.73.refs_4_), channel_id=1, source_target_pairs={{0,12},{1,13},{2,14},{3,15},{4,0},{5,1},{6,2},{7,3},{8,4},{9,5},{1... | collective-permute-start | bytes 1572872 | tf_op jit(solution)/shard_map/ppermute | solution.py:48
  93.7 11.5 %collective-permute-start.24 = (f32[512,256]{1,0:T(8,128)S(1)}, f32[512,256]{1,0:T(8,128)S(1)}, u32[]{:S(2)}, u32[]{:S(2)}) collective-permute-start(f32[512,256]{1,0:T(8,128)S(1)} %collective-permute-done.15.refs_1_), channel_id=1, source_target_pairs={{0,4},{1,5},{2,6},{3,7},{4,8},{5,9},{6,10},{7,11},{8,12},{9,13},{1... | collective-permute-start | bytes 1572872 | tf_op jit(solution)/shard_map/ppermute | solution.py:48
  93.8 11.4 %collective-permute-start.25 = (f32[512,256]{1,0:T(8,128)S(1)}, f32[512,256]{1,0:T(8,128)S(1)}, u32[]{:S(2)}, u32[]{:S(2)}) collective-permute-start(f32[512,256]{1,0:T(8,128)S(1)} %collective-permute-done.16.refs_7_), channel_id=1, source_target_pairs={{0,12},{1,13},{2,14},{3,15},{4,0},{5,1},{6,2},{7,3},{8,4},{9,5},{1... | collective-permute-start | bytes 1572872 | tf_op jit(solution)/shard_map/ppermute | solution.py:48
  105.3 9.4 %collective-permute-start.30 = (f32[256,256]{1,0:T(8,128)S(1)}, f32[256,256]{1,0:T(8,128)S(1)}, u32[]{:S(2)}, u32[]{:S(2)}) collective-permute-start(f32[256,256]{1,0:T(8,128)S(1)} %broadcast_select_fusion), channel_id=1, source_target_pairs={{0,32},{16,112},{32,64},{48,16},{64,96},{80,48},{96,0},{112,80},{1... | collective-permute-start | bytes 786440 | tf_op jit(solution)/shard_map/ppermute | solution.py:101
  (18 other events, 168.6 us)

commit v9 on v7

--- a/solution.py
+++ b/solution.py
@@ -74,15 +74,20 @@
     return lax.ppermute(value, "row", [(r, r ^ 1) for r in range(N_ROW)])
 
 
+def tile_choice(r, line, cross):
+    turned = (cross - r // 4) % SIDE
+    return (turned // 2, turned % 2) if r % 2 else (cross % 2, cross // 2)
+
+
 def to_columns(value):
     pairs = []
     for r in range(N_ROW):
         for x in range(SIDE):
             for z in range(SIDE):
                 line, cross = (z, x) if r % 2 else (x, z)
-                panel, odd = cross // 2, cross % 2
+                odd, panel = tile_choice(r, line, cross)
                 quarter = (line - panel * (r % 2)) % SIDE
-                target = (quarter * 2 + panel) * N_COL + r + N_ROW * odd
+                target = ((quarter + r // 2) % SIDE * 2 + panel) * N_COL + r + N_ROW * odd
                 pairs.append((r * N_COL + x * SIDE + z, target))
     return lax.ppermute(value, ("row", "col"), pairs)
 
@@ -128,24 +133,18 @@
         choose(after, own1, near1, far1, back1),
         choose(cross, own2, near2, far2, back2),
     )
-    half = jnp.where(cross < 2, block1, block2)
-    tile = lax.dynamic_slice(half, (cross % 2 * NB, 0), (NB, NB))
-    block1, block2, tile, pivot = barrier((block1, block2, tile, block1[:NB]))
-
-    corner = [(N_COL + SIDE * a, N_COL + SIDE * a + 2) for a in range(SIDE)]
-    near1, back2, back1, near2, own, pivot_far = barrier((
-        shift_line(block1, 1),
-        shift_line(block2, -1),
-        shift_line(block1, -1),
-        shift_line(block2, 1),
-        to_columns(tile),
-        lax.ppermute(pivot, ("row", "col"), corner),
-    ))
-    pivot = choose(z, pivot, near1[:NB], pivot_far, back1[:NB])
-    near1, back2, own, pivot = barrier((near1, back2, own, pivot))
-    far1, far2, up, down, own_other, pivot_up, pivot_down, pivot_far, pivot_swap = barrier((
-        shift_line(near1, 1),
-        shift_line(back2, -1),
+    turned = (cross - row // 4) % SIDE
+    odd = jnp.where(core == 0, cross % 2, turned // 2)
+    panel = jnp.where(core == 0, cross // 2, turned % 2)
+    tile = lax.dynamic_slice(jnp.where(panel == 0, block1, block2), (odd * NB, 0), (NB, NB))
+    block1, block2, tile = barrier((block1, block2, tile))
+
+    near1, back2 = shift_line(block1, 1), shift_line(block2, -1)
+    back1, near2 = shift_line(block1, -1), shift_line(block2, 1)
+    far1, far2 = shift_line(near1, 1), shift_line(back2, -1)
+    near1, far1, back1, near2, far2, back2, own = barrier((near1, far1, back1, near2, far2, back2, to_columns(tile)))
+    pivot = choose(z, block1[:NB], near1[:NB], far1[:NB], back1[:NB])
+    up, down, own_other, pivot_up, pivot_down, pivot_far, pivot_swap = barrier((
         shift_y(own, 1),
         shift_y(own, -1),
         swap_core(own),
@@ -196,7 +195,9 @@
     copies = []
     for n in range(N_ROW):
         k = lax.rem(y + SIDE - n % SIDE, SIDE) * 2 + lax.rem(core + n // SIDE, 2)
-        target = raw.at[lax.rem(k, 2), rows_at(lax.div(k, 2), NB), :]
+        source_y = lax.div(lax.rem(lax.axis_index("col"), N_ROW), 2)
+        tile = lax.rem(lax.div(k, 2) + SIDE - source_y, SIDE)
+        target = raw.at[lax.rem(k, 2), rows_at(tile, NB), :]
         copies.append(pltpu.make_async_copy(tiles[n], target, sems.at[n]))
     return copies
 

time: 125 us -> 126 us (level); the launches traced: 123 us -> 126 us
  waiting for transfers between devices: 38.9 us -> 53.1 us
  starting transfers between devices: 54.7 us -> 44.5 us
    ppermute x1 -> x0, starting transfers between devices: 11.7 us -> none  [gather_all(): lax.ppermute(pivot, ('row', 'col'), corner)]
    ppermute x1, waiting for transfers between devices: 0.63 us -> 9.79 us  [to_columns(): return lax.ppermute(value, ('row', 'col'), pairs)]
    ppermute x1, starting transfers between devices: 2.78 us -> 10 us  [gather_all(): lax.ppermute(pivot, 'row', [(1, 5)])]
    ppermute x14, waiting for transfers between devices: 22 us -> 27.3 us  [shift_plane(): return lax.ppermute(value, ('row', 'col'), pairs)]
    ppermute x2, waiting for transfers between devices: 1.49 us -> 6.32 us  [shift_y(): return lax.ppermute(value, 'row', pairs)]
    ppermute x1 -> x0, waiting for transfers between devices: 2.91 us -> none  [gather_all(): lax.ppermute(pivot, ('row', 'col'), corner)]
    ppermute x14, starting transfers between devices: 16.3 us -> 14.7 us  [shift_plane(): return lax.ppermute(value, ('row', 'col'), pairs)]
    ppermute x1, starting transfers between devices: 2.34 us -> 0.98 us  [relay_y(): return lax.ppermute(jnp.where(core == 0, near, back), 'row', pairs)]
  transfers between devices with their start and end apart: 29 -> 28, of which waited for: 14 -> 17; matrix products, arithmetic and copies ran while one was open for 0% -> 0% of each run, Pallas kernels for 2% -> 2%
where the time goes in v9:
time: 126 us
  waiting for transfers between devices  53.1 us (42%)
  starting transfers between devices  44.5 us (35%)
  Pallas kernels  19.7 us (16%)
  other arithmetic  3.86 us (3%)
  local copies, waits for them, and re-layouts  3.81 us (3%)
    ppermute x14, waiting for transfers between devices, shift_plane(): return lax.ppermute(value, ('row', 'col'), pairs)  27.3 us
    pallas_call x1, Pallas kernels, finish(): pl.pallas_call(last_kernel, out_shape=(jax.ShapeDtypeStruct((TR, LINES, H...  17.8 us
    ppermute x14, starting transfers between devices, shift_plane(): return lax.ppermute(value, ('row', 'col'), pairs)  14.7 us
    ppermute x1, starting transfers between devices, gather_all(): lax.ppermute(pivot, 'row', [(1, 5)])  10 us
    ppermute x1, waiting for transfers between devices, to_columns(): return lax.ppermute(value, ('row', 'col'), pairs)  9.79 us
    ppermute x1, starting transfers between devices, send_far(): return lax.ppermute(value, ('row', 'col'), pairs)  6.35 us
    ppermute x2, waiting for transfers between devices, shift_y(): return lax.ppermute(value, 'row', pairs)  6.32 us
    ppermute x1, waiting for transfers between devices, send_far(): return lax.ppermute(value, ('row', 'col'), pairs)  4.9 us
  transfers between devices with their start and end apart: 28, of which 17 were waited for; matrix products, arithmetic and copies ran while one was open for 0% of the time, Pallas kernels for 2%

profile of v9, /device:TPU:1, one launch (start us, length us, event | category | flops | bytes accessed | tf_op | source)
XLA Modules:
  0.0 126.0 jit_solution(11899451589797255359)
XLA Ops:
  0.6 1.6 %slice-done = f32[8,256,1,256]{3,2,1,0:T(1,128)S(1)} async-done(((f32[8,256,4,256]{3,2,1,0:T(4,128)}), f32[8,256,1,256]{3,2,1,0:T(1,128)S(1)}, s32[]{:S(2)}) %slice-start) | async-done | bytes 2097176 | tf_op jit(solution)/shard_map/slice | solution.py:388
  3.6 6.3 %collective-permute-start.2 = (f32[512,256]{1,0:T(8,128)}, f32[512,256]{1,0:T(8,128)S(1)}, u32[]{:S(2)}, u32[]{:S(2)}) collective-permute-start(f32[512,256]{1,0:T(8,128)} %get-tuple-element.74), channel_id=1, source_target_pairs={{0,8},{1,9},{16,18},{17,19},{32,40},{33,41},{48,50},{49,51},{64,72... | collective-permute-start | bytes 1572872 | tf_op jit(solution)/shard_map/ppermute | solution.py:65
  10.1 1.5 %collective-permute-start = (f32[512,256]{1,0:T(8,128)}, f32[512,256]{1,0:T(8,128)}, u32[]{:S(2)}, u32[]{:S(2)}) collective-permute-start(f32[512,256]{1,0:T(8,128)} %get-tuple-element.76), channel_id=1, source_target_pairs={{0,4},{1,5},{2,6},{3,7},{4,8},{5,9},{6,10},{7,11},{8,12},{9,13},{1... | collective-permute-start | bytes 1572872 | tf_op jit(solution)/shard_map/ppermute | solution.py:48
  11.5 4.9 %collective-permute-done.2 = f32[512,256]{1,0:T(8,128)S(1)} collective-permute-done((f32[512,256]{1,0:T(8,128)}, f32[512,256]{1,0:T(8,128)S(1)}, u32[]{:S(2)}, u32[]{:S(2)}) %collective-permute-start.2) | collective-permute-done | bytes 524320 | tf_op jit(solution)/shard_map/ppermute | solution.py:65
  16.4 6.7 %collective-permute-done.1 = f32[512,256]{1,0:T(8,128)S(1)} collective-permute-done((f32[512,256]{1,0:T(8,128)}, f32[512,256]{1,0:T(8,128)S(1)}, u32[]{:S(2)}, u32[]{:S(2)}) %collective-permute-start.1) | collective-permute-done | bytes 524320 | tf_op jit(solution)/shard_map/ppermute | solution.py:48
  23.9 1.5 %select_select_fusion.2 = (f32[512,256]{1,0:T(8,128)S(1)}, f32[512,256]{1,0:T(8,128)S(1)}) fusion(f32[512,256]{1,0:T(8,128)} %collective-permute-done, f32[512,256]{1,0:T(8,128)} %copy-done.2, f32[512,256]{1,0:T(8,128)} %copy-done.3, f32[2048,256]{1,0:T(8,128)S(1)} %bitcast.12, pred[]{:T(512)S(6)} %eq.75, pred[]{:T(512)S(6)} %eq.74, pred[]{:T(512)S(6)} %eq.73, ...), kind=kLoop, calls=%fused_computation.2 | loop fusion | flops 786432 | bytes 3145734 | tf_op jit(solution)/shard_map/jit(_where)/select_n | solution.py:101
  27.0 2.6 %collective-permute-start.5 = (f32[512,256]{1,0:T(8,128)S(1)}, f32[512,256]{1,0:T(8,128)S(1)}, u32[]{:S(2)}, u32[]{:S(2)}) collective-permute-start(f32[512,256]{1,0:T(8,128)S(1)} %get-tuple-element.71), channel_id=1, source_target_pairs={{0,3},{1,0},{2,1},{3,2},{4,7},{5,4},{6,5},{7,6},{8,11},{9,8},{10,9... | collective-permute-start | bytes 1572872 | tf_op jit(solution)/shard_map/ppermute | solution.py:48
  29.6 4.2 %collective-permute-done.7 = f32[512,256]{1,0:T(8,128)S(1)} collective-permute-done((f32[512,256]{1,0:T(8,128)S(1)}, f32[512,256]{1,0:T(8,128)S(1)}, u32[]{:S(2)}, u32[]{:S(2)}) %collective-permute-start.7) | collective-permute-done | bytes 524320 | tf_op jit(solution)/shard_map/ppermute | solution.py:48
  35.3 5.5 %collective-permute-done.6 = f32[512,256]{1,0:T(8,128)S(1)} collective-permute-done((f32[512,256]{1,0:T(8,128)S(1)}, f32[512,256]{1,0:T(8,128)S(1)}, u32[]{:S(2)}, u32[]{:S(2)}) %collective-permute-start.6) | collective-permute-done | bytes 524320 | tf_op jit(solution)/shard_map/ppermute | solution.py:48
  40.8 4.3 %collective-permute-done.8 = f32[512,256]{1,0:T(8,128)} collective-permute-done((f32[512,256]{1,0:T(8,128)S(1)}, f32[512,256]{1,0:T(8,128)}, u32[]{:S(2)}, u32[]{:S(2)}) %collective-permute-start.8) | collective-permute-done | bytes 524320 | tf_op jit(solution)/shard_map/ppermute | solution.py:48
  46.3 1.5 %select_select_fusion = (f32[512,256]{1,0:T(8,128)S(1)}, f32[512,256]{1,0:T(8,128)S(1)}) fusion(f32[512,256]{1,0:T(8,128)S(1)} %get-tuple-element.70, f32[512,256]{1,0:T(8,128)} %copy-done.4, f32[512,256]{1,0:T(8,128)} %collective-permute-done.8, f32[512,256]{1,0:T(8,128)S(1)} %collective-permute-done.7, f32[512,256]{1,0:T(8,128)S(1)} %get-tuple-element.71, ...), kind=kLoop, calls=%fused_computation | loop fusion | flops 1310720 | bytes 5242887 | tf_op jit(solution)/shard_map/jit(_where)/select_n | solution.py:131
  48.5 1.9 %collective-permute-start.13 = (f32[512,256]{1,0:T(8,128)S(1)}, f32[512,256]{1,0:T(8,128)}, u32[]{:S(2)}, u32[]{:S(2)}) collective-permute-start(f32[512,256]{1,0:T(8,128)S(1)} %get-tuple-element.45.refs_0_), channel_id=1, source_target_pairs={{0,12},{1,13},{2,14},{3,15},{4,0},{5,1},{6,2},{7,3},{8,4},{9,5},{1... | collective-permute-start | bytes 1572872 | tf_op jit(solution)/shard_map/ppermute | solution.py:48
  50.4 2.7 %collective-permute-start.11 = (f32[512,256]{1,0:T(8,128)S(1)}, f32[512,256]{1,0:T(8,128)S(1)}, u32[]{:S(2)}, u32[]{:S(2)}) collective-permute-start(f32[512,256]{1,0:T(8,128)S(1)} %get-tuple-element.46.refs_0_), channel_id=1, source_target_pairs={{0,12},{1,13},{2,14},{3,15},{4,0},{5,1},{6,2},{7,3},{8,4},{9,5},{1... | collective-permute-start | bytes 1572872 | tf_op jit(solution)/shard_map/ppermute | solution.py:48
  53.1 3.9 %collective-permute-done.13.refs_3_ = f32[512,256]{1,0:T(8,128)} collective-permute-done((f32[512,256]{1,0:T(8,128)S(1)}, f32[512,256]{1,0:T(8,128)}, u32[]{:S(2)}, u32[]{:S(2)}) %collective-permute-start.13) | collective-permute-done | bytes 524320 | tf_op jit(solution)/shard_map/ppermute | solution.py:48
  57.0 3.0 %collective-permute-start.14 = (f32[512,256]{1,0:T(8,128)}, f32[512,256]{1,0:T(8,128)}, u32[]{:S(2)}, u32[]{:S(2)}) collective-permute-start(f32[512,256]{1,0:T(8,128)} %collective-permute-done.13.refs_3_), channel_id=1, source_target_pairs={{0,12},{1,13},{2,14},{3,15},{4,0},{5,1},{6,2},{7,3},{8,4},{9,5},{1... | collective-permute-start | bytes 1572872 | tf_op jit(solution)/shard_map/ppermute | solution.py:48
  60.1 2.5 %collective-permute-start.15 = (f32[256,256]{1,0:T(8,128)}, f32[256,256]{1,0:T(8,128)S(1)}, u32[]{:S(2)}, u32[]{:S(2)}) collective-permute-start(f32[256,256]{1,0:T(8,128)} %dynamic-slice_select_fusion), channel_id=1, source_target_pairs={{0,0},{1,8},{2,16},{3,24},{4,32},{5,40},{6,48},{7,56},{8,64},{9,72... | collective-permute-start | bytes 786440 | tf_op jit(solution)/shard_map/ppermute | solution.py:92
  62.5 9.8 %collective-permute-done.15.refs_4_ = f32[256,256]{1,0:T(8,128)S(1)} collective-permute-done((f32[256,256]{1,0:T(8,128)}, f32[256,256]{1,0:T(8,128)S(1)}, u32[]{:S(2)}, u32[]{:S(2)}) %collective-permute-start.15) | collective-permute-done | bytes 262176 | tf_op jit(solution)/shard_map/ppermute | solution.py:92
  75.1 10.0 %collective-permute-start.21 = (f32[256,256]{1,0:T(8,128)S(1)}, f32[256,256]{1,0:T(8,128)S(1)}, u32[]{:S(2)}, u32[]{:S(2)}) collective-permute-start(f32[256,256]{1,0:T(8,128)S(1)} %select_select_fusion.4.refs_13_), channel_id=1, source_target_pairs={{16,80},{17,81},{18,82},{19,83},{20,84},{21,85},{22,86},{23,87},{2... | collective-permute-start | bytes 786440 | tf_op jit(solution)/shard_map/ppermute | solution.py:153
  91.2 4.2 %collective-permute-done.17.refs_7_ = f32[256,256]{1,0:T(8,128)S(1)} collective-permute-done((f32[256,256]{1,0:T(8,128)S(1)}, f32[256,256]{1,0:T(8,128)S(1)}, u32[]{:S(2)}, u32[]{:S(2)}) %collective-permute-start.17) | collective-permute-done | bytes 262176 | tf_op jit(solution)/shard_map/ppermute | solution.py:70
  95.3 2.2 %collective-permute-done.16.refs_5_ = f32[256,256]{1,0:T(8,128)S(1)} collective-permute-done((f32[256,256]{1,0:T(8,128)S(1)}, f32[256,256]{1,0:T(8,128)S(1)}, u32[]{:S(2)}, u32[]{:S(2)}) %collective-permute-start.16) | collective-permute-done | bytes 262176 | tf_op jit(solution)/shard_map/ppermute | solution.py:70
  100.6 2.5 %collective-permute-done.23.refs_6_ = f32[256,256]{1,0:T(8,128)S(1)} collective-permute-done((f32[256,256]{1,0:T(8,128)S(1)}, f32[256,256]{1,0:T(8,128)S(1)}, u32[]{:S(2)}, u32[]{:S(2)}) %collective-permute-start.23) | collective-permute-done | bytes 262176 | tf_op jit(solution)/shard_map/ppermute | solution.py:97
  103.2 2.9 %collective-permute-start.27 = (f32[256,256]{1,0:T(8,128)S(1)}, f32[256,256]{1,0:T(8,128)S(1)}, u32[]{:S(2)}, u32[]{:S(2)}) collective-permute-start(f32[256,256]{1,0:T(8,128)S(1)} %collective-permute-done.23.refs_6_), channel_id=1, source_target_pairs={{0,16},{16,0},{32,48},{48,32},{64,80},{80,64},{96,112},{112,96},{1... | collective-permute-start | bytes 786440 | tf_op jit(solution)/shard_map/ppermute | solution.py:74
  106.1 1.9 %solve_first.1 = (bf16[8,256,256]{2,1,0:T(8,128)(2,1)S(1)}, bf16[8,256,256]{2,1,0:T(8,128)(2,1)S(1)}) custom-call(f32[512,256]{1,0:T(8,128)S(1)} %get-tuple-element.46.refs_0_, f32[512,256]{1,0:T(8,128)S(1)} %collective-permute-done.9.refs_1_, f32[512,256]{1,0:T(8,128)S(1)} %collective-permute-done.10.refs_2_, ...), custom_call_target="tpu_custom_call" | custom-call | flops 805306368 | bytes 4194304 | tf_op jit(solution)/shard_map/solve_first/pallas_call | solution.py:227
  108.0 17.8 %solve_and_update.1 = (f32[8,2048,128]{2,1,0:T(8,128)}, f32[8,256,256]{2,1,0:T(8,128)}) custom-call(f32[512,256]{1,0:T(8,128)S(1)} %get-tuple-element.45.refs_0_, f32[512,256]{1,0:T(8,128)} %collective-permute-done.12.refs_1_, f32[512,256]{1,0:T(8,128)} %collective-permute-done.14.refs_2_, f32[512,256]{1,0:T(8,128)} %collective-permute-done.13.refs_3_, ...), custom_call_target="tpu_custom_call" | custom-call | flops 6710886400 | bytes 20971520 | tf_op jit(solution)/shard_map/solve_and_update/pallas_call | solution.py:351
  (56 shorter events, 19.2 us)
Async XLA Ops:
  3.6 12.8 %collective-permute-start.2 = (f32[512,256]{1,0:T(8,128)}, f32[512,256]{1,0:T(8,128)S(1)}, u32[]{:S(2)}, u32[]{:S(2)}) collective-permute-start(f32[512,256]{1,0:T(8,128)} %get-tuple-element.74), channel_id=1, source_target_pairs={{0,8},{1,9},{16,18},{17,19},{32,40},{33,41},{48,50},{49,51},{64,72... | collective-permute-start | bytes 1572872 | tf_op jit(solution)/shard_map/ppermute | solution.py:65
  10.0 13.1 %collective-permute-start.1 = (f32[512,256]{1,0:T(8,128)}, f32[512,256]{1,0:T(8,128)S(1)}, u32[]{:S(2)}, u32[]{:S(2)}) collective-permute-start(f32[512,256]{1,0:T(8,128)} %get-tuple-element.75), channel_id=1, source_target_pairs={{0,12},{1,13},{2,14},{3,15},{4,0},{5,1},{6,2},{7,3},{8,4},{9,5},{1... | collective-permute-start | bytes 1572872 | tf_op jit(solution)/shard_map/ppermute | solution.py:48
  10.1 13.8 %collective-permute-start = (f32[512,256]{1,0:T(8,128)}, f32[512,256]{1,0:T(8,128)}, u32[]{:S(2)}, u32[]{:S(2)}) collective-permute-start(f32[512,256]{1,0:T(8,128)} %get-tuple-element.76), channel_id=1, source_target_pairs={{0,4},{1,5},{2,6},{3,7},{4,8},{5,9},{6,10},{7,11},{8,12},{9,13},{1... | collective-permute-start | bytes 1572872 | tf_op jit(solution)/shard_map/ppermute | solution.py:48
  25.4 8.4 %collective-permute-start.7 = (f32[512,256]{1,0:T(8,128)S(1)}, f32[512,256]{1,0:T(8,128)S(1)}, u32[]{:S(2)}, u32[]{:S(2)}) collective-permute-start(f32[512,256]{1,0:T(8,128)S(1)} %get-tuple-element.70), channel_id=1, source_target_pairs={{0,3},{1,0},{2,1},{3,2},{4,7},{5,4},{6,5},{7,6},{8,11},{9,8},{10,9... | collective-permute-start | bytes 1572872 | tf_op jit(solution)/shard_map/ppermute | solution.py:48
  25.5 9.6 %collective-permute-start.3 = (f32[512,256]{1,0:T(8,128)S(1)}, f32[512,256]{1,0:T(8,128)S(1)}, u32[]{:S(2)}, u32[]{:S(2)}) collective-permute-start(f32[512,256]{1,0:T(8,128)S(1)} %get-tuple-element.71), channel_id=1, source_target_pairs={{0,1},{1,2},{2,3},{3,0},{4,5},{5,6},{6,7},{7,4},{8,9},{9,10},{10,1... | collective-permute-start | bytes 1572872 | tf_op jit(solution)/shard_map/ppermute | solution.py:48
  27.0 13.9 %collective-permute-start.6 = (f32[512,256]{1,0:T(8,128)S(1)}, f32[512,256]{1,0:T(8,128)S(1)}, u32[]{:S(2)}, u32[]{:S(2)}) collective-permute-start(f32[512,256]{1,0:T(8,128)S(1)} %get-tuple-element.70), channel_id=1, source_target_pairs={{0,1},{1,2},{2,3},{3,0},{4,5},{5,6},{6,7},{7,4},{8,9},{9,10},{10,1... | collective-permute-start | bytes 1572872 | tf_op jit(solution)/shard_map/ppermute | solution.py:48
  27.0 13.8 %collective-permute-start.5 = (f32[512,256]{1,0:T(8,128)S(1)}, f32[512,256]{1,0:T(8,128)S(1)}, u32[]{:S(2)}, u32[]{:S(2)}) collective-permute-start(f32[512,256]{1,0:T(8,128)S(1)} %get-tuple-element.71), channel_id=1, source_target_pairs={{0,3},{1,0},{2,1},{3,2},{4,7},{5,4},{6,5},{7,6},{8,11},{9,8},{10,9... | collective-permute-start | bytes 1572872 | tf_op jit(solution)/shard_map/ppermute | solution.py:48
  33.8 11.3 %collective-permute-start.8 = (f32[512,256]{1,0:T(8,128)S(1)}, f32[512,256]{1,0:T(8,128)}, u32[]{:S(2)}, u32[]{:S(2)}) collective-permute-start(f32[512,256]{1,0:T(8,128)S(1)} %collective-permute-done.7), channel_id=1, source_target_pairs={{0,3},{1,0},{2,1},{3,2},{4,7},{5,4},{6,5},{7,6},{8,11},{9,8},{10,9... | collective-permute-start | bytes 1572872 | tf_op jit(solution)/shard_map/ppermute | solution.py:48
  35.1 11.2 %collective-permute-start.4 = (f32[512,256]{1,0:T(8,128)S(1)}, f32[512,256]{1,0:T(8,128)}, u32[]{:S(2)}, u32[]{:S(2)}) collective-permute-start(f32[512,256]{1,0:T(8,128)S(1)} %collective-permute-done.3), channel_id=1, source_target_pairs={{0,1},{1,2},{2,3},{3,0},{4,5},{5,6},{6,7},{7,4},{8,9},{9,10},{10,1... | collective-permute-start | bytes 1572872 | tf_op jit(solution)/shard_map/ppermute | solution.py:48
  48.5 8.4 %collective-permute-start.13 = (f32[512,256]{1,0:T(8,128)S(1)}, f32[512,256]{1,0:T(8,128)}, u32[]{:S(2)}, u32[]{:S(2)}) collective-permute-start(f32[512,256]{1,0:T(8,128)S(1)} %get-tuple-element.45.refs_0_), channel_id=1, source_target_pairs={{0,12},{1,13},{2,14},{3,15},{4,0},{5,1},{6,2},{7,3},{8,4},{9,5},{1... | collective-permute-start | bytes 1572872 | tf_op jit(solution)/shard_map/ppermute | solution.py:48
  50.4 9.6 %collective-permute-start.9 = (f32[512,256]{1,0:T(8,128)S(1)}, f32[512,256]{1,0:T(8,128)S(1)}, u32[]{:S(2)}, u32[]{:S(2)}) collective-permute-start(f32[512,256]{1,0:T(8,128)S(1)} %get-tuple-element.46.refs_0_), channel_id=1, source_target_pairs={{0,4},{1,5},{2,6},{3,7},{4,8},{5,9},{6,10},{7,11},{8,12},{9,13},{1... | collective-permute-start | bytes 1572872 | tf_op jit(solution)/shard_map/ppermute | solution.py:48
  50.4 21.9 %collective-permute-start.12 = (f32[512,256]{1,0:T(8,128)S(1)}, f32[512,256]{1,0:T(8,128)}, u32[]{:S(2)}, u32[]{:S(2)}) collective-permute-start(f32[512,256]{1,0:T(8,128)S(1)} %get-tuple-element.45.refs_0_), channel_id=1, source_target_pairs={{0,4},{1,5},{2,6},{3,7},{4,8},{5,9},{6,10},{7,11},{8,12},{9,13},{1... | collective-permute-start | bytes 1572872 | tf_op jit(solution)/shard_map/ppermute | solution.py:48
  50.4 21.9 %collective-permute-start.11 = (f32[512,256]{1,0:T(8,128)S(1)}, f32[512,256]{1,0:T(8,128)S(1)}, u32[]{:S(2)}, u32[]{:S(2)}) collective-permute-start(f32[512,256]{1,0:T(8,128)S(1)} %get-tuple-element.46.refs_0_), channel_id=1, source_target_pairs={{0,12},{1,13},{2,14},{3,15},{4,0},{5,1},{6,2},{7,3},{8,4},{9,5},{1... | collective-permute-start | bytes 1572872 | tf_op jit(solution)/shard_map/ppermute | solution.py:48
  57.0 15.3 %collective-permute-start.14 = (f32[512,256]{1,0:T(8,128)}, f32[512,256]{1,0:T(8,128)}, u32[]{:S(2)}, u32[]{:S(2)}) collective-permute-start(f32[512,256]{1,0:T(8,128)} %collective-permute-done.13.refs_3_), channel_id=1, source_target_pairs={{0,12},{1,13},{2,14},{3,15},{4,0},{5,1},{6,2},{7,3},{8,4},{9,5},{1... | collective-permute-start | bytes 1572872 | tf_op jit(solution)/shard_map/ppermute | solution.py:48
  60.0 13.6 %collective-permute-start.10 = (f32[512,256]{1,0:T(8,128)S(1)}, f32[512,256]{1,0:T(8,128)S(1)}, u32[]{:S(2)}, u32[]{:S(2)}) collective-permute-start(f32[512,256]{1,0:T(8,128)S(1)} %collective-permute-done.9.refs_1_), channel_id=1, source_target_pairs={{0,4},{1,5},{2,6},{3,7},{4,8},{5,9},{6,10},{7,11},{8,12},{9,13},{1... | collective-permute-start | bytes 1572872 | tf_op jit(solution)/shard_map/ppermute | solution.py:48
  60.1 12.3 %collective-permute-start.15 = (f32[256,256]{1,0:T(8,128)}, f32[256,256]{1,0:T(8,128)S(1)}, u32[]{:S(2)}, u32[]{:S(2)}) collective-permute-start(f32[256,256]{1,0:T(8,128)} %dynamic-slice_select_fusion), channel_id=1, source_target_pairs={{0,0},{1,8},{2,16},{3,24},{4,32},{5,40},{6,48},{7,56},{8,64},{9,72... | collective-permute-start | bytes 786440 | tf_op jit(solution)/shard_map/ppermute | solution.py:92
  73.8 14.1 %collective-permute-start.22 = (f32[256,256]{1,0:T(8,128)S(1)}, f32[256,256]{1,0:T(8,128)S(1)}, u32[]{:S(2)}, u32[]{:S(2)}) collective-permute-start(f32[256,256]{1,0:T(8,128)S(1)} %select_select_fusion.4.refs_13_), channel_id=1, source_target_pairs={{16,0},{17,1},{18,2},{19,3},{20,4},{21,5},{22,6},{23,7},{24,8},{25... | collective-permute-start | bytes 786440 | tf_op jit(solution)/shard_map/ppermute | solution.py:154
  75.1 13.3 %collective-permute-start.21 = (f32[256,256]{1,0:T(8,128)S(1)}, f32[256,256]{1,0:T(8,128)S(1)}, u32[]{:S(2)}, u32[]{:S(2)}) collective-permute-start(f32[256,256]{1,0:T(8,128)S(1)} %select_select_fusion.4.refs_13_), channel_id=1, source_target_pairs={{16,80},{17,81},{18,82},{19,83},{20,84},{21,85},{22,86},{23,87},{2... | collective-permute-start | bytes 786440 | tf_op jit(solution)/shard_map/ppermute | solution.py:153
  85.1 5.2 %collective-permute-start.20 = (f32[256,256]{1,0:T(8,128)S(1)}, f32[256,256]{1,0:T(8,128)S(1)}, u32[]{:S(2)}, u32[]{:S(2)}) collective-permute-start(f32[256,256]{1,0:T(8,128)S(1)} %select_select_fusion.4.refs_13_), channel_id=1, source_target_pairs={{16,112},{17,113},{18,114},{19,115},{20,116},{21,117},{22,118},{23... | collective-permute-start | bytes 786440 | tf_op jit(solution)/shard_map/ppermute | solution.py:152
  86.4 4.8 %collective-permute-start.19 = (f32[256,256]{1,0:T(8,128)S(1)}, f32[256,256]{1,0:T(8,128)S(1)}, u32[]{:S(2)}, u32[]{:S(2)}) collective-permute-start(f32[256,256]{1,0:T(8,128)S(1)} %select_select_fusion.4.refs_13_), channel_id=1, source_target_pairs={{16,48},{17,49},{18,50},{19,51},{20,52},{21,53},{22,54},{23,55},{2... | collective-permute-start | bytes 786440 | tf_op jit(solution)/shard_map/ppermute | solution.py:151
  87.8 7.5 %collective-permute-start.17 = (f32[256,256]{1,0:T(8,128)S(1)}, f32[256,256]{1,0:T(8,128)S(1)}, u32[]{:S(2)}, u32[]{:S(2)}) collective-permute-start(f32[256,256]{1,0:T(8,128)S(1)} %collective-permute-done.15.refs_4_), channel_id=1, source_target_pairs={{0,96},{16,112},{32,0},{48,16},{64,32},{80,48},{96,64},{112,80},{1... | collective-permute-start | bytes 786440 | tf_op jit(solution)/shard_map/ppermute | solution.py:70
  88.4 9.1 %collective-permute-start.16 = (f32[256,256]{1,0:T(8,128)S(1)}, f32[256,256]{1,0:T(8,128)S(1)}, u32[]{:S(2)}, u32[]{:S(2)}) collective-permute-start(f32[256,256]{1,0:T(8,128)S(1)} %collective-permute-done.15.refs_4_), channel_id=1, source_target_pairs={{0,32},{16,48},{32,64},{48,80},{64,96},{80,112},{96,0},{112,16},{1... | collective-permute-start | bytes 786440 | tf_op jit(solution)/shard_map/ppermute | solution.py:70
  97.6 5.6 %collective-permute-start.23 = (f32[256,256]{1,0:T(8,128)S(1)}, f32[256,256]{1,0:T(8,128)S(1)}, u32[]{:S(2)}, u32[]{:S(2)}) collective-permute-start(f32[256,256]{1,0:T(8,128)S(1)} %broadcast_select_fusion), channel_id=1, source_target_pairs={{0,32},{16,112},{32,64},{48,16},{64,96},{80,48},{96,0},{112,80},{1... | collective-permute-start | bytes 786440 | tf_op jit(solution)/shard_map/ppermute | solution.py:97
  103.2 4.8 %collective-permute-start.27 = (f32[256,256]{1,0:T(8,128)S(1)}, f32[256,256]{1,0:T(8,128)S(1)}, u32[]{:S(2)}, u32[]{:S(2)}) collective-permute-start(f32[256,256]{1,0:T(8,128)S(1)} %collective-permute-done.23.refs_6_), channel_id=1, source_target_pairs={{0,16},{16,0},{32,48},{48,32},{64,80},{80,64},{96,112},{112,96},{1... | collective-permute-start | bytes 786440 | tf_op jit(solution)/shard_map/ppermute | solution.py:74
  (11 other events, 101.0 us)

commit v10 on v9

--- a/solution.py
+++ b/solution.py
@@ -1,5 +1,3 @@
-import functools
-
 import jax
 import jax.numpy as jnp
 from jax import lax
@@ -144,26 +142,23 @@
     far1, far2 = shift_line(near1, 1), shift_line(back2, -1)
     near1, far1, back1, near2, far2, back2, own = barrier((near1, far1, back1, near2, far2, back2, to_columns(tile)))
     pivot = choose(z, block1[:NB], near1[:NB], far1[:NB], back1[:NB])
-    up, down, own_other, pivot_up, pivot_down, pivot_far, pivot_swap = barrier((
+    up, down, own_other, *odd = barrier((
         shift_y(own, 1),
         shift_y(own, -1),
         swap_core(own),
-        lax.ppermute(pivot, "row", [(1, 3)]),
-        lax.ppermute(pivot, "row", [(1, 7)]),
-        lax.ppermute(pivot, "row", [(1, 5)]),
-        lax.ppermute(pivot, "row", [(1, 0)]),
+        *[lax.ppermute(pivot, "row", [(1, to)]) for to in (3, 5, 7)],
     ))
     panel1 = [block1, near1, far1, back1]
     panel2 = [block2, near2, far2, back2]
-    odd = pivot_up + pivot_down + pivot_far
+    odd = jnp.where(row == 1, pivot, sum(odd))
     last, up_other, down_other, even = barrier((
         relay_y(up, down, core),
         swap_core(up),
         swap_core(down),
-        lax.ppermute(odd, "row", [(3, 2), (5, 4), (7, 6)]),
+        lax.ppermute(odd, "row", [(1, 0), (3, 2), (5, 4), (7, 6)]),
     ))
     cols = [own, up, last, down, own_other, up_other, swap_core(last), down_other]
-    pivots = [pivot_swap, pivot, even, odd]
+    pivots = [even, odd]
     return panel1, panel2, cols, pivots
 
 
@@ -247,7 +242,7 @@
 
 def last_kernel(*refs):
     pieces, cols = refs[:SIDE], refs[SIDE : SIDE + N_ROW]
-    pivots, refs = refs[SIDE + N_ROW : SIDE + N_ROW + 4], refs[SIDE + N_ROW + 4 :]
+    pivots, refs = refs[SIDE + N_ROW : SIDE + N_ROW + 2], refs[SIDE + N_ROW + 2 :]
     matrix, inv_in, high_in, low_in, band, out, panel, *refs = refs
     tiles, raw, raw_cols, row_high1, row_low1, row_high2, row_low2, col_high, col_low, even, odd, *refs = refs
     inv, pivot, sems, col_sems, in_sems, out_sems, panel_sems, small_sems = refs
@@ -258,13 +253,13 @@
     small = [(inv_in, inv), (pivots[0], pivot), (high_in, row_high1), (low_in, row_low1)]
     small = [pltpu.make_async_copy(a, b, small_sems.at[n]) for n, (a, b) in enumerate(small)]
     small[0].start()
-    for n, rows in enumerate(((0,), (1,), (2, 4, 6), (3, 5, 7))):
-
-        @pl.when(functools.reduce(jnp.logical_or, [r == row for row in rows]))
+    for n in range(2):
+
+        @pl.when(lax.rem(r, 2) == n)
         def _():
             pltpu.make_async_copy(pivots[n], pivot, small_sems.at[1]).start()
 
-    for copy in small[2:] + copies + col_copies + loads:
+    for copy in col_copies + small[2:] + copies + loads:
         copy.start()
     small[0].wait()
     weights0 = deep(inv[0].T)
@@ -273,31 +268,37 @@
     one_high, one_low = split(dot3(pivot[...], weights0).T)
     rest_weights = join(one_low, one_high)
 
-    def used(high, low, code):
+    def subtracted(raw_part, high, low, codes):
         full = dot(high, one_high)
         rest = dot(jnp.concatenate([high, low], axis=1), rest_weights)
-        return jnp.where(code == 2, 0.0, full + jnp.where(code == 0, rest, 0.0))
-
-    def column(q, carry):
-        first = dot3(raw_cols[0, rows_at(q, NB), :], weights0)
-        col_high[q, :NB, :], col_low[q, :NB, :] = split(first.T)
-        high, low = split(first)
-        tile = raw_cols[1, rows_at(q, NB), :] - used(high, low, band[q * N_COL + c, 1])
-        col_high[q, NB:, :], col_low[q, NB:, :] = split(dot3(tile, weights1).T)
-        return carry
+        parts = []
+        for n, code in enumerate(codes):
+            at = slice(n * NB, (n + 1) * NB)
+            taken = jnp.where(code == 2, 0.0, full[at] + jnp.where(code == 0, rest[at], 0.0))
+            parts.append(raw_part[at] - taken)
+        return jnp.concatenate(parts, axis=0)
 
     panels = [pltpu.make_async_copy(raw.at[pl.ds(p * NB, NB), :], panel.at[p], panel_sems.at[p]) for p in range(TR)]
 
-    def solve(p):
-        at = pl.ds(p * NB, NB)
-        tile = raw[at, :] - used(row_high1[p], row_low1[p], band[p * N_ROW + r, 1])
-        solved = dot3(tile, weights1)
+    def solve(step):
+        at, tiles_at = pl.ds(step * PAIR, PAIR), pl.ds(step * STEP, STEP)
+        high, low = row_high1[tiles_at].reshape(PAIR, NB), row_low1[tiles_at].reshape(PAIR, NB)
+        codes = [band[(step * STEP + p) * N_ROW + r, 1] for p in range(STEP)]
+        solved = dot3(subtracted(raw[at, :], high, low, codes), weights1)
         raw[at, :] = solved
-        row_high2[p], row_low2[p] = split(solved)
+        high, low = split(solved)
+        row_high2[tiles_at], row_low2[tiles_at] = high.reshape(STEP, NB, NB), low.reshape(STEP, NB, NB)
 
     for copy in col_copies:
         copy.wait()
-    lax.fori_loop(0, TC, column, 0, unroll=2)
+    first = dot3(raw_cols[0], weights0)
+    high, low = split(first)
+    codes = [band[q * N_COL + c, 1] for q in range(TC)]
+    second = dot3(subtracted(raw_cols[1], high, low, codes), weights1)
+    for q in range(TC):
+        at = slice(q * NB, (q + 1) * NB)
+        col_high[q, :NB, :], col_low[q, :NB, :] = split(first[at].T)
+        col_high[q, NB:, :], col_low[q, NB:, :] = split(second[at].T)
     for copy in small[2:] + copies:
         copy.wait()
 
@@ -330,8 +331,8 @@
             for p in range(STEP):
                 loads[(step - 1) * STEP + p].wait()
         for q in range(TC):
-            if step + 1 < steps and q < STEP:
-                solve((step + 1) * STEP + q)
+            if step + 1 < steps and q == 0:
+                solve(step + 1)
             if 0 <= step < steps:
                 multiply(step, q, product)
             if step > 0:
@@ -354,7 +355,7 @@
             jax.ShapeDtypeStruct((TR, LINES, HALF), F32),
             jax.ShapeDtypeStruct((TR, NB, NB), F32),
         ),
-        in_specs=[ANY] * (SIDE + N_ROW + 4 + 4) + [SMEM],
+        in_specs=[ANY] * (SIDE + N_ROW + 2 + 4) + [SMEM],
         out_specs=[ANY] * 2,
         scratch_shapes=[
             pltpu.VMEM((TR, LINES, HALF), F32),

time: 126 us -> 128 us (1.016)
  waiting for transfers between devices: 53.1 us -> 51.1 us
  other arithmetic: 3.86 us -> 5.84 us
    ppermute x5 -> x4, starting transfers between devices: 14.6 us -> 19.1 us  [the longest x3 14.8 us: gather_all(): lax.ppermute(pivot, 'row', [(1, to)])]
    ppermute x4, starting transfers between devices: 4.36 us -> 1.4 us  [swap_core(): return lax.ppermute(value, 'row', [(r, r ^ 1) for r in range(N_ROW)])]
    ppermute x1, waiting for transfers between devices: 2.53 us -> 0.01 us  [relay_y(): return lax.ppermute(jnp.where(core == 0, near, back), 'row', pairs)]
    select_n x0 -> x1, other arithmetic: none -> 1.32 us  [gather_all(): odd = jnp.where(row == 1, pivot, sum(odd))]
    ppermute x5 -> x4, waiting for transfers between devices: 2.3 us -> 3.13 us  [the longest x3 2.6 us: gather_all(): lax.ppermute(pivot, 'row', [(1, to)])]
  transfers between devices with their start and end apart: 28 -> 27, of which waited for: 17 -> 17; matrix products, arithmetic and copies ran while one was open for 0% -> 1% of each run, Pallas kernels for 2% -> 1%
where the time goes in v10:
time: 128 us; the launch traced here: 127 us
  waiting for transfers between devices  51.1 us (40%)
  starting transfers between devices  45.5 us (36%)
  Pallas kernels  19.9 us (16%)
  other arithmetic  5.84 us (5%)
  local copies, waits for them, and re-layouts  3.79 us (3%)
    ppermute x14, waiting for transfers between devices, shift_plane(): return lax.ppermute(value, ('row', 'col'), pairs)  27.2 us
    pallas_call x1, Pallas kernels, finish(): pl.pallas_call(last_kernel, out_shape=(jax.ShapeDtypeStruct((TR, LINES, H...  18.1 us
    ppermute x14, starting transfers between devices, shift_plane(): return lax.ppermute(value, ('row', 'col'), pairs)  14.8 us
    ppermute x3, starting transfers between devices, gather_all(): lax.ppermute(pivot, 'row', [(1, to)])  14.8 us
    ppermute x1, waiting for transfers between devices, to_columns(): return lax.ppermute(value, ('row', 'col'), pairs)  9.82 us
    ppermute x1, starting transfers between devices, send_far(): return lax.ppermute(value, ('row', 'col'), pairs)  6.35 us
    ppermute x2, waiting for transfers between devices, shift_y(): return lax.ppermute(value, 'row', pairs)  5.17 us
    ppermute x1, waiting for transfers between devices, send_far(): return lax.ppermute(value, ('row', 'col'), pairs)  4.9 us
  transfers between devices with their start and end apart: 27, of which 17 were waited for; matrix products, arithmetic and copies ran while one was open for 1% of the time, Pallas kernels for 1%

profile of v10, /device:TPU:1, one launch (start us, length us, event | category | flops | bytes accessed | tf_op | source)
XLA Modules:
  0.0 127.2 jit_solution(1836697169255899692)
XLA Ops:
  0.6 1.6 %slice-done = f32[8,256,1,256]{3,2,1,0:T(1,128)S(1)} async-done(((f32[8,256,4,256]{3,2,1,0:T(4,128)}), f32[8,256,1,256]{3,2,1,0:T(1,128)S(1)}, s32[]{:S(2)}) %slice-start) | async-done | bytes 2097176 | tf_op jit(solution)/shard_map/slice | solution.py:389
  3.6 6.3 %collective-permute-start.2 = (f32[512,256]{1,0:T(8,128)}, f32[512,256]{1,0:T(8,128)S(1)}, u32[]{:S(2)}, u32[]{:S(2)}) collective-permute-start(f32[512,256]{1,0:T(8,128)} %get-tuple-element.72), channel_id=1, source_target_pairs={{0,8},{1,9},{16,18},{17,19},{32,40},{33,41},{48,50},{49,51},{64,72... | collective-permute-start | bytes 1572872 | tf_op jit(solution)/shard_map/ppermute | solution.py:63
  11.5 4.9 %collective-permute-done.2 = f32[512,256]{1,0:T(8,128)S(1)} collective-permute-done((f32[512,256]{1,0:T(8,128)}, f32[512,256]{1,0:T(8,128)S(1)}, u32[]{:S(2)}, u32[]{:S(2)}) %collective-permute-start.2) | collective-permute-done | bytes 524320 | tf_op jit(solution)/shard_map/ppermute | solution.py:63
  16.4 6.7 %collective-permute-done.1 = f32[512,256]{1,0:T(8,128)S(1)} collective-permute-done((f32[512,256]{1,0:T(8,128)}, f32[512,256]{1,0:T(8,128)S(1)}, u32[]{:S(2)}, u32[]{:S(2)}) %collective-permute-start.1) | collective-permute-done | bytes 524320 | tf_op jit(solution)/shard_map/ppermute | solution.py:46
  23.9 1.5 %select_select_fusion.2 = (f32[512,256]{1,0:T(8,128)S(1)}, f32[512,256]{1,0:T(8,128)S(1)}) fusion(f32[512,256]{1,0:T(8,128)} %collective-permute-done, f32[512,256]{1,0:T(8,128)} %copy-done.4, f32[512,256]{1,0:T(8,128)} %copy-done.5, f32[2048,256]{1,0:T(8,128)S(1)} %bitcast.12, pred[]{:T(512)S(6)} %eq.78, pred[]{:T(512)S(6)} %eq.77, pred[]{:T(512)S(6)} %eq.76, ...), kind=kLoop, calls=%fused_computation.2 | loop fusion | flops 786432 | bytes 3145734 | tf_op jit(solution)/shard_map/jit(_where)/select_n | solution.py:99
  27.0 2.6 %collective-permute-start.5 = (f32[512,256]{1,0:T(8,128)S(1)}, f32[512,256]{1,0:T(8,128)S(1)}, u32[]{:S(2)}, u32[]{:S(2)}) collective-permute-start(f32[512,256]{1,0:T(8,128)S(1)} %get-tuple-element.69), channel_id=1, source_target_pairs={{0,3},{1,0},{2,1},{3,2},{4,7},{5,4},{6,5},{7,6},{8,11},{9,8},{10,9... | collective-permute-start | bytes 1572872 | tf_op jit(solution)/shard_map/ppermute | solution.py:46
  29.6 4.2 %collective-permute-done.7 = f32[512,256]{1,0:T(8,128)S(1)} collective-permute-done((f32[512,256]{1,0:T(8,128)S(1)}, f32[512,256]{1,0:T(8,128)S(1)}, u32[]{:S(2)}, u32[]{:S(2)}) %collective-permute-start.7) | collective-permute-done | bytes 524320 | tf_op jit(solution)/shard_map/ppermute | solution.py:46
  35.3 5.5 %collective-permute-done.6 = f32[512,256]{1,0:T(8,128)S(1)} collective-permute-done((f32[512,256]{1,0:T(8,128)S(1)}, f32[512,256]{1,0:T(8,128)S(1)}, u32[]{:S(2)}, u32[]{:S(2)}) %collective-permute-start.6) | collective-permute-done | bytes 524320 | tf_op jit(solution)/shard_map/ppermute | solution.py:46
  40.8 4.3 %collective-permute-done.8 = f32[512,256]{1,0:T(8,128)} collective-permute-done((f32[512,256]{1,0:T(8,128)S(1)}, f32[512,256]{1,0:T(8,128)}, u32[]{:S(2)}, u32[]{:S(2)}) %collective-permute-start.8) | collective-permute-done | bytes 524320 | tf_op jit(solution)/shard_map/ppermute | solution.py:46
  48.5 1.9 %collective-permute-start.13 = (f32[512,256]{1,0:T(8,128)S(1)}, f32[512,256]{1,0:T(8,128)S(1)}, u32[]{:S(2)}, u32[]{:S(2)}) collective-permute-start(f32[512,256]{1,0:T(8,128)S(1)} %get-tuple-element.44.refs_0_), channel_id=1, source_target_pairs={{0,12},{1,13},{2,14},{3,15},{4,0},{5,1},{6,2},{7,3},{8,4},{9,5},{1... | collective-permute-start | bytes 1572872 | tf_op jit(solution)/shard_map/ppermute | solution.py:46
  50.4 2.7 %collective-permute-start.11 = (f32[512,256]{1,0:T(8,128)S(1)}, f32[512,256]{1,0:T(8,128)S(1)}, u32[]{:S(2)}, u32[]{:S(2)}) collective-permute-start(f32[512,256]{1,0:T(8,128)S(1)} %get-tuple-element.45.refs_0_), channel_id=1, source_target_pairs={{0,12},{1,13},{2,14},{3,15},{4,0},{5,1},{6,2},{7,3},{8,4},{9,5},{1... | collective-permute-start | bytes 1572872 | tf_op jit(solution)/shard_map/ppermute | solution.py:46
  53.1 3.8 %collective-permute-done.13.refs_3_ = f32[512,256]{1,0:T(8,128)S(1)} collective-permute-done((f32[512,256]{1,0:T(8,128)S(1)}, f32[512,256]{1,0:T(8,128)S(1)}, u32[]{:S(2)}, u32[]{:S(2)}) %collective-permute-start.13) | collective-permute-done | bytes 524320 | tf_op jit(solution)/shard_map/ppermute | solution.py:46
  56.8 3.1 %collective-permute-start.14 = (f32[512,256]{1,0:T(8,128)S(1)}, f32[512,256]{1,0:T(8,128)}, u32[]{:S(2)}, u32[]{:S(2)}) collective-permute-start(f32[512,256]{1,0:T(8,128)S(1)} %collective-permute-done.13.refs_3_), channel_id=1, source_target_pairs={{0,12},{1,13},{2,14},{3,15},{4,0},{5,1},{6,2},{7,3},{8,4},{9,5},{1... | collective-permute-start | bytes 1572872 | tf_op jit(solution)/shard_map/ppermute | solution.py:46
  60.0 2.4 %collective-permute-start.15 = (f32[256,256]{1,0:T(8,128)}, f32[256,256]{1,0:T(8,128)S(1)}, u32[]{:S(2)}, u32[]{:S(2)}) collective-permute-start(f32[256,256]{1,0:T(8,128)} %dynamic-slice_select_fusion), channel_id=1, source_target_pairs={{0,0},{1,8},{2,16},{3,24},{4,32},{5,40},{6,48},{7,56},{8,64},{9,72... | collective-permute-start | bytes 786440 | tf_op jit(solution)/shard_map/ppermute | solution.py:90
  62.5 9.8 %collective-permute-done.15.refs_4_ = f32[256,256]{1,0:T(8,128)S(1)} collective-permute-done((f32[256,256]{1,0:T(8,128)}, f32[256,256]{1,0:T(8,128)S(1)}, u32[]{:S(2)}, u32[]{:S(2)}) %collective-permute-start.15) | collective-permute-done | bytes 262176 | tf_op jit(solution)/shard_map/ppermute | solution.py:90
  74.4 10.8 %collective-permute-start.21 = (f32[256,256]{1,0:T(8,128)}, f32[256,256]{1,0:T(8,128)}, u32[]{:S(2)}, u32[]{:S(2)}) collective-permute-start(f32[256,256]{1,0:T(8,128)} %select_select_fusion.4), channel_id=1, source_target_pairs={{16,112},{17,113},{18,114},{19,115},{20,116},{21,117},{22,118},{23... | collective-permute-start | bytes 786440 | tf_op jit(solution)/shard_map/ppermute | solution.py:149
  85.2 2.0 %collective-permute-start.20 = (f32[256,256]{1,0:T(8,128)}, f32[256,256]{1,0:T(8,128)}, u32[]{:S(2)}, u32[]{:S(2)}) collective-permute-start(f32[256,256]{1,0:T(8,128)} %select_select_fusion.4), channel_id=1, source_target_pairs={{16,80},{17,81},{18,82},{19,83},{20,84},{21,85},{22,86},{23,87},{2... | collective-permute-start | bytes 786440 | tf_op jit(solution)/shard_map/ppermute | solution.py:149
  87.2 2.0 %collective-permute-start.19 = (f32[256,256]{1,0:T(8,128)}, f32[256,256]{1,0:T(8,128)}, u32[]{:S(2)}, u32[]{:S(2)}) collective-permute-start(f32[256,256]{1,0:T(8,128)} %select_select_fusion.4), channel_id=1, source_target_pairs={{16,48},{17,49},{18,50},{19,51},{20,52},{21,53},{22,54},{23,55},{2... | collective-permute-start | bytes 786440 | tf_op jit(solution)/shard_map/ppermute | solution.py:149
  90.7 2.6 %collective-permute-done.19 = f32[256,256]{1,0:T(8,128)} collective-permute-done((f32[256,256]{1,0:T(8,128)}, f32[256,256]{1,0:T(8,128)}, u32[]{:S(2)}, u32[]{:S(2)}) %collective-permute-start.19) | collective-permute-done | bytes 262176 | tf_op jit(solution)/shard_map/ppermute | solution.py:149
  93.3 3.3 %collective-permute-done.17.refs_7_ = f32[256,256]{1,0:T(8,128)S(1)} collective-permute-done((f32[256,256]{1,0:T(8,128)S(1)}, f32[256,256]{1,0:T(8,128)S(1)}, u32[]{:S(2)}, u32[]{:S(2)}) %collective-permute-start.17) | collective-permute-done | bytes 262176 | tf_op jit(solution)/shard_map/ppermute | solution.py:68
  96.6 1.9 %collective-permute-done.16.refs_5_ = f32[256,256]{1,0:T(8,128)S(1)} collective-permute-done((f32[256,256]{1,0:T(8,128)S(1)}, f32[256,256]{1,0:T(8,128)S(1)}, u32[]{:S(2)}, u32[]{:S(2)}) %collective-permute-start.16) | collective-permute-done | bytes 262176 | tf_op jit(solution)/shard_map/ppermute | solution.py:68
  99.9 4.3 %collective-permute-start.25 = (f32[256,256]{1,0:T(8,128)S(1)}, f32[256,256]{1,0:T(8,128)S(1)}, u32[]{:S(2)}, u32[]{:S(2)}) collective-permute-start(f32[256,256]{1,0:T(8,128)S(1)} %add_select_fusion.refs_13_), channel_id=1, source_target_pairs={{16,0},{48,32},{80,64},{112,96},{17,1},{49,33},{81,65},{113,97},{1... | collective-permute-start | bytes 786440 | tf_op jit(solution)/shard_map/ppermute | solution.py:158
  107.0 1.9 %solve_first.1 = (bf16[8,256,256]{2,1,0:T(8,128)(2,1)S(1)}, bf16[8,256,256]{2,1,0:T(8,128)(2,1)S(1)}) custom-call(f32[512,256]{1,0:T(8,128)S(1)} %get-tuple-element.45.refs_0_, f32[512,256]{1,0:T(8,128)S(1)} %collective-permute-done.9.refs_1_, f32[512,256]{1,0:T(8,128)S(1)} %collective-permute-done.10.refs_2_, ...), custom_call_target="tpu_custom_call" | custom-call | flops 805306368 | bytes 4194304 | tf_op jit(solution)/shard_map/solve_first/pallas_call | solution.py:222
  109.0 18.1 %solve_and_update.1 = (f32[8,2048,128]{2,1,0:T(8,128)}, f32[8,256,256]{2,1,0:T(8,128)}) custom-call(f32[512,256]{1,0:T(8,128)S(1)} %get-tuple-element.44.refs_0_, f32[512,256]{1,0:T(8,128)} %collective-permute-done.12.refs_1_, f32[512,256]{1,0:T(8,128)} %collective-permute-done.14.refs_2_, f32[512,256]{1,0:T(8,128)S(1)} %copy-done.2, ...), custom_call_target="tpu_custom_call" | custom-call | flops 6710886400 | bytes 20971520 | tf_op jit(solution)/shard_map/solve_and_update/pallas_call | solution.py:352
  (58 shorter events, 18.1 us)
Async XLA Ops:
  3.6 12.8 %collective-permute-start.2 = (f32[512,256]{1,0:T(8,128)}, f32[512,256]{1,0:T(8,128)S(1)}, u32[]{:S(2)}, u32[]{:S(2)}) collective-permute-start(f32[512,256]{1,0:T(8,128)} %get-tuple-element.72), channel_id=1, source_target_pairs={{0,8},{1,9},{16,18},{17,19},{32,40},{33,41},{48,50},{49,51},{64,72... | collective-permute-start | bytes 1572872 | tf_op jit(solution)/shard_map/ppermute | solution.py:63
  10.0 13.1 %collective-permute-start.1 = (f32[512,256]{1,0:T(8,128)}, f32[512,256]{1,0:T(8,128)S(1)}, u32[]{:S(2)}, u32[]{:S(2)}) collective-permute-start(f32[512,256]{1,0:T(8,128)} %get-tuple-element.73), channel_id=1, source_target_pairs={{0,12},{1,13},{2,14},{3,15},{4,0},{5,1},{6,2},{7,3},{8,4},{9,5},{1... | collective-permute-start | bytes 1572872 | tf_op jit(solution)/shard_map/ppermute | solution.py:46
  10.1 13.8 %collective-permute-start = (f32[512,256]{1,0:T(8,128)}, f32[512,256]{1,0:T(8,128)}, u32[]{:S(2)}, u32[]{:S(2)}) collective-permute-start(f32[512,256]{1,0:T(8,128)} %get-tuple-element.74), channel_id=1, source_target_pairs={{0,4},{1,5},{2,6},{3,7},{4,8},{5,9},{6,10},{7,11},{8,12},{9,13},{1... | collective-permute-start | bytes 1572872 | tf_op jit(solution)/shard_map/ppermute | solution.py:46
  25.4 8.4 %collective-permute-start.7 = (f32[512,256]{1,0:T(8,128)S(1)}, f32[512,256]{1,0:T(8,128)S(1)}, u32[]{:S(2)}, u32[]{:S(2)}) collective-permute-start(f32[512,256]{1,0:T(8,128)S(1)} %get-tuple-element.68), channel_id=1, source_target_pairs={{0,3},{1,0},{2,1},{3,2},{4,7},{5,4},{6,5},{7,6},{8,11},{9,8},{10,9... | collective-permute-start | bytes 1572872 | tf_op jit(solution)/shard_map/ppermute | solution.py:46
  25.5 9.6 %collective-permute-start.3 = (f32[512,256]{1,0:T(8,128)S(1)}, f32[512,256]{1,0:T(8,128)S(1)}, u32[]{:S(2)}, u32[]{:S(2)}) collective-permute-start(f32[512,256]{1,0:T(8,128)S(1)} %get-tuple-element.69), channel_id=1, source_target_pairs={{0,1},{1,2},{2,3},{3,0},{4,5},{5,6},{6,7},{7,4},{8,9},{9,10},{10,1... | collective-permute-start | bytes 1572872 | tf_op jit(solution)/shard_map/ppermute | solution.py:46
  26.9 13.9 %collective-permute-start.6 = (f32[512,256]{1,0:T(8,128)S(1)}, f32[512,256]{1,0:T(8,128)S(1)}, u32[]{:S(2)}, u32[]{:S(2)}) collective-permute-start(f32[512,256]{1,0:T(8,128)S(1)} %get-tuple-element.68), channel_id=1, source_target_pairs={{0,1},{1,2},{2,3},{3,0},{4,5},{5,6},{6,7},{7,4},{8,9},{9,10},{10,1... | collective-permute-start | bytes 1572872 | tf_op jit(solution)/shard_map/ppermute | solution.py:46
  27.0 13.8 %collective-permute-start.5 = (f32[512,256]{1,0:T(8,128)S(1)}, f32[512,256]{1,0:T(8,128)S(1)}, u32[]{:S(2)}, u32[]{:S(2)}) collective-permute-start(f32[512,256]{1,0:T(8,128)S(1)} %get-tuple-element.69), channel_id=1, source_target_pairs={{0,3},{1,0},{2,1},{3,2},{4,7},{5,4},{6,5},{7,6},{8,11},{9,8},{10,9... | collective-permute-start | bytes 1572872 | tf_op jit(solution)/shard_map/ppermute | solution.py:46
  33.8 11.3 %collective-permute-start.8 = (f32[512,256]{1,0:T(8,128)S(1)}, f32[512,256]{1,0:T(8,128)}, u32[]{:S(2)}, u32[]{:S(2)}) collective-permute-start(f32[512,256]{1,0:T(8,128)S(1)} %collective-permute-done.7), channel_id=1, source_target_pairs={{0,3},{1,0},{2,1},{3,2},{4,7},{5,4},{6,5},{7,6},{8,11},{9,8},{10,9... | collective-permute-start | bytes 1572872 | tf_op jit(solution)/shard_map/ppermute | solution.py:46
  35.1 11.2 %collective-permute-start.4 = (f32[512,256]{1,0:T(8,128)S(1)}, f32[512,256]{1,0:T(8,128)}, u32[]{:S(2)}, u32[]{:S(2)}) collective-permute-start(f32[512,256]{1,0:T(8,128)S(1)} %collective-permute-done.3), channel_id=1, source_target_pairs={{0,1},{1,2},{2,3},{3,0},{4,5},{5,6},{6,7},{7,4},{8,9},{9,10},{10,1... | collective-permute-start | bytes 1572872 | tf_op jit(solution)/shard_map/ppermute | solution.py:46
  48.5 8.3 %collective-permute-start.13 = (f32[512,256]{1,0:T(8,128)S(1)}, f32[512,256]{1,0:T(8,128)S(1)}, u32[]{:S(2)}, u32[]{:S(2)}) collective-permute-start(f32[512,256]{1,0:T(8,128)S(1)} %get-tuple-element.44.refs_0_), channel_id=1, source_target_pairs={{0,12},{1,13},{2,14},{3,15},{4,0},{5,1},{6,2},{7,3},{8,4},{9,5},{1... | collective-permute-start | bytes 1572872 | tf_op jit(solution)/shard_map/ppermute | solution.py:46
  50.4 9.6 %collective-permute-start.9 = (f32[512,256]{1,0:T(8,128)S(1)}, f32[512,256]{1,0:T(8,128)S(1)}, u32[]{:S(2)}, u32[]{:S(2)}) collective-permute-start(f32[512,256]{1,0:T(8,128)S(1)} %get-tuple-element.45.refs_0_), channel_id=1, source_target_pairs={{0,4},{1,5},{2,6},{3,7},{4,8},{5,9},{6,10},{7,11},{8,12},{9,13},{1... | collective-permute-start | bytes 1572872 | tf_op jit(solution)/shard_map/ppermute | solution.py:46
  50.4 21.9 %collective-permute-start.12 = (f32[512,256]{1,0:T(8,128)S(1)}, f32[512,256]{1,0:T(8,128)}, u32[]{:S(2)}, u32[]{:S(2)}) collective-permute-start(f32[512,256]{1,0:T(8,128)S(1)} %get-tuple-element.44.refs_0_), channel_id=1, source_target_pairs={{0,4},{1,5},{2,6},{3,7},{4,8},{5,9},{6,10},{7,11},{8,12},{9,13},{1... | collective-permute-start | bytes 1572872 | tf_op jit(solution)/shard_map/ppermute | solution.py:46
  50.4 21.9 %collective-permute-start.11 = (f32[512,256]{1,0:T(8,128)S(1)}, f32[512,256]{1,0:T(8,128)S(1)}, u32[]{:S(2)}, u32[]{:S(2)}) collective-permute-start(f32[512,256]{1,0:T(8,128)S(1)} %get-tuple-element.45.refs_0_), channel_id=1, source_target_pairs={{0,12},{1,13},{2,14},{3,15},{4,0},{5,1},{6,2},{7,3},{8,4},{9,5},{1... | collective-permute-start | bytes 1572872 | tf_op jit(solution)/shard_map/ppermute | solution.py:46
  56.8 15.4 %collective-permute-start.14 = (f32[512,256]{1,0:T(8,128)S(1)}, f32[512,256]{1,0:T(8,128)}, u32[]{:S(2)}, u32[]{:S(2)}) collective-permute-start(f32[512,256]{1,0:T(8,128)S(1)} %collective-permute-done.13.refs_3_), channel_id=1, source_target_pairs={{0,12},{1,13},{2,14},{3,15},{4,0},{5,1},{6,2},{7,3},{8,4},{9,5},{1... | collective-permute-start | bytes 1572872 | tf_op jit(solution)/shard_map/ppermute | solution.py:46
  60.0 13.6 %collective-permute-start.10 = (f32[512,256]{1,0:T(8,128)S(1)}, f32[512,256]{1,0:T(8,128)S(1)}, u32[]{:S(2)}, u32[]{:S(2)}) collective-permute-start(f32[512,256]{1,0:T(8,128)S(1)} %collective-permute-done.9.refs_1_), channel_id=1, source_target_pairs={{0,4},{1,5},{2,6},{3,7},{4,8},{5,9},{6,10},{7,11},{8,12},{9,13},{1... | collective-permute-start | bytes 1572872 | tf_op jit(solution)/shard_map/ppermute | solution.py:46
  60.0 12.3 %collective-permute-start.15 = (f32[256,256]{1,0:T(8,128)}, f32[256,256]{1,0:T(8,128)S(1)}, u32[]{:S(2)}, u32[]{:S(2)}) collective-permute-start(f32[256,256]{1,0:T(8,128)} %dynamic-slice_select_fusion), channel_id=1, source_target_pairs={{0,0},{1,8},{2,16},{3,24},{4,32},{5,40},{6,48},{7,56},{8,64},{9,72... | collective-permute-start | bytes 786440 | tf_op jit(solution)/shard_map/ppermute | solution.py:90
  74.4 14.8 %collective-permute-start.21 = (f32[256,256]{1,0:T(8,128)}, f32[256,256]{1,0:T(8,128)}, u32[]{:S(2)}, u32[]{:S(2)}) collective-permute-start(f32[256,256]{1,0:T(8,128)} %select_select_fusion.4), channel_id=1, source_target_pairs={{16,112},{17,113},{18,114},{19,115},{20,116},{21,117},{22,118},{23... | collective-permute-start | bytes 786440 | tf_op jit(solution)/shard_map/ppermute | solution.py:149
  85.2 5.5 %collective-permute-start.20 = (f32[256,256]{1,0:T(8,128)}, f32[256,256]{1,0:T(8,128)}, u32[]{:S(2)}, u32[]{:S(2)}) collective-permute-start(f32[256,256]{1,0:T(8,128)} %select_select_fusion.4), channel_id=1, source_target_pairs={{16,80},{17,81},{18,82},{19,83},{20,84},{21,85},{22,86},{23,87},{2... | collective-permute-start | bytes 786440 | tf_op jit(solution)/shard_map/ppermute | solution.py:149
  87.2 6.1 %collective-permute-start.19 = (f32[256,256]{1,0:T(8,128)}, f32[256,256]{1,0:T(8,128)}, u32[]{:S(2)}, u32[]{:S(2)}) collective-permute-start(f32[256,256]{1,0:T(8,128)} %select_select_fusion.4), channel_id=1, source_target_pairs={{16,48},{17,49},{18,50},{19,51},{20,52},{21,53},{22,54},{23,55},{2... | collective-permute-start | bytes 786440 | tf_op jit(solution)/shard_map/ppermute | solution.py:149
  89.2 4.1 %collective-permute-start.18 = (f32[256,256]{1,0:T(8,128)S(1)}, f32[256,256]{1,0:T(8,128)}, u32[]{:S(2)}, u32[]{:S(2)}) collective-permute-start(f32[256,256]{1,0:T(8,128)S(1)} %collective-permute-done.15.refs_4_), channel_id=1, source_target_pairs={{0,16},{16,0},{32,48},{48,32},{64,80},{80,64},{96,112},{112,96},{1... | collective-permute-start | bytes 786440 | tf_op jit(solution)/shard_map/ppermute | solution.py:72
  89.2 7.4 %collective-permute-start.17 = (f32[256,256]{1,0:T(8,128)S(1)}, f32[256,256]{1,0:T(8,128)S(1)}, u32[]{:S(2)}, u32[]{:S(2)}) collective-permute-start(f32[256,256]{1,0:T(8,128)S(1)} %collective-permute-done.15.refs_4_), channel_id=1, source_target_pairs={{0,96},{16,112},{32,0},{48,16},{64,32},{80,48},{96,64},{112,80},{1... | collective-permute-start | bytes 786440 | tf_op jit(solution)/shard_map/ppermute | solution.py:68
  89.2 9.2 %collective-permute-start.16 = (f32[256,256]{1,0:T(8,128)S(1)}, f32[256,256]{1,0:T(8,128)S(1)}, u32[]{:S(2)}, u32[]{:S(2)}) collective-permute-start(f32[256,256]{1,0:T(8,128)S(1)} %collective-permute-done.15.refs_4_), channel_id=1, source_target_pairs={{0,32},{16,48},{32,64},{48,80},{64,96},{80,112},{96,0},{112,16},{1... | collective-permute-start | bytes 786440 | tf_op jit(solution)/shard_map/ppermute | solution.py:68
  98.5 6.3 %collective-permute-start.22 = (f32[256,256]{1,0:T(8,128)S(1)}, f32[256,256]{1,0:T(8,128)S(1)}, u32[]{:S(2)}, u32[]{:S(2)}) collective-permute-start(f32[256,256]{1,0:T(8,128)S(1)} %broadcast_select_fusion), channel_id=1, source_target_pairs={{0,32},{16,112},{32,64},{48,16},{64,96},{80,48},{96,0},{112,80},{1... | collective-permute-start | bytes 786440 | tf_op jit(solution)/shard_map/ppermute | solution.py:95
  99.9 5.4 %collective-permute-start.25 = (f32[256,256]{1,0:T(8,128)S(1)}, f32[256,256]{1,0:T(8,128)S(1)}, u32[]{:S(2)}, u32[]{:S(2)}) collective-permute-start(f32[256,256]{1,0:T(8,128)S(1)} %add_select_fusion.refs_13_), channel_id=1, source_target_pairs={{16,0},{48,32},{80,64},{112,96},{17,1},{49,33},{81,65},{113,97},{1... | collective-permute-start | bytes 786440 | tf_op jit(solution)/shard_map/ppermute | solution.py:158
  (12 other events, 93.6 us)

commit v11 on v7

--- a/solution.py
+++ b/solution.py
@@ -241,14 +241,13 @@
 
 STEP = 2
 LINES = NB * TC * 2
-PART = 32
 
 
 def last_kernel(*refs):
     pieces, cols = refs[:SIDE], refs[SIDE : SIDE + N_ROW]
     pivots, refs = refs[SIDE + N_ROW : SIDE + N_ROW + 4], refs[SIDE + N_ROW + 4 :]
     matrix, inv_in, high_in, low_in, band, out, panel, *refs = refs
-    tiles, raw, raw_cols, row_high1, row_low1, row_high2, row_low2, col_high, col_low, even, odd, *refs = refs
+    tiles, raw, raw_cols, row_high1, row_low1, row_high2, row_low2, col_high, col_low, *refs = refs
     inv, pivot, sems, col_sems, in_sems, out_sems, panel_sems, small_sems = refs
     r, c = lax.axis_index("row"), lax.axis_index("col")
     copies = plane_copies(pieces, raw, sems, 1)
@@ -263,7 +262,7 @@
         def _():
             pltpu.make_async_copy(pivots[n], pivot, small_sems.at[1]).start()
 
-    for copy in small[2:] + copies + col_copies + loads:
+    for copy in col_copies + small[2:] + copies + loads:
         copy.start()
     small[0].wait()
     weights0 = deep(inv[0].T)
@@ -302,7 +301,7 @@
 
     size = STEP * NB
 
-    def multiply(step, q, product):
+    def multiply(step, q):
         at = pl.ds(step * STEP, STEP)
         high = jnp.concatenate([row_high1[at].reshape(size, NB), row_high2[at].reshape(size, NB)], axis=1)
         low = jnp.concatenate([row_low1[at].reshape(size, NB), row_low2[at].reshape(size, NB)], axis=1)
@@ -313,34 +312,26 @@
             at = slice(p * NB, (p + 1) * NB)
             total = jnp.where(code == 2, 0.0, full[at] + jnp.where(code == 0, rest[at], 0.0))
             for b in range(2):
-                product[b * TC + q, at, :] = total[:, b * HALF : (b + 1) * HALF]
-
-    def subtract(step, share, product):
-        for a in range(share * size // TC, (share + 1) * size // TC, PART):
-            turned = product[:, a : a + PART, :].transpose(1, 0, 2).reshape(PART * 2 * TC, HALF)
-            at = pl.ds(a % NB * 2 * TC, PART * 2 * TC)
-            tiles[step * STEP + a // NB, at, :] -= turned
+                lines = pl.ds(b * TC + q, NB, stride=2 * TC)
+                tiles[step * STEP + p, lines, :] -= total[:, b * HALF : (b + 1) * HALF]
 
     steps = TR // STEP
     stores = [pltpu.make_async_copy(tiles.at[p], out.at[p], out_sems.at[p]) for p in range(TR)]
-    for step in range(-1, steps + 1):
-        product, before = (even, odd) if step % 2 == 0 else (odd, even)
-        if step > 0:
+    for step in range(-1, steps):
+        if step >= 0:
             for p in range(STEP):
-                loads[(step - 1) * STEP + p].wait()
+                loads[step * STEP + p].wait()
         for q in range(TC):
             if step + 1 < steps and q < STEP:
                 solve((step + 1) * STEP + q)
-            if 0 <= step < steps:
-                multiply(step, q, product)
-            if step > 0:
-                subtract(step - 1, q, before)
+            if step >= 0:
+                multiply(step, q)
         if step + 1 < steps:
             for p in range(STEP):
                 panels[(step + 1) * STEP + p].start()
-        if step > 0:
+        if step >= 0:
             for p in range(STEP):
-                stores[(step - 1) * STEP + p].start()
+                stores[step * STEP + p].start()
     for copy in stores + panels:
         copy.wait()
 
@@ -365,8 +356,6 @@
             pltpu.VMEM((TR, NB, NB), BF16),
             pltpu.VMEM((TC, PAIR, NB), BF16),
             pltpu.VMEM((TC, PAIR, NB), BF16),
-            pltpu.VMEM((2 * TC, STEP * NB, HALF), F32),
-            pltpu.VMEM((2 * TC, STEP * NB, HALF), F32),
             pltpu.VMEM((2, NB, NB), F32),
             pltpu.VMEM((NB, NB), F32),
             pltpu.SemaphoreType.DMA((SIDE,)),

time: 125 us -> 125 us (level)
  no operation moved by 1% of the time
where the time goes in v11:
time: 125 us; the launch traced here: 123 us
  starting transfers between devices  54.7 us (44%)
  waiting for transfers between devices  38.9 us (31%)
  Pallas kernels  20 us (16%)
  other arithmetic  4.84 us (4%)
  local copies, waits for them, and re-layouts  3.79 us (3%)
    ppermute x14, waiting for transfers between devices, shift_plane(): return lax.ppermute(value, ('row', 'col'), pairs)  22 us
    pallas_call x1, Pallas kernels, finish(): pl.pallas_call(last_kernel, out_shape=(jax.ShapeDtypeStruct((TR, LINES, H...  18.1 us
    ppermute x14, starting transfers between devices, shift_plane(): return lax.ppermute(value, ('row', 'col'), pairs)  16.3 us
    ppermute x1, starting transfers between devices, gather_all(): lax.ppermute(pivot, ('row', 'col'), corner)  11.7 us
    ppermute x1, starting transfers between devices, send_far(): return lax.ppermute(value, ('row', 'col'), pairs)  6.35 us
    ppermute x4, starting transfers between devices, swap_core(): return lax.ppermute(value, 'row', [(r, r ^ 1) for r in range(N_ROW)])  5.13 us
    ppermute x1, waiting for transfers between devices, send_far(): return lax.ppermute(value, ('row', 'col'), pairs)  4.9 us
    ppermute x1, waiting for transfers between devices, relay_y(): return lax.ppermute(jnp.where(core == 0, near, back), 'row', pairs)  3.51 us
  transfers between devices with their start and end apart: 29, of which 14 were waited for; matrix products, arithmetic and copies ran while one was open for 0% of the time, Pallas kernels for 2%

profile of v11, /device:TPU:1, one launch (start us, length us, event | category | flops | bytes accessed | tf_op | source)
XLA Modules:
  0.0 123.2 jit_solution(2608671294791109871)
XLA Ops:
  0.6 1.6 %slice-done = f32[8,256,1,256]{3,2,1,0:T(1,128)S(1)} async-done(((f32[8,256,4,256]{3,2,1,0:T(4,128)}), f32[8,256,1,256]{3,2,1,0:T(1,128)S(1)}, s32[]{:S(2)}) %slice-start) | async-done | bytes 2097176 | tf_op jit(solution)/shard_map/slice | solution.py:376
  3.6 6.3 %collective-permute-start.2 = (f32[512,256]{1,0:T(8,128)}, f32[512,256]{1,0:T(8,128)S(1)}, u32[]{:S(2)}, u32[]{:S(2)}) collective-permute-start(f32[512,256]{1,0:T(8,128)} %get-tuple-element.86), channel_id=1, source_target_pairs={{0,8},{1,9},{16,18},{17,19},{32,40},{33,41},{48,50},{49,51},{64,72... | collective-permute-start | bytes 1572872 | tf_op jit(solution)/shard_map/ppermute | solution.py:65
  11.5 4.9 %collective-permute-done.2 = f32[512,256]{1,0:T(8,128)S(1)} collective-permute-done((f32[512,256]{1,0:T(8,128)}, f32[512,256]{1,0:T(8,128)S(1)}, u32[]{:S(2)}, u32[]{:S(2)}) %collective-permute-start.2) | collective-permute-done | bytes 524320 | tf_op jit(solution)/shard_map/ppermute | solution.py:65
  16.4 6.7 %collective-permute-done.1 = f32[512,256]{1,0:T(8,128)S(1)} collective-permute-done((f32[512,256]{1,0:T(8,128)}, f32[512,256]{1,0:T(8,128)S(1)}, u32[]{:S(2)}, u32[]{:S(2)}) %collective-permute-start.1) | collective-permute-done | bytes 524320 | tf_op jit(solution)/shard_map/ppermute | solution.py:48
  23.9 1.5 %select_select_fusion.2 = (f32[512,256]{1,0:T(8,128)S(1)}, f32[512,256]{1,0:T(8,128)S(1)}) fusion(f32[512,256]{1,0:T(8,128)} %collective-permute-done, f32[512,256]{1,0:T(8,128)} %copy-done.2, f32[512,256]{1,0:T(8,128)} %copy-done.3, f32[2048,256]{1,0:T(8,128)S(1)} %bitcast.12, pred[]{:T(512)S(6)} %eq.68, pred[]{:T(512)S(6)} %eq.67, pred[]{:T(512)S(6)} %eq.66, ...), kind=kLoop, calls=%fused_computation.2 | loop fusion | flops 786432 | bytes 3145734 | tf_op jit(solution)/shard_map/jit(_where)/select_n | solution.py:96
  27.0 2.6 %collective-permute-start.5 = (f32[512,256]{1,0:T(8,128)S(1)}, f32[512,256]{1,0:T(8,128)S(1)}, u32[]{:S(2)}, u32[]{:S(2)}) collective-permute-start(f32[512,256]{1,0:T(8,128)S(1)} %get-tuple-element.83), channel_id=1, source_target_pairs={{0,3},{1,0},{2,1},{3,2},{4,7},{5,4},{6,5},{7,6},{8,11},{9,8},{10,9... | collective-permute-start | bytes 1572872 | tf_op jit(solution)/shard_map/ppermute | solution.py:48
  29.6 4.2 %collective-permute-done.7 = f32[512,256]{1,0:T(8,128)S(1)} collective-permute-done((f32[512,256]{1,0:T(8,128)S(1)}, f32[512,256]{1,0:T(8,128)S(1)}, u32[]{:S(2)}, u32[]{:S(2)}) %collective-permute-start.7) | collective-permute-done | bytes 524320 | tf_op jit(solution)/shard_map/ppermute | solution.py:48
  35.3 5.5 %collective-permute-done.6 = f32[512,256]{1,0:T(8,128)S(1)} collective-permute-done((f32[512,256]{1,0:T(8,128)S(1)}, f32[512,256]{1,0:T(8,128)S(1)}, u32[]{:S(2)}, u32[]{:S(2)}) %collective-permute-start.6) | collective-permute-done | bytes 524320 | tf_op jit(solution)/shard_map/ppermute | solution.py:48
  40.8 4.3 %collective-permute-done.8 = f32[512,256]{1,0:T(8,128)} collective-permute-done((f32[512,256]{1,0:T(8,128)S(1)}, f32[512,256]{1,0:T(8,128)}, u32[]{:S(2)}, u32[]{:S(2)}) %collective-permute-start.8) | collective-permute-done | bytes 524320 | tf_op jit(solution)/shard_map/ppermute | solution.py:48
  48.5 2.2 %collective-permute-start.13 = (f32[256,256]{1,0:T(8,128)S(1)}, f32[256,256]{1,0:T(8,128)S(1)}, u32[]{:S(2)}, u32[]{:S(2)}) collective-permute-start(f32[256,256]{1,0:T(8,128)S(1)} %get-tuple-element.53), channel_id=1, source_target_pairs={{0,0},{1,8},{2,16},{3,24},{4,32},{5,40},{6,48},{7,56},{8,64},{9,72... | collective-permute-start | bytes 786440 | tf_op jit(solution)/shard_map/ppermute | solution.py:87
  52.1 3.6 %collective-permute-start.10 = (f32[512,256]{1,0:T(8,128)S(1)}, f32[512,256]{1,0:T(8,128)}, u32[]{:S(2)}, u32[]{:S(2)}) collective-permute-start(f32[512,256]{1,0:T(8,128)S(1)} %get-tuple-element.51.refs_0_), channel_id=1, source_target_pairs={{0,12},{1,13},{2,14},{3,15},{4,0},{5,1},{6,2},{7,3},{8,4},{9,5},{1... | collective-permute-start | bytes 1572872 | tf_op jit(solution)/shard_map/ppermute | solution.py:48
  57.8 11.7 %collective-permute-start.14 = (f32[256,256]{1,0:T(8,128)}, f32[256,256]{1,0:T(8,128)}, u32[]{:S(2)}, u32[]{:S(2)}) collective-permute-start(f32[256,256]{1,0:T(8,128)} %get-tuple-element.54), channel_id=1, source_target_pairs={{16,18},{20,22},{24,26},{28,30}} | collective-permute-start | bytes 786440 | tf_op jit(solution)/shard_map/ppermute | solution.py:142
  69.5 2.9 %collective-permute-done.14 = f32[256,256]{1,0:T(8,128)} collective-permute-done((f32[256,256]{1,0:T(8,128)}, f32[256,256]{1,0:T(8,128)}, u32[]{:S(2)}, u32[]{:S(2)}) %collective-permute-start.14) | collective-permute-done | bytes 262176 | tf_op jit(solution)/shard_map/ppermute | solution.py:142
  73.4 4.6 %collective-permute-start.19 = (f32[256,256]{1,0:T(8,128)S(1)}, f32[256,256]{1,0:T(8,128)S(1)}, u32[]{:S(2)}, u32[]{:S(2)}) collective-permute-start(f32[256,256]{1,0:T(8,128)S(1)} %collective-permute-done.13.refs_4_), channel_id=1, source_target_pairs={{0,16},{16,0},{32,48},{48,32},{64,80},{80,64},{96,112},{112,96},{1... | collective-permute-start | bytes 786440 | tf_op jit(solution)/shard_map/ppermute | solution.py:74
  78.1 2.3 %collective-permute-start.17 = (f32[256,256]{1,0:T(8,128)S(1)}, f32[256,256]{1,0:T(8,128)S(1)}, u32[]{:S(2)}, u32[]{:S(2)}) collective-permute-start(f32[256,256]{1,0:T(8,128)S(1)} %collective-permute-done.13.refs_4_), channel_id=1, source_target_pairs={{0,32},{16,48},{32,64},{48,80},{64,96},{80,112},{96,0},{112,16},{1... | collective-permute-start | bytes 786440 | tf_op jit(solution)/shard_map/ppermute | solution.py:70
  80.4 2.3 %collective-permute-start.23 = (f32[256,256]{1,0:T(8,128)S(1)}, f32[256,256]{1,0:T(8,128)S(1)}, u32[]{:S(2)}, u32[]{:S(2)}) collective-permute-start(f32[256,256]{1,0:T(8,128)S(1)} %select_select_fusion.4.refs_13_), channel_id=1, source_target_pairs={{16,0},{17,1},{18,2},{19,3},{20,4},{21,5},{22,6},{23,7},{24,8},{25... | collective-permute-start | bytes 786440 | tf_op jit(solution)/shard_map/ppermute | solution.py:155
  82.8 2.7 %collective-permute-start.16 = (f32[512,256]{1,0:T(8,128)}, f32[512,256]{1,0:T(8,128)S(1)}, u32[]{:S(2)}, u32[]{:S(2)}) collective-permute-start(f32[512,256]{1,0:T(8,128)} %collective-permute-done.10.refs_3_), channel_id=1, source_target_pairs={{0,12},{1,13},{2,14},{3,15},{4,0},{5,1},{6,2},{7,3},{8,4},{9,5},{1... | collective-permute-start | bytes 1572872 | tf_op jit(solution)/shard_map/ppermute | solution.py:48
  85.5 1.5 %collective-permute-done.18.refs_7_ = f32[256,256]{1,0:T(8,128)S(1)} collective-permute-done((f32[256,256]{1,0:T(8,128)S(1)}, f32[256,256]{1,0:T(8,128)S(1)}, u32[]{:S(2)}, u32[]{:S(2)}) %collective-permute-start.18) | collective-permute-done | bytes 262176 | tf_op jit(solution)/shard_map/ppermute | solution.py:70
  87.0 2.8 %collective-permute-start.22 = (f32[256,256]{1,0:T(8,128)S(1)}, f32[256,256]{1,0:T(8,128)S(1)}, u32[]{:S(2)}, u32[]{:S(2)}) collective-permute-start(f32[256,256]{1,0:T(8,128)S(1)} %select_select_fusion.4.refs_13_), channel_id=1, source_target_pairs={{16,80},{17,81},{18,82},{19,83},{20,84},{21,85},{22,86},{23,87},{2... | collective-permute-start | bytes 786440 | tf_op jit(solution)/shard_map/ppermute | solution.py:154
  94.4 1.5 %collective-permute-done.20 = f32[256,256]{1,0:T(8,128)S(1)} collective-permute-done((f32[256,256]{1,0:T(8,128)S(1)}, f32[256,256]{1,0:T(8,128)S(1)}, u32[]{:S(2)}, u32[]{:S(2)}) %collective-permute-start.20) | collective-permute-done | bytes 262176 | tf_op jit(solution)/shard_map/ppermute | solution.py:152
  96.7 2.3 %collective-permute-start.24 = (f32[256,256]{1,0:T(8,128)S(1)}, f32[256,256]{1,0:T(8,128)S(1)}, u32[]{:S(2)}, u32[]{:S(2)}) collective-permute-start(f32[256,256]{1,0:T(8,128)S(1)} %broadcast_select_fusion), channel_id=1, source_target_pairs={{0,32},{16,112},{32,64},{48,16},{64,96},{80,48},{96,0},{112,80},{1... | collective-permute-start | bytes 786440 | tf_op jit(solution)/shard_map/ppermute | solution.py:92
  99.5 3.5 %collective-permute-done.24.refs_6_ = f32[256,256]{1,0:T(8,128)S(1)} collective-permute-done((f32[256,256]{1,0:T(8,128)S(1)}, f32[256,256]{1,0:T(8,128)S(1)}, u32[]{:S(2)}, u32[]{:S(2)}) %collective-permute-start.24) | collective-permute-done | bytes 262176 | tf_op jit(solution)/shard_map/ppermute | solution.py:92
  103.1 1.9 %solve_first.1 = (bf16[8,256,256]{2,1,0:T(8,128)(2,1)S(1)}, bf16[8,256,256]{2,1,0:T(8,128)(2,1)S(1)}) custom-call(f32[512,256]{1,0:T(8,128)S(1)} %get-tuple-element.52.refs_0_, f32[512,256]{1,0:T(8,128)S(1)} %collective-permute-done.9.refs_1_, f32[512,256]{1,0:T(8,128)S(1)} %collective-permute-done.15.refs_2_, ...), custom_call_target="tpu_custom_call" | custom-call | flops 805306368 | bytes 4194304 | tf_op jit(solution)/shard_map/solve_first/pallas_call | solution.py:226
  105.0 18.1 %solve_and_update.1 = (f32[8,2048,128]{2,1,0:T(8,128)}, f32[8,256,256]{2,1,0:T(8,128)}) custom-call(f32[512,256]{1,0:T(8,128)S(1)} %get-tuple-element.51.refs_0_, f32[512,256]{1,0:T(8,128)S(1)} %collective-permute-done.12.refs_1_, f32[512,256]{1,0:T(8,128)S(1)} %collective-permute-done.16.refs_2_, f32[512,256]{1,0:T(8,128)} %collective-permute-done.10.refs_3_, ...), custom_call_target="tpu_custom_call" | custom-call | flops 6710886400 | bytes 20971520 | tf_op jit(solution)/shard_map/solve_and_update/pallas_call | solution.py:341
  (58 shorter events, 20.6 us)
Async XLA Ops:
  3.6 12.8 %collective-permute-start.2 = (f32[512,256]{1,0:T(8,128)}, f32[512,256]{1,0:T(8,128)S(1)}, u32[]{:S(2)}, u32[]{:S(2)}) collective-permute-start(f32[512,256]{1,0:T(8,128)} %get-tuple-element.86), channel_id=1, source_target_pairs={{0,8},{1,9},{16,18},{17,19},{32,40},{33,41},{48,50},{49,51},{64,72... | collective-permute-start | bytes 1572872 | tf_op jit(solution)/shard_map/ppermute | solution.py:65
  10.0 13.1 %collective-permute-start.1 = (f32[512,256]{1,0:T(8,128)}, f32[512,256]{1,0:T(8,128)S(1)}, u32[]{:S(2)}, u32[]{:S(2)}) collective-permute-start(f32[512,256]{1,0:T(8,128)} %get-tuple-element.87), channel_id=1, source_target_pairs={{0,12},{1,13},{2,14},{3,15},{4,0},{5,1},{6,2},{7,3},{8,4},{9,5},{1... | collective-permute-start | bytes 1572872 | tf_op jit(solution)/shard_map/ppermute | solution.py:48
  10.1 13.8 %collective-permute-start = (f32[512,256]{1,0:T(8,128)}, f32[512,256]{1,0:T(8,128)}, u32[]{:S(2)}, u32[]{:S(2)}) collective-permute-start(f32[512,256]{1,0:T(8,128)} %get-tuple-element.88), channel_id=1, source_target_pairs={{0,4},{1,5},{2,6},{3,7},{4,8},{5,9},{6,10},{7,11},{8,12},{9,13},{1... | collective-permute-start | bytes 1572872 | tf_op jit(solution)/shard_map/ppermute | solution.py:48
  25.4 8.4 %collective-permute-start.7 = (f32[512,256]{1,0:T(8,128)S(1)}, f32[512,256]{1,0:T(8,128)S(1)}, u32[]{:S(2)}, u32[]{:S(2)}) collective-permute-start(f32[512,256]{1,0:T(8,128)S(1)} %get-tuple-element.82), channel_id=1, source_target_pairs={{0,3},{1,0},{2,1},{3,2},{4,7},{5,4},{6,5},{7,6},{8,11},{9,8},{10,9... | collective-permute-start | bytes 1572872 | tf_op jit(solution)/shard_map/ppermute | solution.py:48
  25.5 9.6 %collective-permute-start.3 = (f32[512,256]{1,0:T(8,128)S(1)}, f32[512,256]{1,0:T(8,128)S(1)}, u32[]{:S(2)}, u32[]{:S(2)}) collective-permute-start(f32[512,256]{1,0:T(8,128)S(1)} %get-tuple-element.83), channel_id=1, source_target_pairs={{0,1},{1,2},{2,3},{3,0},{4,5},{5,6},{6,7},{7,4},{8,9},{9,10},{10,1... | collective-permute-start | bytes 1572872 | tf_op jit(solution)/shard_map/ppermute | solution.py:48
  26.9 13.9 %collective-permute-start.6 = (f32[512,256]{1,0:T(8,128)S(1)}, f32[512,256]{1,0:T(8,128)S(1)}, u32[]{:S(2)}, u32[]{:S(2)}) collective-permute-start(f32[512,256]{1,0:T(8,128)S(1)} %get-tuple-element.82), channel_id=1, source_target_pairs={{0,1},{1,2},{2,3},{3,0},{4,5},{5,6},{6,7},{7,4},{8,9},{9,10},{10,1... | collective-permute-start | bytes 1572872 | tf_op jit(solution)/shard_map/ppermute | solution.py:48
  27.0 13.8 %collective-permute-start.5 = (f32[512,256]{1,0:T(8,128)S(1)}, f32[512,256]{1,0:T(8,128)S(1)}, u32[]{:S(2)}, u32[]{:S(2)}) collective-permute-start(f32[512,256]{1,0:T(8,128)S(1)} %get-tuple-element.83), channel_id=1, source_target_pairs={{0,3},{1,0},{2,1},{3,2},{4,7},{5,4},{6,5},{7,6},{8,11},{9,8},{10,9... | collective-permute-start | bytes 1572872 | tf_op jit(solution)/shard_map/ppermute | solution.py:48
  33.8 11.3 %collective-permute-start.8 = (f32[512,256]{1,0:T(8,128)S(1)}, f32[512,256]{1,0:T(8,128)}, u32[]{:S(2)}, u32[]{:S(2)}) collective-permute-start(f32[512,256]{1,0:T(8,128)S(1)} %collective-permute-done.7), channel_id=1, source_target_pairs={{0,3},{1,0},{2,1},{3,2},{4,7},{5,4},{6,5},{7,6},{8,11},{9,8},{10,9... | collective-permute-start | bytes 1572872 | tf_op jit(solution)/shard_map/ppermute | solution.py:48
  35.1 11.2 %collective-permute-start.4 = (f32[512,256]{1,0:T(8,128)S(1)}, f32[512,256]{1,0:T(8,128)}, u32[]{:S(2)}, u32[]{:S(2)}) collective-permute-start(f32[512,256]{1,0:T(8,128)S(1)} %collective-permute-done.3), channel_id=1, source_target_pairs={{0,1},{1,2},{2,3},{3,0},{4,5},{5,6},{6,7},{7,4},{8,9},{9,10},{10,1... | collective-permute-start | bytes 1572872 | tf_op jit(solution)/shard_map/ppermute | solution.py:48
  48.5 9.3 %collective-permute-start.13 = (f32[256,256]{1,0:T(8,128)S(1)}, f32[256,256]{1,0:T(8,128)S(1)}, u32[]{:S(2)}, u32[]{:S(2)}) collective-permute-start(f32[256,256]{1,0:T(8,128)S(1)} %get-tuple-element.53), channel_id=1, source_target_pairs={{0,0},{1,8},{2,16},{3,24},{4,32},{5,40},{6,48},{7,56},{8,64},{9,72... | collective-permute-start | bytes 786440 | tf_op jit(solution)/shard_map/ppermute | solution.py:87
  50.7 21.7 %collective-permute-start.12 = (f32[512,256]{1,0:T(8,128)S(1)}, f32[512,256]{1,0:T(8,128)S(1)}, u32[]{:S(2)}, u32[]{:S(2)}) collective-permute-start(f32[512,256]{1,0:T(8,128)S(1)} %get-tuple-element.51.refs_0_), channel_id=1, source_target_pairs={{0,4},{1,5},{2,6},{3,7},{4,8},{5,9},{6,10},{7,11},{8,12},{9,13},{1... | collective-permute-start | bytes 1572872 | tf_op jit(solution)/shard_map/ppermute | solution.py:48
  52.1 20.3 %collective-permute-start.10 = (f32[512,256]{1,0:T(8,128)S(1)}, f32[512,256]{1,0:T(8,128)}, u32[]{:S(2)}, u32[]{:S(2)}) collective-permute-start(f32[512,256]{1,0:T(8,128)S(1)} %get-tuple-element.51.refs_0_), channel_id=1, source_target_pairs={{0,12},{1,13},{2,14},{3,15},{4,0},{5,1},{6,2},{7,3},{8,4},{9,5},{1... | collective-permute-start | bytes 1572872 | tf_op jit(solution)/shard_map/ppermute | solution.py:48
  55.7 16.7 %collective-permute-start.11 = (f32[512,256]{1,0:T(8,128)S(1)}, f32[512,256]{1,0:T(8,128)S(1)}, u32[]{:S(2)}, u32[]{:S(2)}) collective-permute-start(f32[512,256]{1,0:T(8,128)S(1)} %get-tuple-element.52.refs_0_), channel_id=1, source_target_pairs={{0,12},{1,13},{2,14},{3,15},{4,0},{5,1},{6,2},{7,3},{8,4},{9,5},{1... | collective-permute-start | bytes 1572872 | tf_op jit(solution)/shard_map/ppermute | solution.py:48
  57.1 15.3 %collective-permute-start.9 = (f32[512,256]{1,0:T(8,128)S(1)}, f32[512,256]{1,0:T(8,128)S(1)}, u32[]{:S(2)}, u32[]{:S(2)}) collective-permute-start(f32[512,256]{1,0:T(8,128)S(1)} %get-tuple-element.52.refs_0_), channel_id=1, source_target_pairs={{0,4},{1,5},{2,6},{3,7},{4,8},{5,9},{6,10},{7,11},{8,12},{9,13},{1... | collective-permute-start | bytes 1572872 | tf_op jit(solution)/shard_map/ppermute | solution.py:48
  57.8 14.6 %collective-permute-start.14 = (f32[256,256]{1,0:T(8,128)}, f32[256,256]{1,0:T(8,128)}, u32[]{:S(2)}, u32[]{:S(2)}) collective-permute-start(f32[256,256]{1,0:T(8,128)} %get-tuple-element.54), channel_id=1, source_target_pairs={{16,18},{20,22},{24,26},{28,30}} | collective-permute-start | bytes 786440 | tf_op jit(solution)/shard_map/ppermute | solution.py:142
  73.4 9.4 %collective-permute-start.19 = (f32[256,256]{1,0:T(8,128)S(1)}, f32[256,256]{1,0:T(8,128)S(1)}, u32[]{:S(2)}, u32[]{:S(2)}) collective-permute-start(f32[256,256]{1,0:T(8,128)S(1)} %collective-permute-done.13.refs_4_), channel_id=1, source_target_pairs={{0,16},{16,0},{32,48},{48,32},{64,80},{80,64},{96,112},{112,96},{1... | collective-permute-start | bytes 786440 | tf_op jit(solution)/shard_map/ppermute | solution.py:74
  78.1 8.9 %collective-permute-start.18 = (f32[256,256]{1,0:T(8,128)S(1)}, f32[256,256]{1,0:T(8,128)S(1)}, u32[]{:S(2)}, u32[]{:S(2)}) collective-permute-start(f32[256,256]{1,0:T(8,128)S(1)} %collective-permute-done.13.refs_4_), channel_id=1, source_target_pairs={{0,96},{16,112},{32,0},{48,16},{64,32},{80,48},{96,64},{112,80},{1... | collective-permute-start | bytes 786440 | tf_op jit(solution)/shard_map/ppermute | solution.py:70
  78.1 11.7 %collective-permute-start.17 = (f32[256,256]{1,0:T(8,128)S(1)}, f32[256,256]{1,0:T(8,128)S(1)}, u32[]{:S(2)}, u32[]{:S(2)}) collective-permute-start(f32[256,256]{1,0:T(8,128)S(1)} %collective-permute-done.13.refs_4_), channel_id=1, source_target_pairs={{0,32},{16,48},{32,64},{48,80},{64,96},{80,112},{96,0},{112,16},{1... | collective-permute-start | bytes 786440 | tf_op jit(solution)/shard_map/ppermute | solution.py:70
  80.4 10.7 %collective-permute-start.23 = (f32[256,256]{1,0:T(8,128)S(1)}, f32[256,256]{1,0:T(8,128)S(1)}, u32[]{:S(2)}, u32[]{:S(2)}) collective-permute-start(f32[256,256]{1,0:T(8,128)S(1)} %select_select_fusion.4.refs_13_), channel_id=1, source_target_pairs={{16,0},{17,1},{18,2},{19,3},{20,4},{21,5},{22,6},{23,7},{24,8},{25... | collective-permute-start | bytes 786440 | tf_op jit(solution)/shard_map/ppermute | solution.py:155
  82.8 13.1 %collective-permute-start.15 = (f32[512,256]{1,0:T(8,128)S(1)}, f32[512,256]{1,0:T(8,128)S(1)}, u32[]{:S(2)}, u32[]{:S(2)}) collective-permute-start(f32[512,256]{1,0:T(8,128)S(1)} %collective-permute-done.9.refs_1_), channel_id=1, source_target_pairs={{0,4},{1,5},{2,6},{3,7},{4,8},{5,9},{6,10},{7,11},{8,12},{9,13},{1... | collective-permute-start | bytes 1572872 | tf_op jit(solution)/shard_map/ppermute | solution.py:48
  82.8 13.0 %collective-permute-start.16 = (f32[512,256]{1,0:T(8,128)}, f32[512,256]{1,0:T(8,128)S(1)}, u32[]{:S(2)}, u32[]{:S(2)}) collective-permute-start(f32[512,256]{1,0:T(8,128)} %collective-permute-done.10.refs_3_), channel_id=1, source_target_pairs={{0,12},{1,13},{2,14},{3,15},{4,0},{5,1},{6,2},{7,3},{8,4},{9,5},{1... | collective-permute-start | bytes 1572872 | tf_op jit(solution)/shard_map/ppermute | solution.py:48
  87.0 6.1 %collective-permute-start.22 = (f32[256,256]{1,0:T(8,128)S(1)}, f32[256,256]{1,0:T(8,128)S(1)}, u32[]{:S(2)}, u32[]{:S(2)}) collective-permute-start(f32[256,256]{1,0:T(8,128)S(1)} %select_select_fusion.4.refs_13_), channel_id=1, source_target_pairs={{16,80},{17,81},{18,82},{19,83},{20,84},{21,85},{22,86},{23,87},{2... | collective-permute-start | bytes 786440 | tf_op jit(solution)/shard_map/ppermute | solution.py:154
  91.1 4.8 %collective-permute-start.20 = (f32[256,256]{1,0:T(8,128)S(1)}, f32[256,256]{1,0:T(8,128)S(1)}, u32[]{:S(2)}, u32[]{:S(2)}) collective-permute-start(f32[256,256]{1,0:T(8,128)S(1)} %select_select_fusion.4.refs_13_), channel_id=1, source_target_pairs={{16,48},{17,49},{18,50},{19,51},{20,52},{21,53},{22,54},{23,55},{2... | collective-permute-start | bytes 786440 | tf_op jit(solution)/shard_map/ppermute | solution.py:152
  96.7 6.4 %collective-permute-start.24 = (f32[256,256]{1,0:T(8,128)S(1)}, f32[256,256]{1,0:T(8,128)S(1)}, u32[]{:S(2)}, u32[]{:S(2)}) collective-permute-start(f32[256,256]{1,0:T(8,128)S(1)} %broadcast_select_fusion), channel_id=1, source_target_pairs={{0,32},{16,112},{32,64},{48,16},{64,96},{80,48},{96,0},{112,80},{1... | collective-permute-start | bytes 786440 | tf_op jit(solution)/shard_map/ppermute | solution.py:92
  (12 other events, 100.3 us)

commit v12 on v7

--- a/solution.py
+++ b/solution.py
@@ -1,5 +1,3 @@
-import functools
-
 import jax
 import jax.numpy as jnp
 from jax import lax
@@ -74,15 +72,20 @@
     return lax.ppermute(value, "row", [(r, r ^ 1) for r in range(N_ROW)])
 
 
+def tile_choice(r, line, cross):
+    turned = (cross - r // 4) % SIDE
+    return (turned // 2, turned % 2) if r % 2 else (cross % 2, cross // 2)
+
+
 def to_columns(value):
     pairs = []
     for r in range(N_ROW):
         for x in range(SIDE):
             for z in range(SIDE):
                 line, cross = (z, x) if r % 2 else (x, z)
-                panel, odd = cross // 2, cross % 2
+                odd, panel = tile_choice(r, line, cross)
                 quarter = (line - panel * (r % 2)) % SIDE
-                target = (quarter * 2 + panel) * N_COL + r + N_ROW * odd
+                target = ((quarter + r // 2) % SIDE * 2 + panel) * N_COL + r + N_ROW * odd
                 pairs.append((r * N_COL + x * SIDE + z, target))
     return lax.ppermute(value, ("row", "col"), pairs)
 
@@ -128,8 +131,10 @@
         choose(after, own1, near1, far1, back1),
         choose(cross, own2, near2, far2, back2),
     )
-    half = jnp.where(cross < 2, block1, block2)
-    tile = lax.dynamic_slice(half, (cross % 2 * NB, 0), (NB, NB))
+    turned = (cross - row // 4) % SIDE
+    odd = jnp.where(core == 0, cross % 2, turned // 2)
+    panel = jnp.where(core == 0, cross // 2, turned % 2)
+    tile = lax.dynamic_slice(jnp.where(panel == 0, block1, block2), (odd * NB, 0), (NB, NB))
     block1, block2, tile, pivot = barrier((block1, block2, tile, block1[:NB]))
 
     corner = [(N_COL + SIDE * a, N_COL + SIDE * a + 2) for a in range(SIDE)]
@@ -143,28 +148,25 @@
     ))
     pivot = choose(z, pivot, near1[:NB], pivot_far, back1[:NB])
     near1, back2, own, pivot = barrier((near1, back2, own, pivot))
-    far1, far2, up, down, own_other, pivot_up, pivot_down, pivot_far, pivot_swap = barrier((
+    far1, far2, up, down, own_other, *odd = barrier((
         shift_line(near1, 1),
         shift_line(back2, -1),
         shift_y(own, 1),
         shift_y(own, -1),
         swap_core(own),
-        lax.ppermute(pivot, "row", [(1, 3)]),
-        lax.ppermute(pivot, "row", [(1, 7)]),
-        lax.ppermute(pivot, "row", [(1, 5)]),
-        lax.ppermute(pivot, "row", [(1, 0)]),
+        *[lax.ppermute(pivot, "row", [(1, to)]) for to in (3, 5, 7)],
     ))
     panel1 = [block1, near1, far1, back1]
     panel2 = [block2, near2, far2, back2]
-    odd = pivot_up + pivot_down + pivot_far
+    odd = jnp.where(row == 1, pivot, sum(odd))
     last, up_other, down_other, even = barrier((
         relay_y(up, down, core),
         swap_core(up),
         swap_core(down),
-        lax.ppermute(odd, "row", [(3, 2), (5, 4), (7, 6)]),
+        lax.ppermute(odd, "row", [(1, 0), (3, 2), (5, 4), (7, 6)]),
     ))
     cols = [own, up, last, down, own_other, up_other, swap_core(last), down_other]
-    pivots = [pivot_swap, pivot, even, odd]
+    pivots = [even, odd]
     return panel1, panel2, cols, pivots
 
 
@@ -196,7 +198,9 @@
     copies = []
     for n in range(N_ROW):
         k = lax.rem(y + SIDE - n % SIDE, SIDE) * 2 + lax.rem(core + n // SIDE, 2)
-        target = raw.at[lax.rem(k, 2), rows_at(lax.div(k, 2), NB), :]
+        source_y = lax.div(lax.rem(lax.axis_index("col"), N_ROW), 2)
+        tile = lax.rem(lax.div(k, 2) + SIDE - source_y, SIDE)
+        target = raw.at[lax.rem(k, 2), rows_at(tile, NB), :]
         copies.append(pltpu.make_async_copy(tiles[n], target, sems.at[n]))
     return copies
 
@@ -246,7 +250,7 @@
 
 def last_kernel(*refs):
     pieces, cols = refs[:SIDE], refs[SIDE : SIDE + N_ROW]
-    pivots, refs = refs[SIDE + N_ROW : SIDE + N_ROW + 4], refs[SIDE + N_ROW + 4 :]
+    pivots, refs = refs[SIDE + N_ROW : SIDE + N_ROW + 2], refs[SIDE + N_ROW + 2 :]
     matrix, inv_in, high_in, low_in, band, out, panel, *refs = refs
     tiles, raw, raw_cols, row_high1, row_low1, row_high2, row_low2, col_high, col_low, even, odd, *refs = refs
     inv, pivot, sems, col_sems, in_sems, out_sems, panel_sems, small_sems = refs
@@ -257,9 +261,9 @@
     small = [(inv_in, inv), (pivots[0], pivot), (high_in, row_high1), (low_in, row_low1)]
     small = [pltpu.make_async_copy(a, b, small_sems.at[n]) for n, (a, b) in enumerate(small)]
     small[0].start()
-    for n, rows in enumerate(((0,), (1,), (2, 4, 6), (3, 5, 7))):
-
-        @pl.when(functools.reduce(jnp.logical_or, [r == row for row in rows]))
+    for n in range(2):
+
+        @pl.when(lax.rem(r, 2) == n)
         def _():
             pltpu.make_async_copy(pivots[n], pivot, small_sems.at[1]).start()
 
@@ -353,7 +357,7 @@
             jax.ShapeDtypeStruct((TR, LINES, HALF), F32),
             jax.ShapeDtypeStruct((TR, NB, NB), F32),
         ),
-        in_specs=[ANY] * (SIDE + N_ROW + 4 + 4) + [SMEM],
+        in_specs=[ANY] * (SIDE + N_ROW + 2 + 4) + [SMEM],
         out_specs=[ANY] * 2,
         scratch_shapes=[
             pltpu.VMEM((TR, LINES, HALF), F32),

time: 125 us -> 125 us (level)
  starting transfers between devices: 54.7 us -> 50.6 us
  other arithmetic: 4.84 us -> 6.99 us
    ppermute x5 -> x4, waiting for transfers between devices: 3.45 us -> 5.74 us  [the longest x3 5.74 us: gather_all(): lax.ppermute(pivot, 'row', [(1, to)])]
    ppermute x1, starting transfers between devices: 2.34 us -> 0.07 us  [relay_y(): return lax.ppermute(jnp.where(core == 0, near, back), 'row', pairs)]
    ppermute x4, starting transfers between devices: 5.13 us -> 3.13 us  [swap_core(): return lax.ppermute(value, 'row', [(r, r ^ 1) for r in range(N_ROW)])]
    ppermute x2, waiting for transfers between devices: 1.49 us -> 0.01 us  [shift_y(): return lax.ppermute(value, 'row', pairs)]
    select_n x0 -> x1, other arithmetic: none -> 1.33 us  [gather_all(): odd = jnp.where(row == 1, pivot, sum(odd))]
    ppermute x5 -> x4, starting transfers between devices: 8.41 us -> 9.56 us  [the longest x3 8.26 us: gather_all(): lax.ppermute(pivot, 'row', [(1, to)])]
  transfers between devices with their start and end apart: 29 -> 28, of which waited for: 14 -> 12; matrix products, arithmetic and copies ran while one was open for 0% -> 1% of each run, Pallas kernels for 2% -> 2%
where the time goes in v12:
time: 125 us; the launch traced here: 122 us
  starting transfers between devices  50.6 us (40%)
  waiting for transfers between devices  38.8 us (31%)
  Pallas kernels  20.5 us (16%)
  other arithmetic  6.99 us (6%)
  local copies, waits for them, and re-layouts  4.52 us (4%)
    ppermute x14, waiting for transfers between devices, shift_plane(): return lax.ppermute(value, ('row', 'col'), pairs)  22 us
    pallas_call x1, Pallas kernels, finish(): pl.pallas_call(last_kernel, out_shape=(jax.ShapeDtypeStruct((TR, LINES, H...  17.8 us
    ppermute x14, starting transfers between devices, shift_plane(): return lax.ppermute(value, ('row', 'col'), pairs)  16.3 us
    ppermute x1, starting transfers between devices, gather_all(): lax.ppermute(pivot, ('row', 'col'), corner)  11.5 us
    ppermute x3, starting transfers between devices, gather_all(): lax.ppermute(pivot, 'row', [(1, to)])  8.26 us
    ppermute x1, starting transfers between devices, send_far(): return lax.ppermute(value, ('row', 'col'), pairs)  6.35 us
    ppermute x3, waiting for transfers between devices, gather_all(): lax.ppermute(pivot, 'row', [(1, to)])  5.74 us
    ppermute x1, waiting for transfers between devices, send_far(): return lax.ppermute(value, ('row', 'col'), pairs)  4.9 us
  transfers between devices with their start and end apart: 28, of which 12 were waited for; matrix products, arithmetic and copies ran while one was open for 1% of the time, Pallas kernels for 2%

profile of v12, /device:TPU:1, one launch (start us, length us, event | category | flops | bytes accessed | tf_op | source)
XLA Modules:
  0.0 122.4 jit_solution(12226926936674207291)
XLA Ops:
  0.6 1.6 %slice-done = f32[8,256,1,256]{3,2,1,0:T(1,128)S(1)} async-done(((f32[8,256,4,256]{3,2,1,0:T(4,128)}), f32[8,256,1,256]{3,2,1,0:T(1,128)S(1)}, s32[]{:S(2)}) %slice-start) | async-done | bytes 2097176 | tf_op jit(solution)/shard_map/slice | solution.py:391
  3.6 6.3 %collective-permute-start.2 = (f32[512,256]{1,0:T(8,128)}, f32[512,256]{1,0:T(8,128)S(1)}, u32[]{:S(2)}, u32[]{:S(2)}) collective-permute-start(f32[512,256]{1,0:T(8,128)} %get-tuple-element.84), channel_id=1, source_target_pairs={{0,8},{1,9},{16,18},{17,19},{32,40},{33,41},{48,50},{49,51},{64,72... | collective-permute-start | bytes 1572872 | tf_op jit(solution)/shard_map/ppermute | solution.py:63
  11.5 4.9 %collective-permute-done.2 = f32[512,256]{1,0:T(8,128)S(1)} collective-permute-done((f32[512,256]{1,0:T(8,128)}, f32[512,256]{1,0:T(8,128)S(1)}, u32[]{:S(2)}, u32[]{:S(2)}) %collective-permute-start.2) | collective-permute-done | bytes 524320 | tf_op jit(solution)/shard_map/ppermute | solution.py:63
  16.4 6.7 %collective-permute-done.1 = f32[512,256]{1,0:T(8,128)S(1)} collective-permute-done((f32[512,256]{1,0:T(8,128)}, f32[512,256]{1,0:T(8,128)S(1)}, u32[]{:S(2)}, u32[]{:S(2)}) %collective-permute-start.1) | collective-permute-done | bytes 524320 | tf_op jit(solution)/shard_map/ppermute | solution.py:46
  23.9 1.5 %select_select_fusion.2 = (f32[512,256]{1,0:T(8,128)S(1)}, f32[512,256]{1,0:T(8,128)S(1)}) fusion(f32[512,256]{1,0:T(8,128)} %collective-permute-done, f32[512,256]{1,0:T(8,128)} %copy-done.6, f32[512,256]{1,0:T(8,128)} %copy-done.7, f32[2048,256]{1,0:T(8,128)S(1)} %bitcast.12, pred[]{:T(512)S(6)} %eq.78, pred[]{:T(512)S(6)} %eq.77, pred[]{:T(512)S(6)} %eq.76, ...), kind=kLoop, calls=%fused_computation.2 | loop fusion | flops 786432 | bytes 3145734 | tf_op jit(solution)/shard_map/jit(_where)/select_n | solution.py:99
  27.0 2.6 %collective-permute-start.5 = (f32[512,256]{1,0:T(8,128)S(1)}, f32[512,256]{1,0:T(8,128)S(1)}, u32[]{:S(2)}, u32[]{:S(2)}) collective-permute-start(f32[512,256]{1,0:T(8,128)S(1)} %get-tuple-element.81), channel_id=1, source_target_pairs={{0,3},{1,0},{2,1},{3,2},{4,7},{5,4},{6,5},{7,6},{8,11},{9,8},{10,9... | collective-permute-start | bytes 1572872 | tf_op jit(solution)/shard_map/ppermute | solution.py:46
  29.6 4.2 %collective-permute-done.7 = f32[512,256]{1,0:T(8,128)S(1)} collective-permute-done((f32[512,256]{1,0:T(8,128)S(1)}, f32[512,256]{1,0:T(8,128)S(1)}, u32[]{:S(2)}, u32[]{:S(2)}) %collective-permute-start.7) | collective-permute-done | bytes 524320 | tf_op jit(solution)/shard_map/ppermute | solution.py:46
  35.3 5.5 %collective-permute-done.6 = f32[512,256]{1,0:T(8,128)S(1)} collective-permute-done((f32[512,256]{1,0:T(8,128)S(1)}, f32[512,256]{1,0:T(8,128)S(1)}, u32[]{:S(2)}, u32[]{:S(2)}) %collective-permute-start.6) | collective-permute-done | bytes 524320 | tf_op jit(solution)/shard_map/ppermute | solution.py:46
  40.8 4.3 %collective-permute-done.8 = f32[512,256]{1,0:T(8,128)} collective-permute-done((f32[512,256]{1,0:T(8,128)S(1)}, f32[512,256]{1,0:T(8,128)}, u32[]{:S(2)}, u32[]{:S(2)}) %collective-permute-start.8) | collective-permute-done | bytes 524320 | tf_op jit(solution)/shard_map/ppermute | solution.py:46
  46.3 1.5 %select_select_fusion = (f32[512,256]{1,0:T(8,128)S(1)}, f32[512,256]{1,0:T(8,128)S(1)}) fusion(f32[512,256]{1,0:T(8,128)S(1)} %get-tuple-element.80, f32[512,256]{1,0:T(8,128)} %copy-done.8, f32[512,256]{1,0:T(8,128)} %collective-permute-done.8, f32[512,256]{1,0:T(8,128)S(1)} %collective-permute-done.7, f32[512,256]{1,0:T(8,128)S(1)} %get-tuple-element.81, ...), kind=kLoop, calls=%fused_computation | loop fusion | flops 1310720 | bytes 5242887 | tf_op jit(solution)/shard_map/jit(_where)/select_n | solution.py:129
  48.5 2.2 %collective-permute-start.13 = (f32[256,256]{1,0:T(8,128)S(1)}, f32[256,256]{1,0:T(8,128)S(1)}, u32[]{:S(2)}, u32[]{:S(2)}) collective-permute-start(f32[256,256]{1,0:T(8,128)S(1)} %get-tuple-element.52), channel_id=1, source_target_pairs={{0,0},{1,8},{2,16},{3,24},{4,32},{5,40},{6,48},{7,56},{8,64},{9,72... | collective-permute-start | bytes 786440 | tf_op jit(solution)/shard_map/ppermute | solution.py:90
  52.1 3.6 %collective-permute-start.10 = (f32[512,256]{1,0:T(8,128)S(1)}, f32[512,256]{1,0:T(8,128)}, u32[]{:S(2)}, u32[]{:S(2)}) collective-permute-start(f32[512,256]{1,0:T(8,128)S(1)} %get-tuple-element.50.refs_0_), channel_id=1, source_target_pairs={{0,12},{1,13},{2,14},{3,15},{4,0},{5,1},{6,2},{7,3},{8,4},{9,5},{1... | collective-permute-start | bytes 1572872 | tf_op jit(solution)/shard_map/ppermute | solution.py:46
  57.8 11.5 %collective-permute-start.14 = (f32[256,256]{1,0:T(8,128)}, f32[256,256]{1,0:T(8,128)}, u32[]{:S(2)}, u32[]{:S(2)}) collective-permute-start(f32[256,256]{1,0:T(8,128)} %get-tuple-element.53), channel_id=1, source_target_pairs={{16,18},{20,22},{24,26},{28,30}} | collective-permute-start | bytes 786440 | tf_op jit(solution)/shard_map/ppermute | solution.py:147
  69.4 2.9 %collective-permute-done.14 = f32[256,256]{1,0:T(8,128)} collective-permute-done((f32[256,256]{1,0:T(8,128)}, f32[256,256]{1,0:T(8,128)}, u32[]{:S(2)}, u32[]{:S(2)}) %collective-permute-start.14) | collective-permute-done | bytes 262176 | tf_op jit(solution)/shard_map/ppermute | solution.py:147
  72.3 1.9 %select_select_fusion.4 = f32[256,256]{1,0:T(8,128)} fusion(f32[256,256]{1,0:T(8,128)} %get-tuple-element.53, f32[256,256]{1,0:T(8,128)} %collective-permute-done.14, f32[512,256]{1,0:T(8,128)S(1)} %collective-permute-done.11.refs_3_, f32[512,256]{1,0:T(8,128)S(1)} %collective-permute-done.9.refs_1_, pred[]{:T(512)S(6)} %eq.86, pred[]{:T(512)S(6)} %eq.85, ...), kind=kLoop, calls=%fused_computation.6 | loop fusion | flops 196608 | bytes 1310723 | tf_op jit(solution)/shard_map/jit(_where)/select_n | solution.py:99
  74.2 2.5 %collective-permute-start.19 = (f32[256,256]{1,0:T(8,128)S(1)}, f32[256,256]{1,0:T(8,128)S(1)}, u32[]{:S(2)}, u32[]{:S(2)}) collective-permute-start(f32[256,256]{1,0:T(8,128)S(1)} %collective-permute-done.13.refs_4_), channel_id=1, source_target_pairs={{0,16},{16,0},{32,48},{48,32},{64,80},{80,64},{96,112},{112,96},{1... | collective-permute-start | bytes 786440 | tf_op jit(solution)/shard_map/ppermute | solution.py:72
  78.1 2.7 %collective-permute-start.16 = (f32[512,256]{1,0:T(8,128)}, f32[512,256]{1,0:T(8,128)}, u32[]{:S(2)}, u32[]{:S(2)}) collective-permute-start(f32[512,256]{1,0:T(8,128)} %collective-permute-done.10.refs_3_), channel_id=1, source_target_pairs={{0,12},{1,13},{2,14},{3,15},{4,0},{5,1},{6,2},{7,3},{8,4},{9,5},{1... | collective-permute-start | bytes 1572872 | tf_op jit(solution)/shard_map/ppermute | solution.py:46
  81.5 3.8 %collective-permute-start.22 = (f32[256,256]{1,0:T(8,128)}, f32[256,256]{1,0:T(8,128)}, u32[]{:S(2)}, u32[]{:S(2)}) collective-permute-start(f32[256,256]{1,0:T(8,128)} %select_select_fusion.4), channel_id=1, source_target_pairs={{16,112},{17,113},{18,114},{19,115},{20,116},{21,117},{22,118},{23... | collective-permute-start | bytes 786440 | tf_op jit(solution)/shard_map/ppermute | solution.py:157
  85.3 2.4 %collective-permute-start.21 = (f32[256,256]{1,0:T(8,128)}, f32[256,256]{1,0:T(8,128)}, u32[]{:S(2)}, u32[]{:S(2)}) collective-permute-start(f32[256,256]{1,0:T(8,128)} %select_select_fusion.4), channel_id=1, source_target_pairs={{16,80},{17,81},{18,82},{19,83},{20,84},{21,85},{22,86},{23,87},{2... | collective-permute-start | bytes 786440 | tf_op jit(solution)/shard_map/ppermute | solution.py:157
  87.8 2.0 %collective-permute-start.20 = (f32[256,256]{1,0:T(8,128)}, f32[256,256]{1,0:T(8,128)}, u32[]{:S(2)}, u32[]{:S(2)}) collective-permute-start(f32[256,256]{1,0:T(8,128)} %select_select_fusion.4), channel_id=1, source_target_pairs={{16,48},{17,49},{18,50},{19,51},{20,52},{21,53},{22,54},{23,55},{2... | collective-permute-start | bytes 786440 | tf_op jit(solution)/shard_map/ppermute | solution.py:157
  90.7 4.8 %collective-permute-done.20 = f32[256,256]{1,0:T(8,128)} collective-permute-done((f32[256,256]{1,0:T(8,128)}, f32[256,256]{1,0:T(8,128)}, u32[]{:S(2)}, u32[]{:S(2)}) %collective-permute-start.20) | collective-permute-done | bytes 262176 | tf_op jit(solution)/shard_map/ppermute | solution.py:157
  98.9 2.6 %collective-permute-done.23.refs_6_ = f32[256,256]{1,0:T(8,128)S(1)} collective-permute-done((f32[256,256]{1,0:T(8,128)S(1)}, f32[256,256]{1,0:T(8,128)S(1)}, u32[]{:S(2)}, u32[]{:S(2)}) %collective-permute-start.23) | collective-permute-done | bytes 262176 | tf_op jit(solution)/shard_map/ppermute | solution.py:95
  101.6 2.7 %solve_first.1 = (bf16[8,256,256]{2,1,0:T(8,128)(2,1)S(1)}, bf16[8,256,256]{2,1,0:T(8,128)(2,1)S(1)}) custom-call(f32[512,256]{1,0:T(8,128)S(1)} %get-tuple-element.51.refs_0_, f32[512,256]{1,0:T(8,128)S(1)} %collective-permute-done.9.refs_1_, f32[512,256]{1,0:T(8,128)} %collective-permute-done.15.refs_2_, f32[512,256]{1,0:T(8,128)S(1)} %collective-permute-done.11.refs_3_, ...), custom_call_target="tpu_custom_call" | custom-call | flops 805306368 | bytes 4194304 | tf_op jit(solution)/shard_map/solve_first/pallas_call | solution.py:230
  104.4 17.8 %solve_and_update.1 = (f32[8,2048,128]{2,1,0:T(8,128)}, f32[8,256,256]{2,1,0:T(8,128)}) custom-call(f32[512,256]{1,0:T(8,128)S(1)} %get-tuple-element.50.refs_0_, f32[512,256]{1,0:T(8,128)S(1)} %copy-done.2, f32[512,256]{1,0:T(8,128)} %collective-permute-done.16.refs_2_, f32[512,256]{1,0:T(8,128)} %collective-permute-done.10.refs_3_, ...), custom_call_target="tpu_custom_call" | custom-call | flops 6710886400 | bytes 20971520 | tf_op jit(solution)/shard_map/solve_and_update/pallas_call | solution.py:354
  (64 shorter events, 18.7 us)
Async XLA Ops:
  3.6 12.8 %collective-permute-start.2 = (f32[512,256]{1,0:T(8,128)}, f32[512,256]{1,0:T(8,128)S(1)}, u32[]{:S(2)}, u32[]{:S(2)}) collective-permute-start(f32[512,256]{1,0:T(8,128)} %get-tuple-element.84), channel_id=1, source_target_pairs={{0,8},{1,9},{16,18},{17,19},{32,40},{33,41},{48,50},{49,51},{64,72... | collective-permute-start | bytes 1572872 | tf_op jit(solution)/shard_map/ppermute | solution.py:63
  10.0 13.1 %collective-permute-start.1 = (f32[512,256]{1,0:T(8,128)}, f32[512,256]{1,0:T(8,128)S(1)}, u32[]{:S(2)}, u32[]{:S(2)}) collective-permute-start(f32[512,256]{1,0:T(8,128)} %get-tuple-element.85), channel_id=1, source_target_pairs={{0,12},{1,13},{2,14},{3,15},{4,0},{5,1},{6,2},{7,3},{8,4},{9,5},{1... | collective-permute-start | bytes 1572872 | tf_op jit(solution)/shard_map/ppermute | solution.py:46
  10.1 13.8 %collective-permute-start = (f32[512,256]{1,0:T(8,128)}, f32[512,256]{1,0:T(8,128)}, u32[]{:S(2)}, u32[]{:S(2)}) collective-permute-start(f32[512,256]{1,0:T(8,128)} %get-tuple-element.86), channel_id=1, source_target_pairs={{0,4},{1,5},{2,6},{3,7},{4,8},{5,9},{6,10},{7,11},{8,12},{9,13},{1... | collective-permute-start | bytes 1572872 | tf_op jit(solution)/shard_map/ppermute | solution.py:46
  25.4 8.4 %collective-permute-start.7 = (f32[512,256]{1,0:T(8,128)S(1)}, f32[512,256]{1,0:T(8,128)S(1)}, u32[]{:S(2)}, u32[]{:S(2)}) collective-permute-start(f32[512,256]{1,0:T(8,128)S(1)} %get-tuple-element.80), channel_id=1, source_target_pairs={{0,3},{1,0},{2,1},{3,2},{4,7},{5,4},{6,5},{7,6},{8,11},{9,8},{10,9... | collective-permute-start | bytes 1572872 | tf_op jit(solution)/shard_map/ppermute | solution.py:46
  25.5 9.6 %collective-permute-start.3 = (f32[512,256]{1,0:T(8,128)S(1)}, f32[512,256]{1,0:T(8,128)S(1)}, u32[]{:S(2)}, u32[]{:S(2)}) collective-permute-start(f32[512,256]{1,0:T(8,128)S(1)} %get-tuple-element.81), channel_id=1, source_target_pairs={{0,1},{1,2},{2,3},{3,0},{4,5},{5,6},{6,7},{7,4},{8,9},{9,10},{10,1... | collective-permute-start | bytes 1572872 | tf_op jit(solution)/shard_map/ppermute | solution.py:46
  26.9 13.9 %collective-permute-start.6 = (f32[512,256]{1,0:T(8,128)S(1)}, f32[512,256]{1,0:T(8,128)S(1)}, u32[]{:S(2)}, u32[]{:S(2)}) collective-permute-start(f32[512,256]{1,0:T(8,128)S(1)} %get-tuple-element.80), channel_id=1, source_target_pairs={{0,1},{1,2},{2,3},{3,0},{4,5},{5,6},{6,7},{7,4},{8,9},{9,10},{10,1... | collective-permute-start | bytes 1572872 | tf_op jit(solution)/shard_map/ppermute | solution.py:46
  27.0 13.8 %collective-permute-start.5 = (f32[512,256]{1,0:T(8,128)S(1)}, f32[512,256]{1,0:T(8,128)S(1)}, u32[]{:S(2)}, u32[]{:S(2)}) collective-permute-start(f32[512,256]{1,0:T(8,128)S(1)} %get-tuple-element.81), channel_id=1, source_target_pairs={{0,3},{1,0},{2,1},{3,2},{4,7},{5,4},{6,5},{7,6},{8,11},{9,8},{10,9... | collective-permute-start | bytes 1572872 | tf_op jit(solution)/shard_map/ppermute | solution.py:46
  33.8 11.3 %collective-permute-start.8 = (f32[512,256]{1,0:T(8,128)S(1)}, f32[512,256]{1,0:T(8,128)}, u32[]{:S(2)}, u32[]{:S(2)}) collective-permute-start(f32[512,256]{1,0:T(8,128)S(1)} %collective-permute-done.7), channel_id=1, source_target_pairs={{0,3},{1,0},{2,1},{3,2},{4,7},{5,4},{6,5},{7,6},{8,11},{9,8},{10,9... | collective-permute-start | bytes 1572872 | tf_op jit(solution)/shard_map/ppermute | solution.py:46
  35.1 11.2 %collective-permute-start.4 = (f32[512,256]{1,0:T(8,128)S(1)}, f32[512,256]{1,0:T(8,128)}, u32[]{:S(2)}, u32[]{:S(2)}) collective-permute-start(f32[512,256]{1,0:T(8,128)S(1)} %collective-permute-done.3), channel_id=1, source_target_pairs={{0,1},{1,2},{2,3},{3,0},{4,5},{5,6},{6,7},{7,4},{8,9},{9,10},{10,1... | collective-permute-start | bytes 1572872 | tf_op jit(solution)/shard_map/ppermute | solution.py:46
  48.5 9.3 %collective-permute-start.13 = (f32[256,256]{1,0:T(8,128)S(1)}, f32[256,256]{1,0:T(8,128)S(1)}, u32[]{:S(2)}, u32[]{:S(2)}) collective-permute-start(f32[256,256]{1,0:T(8,128)S(1)} %get-tuple-element.52), channel_id=1, source_target_pairs={{0,0},{1,8},{2,16},{3,24},{4,32},{5,40},{6,48},{7,56},{8,64},{9,72... | collective-permute-start | bytes 786440 | tf_op jit(solution)/shard_map/ppermute | solution.py:90
  50.7 21.5 %collective-permute-start.12 = (f32[512,256]{1,0:T(8,128)S(1)}, f32[512,256]{1,0:T(8,128)S(1)}, u32[]{:S(2)}, u32[]{:S(2)}) collective-permute-start(f32[512,256]{1,0:T(8,128)S(1)} %get-tuple-element.50.refs_0_), channel_id=1, source_target_pairs={{0,4},{1,5},{2,6},{3,7},{4,8},{5,9},{6,10},{7,11},{8,12},{9,13},{1... | collective-permute-start | bytes 1572872 | tf_op jit(solution)/shard_map/ppermute | solution.py:46
  52.1 20.2 %collective-permute-start.10 = (f32[512,256]{1,0:T(8,128)S(1)}, f32[512,256]{1,0:T(8,128)}, u32[]{:S(2)}, u32[]{:S(2)}) collective-permute-start(f32[512,256]{1,0:T(8,128)S(1)} %get-tuple-element.50.refs_0_), channel_id=1, source_target_pairs={{0,12},{1,13},{2,14},{3,15},{4,0},{5,1},{6,2},{7,3},{8,4},{9,5},{1... | collective-permute-start | bytes 1572872 | tf_op jit(solution)/shard_map/ppermute | solution.py:46
  55.7 16.5 %collective-permute-start.11 = (f32[512,256]{1,0:T(8,128)S(1)}, f32[512,256]{1,0:T(8,128)S(1)}, u32[]{:S(2)}, u32[]{:S(2)}) collective-permute-start(f32[512,256]{1,0:T(8,128)S(1)} %get-tuple-element.51.refs_0_), channel_id=1, source_target_pairs={{0,12},{1,13},{2,14},{3,15},{4,0},{5,1},{6,2},{7,3},{8,4},{9,5},{1... | collective-permute-start | bytes 1572872 | tf_op jit(solution)/shard_map/ppermute | solution.py:46
  57.1 15.2 %collective-permute-start.9 = (f32[512,256]{1,0:T(8,128)S(1)}, f32[512,256]{1,0:T(8,128)S(1)}, u32[]{:S(2)}, u32[]{:S(2)}) collective-permute-start(f32[512,256]{1,0:T(8,128)S(1)} %get-tuple-element.51.refs_0_), channel_id=1, source_target_pairs={{0,4},{1,5},{2,6},{3,7},{4,8},{5,9},{6,10},{7,11},{8,12},{9,13},{1... | collective-permute-start | bytes 1572872 | tf_op jit(solution)/shard_map/ppermute | solution.py:46
  57.8 14.4 %collective-permute-start.14 = (f32[256,256]{1,0:T(8,128)}, f32[256,256]{1,0:T(8,128)}, u32[]{:S(2)}, u32[]{:S(2)}) collective-permute-start(f32[256,256]{1,0:T(8,128)} %get-tuple-element.53), channel_id=1, source_target_pairs={{16,18},{20,22},{24,26},{28,30}} | collective-permute-start | bytes 786440 | tf_op jit(solution)/shard_map/ppermute | solution.py:147
  74.2 6.6 %collective-permute-start.19 = (f32[256,256]{1,0:T(8,128)S(1)}, f32[256,256]{1,0:T(8,128)S(1)}, u32[]{:S(2)}, u32[]{:S(2)}) collective-permute-start(f32[256,256]{1,0:T(8,128)S(1)} %collective-permute-done.13.refs_4_), channel_id=1, source_target_pairs={{0,16},{16,0},{32,48},{48,32},{64,80},{80,64},{96,112},{112,96},{1... | collective-permute-start | bytes 786440 | tf_op jit(solution)/shard_map/ppermute | solution.py:72
  76.7 8.7 %collective-permute-start.18 = (f32[256,256]{1,0:T(8,128)S(1)}, f32[256,256]{1,0:T(8,128)S(1)}, u32[]{:S(2)}, u32[]{:S(2)}) collective-permute-start(f32[256,256]{1,0:T(8,128)S(1)} %collective-permute-done.13.refs_4_), channel_id=1, source_target_pairs={{0,96},{16,112},{32,0},{48,16},{64,32},{80,48},{96,64},{112,80},{1... | collective-permute-start | bytes 786440 | tf_op jit(solution)/shard_map/ppermute | solution.py:68
  76.7 11.1 %collective-permute-start.17 = (f32[256,256]{1,0:T(8,128)S(1)}, f32[256,256]{1,0:T(8,128)S(1)}, u32[]{:S(2)}, u32[]{:S(2)}) collective-permute-start(f32[256,256]{1,0:T(8,128)S(1)} %collective-permute-done.13.refs_4_), channel_id=1, source_target_pairs={{0,32},{16,48},{32,64},{48,80},{64,96},{80,112},{96,0},{112,16},{1... | collective-permute-start | bytes 786440 | tf_op jit(solution)/shard_map/ppermute | solution.py:68
  78.1 17.4 %collective-permute-start.15 = (f32[512,256]{1,0:T(8,128)S(1)}, f32[512,256]{1,0:T(8,128)}, u32[]{:S(2)}, u32[]{:S(2)}) collective-permute-start(f32[512,256]{1,0:T(8,128)S(1)} %collective-permute-done.9.refs_1_), channel_id=1, source_target_pairs={{0,4},{1,5},{2,6},{3,7},{4,8},{5,9},{6,10},{7,11},{8,12},{9,13},{1... | collective-permute-start | bytes 1572872 | tf_op jit(solution)/shard_map/ppermute | solution.py:46
  78.1 17.4 %collective-permute-start.16 = (f32[512,256]{1,0:T(8,128)}, f32[512,256]{1,0:T(8,128)}, u32[]{:S(2)}, u32[]{:S(2)}) collective-permute-start(f32[512,256]{1,0:T(8,128)} %collective-permute-done.10.refs_3_), channel_id=1, source_target_pairs={{0,12},{1,13},{2,14},{3,15},{4,0},{5,1},{6,2},{7,3},{8,4},{9,5},{1... | collective-permute-start | bytes 1572872 | tf_op jit(solution)/shard_map/ppermute | solution.py:46
  81.5 8.3 %collective-permute-start.22 = (f32[256,256]{1,0:T(8,128)}, f32[256,256]{1,0:T(8,128)}, u32[]{:S(2)}, u32[]{:S(2)}) collective-permute-start(f32[256,256]{1,0:T(8,128)} %select_select_fusion.4), channel_id=1, source_target_pairs={{16,112},{17,113},{18,114},{19,115},{20,116},{21,117},{22,118},{23... | collective-permute-start | bytes 786440 | tf_op jit(solution)/shard_map/ppermute | solution.py:157
  85.3 5.3 %collective-permute-start.21 = (f32[256,256]{1,0:T(8,128)}, f32[256,256]{1,0:T(8,128)}, u32[]{:S(2)}, u32[]{:S(2)}) collective-permute-start(f32[256,256]{1,0:T(8,128)} %select_select_fusion.4), channel_id=1, source_target_pairs={{16,80},{17,81},{18,82},{19,83},{20,84},{21,85},{22,86},{23,87},{2... | collective-permute-start | bytes 786440 | tf_op jit(solution)/shard_map/ppermute | solution.py:157
  87.8 7.7 %collective-permute-start.20 = (f32[256,256]{1,0:T(8,128)}, f32[256,256]{1,0:T(8,128)}, u32[]{:S(2)}, u32[]{:S(2)}) collective-permute-start(f32[256,256]{1,0:T(8,128)} %select_select_fusion.4), channel_id=1, source_target_pairs={{16,48},{17,49},{18,50},{19,51},{20,52},{21,53},{22,54},{23,55},{2... | collective-permute-start | bytes 786440 | tf_op jit(solution)/shard_map/ppermute | solution.py:157
  95.6 5.9 %collective-permute-start.23 = (f32[256,256]{1,0:T(8,128)S(1)}, f32[256,256]{1,0:T(8,128)S(1)}, u32[]{:S(2)}, u32[]{:S(2)}) collective-permute-start(f32[256,256]{1,0:T(8,128)S(1)} %broadcast_select_fusion), channel_id=1, source_target_pairs={{0,32},{16,112},{32,64},{48,16},{64,96},{80,48},{96,0},{112,80},{1... | collective-permute-start | bytes 786440 | tf_op jit(solution)/shard_map/ppermute | solution.py:95
  (15 other events, 114.5 us)

commit v13 on v12

--- a/solution.py
+++ b/solution.py
@@ -165,7 +165,7 @@
         swap_core(down),
         lax.ppermute(odd, "row", [(1, 0), (3, 2), (5, 4), (7, 6)]),
     ))
-    cols = [own, up, last, down, own_other, up_other, swap_core(last), down_other]
+    cols = (own, up, last, down, own_other, up_other, down_other)
     pivots = [even, odd]
     return panel1, panel2, cols, pivots
 
@@ -391,6 +391,9 @@
     raw = lax.optimization_barrier(matrix[:, :, 0, :].reshape(ROWS, NB))
     panel1, panel2, cols, pivots = gather_all(raw, lax.axis_index("row"), lax.axis_index("col"))
     first = solve_first(panel1, diag_inverses)
+    cols, first = lax.optimization_barrier((cols, first))
+    own, up, last, down, own_other, up_other, down_other = cols
+    cols = [own, up, last, down, own_other, up_other, swap_core(last), down_other]
     return finish(panel2, cols, pivots, matrix, diag_inverses, first, band)
 
 

time: 125 us -> 124 us (level)
  the two profiles are of different devices: /device:TPU:1 before, /device:TPU:19 now
where the time goes in v13:
time: 124 us
  waiting for transfers between devices  47.5 us (38%)
  starting transfers between devices  43.5 us (35%)
  Pallas kernels  20.5 us (17%)
  other arithmetic  6.81 us (5%)
  local copies, waits for them, and re-layouts  4.51 us (4%)
    ppermute x14, waiting for transfers between devices, shift_plane(): return lax.ppermute(value, ('row', 'col'), pairs)  34.4 us
    ppermute x14, starting transfers between devices, shift_plane(): return lax.ppermute(value, ('row', 'col'), pairs)  20.1 us
    pallas_call x1, Pallas kernels, finish(): pl.pallas_call(last_kernel, out_shape=(jax.ShapeDtypeStruct((TR, LINES, H...  17.8 us
    ppermute x3, waiting for transfers between devices, gather_all(): lax.ppermute(pivot, 'row', [(1, to)])  7.54 us
    ppermute x1, starting transfers between devices, relay_y(): return lax.ppermute(jnp.where(core == 0, near, back), 'row', pairs)  4.75 us
    ppermute x3, starting transfers between devices, gather_all(): lax.ppermute(pivot, 'row', [(1, to)])  4.01 us
    ppermute x1, starting transfers between devices, to_columns(): return lax.ppermute(value, ('row', 'col'), pairs)  3.92 us
    ppermute x4, starting transfers between devices, swap_core(): return lax.ppermute(value, 'row', [(r, r ^ 1) for r in range(N_ROW)])  3.72 us
  transfers between devices with their start and end apart: 28, of which 13 were waited for; matrix products, arithmetic and copies ran while one was open for 1% of the time, Pallas kernels for 2%

profile of v13, /device:TPU:19, one launch (start us, length us, event | category | flops | bytes accessed | tf_op | source)
XLA Modules:
  0.0 123.8 jit_solution(7145249468054354621)
XLA Ops:
  4.3 3.8 %collective-permute-start.1 = (f32[512,256]{1,0:T(8,128)}, f32[512,256]{1,0:T(8,128)S(1)}, u32[]{:S(2)}, u32[]{:S(2)}) collective-permute-start(f32[512,256]{1,0:T(8,128)} %get-tuple-element.103), channel_id=1, source_target_pairs={{0,12},{1,13},{2,14},{3,15},{4,0},{5,1},{6,2},{7,3},{8,4},{9,5},{1... | collective-permute-start | bytes 1572872 | tf_op jit(solution)/shard_map/ppermute | solution.py:46
  8.2 6.4 %collective-permute-done.1 = f32[512,256]{1,0:T(8,128)S(1)} collective-permute-done((f32[512,256]{1,0:T(8,128)}, f32[512,256]{1,0:T(8,128)S(1)}, u32[]{:S(2)}, u32[]{:S(2)}) %collective-permute-start.1) | collective-permute-done | bytes 524320 | tf_op jit(solution)/shard_map/ppermute | solution.py:46
  15.4 2.3 %collective-permute-done = f32[512,256]{1,0:T(8,128)} collective-permute-done((f32[512,256]{1,0:T(8,128)}, f32[512,256]{1,0:T(8,128)}, u32[]{:S(2)}, u32[]{:S(2)}) %collective-permute-start) | collective-permute-done | bytes 524320 | tf_op jit(solution)/shard_map/ppermute | solution.py:46
  19.2 5.7 %collective-permute-start.7 = (f32[512,256]{1,0:T(8,128)S(1)}, f32[512,256]{1,0:T(8,128)S(1)}, u32[]{:S(2)}, u32[]{:S(2)}) collective-permute-start(f32[512,256]{1,0:T(8,128)S(1)} %get-tuple-element.98), channel_id=1, source_target_pairs={{0,3},{1,0},{2,1},{3,2},{4,7},{5,4},{6,5},{7,6},{8,11},{9,8},{10,9... | collective-permute-start | bytes 1572872 | tf_op jit(solution)/shard_map/ppermute | solution.py:46
  26.4 4.6 %collective-permute-done.7 = f32[512,256]{1,0:T(8,128)S(1)} collective-permute-done((f32[512,256]{1,0:T(8,128)S(1)}, f32[512,256]{1,0:T(8,128)S(1)}, u32[]{:S(2)}, u32[]{:S(2)}) %collective-permute-start.7) | collective-permute-done | bytes 524320 | tf_op jit(solution)/shard_map/ppermute | solution.py:46
  31.0 2.2 %collective-permute-start.8 = (f32[512,256]{1,0:T(8,128)S(1)}, f32[512,256]{1,0:T(8,128)}, u32[]{:S(2)}, u32[]{:S(2)}) collective-permute-start(f32[512,256]{1,0:T(8,128)S(1)} %collective-permute-done.7), channel_id=1, source_target_pairs={{0,3},{1,0},{2,1},{3,2},{4,7},{5,4},{6,5},{7,6},{8,11},{9,8},{10,9... | collective-permute-start | bytes 1572872 | tf_op jit(solution)/shard_map/ppermute | solution.py:46
  33.2 5.7 %collective-permute-done.6 = f32[512,256]{1,0:T(8,128)S(1)} collective-permute-done((f32[512,256]{1,0:T(8,128)S(1)}, f32[512,256]{1,0:T(8,128)S(1)}, u32[]{:S(2)}, u32[]{:S(2)}) %collective-permute-start.6) | collective-permute-done | bytes 524320 | tf_op jit(solution)/shard_map/ppermute | solution.py:46
  39.0 3.3 %collective-permute-done.8 = f32[512,256]{1,0:T(8,128)} collective-permute-done((f32[512,256]{1,0:T(8,128)S(1)}, f32[512,256]{1,0:T(8,128)}, u32[]{:S(2)}, u32[]{:S(2)}) %collective-permute-start.8) | collective-permute-done | bytes 524320 | tf_op jit(solution)/shard_map/ppermute | solution.py:46
  42.3 2.3 %collective-permute-done.4 = f32[512,256]{1,0:T(8,128)} collective-permute-done((f32[512,256]{1,0:T(8,128)S(1)}, f32[512,256]{1,0:T(8,128)}, u32[]{:S(2)}, u32[]{:S(2)}) %collective-permute-start.4) | collective-permute-done | bytes 524320 | tf_op jit(solution)/shard_map/ppermute | solution.py:46
  44.6 1.6 %select_select_fusion = (f32[512,256]{1,0:T(8,128)S(1)}, f32[512,256]{1,0:T(8,128)S(1)}) fusion(f32[512,256]{1,0:T(8,128)S(1)} %get-tuple-element.98, f32[512,256]{1,0:T(8,128)} %copy-done.8, f32[512,256]{1,0:T(8,128)} %collective-permute-done.8, f32[512,256]{1,0:T(8,128)S(1)} %collective-permute-done.7, f32[512,256]{1,0:T(8,128)S(1)} %get-tuple-element.99, ...), kind=kLoop, calls=%fused_computation | loop fusion | flops 1310720 | bytes 5242887 | tf_op jit(solution)/shard_map/jit(_where)/select_n | solution.py:129
  47.0 3.9 %collective-permute-start.13 = (f32[256,256]{1,0:T(8,128)S(1)}, f32[256,256]{1,0:T(8,128)S(1)}, u32[]{:S(2)}, u32[]{:S(2)}) collective-permute-start(f32[256,256]{1,0:T(8,128)S(1)} %get-tuple-element.61), channel_id=1, source_target_pairs={{0,0},{1,8},{2,16},{3,24},{4,32},{5,40},{6,48},{7,56},{8,64},{9,72... | collective-permute-start | bytes 786440 | tf_op jit(solution)/shard_map/ppermute | solution.py:90
  52.0 1.7 %collective-permute-start.10 = (f32[512,256]{1,0:T(8,128)S(1)}, f32[512,256]{1,0:T(8,128)}, u32[]{:S(2)}, u32[]{:S(2)}) collective-permute-start(f32[512,256]{1,0:T(8,128)S(1)} %get-tuple-element.59.refs_0_), channel_id=1, source_target_pairs={{0,12},{1,13},{2,14},{3,15},{4,0},{5,1},{6,2},{7,3},{8,4},{9,5},{1... | collective-permute-start | bytes 1572872 | tf_op jit(solution)/shard_map/ppermute | solution.py:46
  55.1 2.1 %collective-permute-done.13.refs_4_ = f32[256,256]{1,0:T(8,128)S(1)} collective-permute-done((f32[256,256]{1,0:T(8,128)S(1)}, f32[256,256]{1,0:T(8,128)S(1)}, u32[]{:S(2)}, u32[]{:S(2)}) %collective-permute-start.13) | collective-permute-done | bytes 262176 | tf_op jit(solution)/shard_map/ppermute | solution.py:90
  58.6 4.1 %collective-permute-done.12.refs_1_ = f32[512,256]{1,0:T(8,128)S(1)} collective-permute-done((f32[512,256]{1,0:T(8,128)S(1)}, f32[512,256]{1,0:T(8,128)S(1)}, u32[]{:S(2)}, u32[]{:S(2)}) %collective-permute-start.12) | collective-permute-done | bytes 524320 | tf_op jit(solution)/shard_map/ppermute | solution.py:46
  62.7 4.5 %collective-permute-done.11.refs_3_ = f32[512,256]{1,0:T(8,128)S(1)} collective-permute-done((f32[512,256]{1,0:T(8,128)S(1)}, f32[512,256]{1,0:T(8,128)S(1)}, u32[]{:S(2)}, u32[]{:S(2)}) %collective-permute-start.11) | collective-permute-done | bytes 524320 | tf_op jit(solution)/shard_map/ppermute | solution.py:46
  68.3 1.7 %select_select_fusion.4 = f32[256,256]{1,0:T(8,128)} fusion(f32[256,256]{1,0:T(8,128)} %get-tuple-element.62, f32[256,256]{1,0:T(8,128)} %collective-permute-done.14, f32[512,256]{1,0:T(8,128)S(1)} %collective-permute-done.11.refs_3_, f32[512,256]{1,0:T(8,128)S(1)} %collective-permute-done.9.refs_1_, pred[]{:T(512)S(6)} %eq.86, pred[]{:T(512)S(6)} %eq.85, ...), kind=kLoop, calls=%fused_computation.6 | loop fusion | flops 196608 | bytes 1310723 | tf_op jit(solution)/shard_map/jit(_where)/select_n | solution.py:99
  70.0 3.0 %collective-permute-start.19 = (f32[256,256]{1,0:T(8,128)S(1)}, f32[256,256]{1,0:T(8,128)S(1)}, u32[]{:S(2)}, u32[]{:S(2)}) collective-permute-start(f32[256,256]{1,0:T(8,128)S(1)} %collective-permute-done.13.refs_4_), channel_id=1, source_target_pairs={{0,16},{16,0},{32,48},{48,32},{64,80},{80,64},{96,112},{112,96},{1... | collective-permute-start | bytes 786440 | tf_op jit(solution)/shard_map/ppermute | solution.py:72
  73.0 3.6 %collective-permute-start.17 = (f32[256,256]{1,0:T(8,128)S(1)}, f32[256,256]{1,0:T(8,128)S(1)}, u32[]{:S(2)}, u32[]{:S(2)}) collective-permute-start(f32[256,256]{1,0:T(8,128)S(1)} %collective-permute-done.13.refs_4_), channel_id=1, source_target_pairs={{0,32},{16,48},{32,64},{48,80},{64,96},{80,112},{96,0},{112,16},{1... | collective-permute-start | bytes 786440 | tf_op jit(solution)/shard_map/ppermute | solution.py:68
  76.5 2.7 %collective-permute-start.16 = (f32[512,256]{1,0:T(8,128)}, f32[512,256]{1,0:T(8,128)}, u32[]{:S(2)}, u32[]{:S(2)}) collective-permute-start(f32[512,256]{1,0:T(8,128)} %collective-permute-done.10.refs_3_), channel_id=1, source_target_pairs={{0,12},{1,13},{2,14},{3,15},{4,0},{5,1},{6,2},{7,3},{8,4},{9,5},{1... | collective-permute-start | bytes 1572872 | tf_op jit(solution)/shard_map/ppermute | solution.py:46
  81.3 2.0 %collective-permute-done.18.refs_7_ = f32[256,256]{1,0:T(8,128)S(1)} collective-permute-done((f32[256,256]{1,0:T(8,128)S(1)}, f32[256,256]{1,0:T(8,128)S(1)}, u32[]{:S(2)}, u32[]{:S(2)}) %collective-permute-start.18) | collective-permute-done | bytes 262176 | tf_op jit(solution)/shard_map/ppermute | solution.py:68
  86.0 7.5 %collective-permute-done.21 = f32[256,256]{1,0:T(8,128)} collective-permute-done((f32[256,256]{1,0:T(8,128)}, f32[256,256]{1,0:T(8,128)}, u32[]{:S(2)}, u32[]{:S(2)}) %collective-permute-start.21) | collective-permute-done | bytes 262176 | tf_op jit(solution)/shard_map/ppermute | solution.py:157
  93.6 4.7 %collective-permute-start.23 = (f32[256,256]{1,0:T(8,128)S(1)}, f32[256,256]{1,0:T(8,128)S(1)}, u32[]{:S(2)}, u32[]{:S(2)}) collective-permute-start(f32[256,256]{1,0:T(8,128)S(1)} %broadcast_select_fusion), channel_id=1, source_target_pairs={{0,32},{16,112},{32,64},{48,16},{64,96},{80,48},{96,0},{112,80},{1... | collective-permute-start | bytes 786440 | tf_op jit(solution)/shard_map/ppermute | solution.py:95
  101.5 2.7 %solve_first.1 = (bf16[8,256,256]{2,1,0:T(8,128)(2,1)S(1)}, bf16[8,256,256]{2,1,0:T(8,128)(2,1)S(1)}) custom-call(f32[512,256]{1,0:T(8,128)S(1)} %get-tuple-element.60.refs_0_, f32[512,256]{1,0:T(8,128)S(1)} %collective-permute-done.9.refs_1_, f32[512,256]{1,0:T(8,128)} %collective-permute-done.15.refs_2_, f32[512,256]{1,0:T(8,128)S(1)} %collective-permute-done.11.refs_3_, ...), custom_call_target="tpu_custom_call" | custom-call | flops 805306368 | bytes 4194304 | tf_op jit(solution)/shard_map/solve_first/pallas_call | solution.py:230
  105.9 17.8 %solve_and_update.1 = (f32[8,2048,128]{2,1,0:T(8,128)}, f32[8,256,256]{2,1,0:T(8,128)}) custom-call(f32[512,256]{1,0:T(8,128)S(1)} %get-tuple-element.59.refs_0_, f32[512,256]{1,0:T(8,128)S(1)} %copy-done.2, f32[512,256]{1,0:T(8,128)} %collective-permute-done.16.refs_2_, f32[512,256]{1,0:T(8,128)} %collective-permute-done.10.refs_3_, ...), custom_call_target="tpu_custom_call" | custom-call | flops 6710886400 | bytes 20971520 | tf_op jit(solution)/shard_map/solve_and_update/pallas_call | solution.py:354
  (64 shorter events, 22.7 us)
Async XLA Ops:
  3.6 4.5 %collective-permute-start.2 = (f32[512,256]{1,0:T(8,128)}, f32[512,256]{1,0:T(8,128)S(1)}, u32[]{:S(2)}, u32[]{:S(2)}) collective-permute-start(f32[512,256]{1,0:T(8,128)} %get-tuple-element.102), channel_id=1, source_target_pairs={{0,8},{1,9},{16,18},{17,19},{32,40},{33,41},{48,50},{49,51},{64,72... | collective-permute-start | bytes 1572872 | tf_op jit(solution)/shard_map/ppermute | solution.py:63
  4.3 10.3 %collective-permute-start.1 = (f32[512,256]{1,0:T(8,128)}, f32[512,256]{1,0:T(8,128)S(1)}, u32[]{:S(2)}, u32[]{:S(2)}) collective-permute-start(f32[512,256]{1,0:T(8,128)} %get-tuple-element.103), channel_id=1, source_target_pairs={{0,12},{1,13},{2,14},{3,15},{4,0},{5,1},{6,2},{7,3},{8,4},{9,5},{1... | collective-permute-start | bytes 1572872 | tf_op jit(solution)/shard_map/ppermute | solution.py:46
  8.1 9.6 %collective-permute-start = (f32[512,256]{1,0:T(8,128)}, f32[512,256]{1,0:T(8,128)}, u32[]{:S(2)}, u32[]{:S(2)}) collective-permute-start(f32[512,256]{1,0:T(8,128)} %get-tuple-element.104), channel_id=1, source_target_pairs={{0,4},{1,5},{2,6},{3,7},{4,8},{5,9},{6,10},{7,11},{8,12},{9,13},{1... | collective-permute-start | bytes 1572872 | tf_op jit(solution)/shard_map/ppermute | solution.py:46
  19.2 11.8 %collective-permute-start.7 = (f32[512,256]{1,0:T(8,128)S(1)}, f32[512,256]{1,0:T(8,128)S(1)}, u32[]{:S(2)}, u32[]{:S(2)}) collective-permute-start(f32[512,256]{1,0:T(8,128)S(1)} %get-tuple-element.98), channel_id=1, source_target_pairs={{0,3},{1,0},{2,1},{3,2},{4,7},{5,4},{6,5},{7,6},{8,11},{9,8},{10,9... | collective-permute-start | bytes 1572872 | tf_op jit(solution)/shard_map/ppermute | solution.py:46
  24.9 8.3 %collective-permute-start.3 = (f32[512,256]{1,0:T(8,128)S(1)}, f32[512,256]{1,0:T(8,128)S(1)}, u32[]{:S(2)}, u32[]{:S(2)}) collective-permute-start(f32[512,256]{1,0:T(8,128)S(1)} %get-tuple-element.99), channel_id=1, source_target_pairs={{0,1},{1,2},{2,3},{3,0},{4,5},{5,6},{6,7},{7,4},{8,9},{9,10},{10,1... | collective-permute-start | bytes 1572872 | tf_op jit(solution)/shard_map/ppermute | solution.py:46
  24.9 14.0 %collective-permute-start.6 = (f32[512,256]{1,0:T(8,128)S(1)}, f32[512,256]{1,0:T(8,128)S(1)}, u32[]{:S(2)}, u32[]{:S(2)}) collective-permute-start(f32[512,256]{1,0:T(8,128)S(1)} %get-tuple-element.98), channel_id=1, source_target_pairs={{0,1},{1,2},{2,3},{3,0},{4,5},{5,6},{6,7},{7,4},{8,9},{9,10},{10,1... | collective-permute-start | bytes 1572872 | tf_op jit(solution)/shard_map/ppermute | solution.py:46
  24.9 14.0 %collective-permute-start.5 = (f32[512,256]{1,0:T(8,128)S(1)}, f32[512,256]{1,0:T(8,128)S(1)}, u32[]{:S(2)}, u32[]{:S(2)}) collective-permute-start(f32[512,256]{1,0:T(8,128)S(1)} %get-tuple-element.99), channel_id=1, source_target_pairs={{0,3},{1,0},{2,1},{3,2},{4,7},{5,4},{6,5},{7,6},{8,11},{9,8},{10,9... | collective-permute-start | bytes 1572872 | tf_op jit(solution)/shard_map/ppermute | solution.py:46
  31.0 11.2 %collective-permute-start.8 = (f32[512,256]{1,0:T(8,128)S(1)}, f32[512,256]{1,0:T(8,128)}, u32[]{:S(2)}, u32[]{:S(2)}) collective-permute-start(f32[512,256]{1,0:T(8,128)S(1)} %collective-permute-done.7), channel_id=1, source_target_pairs={{0,3},{1,0},{2,1},{3,2},{4,7},{5,4},{6,5},{7,6},{8,11},{9,8},{10,9... | collective-permute-start | bytes 1572872 | tf_op jit(solution)/shard_map/ppermute | solution.py:46
  33.2 11.3 %collective-permute-start.4 = (f32[512,256]{1,0:T(8,128)S(1)}, f32[512,256]{1,0:T(8,128)}, u32[]{:S(2)}, u32[]{:S(2)}) collective-permute-start(f32[512,256]{1,0:T(8,128)S(1)} %collective-permute-done.3), channel_id=1, source_target_pairs={{0,1},{1,2},{2,3},{3,0},{4,5},{5,6},{6,7},{7,4},{8,9},{9,10},{10,1... | collective-permute-start | bytes 1572872 | tf_op jit(solution)/shard_map/ppermute | solution.py:46
  47.0 10.2 %collective-permute-start.13 = (f32[256,256]{1,0:T(8,128)S(1)}, f32[256,256]{1,0:T(8,128)S(1)}, u32[]{:S(2)}, u32[]{:S(2)}) collective-permute-start(f32[256,256]{1,0:T(8,128)S(1)} %get-tuple-element.61), channel_id=1, source_target_pairs={{0,0},{1,8},{2,16},{3,24},{4,32},{5,40},{6,48},{7,56},{8,64},{9,72... | collective-permute-start | bytes 786440 | tf_op jit(solution)/shard_map/ppermute | solution.py:90
  50.9 11.8 %collective-permute-start.12 = (f32[512,256]{1,0:T(8,128)S(1)}, f32[512,256]{1,0:T(8,128)S(1)}, u32[]{:S(2)}, u32[]{:S(2)}) collective-permute-start(f32[512,256]{1,0:T(8,128)S(1)} %get-tuple-element.59.refs_0_), channel_id=1, source_target_pairs={{0,4},{1,5},{2,6},{3,7},{4,8},{5,9},{6,10},{7,11},{8,12},{9,13},{1... | collective-permute-start | bytes 1572872 | tf_op jit(solution)/shard_map/ppermute | solution.py:46
  52.0 10.7 %collective-permute-start.10 = (f32[512,256]{1,0:T(8,128)S(1)}, f32[512,256]{1,0:T(8,128)}, u32[]{:S(2)}, u32[]{:S(2)}) collective-permute-start(f32[512,256]{1,0:T(8,128)S(1)} %get-tuple-element.59.refs_0_), channel_id=1, source_target_pairs={{0,12},{1,13},{2,14},{3,15},{4,0},{5,1},{6,2},{7,3},{8,4},{9,5},{1... | collective-permute-start | bytes 1572872 | tf_op jit(solution)/shard_map/ppermute | solution.py:46
  53.6 13.6 %collective-permute-start.11 = (f32[512,256]{1,0:T(8,128)S(1)}, f32[512,256]{1,0:T(8,128)S(1)}, u32[]{:S(2)}, u32[]{:S(2)}) collective-permute-start(f32[512,256]{1,0:T(8,128)S(1)} %get-tuple-element.60.refs_0_), channel_id=1, source_target_pairs={{0,12},{1,13},{2,14},{3,15},{4,0},{5,1},{6,2},{7,3},{8,4},{9,5},{1... | collective-permute-start | bytes 1572872 | tf_op jit(solution)/shard_map/ppermute | solution.py:46
  54.7 13.6 %collective-permute-start.9 = (f32[512,256]{1,0:T(8,128)S(1)}, f32[512,256]{1,0:T(8,128)S(1)}, u32[]{:S(2)}, u32[]{:S(2)}) collective-permute-start(f32[512,256]{1,0:T(8,128)S(1)} %get-tuple-element.60.refs_0_), channel_id=1, source_target_pairs={{0,4},{1,5},{2,6},{3,7},{4,8},{5,9},{6,10},{7,11},{8,12},{9,13},{1... | collective-permute-start | bytes 1572872 | tf_op jit(solution)/shard_map/ppermute | solution.py:46
  70.0 9.2 %collective-permute-start.19 = (f32[256,256]{1,0:T(8,128)S(1)}, f32[256,256]{1,0:T(8,128)S(1)}, u32[]{:S(2)}, u32[]{:S(2)}) collective-permute-start(f32[256,256]{1,0:T(8,128)S(1)} %collective-permute-done.13.refs_4_), channel_id=1, source_target_pairs={{0,16},{16,0},{32,48},{48,32},{64,80},{80,64},{96,112},{112,96},{1... | collective-permute-start | bytes 786440 | tf_op jit(solution)/shard_map/ppermute | solution.py:72
  73.0 10.3 %collective-permute-start.18 = (f32[256,256]{1,0:T(8,128)S(1)}, f32[256,256]{1,0:T(8,128)S(1)}, u32[]{:S(2)}, u32[]{:S(2)}) collective-permute-start(f32[256,256]{1,0:T(8,128)S(1)} %collective-permute-done.13.refs_4_), channel_id=1, source_target_pairs={{0,96},{16,112},{32,0},{48,16},{64,32},{80,48},{96,64},{112,80},{1... | collective-permute-start | bytes 786440 | tf_op jit(solution)/shard_map/ppermute | solution.py:68
  73.0 11.6 %collective-permute-start.17 = (f32[256,256]{1,0:T(8,128)S(1)}, f32[256,256]{1,0:T(8,128)S(1)}, u32[]{:S(2)}, u32[]{:S(2)}) collective-permute-start(f32[256,256]{1,0:T(8,128)S(1)} %collective-permute-done.13.refs_4_), channel_id=1, source_target_pairs={{0,32},{16,48},{32,64},{48,80},{64,96},{80,112},{96,0},{112,16},{1... | collective-permute-start | bytes 786440 | tf_op jit(solution)/shard_map/ppermute | solution.py:68
  76.5 17.0 %collective-permute-start.15 = (f32[512,256]{1,0:T(8,128)S(1)}, f32[512,256]{1,0:T(8,128)}, u32[]{:S(2)}, u32[]{:S(2)}) collective-permute-start(f32[512,256]{1,0:T(8,128)S(1)} %collective-permute-done.9.refs_1_), channel_id=1, source_target_pairs={{0,4},{1,5},{2,6},{3,7},{4,8},{5,9},{6,10},{7,11},{8,12},{9,13},{1... | collective-permute-start | bytes 1572872 | tf_op jit(solution)/shard_map/ppermute | solution.py:46
  76.5 17.0 %collective-permute-start.16 = (f32[512,256]{1,0:T(8,128)}, f32[512,256]{1,0:T(8,128)}, u32[]{:S(2)}, u32[]{:S(2)}) collective-permute-start(f32[512,256]{1,0:T(8,128)} %collective-permute-done.10.refs_3_), channel_id=1, source_target_pairs={{0,12},{1,13},{2,14},{3,15},{4,0},{5,1},{6,2},{7,3},{8,4},{9,5},{1... | collective-permute-start | bytes 1572872 | tf_op jit(solution)/shard_map/ppermute | solution.py:46
  79.9 6.1 %collective-permute-start.22 = (f32[256,256]{1,0:T(8,128)}, f32[256,256]{1,0:T(8,128)}, u32[]{:S(2)}, u32[]{:S(2)}) collective-permute-start(f32[256,256]{1,0:T(8,128)} %select_select_fusion.4), channel_id=1, source_target_pairs={{16,112},{17,113},{18,114},{19,115},{20,116},{21,117},{22,118},{23... | collective-permute-start | bytes 786440 | tf_op jit(solution)/shard_map/ppermute | solution.py:157
  83.3 10.2 %collective-permute-start.21 = (f32[256,256]{1,0:T(8,128)}, f32[256,256]{1,0:T(8,128)}, u32[]{:S(2)}, u32[]{:S(2)}) collective-permute-start(f32[256,256]{1,0:T(8,128)} %select_select_fusion.4), channel_id=1, source_target_pairs={{16,80},{17,81},{18,82},{19,83},{20,84},{21,85},{22,86},{23,87},{2... | collective-permute-start | bytes 786440 | tf_op jit(solution)/shard_map/ppermute | solution.py:157
  84.6 8.9 %collective-permute-start.20 = (f32[256,256]{1,0:T(8,128)}, f32[256,256]{1,0:T(8,128)}, u32[]{:S(2)}, u32[]{:S(2)}) collective-permute-start(f32[256,256]{1,0:T(8,128)} %select_select_fusion.4), channel_id=1, source_target_pairs={{16,48},{17,49},{18,50},{19,51},{20,52},{21,53},{22,54},{23,55},{2... | collective-permute-start | bytes 786440 | tf_op jit(solution)/shard_map/ppermute | solution.py:157
  93.6 10.6 %collective-permute-start.23 = (f32[256,256]{1,0:T(8,128)S(1)}, f32[256,256]{1,0:T(8,128)S(1)}, u32[]{:S(2)}, u32[]{:S(2)}) collective-permute-start(f32[256,256]{1,0:T(8,128)S(1)} %broadcast_select_fusion), channel_id=1, source_target_pairs={{0,32},{16,112},{32,64},{48,16},{64,96},{80,48},{96,0},{112,80},{1... | collective-permute-start | bytes 786440 | tf_op jit(solution)/shard_map/ppermute | solution.py:95
  99.6 4.6 %collective-permute-start.26 = (f32[256,256]{1,0:T(8,128)S(1)}, f32[256,256]{1,0:T(8,128)S(1)}, u32[]{:S(2)}, u32[]{:S(2)}) collective-permute-start(f32[256,256]{1,0:T(8,128)S(1)} %add_select_fusion.refs_13_), channel_id=1, source_target_pairs={{16,0},{48,32},{80,64},{112,96},{17,1},{49,33},{81,65},{113,97},{1... | collective-permute-start | bytes 786440 | tf_op jit(solution)/shard_map/ppermute | solution.py:166
  (15 other events, 125.1 us)
